TPU v7x, 32 devices: a whole 2x2x4 slice. The times are simulated.
32 devices in a mesh: dp: 4 (over z), tensor: 8 (over y, x, core).
Axes of the slice: x: 2, y: 2, z: 4, core: 2. Of those that a mesh axis runs over, the one named last changes fastest.
Arguments:
- tokens: bfloat16 [4, 2048, 2048], P('dp', 'tensor'), may hold values from -6 to 6
- start_state: float32 [4, 16, 128, 256], P('dp', 'tensor'), may hold values from -3 to 3
- gain_attn: bfloat16 [2048], replicated, may hold values from 0.5 to 1.5
- w_query: bfloat16 [2048, 2048], P(None, 'tensor'), may hold values from -0.125 to 0.125
- w_key: bfloat16 [2048, 2048], P(None, 'tensor'), may hold values from -0.125 to 0.125
- w_value: bfloat16 [2048, 4096], P(None, 'tensor'), may hold values from -0.125 to 0.125
- w_alpha: bfloat16 [2048, 16], P(None, 'tensor'), may hold values from -0.25 to 0.25
- w_beta: bfloat16 [2048, 16], P(None, 'tensor'), may hold values from -0.125 to 0.125
- w_gate_out: bfloat16 [2048, 4096], P(None, 'tensor'), may hold values from -0.125 to 0.125
- conv_query: bfloat16 [4, 2048], P(None, 'tensor'), may hold values from -3 to 3
- conv_key: bfloat16 [4, 2048], P(None, 'tensor'), may hold values from -3 to 3
- conv_value: bfloat16 [4, 4096], P(None, 'tensor'), may hold values from -3 to 3
- decay_log: float32 [16], P('tensor'), may hold values from -9 to -3
- decay_bias: float32 [16], P('tensor'), may hold values from -2 to 1
- out_gain: bfloat16 [256], replicated, may hold values from 0.5 to 1.5
- w_out: bfloat16 [4096, 2048], P('tensor'), may hold values from -0.1875 to 0.1875
- gain_ffn: bfloat16 [2048], replicated, may hold values from 0.5 to 1.5
- w_ffn_gate: bfloat16 [2048, 5504], P(None, 'tensor'), may hold values from -0.125 to 0.125
- w_ffn_up: bfloat16 [2048, 5504], P(None, 'tensor'), may hold values from -0.125 to 0.125
- w_ffn_down: bfloat16 [5504, 2048], P('tensor'), may hold values from -0.15625 to 0.15625
- cotangent: bfloat16 [4, 2048, 2048], P('dp', 'tensor'), may hold values from -6 to 6
Outputs:
- output: bfloat16 [4, 2048, 2048], P('dp', 'tensor')
- final_state: float32 [4, 16, 128, 256], P('dp', 'tensor')
- grad_tokens: float32 [4, 2048, 2048], P('dp', 'tensor')
- grad_gain_attn: float32 [2048], replicated
- grad_query: float32 [2048, 2048], P(None, 'tensor')
- grad_key: float32 [2048, 2048], P(None, 'tensor')
- grad_value: float32 [2048, 4096], P(None, 'tensor')
- grad_alpha: float32 [2048, 16], P(None, 'tensor')
- grad_beta: float32 [2048, 16], P(None, 'tensor')
- grad_gate_out: float32 [2048, 4096], P(None, 'tensor')
- grad_conv_query: float32 [4, 2048], P(None, 'tensor')
- grad_conv_key: float32 [4, 2048], P(None, 'tensor')
- grad_conv_value: float32 [4, 4096], P(None, 'tensor')
- grad_decay_log: float32 [16], P('tensor')
- grad_decay_bias: float32 [16], P('tensor')
- grad_out_gain: float32 [256], replicated
- grad_out: float32 [4096, 2048], P('tensor')
- grad_gain_ffn: float32 [2048], replicated
- grad_ffn_gate: float32 [2048, 5504], P(None, 'tensor')
- grad_ffn_up: float32 [2048, 5504], P(None, 'tensor')
- grad_ffn_down: float32 [5504, 2048], P('tensor')
All inputs are finite; a program needn't handle non-finite values.
Results may differ from a plain program's by a relative error of at most 0.02.
Values may be sent and summed in bfloat16 or wider, within the bound.
A program may use at most 384 MiB of HBM per device.

v0:
```python
import jax
import jax.numpy as jnp
from jax import lax
from jax.sharding import PartitionSpec as P

GROUP = 64


norm_eps = 1e-05
unit_eps = 1e-06


def for_sending(x):
    return jax.tree.map(lambda a: a.astype(jnp.bfloat16) if a.dtype == jnp.float32 else a, x)


def exact_einsum(form, left, right):
    return jnp.einsum(form, left, right, precision=lax.Precision.HIGHEST)


def causal_conv(columns, taps):
    kernel_width = taps.shape[0]
    length = columns.shape[0]
    padded = jnp.pad(columns, ((kernel_width - 1, 0), (0, 0)))
    result = jnp.zeros_like(columns)
    for offset in range(kernel_width):
        result = result + taps[offset] * padded[offset : offset + length]
    return result


def unit_rows(matrix):
    return matrix * lax.rsqrt(jnp.sum(matrix * matrix, -1, keepdims=True) + unit_eps)


def delta_rule(queries, keys_in, values, beta_rows, log_decay, state_in):
    length, head_count, key_dim = queries.shape
    value_dim = values.shape[2]
    blocks = length // GROUP

    def split_blocks(array):
        return jnp.moveaxis(array.reshape((blocks, GROUP, head_count) + array.shape[2:]), 2, 0)

    query_blocks = split_blocks(queries)
    key_blocks = split_blocks(keys_in)
    value_blocks = split_blocks(values)
    beta_blocks = split_blocks(beta_rows)
    cumulative = jnp.cumsum(split_blocks(log_decay), axis=-1)
    positions = jnp.arange(GROUP)
    lower_incl = positions[:, None] >= positions[None, :]
    strict_lower = positions[:, None] > positions[None, :]
    spread_log = cumulative[..., :, None] - cumulative[..., None, :]
    within = jnp.where(lower_incl, jnp.exp(jnp.where(lower_incl, spread_log, 0.0)), 0.0)
    key_gram = exact_einsum("hnid,hnjd->hnij", key_blocks, key_blocks)
    coupling = jnp.where(strict_lower, beta_blocks[..., :, None] * key_gram * within, 0.0)
    system = coupling + jnp.eye(GROUP, dtype=jnp.float32)
    growth = jnp.exp(cumulative)
    stacked = jnp.concatenate(
        [beta_blocks[..., None] * value_blocks, (beta_blocks * growth)[..., None] * key_blocks],
        axis=-1,
    )
    solved = lax.linalg.triangular_solve(
        system, stacked, left_side=True, lower=True, unit_diagonal=True
    )
    fresh = solved[..., :value_dim]
    carried = solved[..., value_dim:]
    attend = jnp.where(
        lower_incl, exact_einsum("hnid,hnjd->hnij", query_blocks, key_blocks) * within, 0.0
    )
    tail_keys = jnp.exp(cumulative[..., -1:] - cumulative)[..., None] * key_blocks
    block_decay = jnp.exp(cumulative[..., -1])

    def advance(state, item):
        fresh_b, carried_b, query_b, attend_b, tail_b, growth_b, decay_b = item
        update = fresh_b - exact_einsum("hid,hde->hie", carried_b, state)
        result = growth_b[..., None] * exact_einsum("hid,hde->hie", query_b, state) + exact_einsum(
            "hij,hje->hie", attend_b, update
        )
        state_next = decay_b[:, None, None] * state + exact_einsum("hid,hie->hde", tail_b, update)
        return (state_next, result)

    items = tuple(
        (
            jnp.moveaxis(array, 1, 0)
            for array in (fresh, carried, query_blocks, attend, tail_keys, growth, block_decay)
        )
    )
    final, outputs = lax.scan(jax.checkpoint(advance), state_in, items)
    outputs = jnp.moveaxis(outputs, 1, 2).reshape(length, head_count, value_dim)
    return (outputs, final)


def mixer_block(
    proj_query,
    proj_key,
    proj_value,
    proj_alpha,
    proj_beta,
    proj_gate,
    taps_query,
    taps_key,
    taps_value,
    decay_log,
    decay_bias,
    out_gain,
    state_in,
):
    length = proj_query.shape[0]
    head_count = proj_alpha.shape[1]
    key_dim = proj_query.shape[1] // head_count
    value_dim = proj_value.shape[1] // head_count
    queries = unit_rows(
        jax.nn.silu(causal_conv(proj_query, taps_query)).reshape(length, head_count, key_dim)
    ) * key_dim ** (-0.5)
    keys_in = unit_rows(
        jax.nn.silu(causal_conv(proj_key, taps_key)).reshape(length, head_count, key_dim)
    )
    values = jax.nn.silu(causal_conv(proj_value, taps_value)).reshape(length, head_count, value_dim)
    beta_rows = jax.nn.sigmoid(proj_beta)
    log_decay = -jnp.exp(decay_log) * jax.nn.softplus(proj_alpha + decay_bias)
    outputs, final = delta_rule(queries, keys_in, values, beta_rows, log_decay, state_in)
    normed = (
        outputs * lax.rsqrt(jnp.mean(outputs * outputs, -1, keepdims=True) + norm_eps) * out_gain
    )
    gated = normed * jax.nn.silu(proj_gate.reshape(length, head_count, value_dim))
    return (gated.reshape(length, head_count * value_dim), final)


def rms_factor(matrix):
    return lax.rsqrt(jnp.mean(matrix * matrix, -1, keepdims=True) + norm_eps)


def cross_rows(left, right):
    return lax.dot_general(
        left, right, (((0,), (0,)), ((), ())), preferred_element_type=jnp.float32
    )


def times_transposed(left, right):
    return lax.dot_general(
        left, right, (((1,), (1,)), ((), ())), preferred_element_type=jnp.float32
    )


def norm_backward(grad_normed, scaled, factor, gain_value):
    weighted = grad_normed * gain_value
    return factor * (weighted - scaled * jnp.mean(weighted * scaled, -1, keepdims=True))


def shards(
    tokens,
    start_state,
    gain_attn,
    w_query,
    w_key,
    w_value,
    w_alpha,
    w_beta,
    w_gate_out,
    conv_query,
    conv_key,
    conv_value,
    decay_log,
    decay_bias,
    out_gain,
    w_out,
    gain_ffn,
    w_ffn_gate,
    w_ffn_up,
    w_ffn_down,
    cotangent,
):
    inputs = tokens[0].astype(jnp.float32)
    own_rows = inputs.shape[0]
    factor_attn = rms_factor(inputs)
    scaled_attn = inputs * factor_attn
    gain_first = gain_attn.astype(jnp.float32)
    gain_second = gain_ffn.astype(jnp.float32)
    normed = (scaled_attn * gain_first).astype(jnp.bfloat16)
    gathered = lax.all_gather(normed, "tensor", axis=0, tiled=True)
    in_weights = (w_query, w_key, w_value, w_alpha, w_beta, w_gate_out)
    projected = tuple(
        (jnp.dot(gathered, weight, preferred_element_type=jnp.float32) for weight in in_weights)
    )
    extras = (
        conv_query.astype(jnp.float32),
        conv_key.astype(jnp.float32),
        conv_value.astype(jnp.float32),
        decay_log,
        decay_bias,
        out_gain.astype(jnp.float32),
    )
    state_begin = start_state[0]

    def local_mixer(*pieces):
        return mixer_block(*pieces, state_begin)

    (mixed, final), mixer_back = jax.vjp(local_mixer, *projected, *extras)
    mixed_low = mixed.astype(jnp.bfloat16)
    grad_out_rows = cotangent[0]
    grad_gathered = lax.all_gather(grad_out_rows, "tensor", axis=0, tiled=True)
    attended = lax.psum_scatter(
        jnp.dot(mixed_low, w_out, preferred_element_type=jnp.float32),
        "tensor",
        scatter_dimension=0,
        tiled=True,
    )
    hidden = inputs + attended
    factor_ffn = rms_factor(hidden)
    scaled_ffn = hidden * factor_ffn
    normed_ffn = (scaled_ffn * gain_second).astype(jnp.bfloat16)
    gathered_ffn = lax.all_gather(normed_ffn, "tensor", axis=0, tiled=True)
    gate_proj = jnp.dot(gathered_ffn, w_ffn_gate, preferred_element_type=jnp.float32)
    up_proj = jnp.dot(gathered_ffn, w_ffn_up, preferred_element_type=jnp.float32)
    sigmoid_gate = jax.nn.sigmoid(gate_proj)
    activated = gate_proj * sigmoid_gate
    inner = (activated * up_proj).astype(jnp.bfloat16)
    ffn_out = lax.psum_scatter(
        jnp.dot(inner, w_ffn_down, preferred_element_type=jnp.float32).astype(jnp.bfloat16),
        "tensor",
        scatter_dimension=0,
        tiled=True,
    ).astype(jnp.float32)
    output = (hidden + ffn_out).astype(jnp.bfloat16)
    grad_inner = times_transposed(grad_gathered, w_ffn_down)
    grad_down = cross_rows(inner, grad_gathered)
    grad_gate_rows = (
        grad_inner * up_proj * sigmoid_gate * (1.0 + gate_proj * (1.0 - sigmoid_gate))
    ).astype(jnp.bfloat16)
    grad_up_rows = (grad_inner * activated).astype(jnp.bfloat16)
    grad_gate_weight = cross_rows(gathered_ffn, grad_gate_rows)
    grad_up_weight = cross_rows(gathered_ffn, grad_up_rows)
    grad_normed_ffn = lax.psum_scatter(
        times_transposed(grad_gate_rows, w_ffn_gate) + times_transposed(grad_up_rows, w_ffn_up),
        "tensor",
        scatter_dimension=0,
        tiled=True,
    )
    part_gain_ffn = jnp.sum(grad_normed_ffn * scaled_ffn, 0)
    grad_hidden = grad_out_rows.astype(jnp.float32) + norm_backward(
        grad_normed_ffn, scaled_ffn, factor_ffn, gain_second
    )
    grad_attended = grad_hidden.astype(jnp.bfloat16)
    grad_attended_all = lax.all_gather(grad_attended, "tensor", axis=0, tiled=True)
    grad_mixed = times_transposed(grad_attended_all, w_out)
    grad_out_weight = cross_rows(mixed_low, grad_attended_all)
    mixer_grads = mixer_back((grad_mixed, jnp.zeros_like(final)))
    grad_projected = tuple((piece.astype(jnp.bfloat16) for piece in mixer_grads[:6]))
    grad_in_weights = tuple((cross_rows(gathered, piece) for piece in grad_projected))
    totals = jnp.zeros((lax.axis_size("tensor") * own_rows, inputs.shape[1]), jnp.float32)
    for piece, weight in zip(grad_projected, in_weights):
        totals = totals + times_transposed(piece, weight)
    grad_normed = lax.psum_scatter(
        totals.astype(jnp.bfloat16), "tensor", scatter_dimension=0, tiled=True
    ).astype(jnp.float32)
    part_gain_attn = jnp.sum(grad_normed * scaled_attn, 0)
    grad_inputs = grad_hidden + norm_backward(grad_normed, scaled_attn, factor_attn, gain_first)
    gain_grads = lax.psum((part_gain_attn, part_gain_ffn, mixer_grads[11]), ("dp", "tensor"))
    mixer_local = grad_in_weights + (
        mixer_grads[6],
        mixer_grads[7],
        mixer_grads[8],
        mixer_grads[9],
        mixer_grads[10],
        grad_out_weight,
    )
    every_summed = jax.tree.map(
        lambda part: part.astype(jnp.float32),
        lax.psum(for_sending(mixer_local + (grad_gate_weight, grad_up_weight, grad_down)), "dp"),
    )
    mixer_summed = every_summed[:12]
    ffn_summed = every_summed[12:]
    return (
        output[None],
        final[None],
        grad_inputs[None],
        gain_grads[0],
        mixer_summed[0],
        mixer_summed[1],
        mixer_summed[2],
        mixer_summed[3],
        mixer_summed[4],
        mixer_summed[5],
        mixer_summed[6],
        mixer_summed[7],
        mixer_summed[8],
        mixer_summed[9],
        mixer_summed[10],
        gain_grads[2],
        mixer_summed[11],
        gain_grads[1],
        ffn_summed[0],
        ffn_summed[1],
        ffn_summed[2],
    )


def solution(mesh):
    return jax.shard_map(
        shards,
        mesh=mesh,
        in_specs=(
            P("dp", "tensor", None),
            P("dp", "tensor", None, None),
            P(),
            P(None, "tensor"),
            P(None, "tensor"),
            P(None, "tensor"),
            P(None, "tensor"),
            P(None, "tensor"),
            P(None, "tensor"),
            P(None, "tensor"),
            P(None, "tensor"),
            P(None, "tensor"),
            P("tensor"),
            P("tensor"),
            P(),
            P("tensor", None),
            P(),
            P(None, "tensor"),
            P(None, "tensor"),
            P("tensor", None),
            P("dp", "tensor", None),
        ),
        out_specs=(
            P("dp", "tensor", None),
            P("dp", "tensor", None, None),
            P("dp", "tensor", None),
            P(),
            P(None, "tensor"),
            P(None, "tensor"),
            P(None, "tensor"),
            P(None, "tensor"),
            P(None, "tensor"),
            P(None, "tensor"),
            P(None, "tensor"),
            P(None, "tensor"),
            P(None, "tensor"),
            P("tensor"),
            P("tensor"),
            P(),
            P("tensor", None),
            P(),
            P(None, "tensor"),
            P(None, "tensor"),
            P("tensor", None),
        ),
        check_vma=False,
    )
```

profile of v0, /device:TPU:0, one launch (start us, length us, event | category | flops | bytes accessed | tf_op | source)
XLA Modules:
  0.0 2882.9 jit_solution(83457524146409884)
XLA Ops:
  12.3 56.5 %all-gather.6.cloned.1.call-done = bf16[2048,2048]{1,0:T(8,128)(2,1)} async-done(((bf16[256,2048]{1,0:T(8,128)(2,1)}), bf16[2048,2048]{1,0:T(8,128)(2,1)}) %all-gather.6.cloned.1.call-update) | async-done | bytes 8388624 | tf_op jit(solution)/shard_map/all_gather | solution.py:179
  68.8 6.1 fusion.154
  84.9 5.6 multiply_reduce_fusion.21
  92.8 7.6 fusion.99
  100.4 5.6 copy.283
  106.0 6.3 broadcast_multiply_fusion.13
  112.9 5.7 fusion.68
  119.4 7.9 add_bitcast_fusion
  127.3 134.4 %custom-call.7 = f32[2,32,1,64,64]{1,3,4,2,0:T(8,128)} custom-call(f32[2,32,1,64,64]{1,4,3,2,0:T(8,128)} %add_bitcast_fusion), custom_call_target="InvertDiagBlocksLowerTriangular" | custom-call | tf_op jit(solution)/shard_map/jvp()/triangular_solve | solution.py:61
  271.3 6.8 fusion.155
  282.9 5.9 reshape.351
  292.3 6.7 fusion.33
  316.8 5.8 multiply_reduce_fusion.20
  324.9 7.7 fusion.90
  343.3 5.9 fusion.53
  363.6 238.9 %while.43 = (s32[]{:T(128)}, f32[2,128,256]{2,1,0:T(8,128)S(1)}, f32[32,2,64,256]{3,2,1,0:T(8,128)}, f32[32,2,128,256]{3,2,1,0:T(8,128)}, f32[32,2]{1,0:T(8,128)...) while((s32[]{:T(128)}, f32[2,128,256]{2,1,0:T(8,128)S(1)}, ...), condition=%wide.region_5.6_spmd, body=%wide.region_4.5_spmd.sunk | while | flops 176390144 | bytes 2757781 | solution.py:87
  622.3 6.7 multiply_convert_fusion.3
  630.4 8.1 fusion.157
  639.2 115.5 %reduce-scatter.5.cloned.1.call-done = f32[256,2048]{1,0:T(8,128)} async-done(((f32[2048,2048]{1,0:T(8,128)}), f32[256,2048]{1,0:T(8,128)}) %reduce-scatter.5.cloned.1.call-update) | async-done | bytes 2097168 | tf_op jit(solution)/shard_map/reduce_scatter | solution.py:201
  760.0 53.9 %all-gather.8.cloned.1.call-done = bf16[2048,2048]{1,0:T(8,128)(2,1)} async-done(((bf16[256,2048]{1,0:T(8,128)(2,1)}), bf16[2048,2048]{1,0:T(8,128)(2,1)}) %all-gather.8.cloned.1.call-update) | async-done | bytes 8388624 | tf_op jit(solution)/shard_map/all_gather | solution.py:211
  813.9 11.5 fusion.158
  825.4 7.8 fusion.159
  833.2 36.9 %all-gather.12.cloned.1.call-done = bf16[1,2048,2048]{2,1,0:T(8,128)(2,1)} async-done(((bf16[1,256,2048]{2,1,0:T(8,128)(2,1)}), bf16[1,2048,2048]{2,1,0:T(8,128)(2,1)}) %all-gather.12.cloned.1.call-update) | async-done | bytes 8388624 | tf_op jit(solution)/shard_map/all_gather | solution.py:200
  870.1 14.2 multiply_convert_fusion
  884.4 10.4 fusion.160
  894.8 13.7 convolution_add_fusion.5
  908.6 116.1 %reduce-scatter.9.cloned.1.call-done = f32[256,2048]{1,0:T(8,128)} async-done(((f32[2048,2048]{1,0:T(8,128)}), f32[256,2048]{1,0:T(8,128)}) %reduce-scatter.9.cloned.1.call-update) | async-done | bytes 2097168 | tf_op jit(solution)/shard_map/reduce_scatter | solution.py:232
  1031.2 5.5 copy.313
  1042.5 5.9 reshape.356
  1048.4 37.3 %all-gather.10.cloned.1.call-done = bf16[2048,2048]{1,0:T(8,128)(2,1)} async-done(((bf16[256,2048]{1,0:T(8,128)(2,1)}), bf16[2048,2048]{1,0:T(8,128)(2,1)}) %all-gather.10.cloned.1.call-update) | async-done | bytes 8388624 | tf_op jit(solution)/shard_map/all_gather | solution.py:243
  1085.7 16.4 fusion.47
  1102.0 5.9 reshape.355
  1107.9 6.8 multiply_reduce_fusion.1
  1128.4 731.4 %while.44 = (s32[]{:T(128)}, f32[2,128,256]{2,1,0:T(8,128)}, f32[32,2,64,256]{3,2,1,0:T(8,128)}, f32[32,2,64,128]{3,2,1,0:T(8,128)}, f32[32,2,64,128]{3,2,0,1:T(...) while((s32[]{:T(128)}, f32[2,128,256]{2,1,0:T(8,128)}, ...), condition=%wide.region_16.17_spmd.clone, body=%wide.region_13.16_spmd.clone.sunk | while | flops 453640064 | bytes 8326999 | solution.py:87
  1859.8 10.9 fusion.37
  1870.8 6.7 fusion.39
  1889.4 5.6 copy.332
  1899.0 11.7 fusion.52
  1910.6 5.4 copy.326
  1916.1 5.8 fusion.88
  1934.6 6.9 fusion.86
  1942.8 11.7 fusion.102
  1962.3 6.6 broadcast_multiply_fusion.4
  1968.8 11.5 fusion.103
  2032.8 5.6 broadcast_multiply_fusion
  2042.7 8.2 fusion.161
  2050.9 7.0 fusion.48
  2057.9 12.6 fusion.163
  2071.2 8.4 fusion.134
  2079.6 8.3 fusion.151
  2087.9 8.2 fusion.164
  2097.8 30.9 %add_convert_fusion = bf16[2048,2048]{1,0:T(8,128)(2,1)} fusion(f32[2048,2048]{1,0:T(8,128)} %fusion.164, f32[2048,2048]{1,0:T(8,128)} %fusion.151, f32[2048,2048]{1,0:T(8,128)} %fusion.134, f32[2048,2048]{1,0:T(8,128)} %fusion.163, f32[2048,2048]{1,0:T(8,128)} %fusion.161, bf16[2048,256]{1,0:T(8,128)(2,1)} %fusion.81, bf16[2048,256]{1,0:T(8,128)(2,1)} %param.29), kind=kOutput, calls=%fused_computation.57 | convolution fusion | flops 2172649472 | bytes 94371840 | tf_op jit(solution)/shard_map/dot_general | solution.py:139
  2128.8 11.0 convolution_convert_fusion
  2139.9 12.2 convolution_convert_fusion.1
  2152.1 11.5 convolution_convert_fusion.2
  2163.7 7.7 fusion.58
  2178.8 5.7 convolution_convert_fusion.3
  2184.5 5.7 convolution_convert_fusion.5
  2190.2 5.9 convolution_convert_fusion.4
  2206.2 19.2 all-reduce.32
  2231.9 38.3 %all-reduce.31 = (f32[2048]{0:T(1024)}, f32[256]{0:T(256)}, f32[2048]{0:T(1024)}) all-reduce(f32[2048]{0:T(1024)S(1)} %get-tuple-element.688, f32[256]{0:T(256)S(1)} %copy-done.148, f32[2048]{0:T(1024)S(1)} %copy-done.103), channel_id=1, replica_groups=mesh['dp'=4,'tensor'=8] {'dp','tensor'}, use_global_device_ids=true, to_apply=%region_30.31 | all-reduce | flops 4352 | bytes 34816 | tf_op jit(solution)/shard_map/psum | solution.py:257
  2270.3 6.4 reduce-scatter.7.cloned.1.call-done
  2276.6 6.2 fusion.72
  2282.8 570.9 %all-reduce.36.cloned.1.call-done = (bf16[2048,256]{1,0:T(8,128)(2,1)}, bf16[2048,256]{1,0:T(8,128)(2,1)}, bf16[2048,512]{1,0:T(8,128)(2,1)}, bf16[2048,512]{1,0...) async-done(((bf16[2048,256]{1,0:T(8,128)(2,1)}, bf16[2048,256]{1,0:T(8,128)(2,1)}, ...) | async-done | bytes 16842768 | tf_op jit(solution)/shard_map/psum | solution.py:268
  (1509 shorter events, 1244.7 us)
Async XLA Ops:
  7.2 862.9 %copy-start = (bf16[688,2048]{1,0:T(8,128)(2,1)S(1)}, bf16[688,2048]{1,0:T(8,128)(2,1)}, u32[]{:S(2)}) copy-start(bf16[688,2048]{1,0:T(8,128)(2,1)} %param.44) | copy-start | bytes 8454148
  7.2 61.6 %all-gather.6.cloned.1.call-start = ((), (), s32[]{:S(2)}) async-start(), calls=%async_computation.4 | async-start | bytes 9437184 | tf_op jit(solution)/shard_map/all_gather | solution.py:179
  11.6 743.1 %reduce-scatter.5.cloned.1.call-start = ((), (), s32[]{:S(2)}) async-start(), calls=%async_computation.5 | async-start | bytes 18874368 | tf_op jit(solution)/shard_map/reduce_scatter | solution.py:201
  11.7 107.6 %copy-start.94 = (pred[64,64]{1,0:T(8,128)(4,1)}, pred[64,64]{1,0:T(8,128)(4,1)S(1)}, u32[]{:S(2)}) copy-start(pred[64,64]{1,0:T(8,128)(4,1)S(1)} %get-tuple-element.839) | copy-start | bytes 12292
  11.7 331.6 %copy-start.80 = (pred[64,64]{1,0:T(8,128)(4,1)}, pred[64,64]{1,0:T(8,128)(4,1)S(1)}, u32[]{:S(2)}) copy-start(pred[64,64]{1,0:T(8,128)(4,1)S(1)} %get-tuple-element.838) | copy-start | bytes 12292
  11.8 94.2 %copy-start.141 = (f32[2]{0:T(128)}, f32[2]{0:T(128)S(1)}, u32[]{:S(2)}) copy-start(f32[2]{0:T(128)S(1)} %exponential_negate_fusion) | copy-start | bytes 28
  11.8 63.1 %copy-start.129 = (f32[1,256]{1,0:T(1,128)}, f32[1,256]{1,0:T(1,128)S(1)}, u32[]{:S(2)}) copy-start(f32[1,256]{1,0:T(1,128)S(1)} %get-tuple-element.826) | copy-start | bytes 3076
  11.8 63.1 %copy-start.131 = (f32[1,256]{1,0:T(1,128)}, f32[1,256]{1,0:T(1,128)S(1)}, u32[]{:S(2)}) copy-start(f32[1,256]{1,0:T(1,128)S(1)} %get-tuple-element.827) | copy-start | bytes 3076
  11.8 63.1 %copy-start.133 = (f32[1,256]{1,0:T(1,128)}, f32[1,256]{1,0:T(1,128)S(1)}, u32[]{:S(2)}) copy-start(f32[1,256]{1,0:T(1,128)S(1)} %get-tuple-element.828) | copy-start | bytes 3076
  11.9 63.1 %copy-start.135 = (f32[1,256]{1,0:T(1,128)}, f32[1,256]{1,0:T(1,128)S(1)}, u32[]{:S(2)}) copy-start(f32[1,256]{1,0:T(1,128)S(1)} %get-tuple-element.829) | copy-start | bytes 3076
  11.9 295.0 %copy-start.121 = (f32[1,256]{1,0:T(1,128)}, f32[1,256]{1,0:T(1,128)S(1)}, u32[]{:S(2)}) copy-start(f32[1,256]{1,0:T(1,128)S(1)} %get-tuple-element.822) | copy-start | bytes 3076
  11.9 295.0 %copy-start.123 = (f32[1,256]{1,0:T(1,128)}, f32[1,256]{1,0:T(1,128)S(1)}, u32[]{:S(2)}) copy-start(f32[1,256]{1,0:T(1,128)S(1)} %get-tuple-element.823) | copy-start | bytes 3076
  11.9 295.0 %copy-start.125 = (f32[1,256]{1,0:T(1,128)}, f32[1,256]{1,0:T(1,128)S(1)}, u32[]{:S(2)}) copy-start(f32[1,256]{1,0:T(1,128)S(1)} %get-tuple-element.824) | copy-start | bytes 3076
  11.9 295.0 %copy-start.127 = (f32[1,256]{1,0:T(1,128)}, f32[1,256]{1,0:T(1,128)S(1)}, u32[]{:S(2)}) copy-start(f32[1,256]{1,0:T(1,128)S(1)} %get-tuple-element.825) | copy-start | bytes 3076
  12.2 266.0 %copy-start.108 = (f32[1,512]{1,0:T(1,128)}, f32[1,512]{1,0:T(1,128)S(1)}, u32[]{:S(2)}) copy-start(f32[1,512]{1,0:T(1,128)S(1)} %get-tuple-element.818) | copy-start | bytes 6148
  12.2 266.0 %copy-start.110 = (f32[1,512]{1,0:T(1,128)}, f32[1,512]{1,0:T(1,128)S(1)}, u32[]{:S(2)}) copy-start(f32[1,512]{1,0:T(1,128)S(1)} %get-tuple-element.819) | copy-start | bytes 6148
  12.2 266.0 %copy-start.112 = (f32[1,512]{1,0:T(1,128)}, f32[1,512]{1,0:T(1,128)S(1)}, u32[]{:S(2)}) copy-start(f32[1,512]{1,0:T(1,128)S(1)} %get-tuple-element.820) | copy-start | bytes 6148
  12.2 266.0 %copy-start.114 = (f32[1,512]{1,0:T(1,128)}, f32[1,512]{1,0:T(1,128)S(1)}, u32[]{:S(2)}) copy-start(f32[1,512]{1,0:T(1,128)S(1)} %get-tuple-element.821) | copy-start | bytes 6148
  12.3 107.0 %copy-start.96 = (pred[64,64]{1,0:T(8,128)(4,1)}, pred[64,64]{1,0:T(8,128)(4,1)S(1)}, u32[]{:S(2)}) copy-start(pred[64,64]{1,0:T(8,128)(4,1)S(1)} %get-tuple-element.840) | copy-start | bytes 12292
  92.8 260.7 %copy-start.56 = (f32[32,64,2]{1,0,2:T(8,128)}, f32[32,64,2]{1,0,2:T(8,128)S(1)}, u32[]{:S(2)}) copy-start(f32[32,64,2]{1,0,2:T(8,128)S(1)} %rsqrt.61) | copy-start | bytes 49156
  112.8 240.5 %copy-start.62 = (f32[2,32,64]{2,1,0:T(8,128)}, f32[2,32,64]{2,1,0:T(8,128)S(1)}, u32[]{:S(2)}) copy-start(f32[2,32,64]{2,1,0:T(8,128)S(1)} %reduce_window_sum.22) | copy-start | bytes 49156
  118.7 170.0 %copy-start.66 = (f32[32,64,2]{1,0,2:T(8,128)}, f32[32,64,2]{1,0,2:T(8,128)S(1)}, u32[]{:S(2)}) copy-start(f32[32,64,2]{1,0,2:T(8,128)S(1)} %reshape.350) | copy-start | bytes 49156
  119.2 147.7 %copy-start.78 = (f32[2,32,64]{2,1,0:T(8,128)}, f32[2,32,64]{2,1,0:T(8,128)S(1)}, u32[]{:S(2)}) copy-start(f32[2,32,64]{2,1,0:T(8,128)S(1)} %exponential_multiply_fusion) | copy-start | bytes 49156
  288.8 15.6 slice-start
  292.2 12.1 slice-start.1
  316.8 36.5 %copy-start.99 = (f32[2,32]{1,0:T(2,128)}, f32[2,32]{1,0:T(2,128)S(1)}, u32[]{:S(2)}) copy-start(f32[2,32]{1,0:T(2,128)S(1)} %slice_reduce_fusion) | copy-start | bytes 772
  618.5 10.5 copy-start.53
  638.5 175.4 %all-gather.8.cloned.1.call-start = ((), (), s32[]{:S(2)}) async-start(), calls=%async_computation.6 | async-start | bytes 9437184 | tf_op jit(solution)/shard_map/all_gather | solution.py:211
  639.2 389.0 %copy-start.82 = (f32[2048]{0:T(1024)}, f32[2048]{0:T(1024)S(1)}, u32[]{:S(2)}) copy-start(f32[2048]{0:T(1024)S(1)} %convert_element_type.187) | copy-start | bytes 24580
  756.9 271.3 %copy-start.106 = (f32[256]{0:T(256)}, f32[256]{0:T(256)S(1)}, u32[]{:S(2)}) copy-start(f32[256]{0:T(256)S(1)} %add_rsqrt_fusion.2) | copy-start | bytes 3076
  759.4 110.7 %all-gather.12.cloned.1.call-start = ((), (), s32[]{:S(2)}) async-start(), calls=%async_computation.11 | async-start | bytes 9437184 | tf_op jit(solution)/shard_map/all_gather | solution.py:200
  760.0 264.7 %reduce-scatter.9.cloned.1.call-start = ((), (), s32[]{:S(2)}) async-start(), calls=%async_computation.8 | async-start | bytes 18874368 | tf_op jit(solution)/shard_map/reduce_scatter | solution.py:232
  813.9 11.5 copy-start.159
  813.9 11.5 copy-start.161
  870.1 14.2 copy-start.160
  884.3 10.5 copy-start.175
  884.3 10.5 copy-start.174
  884.3 10.5 copy-start.162
  908.5 177.2 %all-gather.10.cloned.1.call-start = ((), (), s32[]{:S(2)}) async-start(), calls=%async_computation.9 | async-start | bytes 9437184 | tf_op jit(solution)/shard_map/all_gather | solution.py:243
  1031.1 1198.4 %reduce-scatter.11.cloned.1.call-start = ((), (), s32[]{:S(2)}) async-start(), calls=%async_computation.10 | async-start | bytes 9437184 | tf_op jit(solution)/shard_map/reduce_scatter | solution.py:252
  1859.8 10.9 copy-start.10
  1859.8 10.9 copy-start.19
  1859.8 11.0 copy-start.31
  1942.8 13.3 copy-start.85
  1968.8 13.1 copy-start.89
  1993.9 10.4 copy-start.42
  1993.9 10.4 copy-start.43
  2057.9 12.6 copy-start.93
  2057.9 12.6 copy-start.142
  2057.9 13.3 copy-start.105
  2128.7 147.9 %reduce-scatter.7.cloned.1.call-start = ((), (), s32[]{:S(2)}) async-start(), calls=%async_computation.7 | async-start | bytes 9437184 | tf_op jit(solution)/shard_map/reduce_scatter | solution.py:217
  2139.8 713.9 %all-reduce.36.cloned.1.call-start = ((), (), s32[]{:S(2)}) async-start(), calls=%async_computation.12 | async-start | bytes 33685504 | tf_op jit(solution)/shard_map/psum | solution.py:268
  2139.9 12.2 copy-start.176
  2139.9 23.7 slice-start.6
  2152.1 11.6 slice-start.7
  2152.1 11.6 copy-start.177
  2152.1 19.3 slice-start.4
  2201.6 27.9 copy-start.92
  2201.6 27.9 copy-start.118
  2206.2 25.7 copy-start.103
  2206.2 25.7 copy-start.148
  2206.2 70.4 %copy-start.83 = (f32[2048]{0:T(1024)S(1)}, f32[2048]{0:T(1024)}, u32[]{:S(2)}) copy-start(f32[2048]{0:T(1024)} %copy-done.82) | copy-start | bytes 24580
  2206.2 70.4 %copy-start.107 = (f32[256]{0:T(256)S(1)}, f32[256]{0:T(256)}, u32[]{:S(2)}) copy-start(f32[256]{0:T(256)} %copy-done.106) | copy-start | bytes 3076
  2206.2 70.4 %copy-start.138 = (f32[256]{0:T(256)S(1)}, f32[256]{0:T(256)}, u32[]{:S(2)}) copy-start(f32[256]{0:T(256)} %copy-done.137) | copy-start | bytes 3076
  (164 other events, 699.5 us)
Sparse Core Ops, SparseCore 0:
  11.7 57.0 all-gather.5
  638.6 115.9 reduce-scatter.4
  759.5 54.3 all-gather.7
  815.7 54.3 all-gather.11
  908.6 115.9 reduce-scatter.8
  1031.2 54.3 all-gather.9
  2128.9 71.2 reduce-scatter.10
  2204.0 72.5 reduce-scatter.6
  2281.9 571.8 all-reduce.35
where the time goes:
time: 2920 us; the launch traced here: 2880 us
  waiting for transfers between devices  994 us (34%)
  matrix products  850 us (29%)
  local copies, waits for them, and re-layouts  602 us (21%)
  other arithmetic  361 us (12%)
  blocking collectives  57.5 us (2%)
    psum x1, waiting for transfers between devices, shards(): lax.psum(for_sending(mixer_local + (grad_gate_weight, grad_up_weight, gra...  571 us
    dot_general x454, matrix products, exact_einsum(): return jnp.einsum(form, left, right, precision=lax.Precision.HIGHEST)  553 us
    squeeze x224, local copies, waits for them, and re-layouts, delta_rule(): final, outputs = lax.scan(jax.checkpoint(advance), state_in, items)  268 us
    another operation x5, other arithmetic, delta_rule(): lax.linalg.triangular_solve(system, stacked, left_side=True, lower=True,...  142 us
    dot_general x10, matrix products, times_transposed(): lax.dot_general(left, right, (((1,), (1,)), ((), ())), preferred_element_...  131 us
    reduce_scatter x1, waiting for transfers between devices, shards(): lax.psum_scatter(times_transposed(grad_gate_rows, w_ffn_gate) + times_tra...  116 us
    reduce_scatter x1, waiting for transfers between devices, shards(): lax.psum_scatter(jnp.dot(mixed_low, w_out, preferred_element_type=jnp.flo...  115 us
    dynamic_update_slice x96, local copies, waits for them, and re-layouts, delta_rule(): final, outputs = lax.scan(jax.checkpoint(advance), state_in, items)  106 us
  transfers between devices with their start and end apart: 9, of which 8 were waited for; matrix products, arithmetic and copies ran while one was open for 4% of the time, Pallas kernels for 0%

commit v1 on v0

v1 whole, which is shorter than its diff:
```python
import functools

import jax
import jax.numpy as jnp
from jax import lax
from jax.experimental import pallas as pl
from jax.experimental.pallas import tpu as pltpu
from jax.sharding import PartitionSpec as P

norm_eps = 1e-05
unit_eps = 1e-06
BLOCK = 256
TAPS = 4
EDGE = 8
HALF = 128
EXTRA = 128

f32 = jnp.float32
bf16 = jnp.bfloat16


def dot_nn(left, right):
    return lax.dot_general(
        left.astype(bf16), right.astype(bf16), (((1,), (0,)), ((), ())), preferred_element_type=f32
    )


def dot_nt(left, right):
    return lax.dot_general(
        left.astype(bf16), right.astype(bf16), (((1,), (1,)), ((), ())), preferred_element_type=f32
    )


def dot_tn(left, right):
    return lax.dot_general(
        left.astype(bf16), right.astype(bf16), (((0,), (0,)), ((), ())), preferred_element_type=f32
    )


def dot_exact(left, right):
    return lax.dot_general(
        left, right, (((1,), (0,)), ((), ())), precision=lax.Precision.HIGHEST, preferred_element_type=f32
    )


def sigmoid(x):
    return 1.0 / (1.0 + jnp.exp(-x))


def softplus(x):
    return jnp.maximum(x, 0.0) + jnp.log1p(jnp.exp(-jnp.abs(x)))


def iota(shape, axis):
    return lax.broadcasted_iota(jnp.int32, shape, axis)


def unit_lower_inverse(lower):
    size = lower.shape[0]
    half = min(size, HALF)

    def small(part):
        rows, cols = iota((half, half), 0), iota((half, half), 1)
        eye = jnp.where(rows == cols, 1.0, 0.0)
        differ = rows ^ cols
        inverse = eye - jnp.where(differ == 1, part, 0.0)
        step = 2
        while step < half:
            level = jnp.where((differ >= step) & (differ < 2 * step), part, 0.0)
            inverse = inverse - dot_nn(inverse, dot_nn(level, inverse))
            step *= 2
        return inverse

    blocks = [small(lower[i : i + half, i : i + half]) for i in range(0, size, half)]
    if len(blocks) == 1:
        return blocks[0]
    first, second = blocks
    corner = -dot_nn(second, dot_nn(lower[half:, :half], first))
    top = jnp.concatenate([first, jnp.zeros((half, half), f32)], axis=1)
    return jnp.concatenate([top, jnp.concatenate([corner, second], axis=1)], axis=0)


def refined_inverse(lower):
    size = lower.shape[0]
    rough = unit_lower_inverse(lower).astype(bf16)
    high = lower.astype(bf16)
    low = (lower - high.astype(f32)).astype(bf16)
    eye = jnp.where(iota((size, size), 0) == iota((size, size), 1), 1.0, 0.0)
    rough32 = rough.astype(f32)
    rest = eye - rough32 - dot_nn(high, rough) - dot_nn(low, rough)
    return rough32 + dot_nn(rough, rest)


def conv_from(ext_ref, taps, size):
    total = None
    for j in range(TAPS):
        term = taps[j : j + 1, :] * ext_ref[pl.ds(EDGE - TAPS + 1 + j, size), :]
        total = term if total is None else total + term
    return total


def split_columns(ref, heads, key_dim, value_dim):
    widths = (heads * key_dim, heads * key_dim, heads * value_dim, heads * value_dim, EXTRA)
    parts, at = [], 0
    for width in widths:
        parts.append(ref.at[:, at : at + width])
        at += width
    return parts


def decay_parts(ab, dl_row, db_row, dl_col, db_col, heads, size):
    ab_row = jnp.transpose(ab)[: 2 * heads, :]
    ab_col = ab[:, : 2 * heads]
    rows, cols = iota((size, size), 0), iota((size, size), 1)
    incl = rows >= cols
    tril = jnp.where(incl, 1.0, 0.0)
    triu = jnp.where(rows <= cols, 1.0, 0.0)
    alpha_col = ab_col[:, :heads] + db_row
    ld_col = -jnp.exp(dl_row) * softplus(alpha_col)
    ld_row = -jnp.exp(dl_col) * softplus(ab_row[:heads, :] + db_col)
    cum_col = dot_exact(tril, ld_col)
    cum_row = dot_exact(ld_row, triu)
    beta_col = sigmoid(ab_col[:, heads:])
    return incl, rows > cols, alpha_col, ld_col, cum_col, cum_row, beta_col


def forward_kernel(
    heads,
    key_dim,
    value_dim,
    blocks,
    proj_ref,
    tq_ref,
    tk_ref,
    tv_ref,
    dl_row_ref,
    db_row_ref,
    dl_col_ref,
    db_col_ref,
    gain_ref,
    start_ref,
    gated_ref,
    final_ref,
    states_ref,
    inverse_ref,
    update_ref,
    raw_ref,
    state,
    ext_q,
    ext_k,
    ext_v,
):
    step = pl.program_id(0)
    size = proj_ref.shape[0]
    pq_ref, pk_ref, pv_ref, pg_ref, ab_ref = split_columns(proj_ref, heads, key_dim, value_dim)

    @pl.when(step == 0)
    def _():
        state[...] = start_ref[...]
        for ext in (ext_q, ext_k, ext_v):
            ext[0:EDGE, :] = jnp.zeros((EDGE, ext.shape[1]), f32)

    convs = []
    for ext, src, taps in ((ext_q, pq_ref, tq_ref), (ext_k, pk_ref, tk_ref), (ext_v, pv_ref, tv_ref)):
        ext[EDGE : EDGE + size, :] = src[...]
        convs.append(conv_from(ext, taps[...], size))
        ext[0:EDGE, :] = ext[size : size + EDGE, :]
    conv_q, conv_k, conv_v = convs
    act_q = conv_q * sigmoid(conv_q)
    act_k = conv_k * sigmoid(conv_k)
    values = conv_v * sigmoid(conv_v)
    gate = pg_ref[...]
    gate = gate * sigmoid(gate)
    incl, strict, _, _, cum_col, cum_row, beta_col = decay_parts(
        ab_ref[...], dl_row_ref[...], db_row_ref[...], dl_col_ref[...], db_col_ref[...], heads, size
    )
    gain = gain_ref[...]
    for h in range(heads):
        keys = slice(h * key_dim, (h + 1) * key_dim)
        vals = slice(h * value_dim, (h + 1) * value_dim)
        q = act_q[:, keys]
        q = q * (lax.rsqrt(jnp.sum(q * q, -1, keepdims=True) + unit_eps) * key_dim**-0.5)
        k = act_k[:, keys]
        k = k * lax.rsqrt(jnp.sum(k * k, -1, keepdims=True) + unit_eps)
        v = values[:, vals]
        beta = beta_col[:, h : h + 1]
        cum = cum_col[:, h : h + 1]
        last = cum_row[h : h + 1, size - 1 : size]
        growth = jnp.exp(cum)
        tail = jnp.exp(last - cum)
        within = jnp.exp(jnp.where(incl, cum - cum_row[h : h + 1, :], -1e30))
        kb = k.astype(bf16)
        lower = jnp.where(strict, dot_nt(kb, kb) * within * beta, 0.0)
        inverse = refined_inverse(lower).astype(bf16)
        attend = dot_nt(q, kb) * within
        current = state[h]
        current_low = current.astype(bf16)
        rhs = beta * (v - growth * dot_nn(kb, current_low))
        update = dot_nn(inverse, rhs)
        update_low = update.astype(bf16)
        out = growth * dot_nn(q, current_low) + dot_nn(attend, update_low)
        state[h] = jnp.exp(last) * current + dot_tn(tail * k, update_low)
        states_ref[0, h] = current_low
        inverse_ref[0, h] = inverse
        update_ref[:, vals] = update_low
        raw_ref[:, vals] = out.astype(raw_ref.dtype)
        scale = lax.rsqrt(jnp.mean(out * out, -1, keepdims=True) + norm_eps)
        gated_ref[:, vals] = (out * scale * gain * gate[:, vals]).astype(bf16)

    @pl.when(step == blocks - 1)
    def _():
        final_ref[...] = state[...]


def full_spec(shape):
    return pl.BlockSpec(shape, lambda i: (0,) * len(shape))


def mixer_forward(proj, tq, tk, tv, decay_log, decay_bias, gain, start):
    heads, key_dim, value_dim = start.shape
    length, width = proj.shape
    size = min(BLOCK, length)
    blocks = length // size
    kw, vw = heads * key_dim, heads * value_dim

    def rows(width):
        return pl.BlockSpec((size, width), lambda i: (i, 0))

    per_block = lambda *dims: pl.BlockSpec((1,) + dims, lambda i: (i,) + (0,) * len(dims))
    return pl.pallas_call(
        functools.partial(forward_kernel, heads, key_dim, value_dim, blocks),
        grid=(blocks,),
        out_shape=(
            jax.ShapeDtypeStruct((length, vw), bf16),
            jax.ShapeDtypeStruct((heads, key_dim, value_dim), f32),
            jax.ShapeDtypeStruct((blocks, heads, key_dim, value_dim), bf16),
            jax.ShapeDtypeStruct((blocks, heads, size, size), bf16),
            jax.ShapeDtypeStruct((length, vw), bf16),
            jax.ShapeDtypeStruct((length, vw), f32),
        ),
        in_specs=[
            rows(width),
            full_spec(tq.shape),
            full_spec(tk.shape),
            full_spec(tv.shape),
            full_spec((1, heads)),
            full_spec((1, heads)),
            full_spec((heads, 1)),
            full_spec((heads, 1)),
            full_spec((1, value_dim)),
            full_spec(start.shape),
        ],
        out_specs=(
            rows(vw),
            full_spec(start.shape),
            per_block(heads, key_dim, value_dim),
            per_block(heads, size, size),
            rows(vw),
            rows(vw),
        ),
        scratch_shapes=[
            pltpu.VMEM((heads, key_dim, value_dim), f32),
            pltpu.VMEM((size + EDGE, kw), f32),
            pltpu.VMEM((size + EDGE, kw), f32),
            pltpu.VMEM((size + EDGE, vw), f32),
        ],
        compiler_params=pltpu.CompilerParams(
            dimension_semantics=("arbitrary",), vmem_limit_bytes=48 * 1024 * 1024
        ),
        name="mixer_forward",
    )(
        proj,
        tq,
        tk,
        tv,
        decay_log[None, :],
        decay_bias[None, :],
        decay_log[:, None],
        decay_bias[:, None],
        gain[None, :],
        start,
    )


def backward_kernel(
    heads,
    key_dim,
    value_dim,
    blocks,
    proj_ref,
    eq_ref,
    ek_ref,
    ev_ref,
    tq_ref,
    tk_ref,
    tv_ref,
    dl_row_ref,
    db_row_ref,
    dl_col_ref,
    db_col_ref,
    gain_ref,
    states_ref,
    inverse_ref,
    update_ref,
    raw_ref,
    grad_ref,
    dproj_ref,
    dtq_ref,
    dtk_ref,
    dtv_ref,
    ddl_ref,
    ddb_ref,
    dgain_ref,
    dstate,
    ext_q,
    ext_k,
    ext_v,
    back_q,
    back_k,
    back_v,
):
    step = pl.program_id(0)
    size = proj_ref.shape[0]
    pq_ref, pk_ref, pv_ref, pg_ref, ab_ref = split_columns(proj_ref, heads, key_dim, value_dim)
    dpq_ref, dpk_ref, dpv_ref, dpg_ref, dab_ref = split_columns(dproj_ref, heads, key_dim, value_dim)
    exts = (ext_q, ext_k, ext_v)
    backs = (back_q, back_k, back_v)

    @pl.when(step == 0)
    def _():
        dstate[...] = jnp.zeros_like(dstate)
        for back in backs:
            back[size : size + EDGE, :] = jnp.zeros((EDGE, back.shape[1]), f32)
        for out in (dtq_ref, dtk_ref, dtv_ref, ddl_ref, ddb_ref, dgain_ref):
            out[...] = jnp.zeros_like(out)

    is_first = step == blocks - 1
    convs = []
    for ext, src, edge, taps in (
        (ext_q, pq_ref, eq_ref, tq_ref),
        (ext_k, pk_ref, ek_ref, tk_ref),
        (ext_v, pv_ref, ev_ref, tv_ref),
    ):
        ext[EDGE : EDGE + size, :] = src[...]
        ext[0:EDGE, :] = jnp.where(is_first, 0.0, edge[...])
        convs.append(conv_from(ext, taps[...], size))
    sig = [sigmoid(c) for c in convs]
    acts = [c * s for c, s in zip(convs, sig)]
    slopes = [s * (1.0 + c * (1.0 - s)) for c, s in zip(convs, sig)]
    gate_in = pg_ref[...]
    gate_sig = sigmoid(gate_in)
    gate = gate_in * gate_sig
    gate_slope = gate_sig * (1.0 + gate_in * (1.0 - gate_sig))
    incl, strict, alpha_col, ld_col, cum_col, cum_row, beta_col = decay_parts(
        ab_ref[...], dl_row_ref[...], db_row_ref[...], dl_col_ref[...], db_col_ref[...], heads, size
    )
    gain = gain_ref[...]
    cum_cols, cum_rows, lasts, dbetas = [], [], [], []
    grad_gain = jnp.zeros((1, value_dim), f32)
    for h in range(heads):
        keys = slice(h * key_dim, (h + 1) * key_dim)
        vals = slice(h * value_dim, (h + 1) * value_dim)
        out = raw_ref[:, vals].astype(f32)
        grad = grad_ref[:, vals].astype(f32)
        scale = lax.rsqrt(jnp.mean(out * out, -1, keepdims=True) + norm_eps)
        unit = out * scale
        dpg_ref[:, vals] = (grad * unit * gain * gate_slope[:, vals]).astype(bf16)
        dn = grad * gate[:, vals]
        grad_gain = grad_gain + jnp.sum(dn * unit, 0, keepdims=True)
        e = dn * gain
        do = scale * (e - unit * jnp.mean(e * unit, -1, keepdims=True))
        do = do.astype(bf16)
        aq = acts[0][:, keys]
        rq = lax.rsqrt(jnp.sum(aq * aq, -1, keepdims=True) + unit_eps)
        uq = aq * rq
        q = uq * key_dim**-0.5
        ak = acts[1][:, keys]
        rk = lax.rsqrt(jnp.sum(ak * ak, -1, keepdims=True) + unit_eps)
        k = ak * rk
        v = acts[2][:, vals]
        beta = beta_col[:, h : h + 1]
        cum = cum_col[:, h : h + 1]
        last = cum_row[h : h + 1, size - 1 : size]
        growth = jnp.exp(cum)
        tail = jnp.exp(last - cum)
        dec = jnp.exp(last)
        within = jnp.exp(jnp.where(incl, cum - cum_row[h : h + 1, :], -1e30))
        within_strict = jnp.where(strict, within, 0.0)
        qb, kb = q.astype(bf16), k.astype(bf16)
        attend = dot_nt(qb, kb) * within
        gram = dot_nt(kb, kb) * within_strict
        state = states_ref[0, h]
        update = update_ref[:, vals]
        ds = dstate[h]
        dsb = ds.astype(bf16)
        du = dot_tn(attend, do) + dot_nn(tail * k, dsb)
        db = dot_tn(inverse_ref[0, h], du)
        dbb = db.astype(bf16)
        dstate[h] = dec * ds + dot_tn(growth * q, do) - dot_tn(beta * growth * k, dbb)
        dqg = dot_nt(do, state)
        dkb = -dot_nt(dbb, state)
        da = dot_nt(do, update)
        dl = -dot_nt(dbb, update)
        dkt = dot_nt(update, dsb)
        dgq = (da * within).astype(bf16)
        dl_gram = dl * gram
        dgk = (dl * within_strict * beta).astype(bf16)
        dq = dot_nn(dgq, kb) + growth * dqg
        bg = beta * growth
        dk = dot_tn(dgq, qb) + dot_nn(dgk, kb) + dot_tn(dgk, kb) + tail * dkt + bg * dkb
        dv = beta * db
        sum_bk = jnp.sum(dkb * k, -1, keepdims=True)
        row_gram = jnp.sum(dl_gram, -1, keepdims=True)
        dbetas.append(jnp.sum(db * v, -1, keepdims=True) + growth * sum_bk + row_gram)
        mix = da * attend + dl_gram * beta
        tail_sum = tail * jnp.sum(dkt * k, -1, keepdims=True)
        cum_cols.append(
            jnp.sum(mix, -1, keepdims=True) + growth * jnp.sum(dqg * q, -1, keepdims=True) + bg * sum_bk - tail_sum
        )
        cum_rows.append(jnp.sum(mix, 0, keepdims=True))
        lasts.append(
            jnp.sum(tail_sum, 0, keepdims=True)
            + dec * jnp.sum(jnp.sum(state.astype(f32) * ds, -1, keepdims=True), 0, keepdims=True)
        )
        dq = dq * (key_dim**-0.5)
        back_q[0:size, keys] = rq * (dq - uq * jnp.sum(dq * uq, -1, keepdims=True)) * slopes[0][:, keys]
        back_k[0:size, keys] = rk * (dk - k * jnp.sum(dk * k, -1, keepdims=True)) * slopes[1][:, keys]
        back_v[0:size, vals] = dv * slopes[2][:, vals]

    dgain_ref[...] += grad_gain
    rows, cols = iota((size, size), 0), iota((size, size), 1)
    late = jnp.where(rows <= cols, 1.0, 0.0)
    cum_all = jnp.concatenate(cum_cols, axis=1)
    row_all = jnp.concatenate(cum_rows + [jnp.zeros((EDGE - heads, size), f32)], axis=0)
    cum_all = cum_all - jnp.transpose(row_all)[:, :heads]
    dld = dot_exact(late, cum_all) + jnp.concatenate(lasts, axis=1)
    dalpha = dld * (-jnp.exp(dl_row_ref[...])) * sigmoid(alpha_col)
    ddb_ref[...] += jnp.sum(dalpha, 0, keepdims=True)
    ddl_ref[...] += jnp.sum(dld * ld_col, 0, keepdims=True)
    dbeta = jnp.concatenate(dbetas, axis=1) * beta_col * (1.0 - beta_col)
    dab_ref[...] = jnp.concatenate(
        [dalpha, dbeta, jnp.zeros((size, EXTRA - 2 * heads), f32)], axis=1
    ).astype(bf16)
    for ext, back, taps_ref, dp_ref, dt_ref in (
        (ext_q, back_q, tq_ref, dpq_ref, dtq_ref),
        (ext_k, back_k, tk_ref, dpk_ref, dtk_ref),
        (ext_v, back_v, tv_ref, dpv_ref, dtv_ref),
    ):
        taps = taps_ref[...]
        total = None
        here = back[0:size, :]
        sums = []
        for j in range(TAPS):
            term = taps[j : j + 1, :] * back[pl.ds(TAPS - 1 - j, size), :]
            total = term if total is None else total + term
            sums.append(jnp.sum(here * ext[pl.ds(EDGE - TAPS + 1 + j, size), :], 0, keepdims=True))
        dp_ref[...] = total.astype(bf16)
        dt_ref[...] += jnp.concatenate(sums, axis=0)
        back[size : size + EDGE, :] = back[0:EDGE, :]


def mixer_backward(
    proj, tq, tk, tv, decay_log, decay_bias, gain, states, inverse, update, raw, grad
):
    blocks, heads, key_dim, value_dim = states.shape
    length, width = proj.shape
    size = inverse.shape[-1]
    kw, vw = heads * key_dim, heads * value_dim
    per_edge = size // EDGE

    def at(i):
        return blocks - 1 - i

    def rows(width):
        return pl.BlockSpec((size, width), lambda i: (at(i), 0))

    def edge(width, column):
        return pl.BlockSpec((EDGE, width), lambda i: (jnp.maximum(at(i) * per_edge - 1, 0), column))

    per_block = lambda *dims: pl.BlockSpec((1,) + dims, lambda i: (at(i),) + (0,) * len(dims))
    return pl.pallas_call(
        functools.partial(backward_kernel, heads, key_dim, value_dim, blocks),
        grid=(blocks,),
        out_shape=(
            jax.ShapeDtypeStruct((length, width), bf16),
            jax.ShapeDtypeStruct(tq.shape, f32),
            jax.ShapeDtypeStruct(tk.shape, f32),
            jax.ShapeDtypeStruct(tv.shape, f32),
            jax.ShapeDtypeStruct((1, heads), f32),
            jax.ShapeDtypeStruct((1, heads), f32),
            jax.ShapeDtypeStruct((1, value_dim), f32),
        ),
        in_specs=[
            rows(width),
            edge(kw, 0),
            edge(kw, 1),
            edge(vw, 2 * kw // vw),
            full_spec(tq.shape),
            full_spec(tk.shape),
            full_spec(tv.shape),
            full_spec((1, heads)),
            full_spec((1, heads)),
            full_spec((heads, 1)),
            full_spec((heads, 1)),
            full_spec((1, value_dim)),
            per_block(heads, key_dim, value_dim),
            per_block(heads, size, size),
            rows(vw),
            rows(vw),
            rows(vw),
        ],
        out_specs=(
            rows(width),
            full_spec(tq.shape),
            full_spec(tk.shape),
            full_spec(tv.shape),
            full_spec((1, heads)),
            full_spec((1, heads)),
            full_spec((1, value_dim)),
        ),
        scratch_shapes=[
            pltpu.VMEM((heads, key_dim, value_dim), f32),
            pltpu.VMEM((size + EDGE, kw), f32),
            pltpu.VMEM((size + EDGE, kw), f32),
            pltpu.VMEM((size + EDGE, vw), f32),
            pltpu.VMEM((size + EDGE, kw), f32),
            pltpu.VMEM((size + EDGE, kw), f32),
            pltpu.VMEM((size + EDGE, vw), f32),
        ],
        compiler_params=pltpu.CompilerParams(
            dimension_semantics=("arbitrary",), vmem_limit_bytes=56 * 1024 * 1024
        ),
        name="mixer_backward",
    )(
        proj,
        proj,
        proj,
        proj,
        tq,
        tk,
        tv,
        decay_log[None, :],
        decay_bias[None, :],
        decay_log[:, None],
        decay_bias[:, None],
        gain[None, :],
        states,
        inverse,
        update,
        raw,
        grad,
    )


def rms_factor(matrix):
    return lax.rsqrt(jnp.mean(matrix * matrix, -1, keepdims=True) + norm_eps)


def cross_rows(left, right):
    return lax.dot_general(left, right, (((0,), (0,)), ((), ())), preferred_element_type=f32)


def times_transposed(left, right):
    return lax.dot_general(left, right, (((1,), (1,)), ((), ())), preferred_element_type=f32)


def norm_backward(grad_normed, scaled, factor, gain_value):
    weighted = grad_normed * gain_value
    return factor * (weighted - scaled * jnp.mean(weighted * scaled, -1, keepdims=True))


def scatter_rows(partial):
    return lax.psum_scatter(partial.astype(bf16), "tensor", scatter_dimension=0, tiled=True).astype(f32)


def gather_rows(rows):
    return lax.all_gather(rows, "tensor", axis=0, tiled=True)


def shards(
    tokens,
    start_state,
    gain_attn,
    w_query,
    w_key,
    w_value,
    w_alpha,
    w_beta,
    w_gate_out,
    conv_query,
    conv_key,
    conv_value,
    decay_log,
    decay_bias,
    out_gain,
    w_out,
    gain_ffn,
    w_ffn_gate,
    w_ffn_up,
    w_ffn_down,
    cotangent,
):
    inputs = tokens[0].astype(f32)
    heads = decay_log.shape[0]
    factor_attn = rms_factor(inputs)
    scaled_attn = inputs * factor_attn
    gain_first = gain_attn.astype(f32)
    gain_second = gain_ffn.astype(f32)
    normed = (scaled_attn * gain_first).astype(bf16)
    gathered = gather_rows(normed)
    padding = jnp.zeros((w_alpha.shape[0], EXTRA - 2 * heads), bf16)
    w_in = jnp.concatenate([w_query, w_key, w_value, w_gate_out, w_alpha, w_beta, padding], axis=1)
    projected = jnp.dot(gathered, w_in, preferred_element_type=f32)
    extras = (
        conv_query.astype(f32),
        conv_key.astype(f32),
        conv_value.astype(f32),
        decay_log,
        decay_bias,
        out_gain.astype(f32),
    )
    mixed, final, states, inverse, update, raw = mixer_forward(projected, *extras, start_state[0])
    grad_out_rows = cotangent[0]
    grad_gathered = gather_rows(grad_out_rows)
    attended = scatter_rows(jnp.dot(mixed, w_out, preferred_element_type=f32))
    hidden = inputs + attended
    factor_ffn = rms_factor(hidden)
    scaled_ffn = hidden * factor_ffn
    normed_ffn = (scaled_ffn * gain_second).astype(bf16)
    gathered_ffn = gather_rows(normed_ffn)
    gate_proj = jnp.dot(gathered_ffn, w_ffn_gate, preferred_element_type=f32)
    up_proj = jnp.dot(gathered_ffn, w_ffn_up, preferred_element_type=f32)
    sigmoid_gate = jax.nn.sigmoid(gate_proj)
    activated = gate_proj * sigmoid_gate
    inner = (activated * up_proj).astype(bf16)
    ffn_out = scatter_rows(jnp.dot(inner, w_ffn_down, preferred_element_type=f32))
    output = (hidden + ffn_out).astype(bf16)
    grad_inner = times_transposed(grad_gathered, w_ffn_down)
    grad_gate_rows = (
        grad_inner * up_proj * sigmoid_gate * (1.0 + gate_proj * (1.0 - sigmoid_gate))
    ).astype(bf16)
    grad_up_rows = (grad_inner * activated).astype(bf16)
    grad_normed_ffn = scatter_rows(
        times_transposed(grad_gate_rows, w_ffn_gate) + times_transposed(grad_up_rows, w_ffn_up)
    )
    part_gain_ffn = jnp.sum(grad_normed_ffn * scaled_ffn, 0)
    grad_hidden = grad_out_rows.astype(f32) + norm_backward(
        grad_normed_ffn, scaled_ffn, factor_ffn, gain_second
    )
    grad_attended = gather_rows(grad_hidden.astype(bf16))
    early = (
        cross_rows(gathered_ffn, grad_gate_rows).astype(bf16),
        cross_rows(gathered_ffn, grad_up_rows).astype(bf16),
        cross_rows(inner, grad_gathered).astype(bf16),
    )
    early = lax.psum(early, "dp")
    grad_mixed = times_transposed(grad_attended, w_out)
    middle = cross_rows(mixed, grad_attended).astype(bf16)
    grad_projected, grad_tq, grad_tk, grad_tv, grad_dl, grad_db, grad_gain = mixer_backward(
        projected, *extras, states, inverse, update, raw, grad_mixed
    )
    grad_in = cross_rows(gathered, grad_projected).astype(bf16)
    grad_in, early = lax.optimization_barrier((grad_in, early))
    grad_in, middle = lax.psum((grad_in, middle), "dp")
    grad_normed = scatter_rows(times_transposed(grad_projected, w_in))
    part_gain_attn = jnp.sum(grad_normed * scaled_attn, 0)
    grad_inputs = grad_hidden + norm_backward(grad_normed, scaled_attn, factor_attn, gain_first)
    gain_grads = lax.psum(
        jnp.concatenate([part_gain_attn, part_gain_ffn, grad_gain[0]]), ("dp", "tensor")
    )
    width = inputs.shape[1]
    small = lax.psum(
        jnp.concatenate([a.reshape(-1) for a in (grad_tq, grad_tk, grad_tv, grad_dl, grad_db)]), "dp"
    )
    smalls, at = [], 0
    for a in (grad_tq, grad_tk, grad_tv, grad_dl[0], grad_db[0]):
        smalls.append(small[at : at + a.size].reshape(a.shape))
        at += a.size
    pieces, at = [], 0
    for w in (w_query, w_key, w_value, w_gate_out, w_alpha, w_beta):
        pieces.append(grad_in[:, at : at + w.shape[1]].astype(f32))
        at += w.shape[1]
    return (
        output[None],
        final[None],
        grad_inputs[None],
        gain_grads[:width],
        pieces[0],
        pieces[1],
        pieces[2],
        pieces[4],
        pieces[5],
        pieces[3],
        smalls[0],
        smalls[1],
        smalls[2],
        smalls[3],
        smalls[4],
        gain_grads[2 * width :],
        middle.astype(f32),
        gain_grads[width : 2 * width],
        early[0].astype(f32),
        early[1].astype(f32),
        early[2].astype(f32),
    )


def solution(mesh):
    return jax.shard_map(
        shards,
        mesh=mesh,
        in_specs=(
            P("dp", "tensor", None),
            P("dp", "tensor", None, None),
            P(),
            P(None, "tensor"),
            P(None, "tensor"),
            P(None, "tensor"),
            P(None, "tensor"),
            P(None, "tensor"),
            P(None, "tensor"),
            P(None, "tensor"),
            P(None, "tensor"),
            P(None, "tensor"),
            P("tensor"),
            P("tensor"),
            P(),
            P("tensor", None),
            P(),
            P(None, "tensor"),
            P(None, "tensor"),
            P("tensor", None),
            P("dp", "tensor", None),
        ),
        out_specs=(
            P("dp", "tensor", None),
            P("dp", "tensor", None, None),
            P("dp", "tensor", None),
            P(),
            P(None, "tensor"),
            P(None, "tensor"),
            P(None, "tensor"),
            P(None, "tensor"),
            P(None, "tensor"),
            P(None, "tensor"),
            P(None, "tensor"),
            P(None, "tensor"),
            P(None, "tensor"),
            P("tensor"),
            P("tensor"),
            P(),
            P("tensor", None),
            P(),
            P(None, "tensor"),
            P(None, "tensor"),
            P("tensor", None),
        ),
        check_vma=False,
    )
```

time: 2920 us -> 1320 us (0.45); the launches traced: 2880 us -> 1310 us
  matrix products: 850 us -> 187 us
  local copies, waits for them, and re-layouts: 602 us -> 28.3 us
  other arithmetic: 361 us -> 54.4 us
  waiting for transfers between devices: 994 us -> 831 us
  Pallas kernels: 0 us -> 138 us
    dot_general x465 -> x5, matrix products: 637 us -> 57.7 us  [the longest x1 21.2 us: shards(): projected = jnp.dot(gathered, w_in, preferred_element_type=f32)]
    squeeze x224 -> x0, local copies, waits for them, and re-layouts: 268 us -> none  [delta_rule(): final, outputs = lax.scan(jax.checkpoint(advance), state_in, items)]
    another operation x42 -> x0, other arithmetic: 188 us -> none  [the longest x5 142 us: delta_rule(): lax.linalg.triangular_solve(system, stacked, left_side=True, lower=True,...]
    pallas_call x0 -> x2, Pallas kernels: none -> 138 us  [the longest x1 75.8 us: mixer_forward(): pl.pallas_call(functools.partial(forward_kernel, heads, key_dim, value_di...]
    psum x1 -> x2, waiting for transfers between devices: 571 us -> 446 us  [the longest x1 243 us: shards(): grad_in, middle = lax.psum((grad_in, middle), 'dp')]
    dynamic_update_slice x96 -> x0, local copies, waits for them, and re-layouts: 106 us -> none  [delta_rule(): final, outputs = lax.scan(jax.checkpoint(advance), state_in, items)]
    mul x72 -> x0, local copies, waits for them, and re-layouts: 70.7 us -> none  [the longest x32 22.1 us: advance(): decay_b[:, None, None] * state]
    reduce_sum x44 -> x0, other arithmetic: 65.8 us -> none  [the longest x2 23.2 us: unit_rows(): matrix * lax.rsqrt(jnp.sum(matrix * matrix, -1, keepdims=True) + unit_eps)]
  transfers between devices with their start and end apart: 9 -> 10, of which waited for: 8 -> 10; matrix products, arithmetic and copies ran while one was open for 4% -> 13% of each run, Pallas kernels for 0% -> 5%
where the time goes in v1:
time: 1320 us; the launch traced here: 1310 us
  waiting for transfers between devices  831 us (63%)
  matrix products  187 us (14%)
  Pallas kernels  138 us (10%)
  blocking collectives  58.8 us (4%)
  other arithmetic  54.4 us (4%)
  local copies, waits for them, and re-layouts  28.3 us (2%)
  between operations  15.1 us (1%)
    psum x1, waiting for transfers between devices, shards(): grad_in, middle = lax.psum((grad_in, middle), 'dp')  243 us
    reduce_scatter x4, waiting for transfers between devices, scatter_rows(): lax.psum_scatter(partial.astype(bf16), 'tensor', scatter_dimension=0, til...  225 us
    psum x1, waiting for transfers between devices, shards(): early = lax.psum(early, 'dp')  204 us
    all_gather x4, waiting for transfers between devices, gather_rows(): return lax.all_gather(rows, 'tensor', axis=0, tiled=True)  160 us
    pallas_call x1, Pallas kernels, mixer_forward(): pl.pallas_call(functools.partial(forward_kernel, heads, key_dim, value_di...  75.8 us
    dot_general x5, matrix products, times_transposed(): lax.dot_general(left, right, (((1,), (1,)), ((), ())), preferred_element_...  69 us
    pallas_call x1, Pallas kernels, mixer_backward(): pl.pallas_call(functools.partial(backward_kernel, heads, key_dim, value_d...  62.4 us
    dot_general x5, matrix products, cross_rows(): lax.dot_general(left, right, (((0,), (0,)), ((), ())), preferred_element_...  60.1 us
  transfers between devices with their start and end apart: 10, of which 10 were waited for; matrix products, arithmetic and copies ran while one was open for 13% of the time, Pallas kernels for 5%

profile of v1, /device:TPU:0, one launch (start us, length us, event | category | flops | bytes accessed | tf_op | source)
XLA Modules:
  0.0 1313.5 jit_solution(1266325801078162166)
XLA Ops:
  7.3 1.7 fusion.25
  9.0 0.7 convert_element_type.117
  9.7 0.6 copy-done.22
  10.3 2.5 fusion.22
  13.6 1.1 copy.43
  14.7 0.9 broadcast_in_dim.20
  15.5 11.3 concatenate.9
  26.8 43.3 %all-gather.6.cloned.1.call-done = bf16[2048,2048]{1,0:T(8,128)(2,1)} async-done(((bf16[256,2048]{1,0:T(8,128)(2,1)}), bf16[2048,2048]{1,0:T(8,128)(2,1)}) %all-gather.6.cloned.1.call-update) | async-done | bytes 8388624 | tf_op jit(solution)/shard_map/all_gather | solution.py:577
  70.1 21.2 %fusion.32.proj_ref.eq_ref.ek_ref.ev_ref = f32[2048,1664]{1,0:T(8,128)} fusion(bf16[2048,2048]{1,0:T(8,128)(2,1)} %all-gather.6.cloned.1.call-done, bf16[2048,1664]{1,0:T(8,128)(2,1)} %concatenate.9), kind=kOutput, calls=%fused_computation.62 | convolution fusion | flops 13958643712 | bytes 28835840 | tf_op jit(solution)/shard_map/dot_general | solution.py:613
  91.4 75.8 %mixer_forward.1 = (bf16[2048,512]{1,0:T(8,128)(2,1)S(1)}, f32[2,128,256]{2,1,0:T(8,128)}, bf16[8,2,128,256]{3,2,1,0:T(8,128)(2,1)S(1)}, bf16[8,2,256,256]{3,2,1...) custom-call(f32[2048,1664]{1,0:T(8,128)} %fusion.32.proj_ref.eq_ref.ek_ref.ev_ref, ...), custom_call_target="tpu_custom_call" | custom-call | tf_op jit(solution)/shard_map/mixer_forward/pallas_call | solution.py:230
  167.2 1.3 copy-done.1
  168.5 1.0 copy-done.2
  169.5 1.3 copy-done.12
  170.8 6.8 convolution_convert_fusion.1
  177.9 0.4 copy-done.35
  178.3 70.8 %reduce-scatter.5.cloned.1.call-done = bf16[256,2048]{1,0:T(8,128)(2,1)} async-done(((bf16[2048,2048]{1,0:T(8,128)(2,1)}), bf16[256,2048]{1,0:T(8,128)(2,1)}) %reduce-scatter.5.cloned.1.call-update) | async-done | bytes 1048592 | tf_op jit(solution)/shard_map/reduce_scatter | solution.py:573
  249.1 2.1 multiply_reduce_fusion
  251.3 1.5 multiply_convert_fusion.3
  252.8 0.5 all-gather.12.cloned.1.call-update
  253.4 53.9 %all-gather.8.cloned.1.call-done = bf16[2048,2048]{1,0:T(8,128)(2,1)} async-done(((bf16[256,2048]{1,0:T(8,128)(2,1)}), bf16[2048,2048]{1,0:T(8,128)(2,1)}) %all-gather.8.cloned.1.call-update) | async-done | bytes 8388624 | tf_op jit(solution)/shard_map/all_gather | solution.py:577
  307.3 11.0 fusion.34
  318.3 7.8 fusion.33
  326.1 37.5 %all-gather.12.cloned.1.call-done = bf16[1,2048,2048]{2,1,0:T(8,128)(2,1)} async-done(((bf16[1,256,2048]{2,1,0:T(8,128)(2,1)}), bf16[1,2048,2048]{2,1,0:T(8,128)(2,1)}) %all-gather.12.cloned.1.call-update) | async-done | bytes 8388624 | tf_op jit(solution)/shard_map/all_gather | solution.py:577
  363.6 14.2 %multiply_convert_fusion = (bf16[2048,688]{0,1:T(8,128)(2,1)S(1)}, bf16[2048,688]{0,1:T(8,128)(2,1)S(1)}, bf16[2048,688]{0,1:T(8,128)(2,1)}) fusion(f32[2048,688]{0,1:T(8,128)} %fusion.33, f32[2048,688]{0,1:T(8,128)} %fusion.34, bf16[688,2048]{1,0:T(8,128)(2,1)S(1)} %copy-done, bf16[1,2048,2048]{2,1,0:T(8,128)(2,1)} %all-gather.12.cloned.1.call-done), kind=kOutput, calls=%fused_computation.9 | convolution fusion | flops 5792497664 | bytes 30932992 | tf_op jit(solution)/shard_map/dot_general | solution.py:564
  377.9 10.5 fusion.35
  388.4 12.6 add_convert_fusion
  401.1 71.4 %reduce-scatter.9.cloned.1.call-done = bf16[256,2048]{1,0:T(8,128)(2,1)} async-done(((bf16[2048,2048]{1,0:T(8,128)(2,1)}), bf16[256,2048]{1,0:T(8,128)(2,1)}) %reduce-scatter.9.cloned.1.call-update) | async-done | bytes 1048592 | tf_op jit(solution)/shard_map/reduce_scatter | solution.py:573
  472.5 3.5 fusion.21
  476.0 0.6 copy-done.29
  476.6 3.3 fusion.28
  480.0 10.9 convolution_convert_fusion.4
  491.0 10.8 convolution_convert_fusion.5
  501.8 7.3 fusion.5
  509.1 25.3 %all-gather.10.cloned.1.call-done = bf16[2048,2048]{1,0:T(8,128)(2,1)} async-done(((bf16[256,2048]{1,0:T(8,128)(2,1)}), bf16[2048,2048]{1,0:T(8,128)(2,1)}) %all-gather.10.cloned.1.call-update) | async-done | bytes 8388624 | tf_op jit(solution)/shard_map/all_gather | solution.py:577
  534.5 10.6 fusion.36.grad_ref
  545.0 62.4 %mixer_backward.1 = (bf16[2048,1664]{1,0:T(8,128)(2,1)}, f32[4,256]{1,0:T(4,128)}, f32[4,256]{1,0:T(4,128)}, f32[4,512]{1,0:T(4,128)}, f32[1,2]{1,0:T(1,128)}, /*index=5*/f32[1,2]{1,0:T(1,128)}, f32[1,256]{1,0:T(1,128)}) custom-call(f32[2048,1664]{1,0:T(8,128)} %fusion.32.proj_ref.eq_ref.ek_ref.ev_ref, f32[2048,1664]{1,0:T(8,128)} %fusion.32.proj_ref.eq_ref.ek_ref.ev_ref, ...), custom_call_target="tpu_custom_call" | custom-call | tf_op jit(solution)/shard_map/mixer_backward/pallas_call | solution.py:481
  607.5 21.2 %convolution_convert_fusion.2 = bf16[2048,1664]{1,0:T(8,128)(2,1)} fusion(bf16[2048,2048]{1,0:T(8,128)(2,1)} %all-gather.6.cloned.1.call-done, bf16[2048,1664]{1,0:T(8,128)(2,1)} %get-tuple-element.44), kind=kOutput, calls=%fused_computation.7 | convolution fusion | flops 13962051584 | bytes 22020096 | tf_op jit(solution)/shard_map/dot_general | solution.py:560
  628.7 203.5 %all-reduce.7.cloned.1.call-done = (bf16[2048,688]{0,1:T(8,128)(2,1)}, bf16[2048,688]{0,1:T(8,128)(2,1)}, bf16[688,2048]{1,0:T(8,128)(2,1)}) async-done(((bf16[2048,688]{0,1:T(8,128)(2,1)}, bf16[2048,688]{0,1:T(8,128)(2,1)}, bf16[688,2048]{1,0:T(8,128)(2,1)}), (bf16[2048,688]{0,1:T(8,128)(2,1)}, bf16[2048,688]{0,1:T(8,128)(2,1)}, bf16[688,2048]{1,0:T(8,128)(2,1)})) %all-reduce.7.cloned.1.call-update) | async-done | bytes 8454160 | tf_op jit(solution)/shard_map/psum | solution.py:656
  832.2 9.9 convolution_convert_fusion.6
  842.2 21.1 %convolution_convert_fusion.3 = bf16[2048,2048]{1,0:T(8,128)(2,1)} fusion(bf16[2048,1664]{1,0:T(8,128)(2,1)} %get-tuple-element.44, bf16[2048,1664]{1,0:T(8,128)(2,1)} %concatenate.9), kind=kOutput, calls=%fused_computation.8 | convolution fusion | flops 13962838016 | bytes 22020096 | tf_op jit(solution)/shard_map/dot_general | solution.py:564
  863.4 10.8 convolution_convert_fusion
  874.2 0.6 copy-done.37
  875.0 19.0 %psum.54 = f32[4100]{0:T(1024)S(1)} all-reduce(f32[4100]{0:T(1024)S(1)} %concatenate.11), channel_id=1, replica_groups=mesh['dp'=4,'tensor'=8] {'dp'}, use_global_device_ids=true, to_apply=%region_15.0 | all-reduce | flops 4100 | bytes 32800 | tf_op jit(solution)/shard_map/psum | solution.py:672
  894.0 0.6 reshape.100
  894.6 0.6 reshape.101
  895.2 0.6 reshape.99
  895.8 5.3 convert_element_type.150
  901.1 3.2 convert_element_type.151
  904.3 3.2 convert_element_type.152
  907.6 0.6 fusion.30
  908.2 242.5 %all-reduce.5.cloned.1.call-done = (bf16[2048,1664]{1,0:T(8,128)(2,1)}, bf16[512,2048]{1,0:T(8,128)(2,1)}) async-done(((bf16[2048,1664]{1,0:T(8,128)(2,1)}, bf16[512,2048]{1,0:T(8,128)(2,1)}), (bf16[2048,1664]{1,0:T(8,128)(2,1)}, bf16[512,2048]{1,0:T(8,128)(2,1)})) %all-reduce.5.cloned.1.call-update) | async-done | bytes 8912912 | tf_op jit(solution)/shard_map/psum | solution.py:664
  1150.7 4.1 convert_element_type.149
  1154.8 2.8 slice_convert_fusion.4
  1157.6 2.4 copy.49
  1160.0 2.3 copy.48
  1162.3 4.5 slice_convert_fusion.2
  1166.8 7.4 slice_convert_fusion
  1174.3 50.2 %reduce-scatter.11.cloned.1.call-done = bf16[256,2048]{1,0:T(8,128)(2,1)} async-done(((bf16[2048,2048]{1,0:T(8,128)(2,1)}), bf16[256,2048]{1,0:T(8,128)(2,1)}) %reduce-scatter.11.cloned.1.call-update) | async-done | bytes 1048592 | tf_op jit(solution)/shard_map/reduce_scatter | solution.py:573
  1224.5 2.4 fusion.24
  1226.9 39.8 %psum.49 = f32[4352]{0:T(1024)S(1)} all-reduce(f32[4352]{0:T(1024)S(1)} %pad_maximum_fusion), channel_id=1, replica_groups=mesh['dp'=4,'tensor'=8] {'dp','tensor'}, use_global_device_ids=true, to_apply=%region_10.0 | all-reduce | flops 4352 | bytes 34816 | tf_op jit(solution)/shard_map/psum | solution.py:668
  1266.7 0.6 slice.68
  1267.3 0.6 fusion.29
  1267.9 32.2 %reduce-scatter.7.cloned.1.call-done = bf16[256,2048]{1,0:T(8,128)(2,1)} async-done(((bf16[2048,2048]{1,0:T(8,128)(2,1)}), bf16[256,2048]{1,0:T(8,128)(2,1)}) %reduce-scatter.7.cloned.1.call-update) | async-done | bytes 1048592 | tf_op jit(solution)/shard_map/reduce_scatter | solution.py:573
  1300.1 6.1 fusion.17
  (142 shorter events, 1.7 us)
Async XLA Ops:
  7.2 356.4 %copy-start = (bf16[688,2048]{1,0:T(8,128)(2,1)S(1)}, bf16[688,2048]{1,0:T(8,128)(2,1)}, u32[]{:S(2)}) copy-start(bf16[688,2048]{1,0:T(8,128)(2,1)} %param.40) | copy-start | bytes 8454148
  7.2 5.7 copy-start.11
  7.2 5.8 copy-start.10
  7.2 5.9 copy-start.48
  7.2 5.9 copy-start.38
  7.3 5.9 copy-start.39
  7.3 5.9 copy-start.34
  7.3 5.9 copy-start.31
  7.3 6.3 copy-start.32
  7.3 62.8 %all-gather.6.cloned.1.call-start = ((), (), s32[]{:S(2)}) async-start(), calls=%async_computation.4 | async-start | bytes 9437184 | tf_op jit(solution)/shard_map/all_gather | solution.py:577
  9.0 0.7 copy-start.27
  9.7 0.6 copy-start.22
  12.8 236.3 %reduce-scatter.5.cloned.1.call-start = ((), (), s32[]{:S(2)}) async-start(), calls=%async_computation.5 | async-start | bytes 9437184 | tf_op jit(solution)/shard_map/reduce_scatter | solution.py:573
  13.0 78.3 %copy-start.7 = (f32[2,1]{1,0:T(2,128)}, f32[2,1]{1,0:T(2,128)S(1)}, u32[]{:S(2)}) copy-start(f32[2,1]{1,0:T(2,128)S(1)} %copy.45.db_col_ref) | copy-start | bytes 28
  13.1 78.2 %copy-start.8 = (f32[2,1]{1,0:T(2,128)}, f32[2,1]{1,0:T(2,128)S(1)}, u32[]{:S(2)}) copy-start(f32[2,1]{1,0:T(2,128)S(1)} %copy.44.dl_col_ref) | copy-start | bytes 28
  13.1 78.2 %copy-start.9 = (f32[256]{0:T(256)}, f32[256]{0:T(256)S(1)}, u32[]{:S(2)}) copy-start(f32[256]{0:T(256)S(1)} %broadcast_in_dim.52) | copy-start | bytes 3076
  13.1 78.2 %copy-start.5 = (f32[4,256]{1,0:T(4,128)}, f32[4,256]{1,0:T(4,128)S(1)}, u32[]{:S(2)}) copy-start(f32[4,256]{1,0:T(4,128)S(1)} %convert_element_type.119.tq_ref) | copy-start | bytes 12292
  13.2 78.2 %copy-start.6 = (f32[4,256]{1,0:T(4,128)}, f32[4,256]{1,0:T(4,128)S(1)}, u32[]{:S(2)}) copy-start(f32[4,256]{1,0:T(4,128)S(1)} %convert_element_type.120.tk_ref) | copy-start | bytes 12292
  13.2 78.2 %copy-start.4 = (f32[4,512]{1,0:T(4,128)}, f32[4,512]{1,0:T(4,128)S(1)}, u32[]{:S(2)}) copy-start(f32[4,512]{1,0:T(4,128)S(1)} %convert_element_type.121.tv_ref) | copy-start | bytes 24580
  26.8 64.6 %copy-start.3 = (f32[1,2,128,256]{3,2,1,0:T(8,128)S(1)}, f32[1,2,128,256]{3,2,1,0:T(8,128)}, u32[]{:S(2)}) copy-start(f32[1,2,128,256]{3,2,1,0:T(8,128)} %param.22) | copy-start | bytes 786436
  91.4 79.4 %copy-start.47 = (bf16[512,2048]{1,0:T(8,128)(2,1)S(1)}, bf16[512,2048]{1,0:T(8,128)(2,1)}, u32[]{:S(2)}) copy-start(bf16[512,2048]{1,0:T(8,128)(2,1)} %param.36) | copy-start | bytes 6291460
  167.2 1.3 copy-start.1
  168.5 1.0 copy-start.2
  169.5 1.3 copy-start.12
  177.6 0.7 copy-start.35
  177.7 129.6 %all-gather.8.cloned.1.call-start = ((), (), s32[]{:S(2)}) async-start(), calls=%async_computation.6 | async-start | bytes 9437184 | tf_op jit(solution)/shard_map/all_gather | solution.py:577
  178.3 297.7 %copy-start.20 = (f32[2048]{0:T(1024)}, f32[2048]{0:T(1024)S(1)}, u32[]{:S(2)}) copy-start(f32[2048]{0:T(1024)S(1)} %convert_element_type.124) | copy-start | bytes 24580
  249.1 2.1 copy-start.13
  249.1 2.2 copy-start.15
  251.3 224.7 %copy-start.25 = (f32[256]{0:T(256)}, f32[256]{0:T(256)S(1)}, u32[]{:S(2)}) copy-start(f32[256]{0:T(256)S(1)} %add_rsqrt_fusion) | copy-start | bytes 3076
  252.8 110.9 %all-gather.12.cloned.1.call-start = ((), (), s32[]{:S(2)}) async-start(), calls=%async_computation.11 | async-start | bytes 9437184 | tf_op jit(solution)/shard_map/all_gather | solution.py:577
  253.4 219.1 %reduce-scatter.9.cloned.1.call-start = ((), (), s32[]{:S(2)}) async-start(), calls=%async_computation.8 | async-start | bytes 9437184 | tf_op jit(solution)/shard_map/reduce_scatter | solution.py:573
  307.3 11.0 copy-start.43
  307.3 11.0 copy-start.44
  363.6 14.2 %copy-start.45 = (bf16[2048,688]{0,1:T(8,128)(2,1)S(1)}, bf16[2048,688]{0,1:T(8,128)(2,1)}, u32[]{:S(2)}) copy-start(bf16[2048,688]{0,1:T(8,128)(2,1)} %param.38) | copy-start | bytes 8454148
  377.9 10.5 copy-start.50
  377.9 10.5 copy-start.49
  377.9 10.5 copy-start.46
  401.0 133.4 %all-gather.10.cloned.1.call-start = ((), (), s32[]{:S(2)}) async-start(), calls=%async_computation.9 | async-start | bytes 9437184 | tf_op jit(solution)/shard_map/all_gather | solution.py:577
  472.5 4.1 copy-start.14
  472.5 4.1 copy-start.16
  472.5 4.1 copy-start.17
  479.9 352.3 %all-reduce.7.cloned.1.call-start = ((), (), s32[]{:S(2)}) async-start(), calls=%async_computation.13 | async-start | bytes 16908288 | tf_op jit(solution)/shard_map/psum | solution.py:656
  480.0 11.0 copy-start.51
  480.0 21.8 %slice-start = ((s8[8388608]{0:T(1024)(128)(4,1)}), s8[4194304]{0:T(1024)(128)(4,1)S(1)}, s32[]{:S(2)}) async-start(s8[8388608]{0:T(1024)(128)(4,1)} %bitcast.99), calls=%async_computation.14 | async-start | bytes 8388608
  491.0 10.8 slice-start.1
  491.0 10.8 copy-start.52
  509.1 641.6 %all-reduce.5.cloned.1.call-start = ((), (), s32[]{:S(2)}) async-start(), calls=%async_computation.12 | async-start | bytes 17825792 | tf_op jit(solution)/shard_map/psum | solution.py:664
  842.1 382.3 %reduce-scatter.11.cloned.1.call-start = ((), (), s32[]{:S(2)}) async-start(), calls=%async_computation.10 | async-start | bytes 9437184 | tf_op jit(solution)/shard_map/reduce_scatter | solution.py:573
  863.3 436.8 %reduce-scatter.7.cloned.1.call-start = ((), (), s32[]{:S(2)}) async-start(), calls=%async_computation.7 | async-start | bytes 9437184 | tf_op jit(solution)/shard_map/reduce_scatter | solution.py:573
  874.2 0.7 copy-start.37
  874.2 0.7 copy-start.36
  874.2 0.7 copy-start.33
  874.2 0.7 copy-start.41
  874.2 0.7 copy-start.42
  895.8 5.3 copy-start.19
  901.1 3.2 copy-start.18
  1166.8 57.7 %copy-start.23 = (f32[2048]{0:T(1024)S(1)}, f32[2048]{0:T(1024)}, u32[]{:S(2)}) copy-start(f32[2048]{0:T(1024)} %copy-done.22) | copy-start | bytes 24580
  1166.8 57.7 %copy-start.28 = (f32[256]{0:T(256)S(1)}, f32[256]{0:T(256)}, u32[]{:S(2)}) copy-start(f32[256]{0:T(256)} %copy-done.27) | copy-start | bytes 3076
  1166.8 60.0 %copy-start.24 = (f32[2048]{0:T(1024)S(1)}, f32[2048]{0:T(1024)}, u32[]{:S(2)}) copy-start(f32[2048]{0:T(1024)} %get-tuple-element.76) | copy-start | bytes 24580
  1166.8 60.1 %copy-start.40 = (f32[1,256]{1,0:T(1,128)S(1)}, f32[1,256]{1,0:T(1,128)}, u32[]{:S(2)}) copy-start(f32[1,256]{1,0:T(1,128)} %get-tuple-element.45) | copy-start | bytes 3076
  1166.8 133.3 %copy-start.21 = (f32[2048]{0:T(1024)S(1)}, f32[2048]{0:T(1024)}, u32[]{:S(2)}) copy-start(f32[2048]{0:T(1024)} %copy-done.20) | copy-start | bytes 24580
  1166.8 133.3 %copy-start.26 = (f32[256]{0:T(256)S(1)}, f32[256]{0:T(256)}, u32[]{:S(2)}) copy-start(f32[256]{0:T(256)} %copy-done.25) | copy-start | bytes 3076
  1166.8 133.2 %copy-start.30 = (f32[256]{0:T(256)S(1)}, f32[256]{0:T(256)}, u32[]{:S(2)}) copy-start(f32[256]{0:T(256)} %copy-done.29) | copy-start | bytes 3076
  (1 other events, 0.6 us)
Sparse Core Ops, SparseCore 0:
  13.0 57.0 all-gather.5
  177.8 71.2 reduce-scatter.4
  252.9 54.3 all-gather.7
  309.2 54.3 all-gather.11
  401.1 71.2 reduce-scatter.8
  480.1 54.3 all-gather.9
  537.9 294.3 all-reduce.6
  842.3 308.3 all-reduce.4
  1154.2 70.2 reduce-scatter.10
  1228.2 71.8 reduce-scatter.6

commit v2 on v1

--- a/solution.py
+++ b/solution.py
@@ -267,6 +267,7 @@
         compiler_params=pltpu.CompilerParams(
             dimension_semantics=("arbitrary",), vmem_limit_bytes=48 * 1024 * 1024
         ),
+        cost_estimate=pl.CostEstimate(flops=0, bytes_accessed=200_000_000, transcendentals=0),
         name="mixer_forward",
     )(
         proj,
@@ -530,6 +531,7 @@
         compiler_params=pltpu.CompilerParams(
             dimension_semantics=("arbitrary",), vmem_limit_bytes=56 * 1024 * 1024
         ),
+        cost_estimate=pl.CostEstimate(flops=0, bytes_accessed=200_000_000, transcendentals=0),
         name="mixer_backward",
     )(
         proj,
@@ -552,6 +554,340 @@
     )
 
 
+def copy_to(src, dst, send, recv, axis, index):
+    return pltpu.make_async_remote_copy(
+        src_ref=src,
+        dst_ref=dst,
+        send_sem=send,
+        recv_sem=recv,
+        device_id={axis: index},
+        device_id_type=pl.DeviceIdType.MESH,
+    )
+
+
+def greet(axis, others):
+    barrier = pltpu.get_barrier_semaphore()
+    for other in others:
+        pl.semaphore_signal(
+            barrier, inc=1, device_id={axis: other}, device_id_type=pl.DeviceIdType.MESH
+        )
+    pl.semaphore_wait(barrier, len(others))
+
+
+def neighbours(axis):
+    me = lax.axis_index(axis)
+    other = me + 1 - 2 * (me % 2)
+    along_x = me + 2 - 4 * ((me // 2) % 2)
+    along_y = me + 4 - 8 * (me // 4)
+    return me, other, along_x, along_y
+
+
+PIECES = 4
+
+
+def gather_kernel(axis, x_ref, out_ref, send, recv, local):
+    me, other, along_x, along_y = neighbours(axis)
+    rows = x_ref.shape[0]
+    part = rows // PIECES
+    diagonal = along_x + along_y - me
+    greet(axis, (other, along_x, along_y))
+
+    def place(shard, j):
+        return out_ref.at[pl.ds(pl.multiple_of(shard * rows + j * part, part), part), :]
+
+    own = pltpu.make_async_copy(x_ref, out_ref.at[pl.ds(pl.multiple_of(me * rows, rows), rows), :], local)
+    own.start()
+    copies = {}
+
+    def begin(kind, j, target, shard):
+        index = len(copies)
+        src = x_ref.at[pl.ds(j * part, part), :] if kind[0] == "o" else place(shard, j)
+        copies[kind, j] = copy_to(src, place(shard, j), send.at[index], recv.at[index], axis, target)
+        copies[kind, j].start()
+
+    for j in range(PIECES):
+        begin("ox", j, along_x, me)
+        begin("oy", (j + PIECES // 2) % PIECES, along_y, me)
+    for j in range(PIECES):
+        begin("oc", j, other, me)
+    for j in range(PIECES):
+        copies["ox", j].wait_recv()
+        if j < PIECES // 2:
+            begin("xy", j, along_y, along_x)
+        begin("xc", j, other, along_x)
+        k = (j + PIECES // 2) % PIECES
+        copies["oy", k].wait_recv()
+        if k >= PIECES // 2:
+            begin("yx", k, along_x, along_y)
+        begin("yc", k, other, along_y)
+    for j in range(PIECES // 2):
+        copies["xy", j].wait_recv()
+        begin("dc", j, other, diagonal)
+        k = j + PIECES // 2
+        copies["yx", k].wait_recv()
+        begin("dc", k, other, diagonal)
+    for j in range(PIECES):
+        for kind in ("oc", "xc", "yc", "dc"):
+            copies[kind, j].wait_recv()
+    for copy in copies.values():
+        copy.wait_send()
+    own.wait()
+
+
+def square(axis_sizes):
+    return axis_sizes["tensor"] == 8 and axis_sizes["dp"] == 4
+
+
+def gather_rows(rows, identity, sizes):
+    if not square(sizes):
+        return lax.all_gather(rows, "tensor", axis=0, tiled=True)
+    height, width = rows.shape
+    count = 7 * PIECES
+    return pl.pallas_call(
+        functools.partial(gather_kernel, "tensor"),
+        out_shape=jax.ShapeDtypeStruct((8 * height, width), rows.dtype),
+        in_specs=[pl.BlockSpec(memory_space=pl.ANY)],
+        out_specs=pl.BlockSpec(memory_space=pl.ANY),
+        scratch_shapes=[
+            pltpu.SemaphoreType.DMA((count,)),
+            pltpu.SemaphoreType.DMA((count,)),
+            pltpu.SemaphoreType.DMA,
+        ],
+        compiler_params=pltpu.CompilerParams(collective_id=identity, has_side_effects=True),
+        cost_estimate=pl.CostEstimate(flops=0, bytes_accessed=1_000_000, transcendentals=0),
+        name="gather_rows",
+    )(rows)
+
+
+def scatter_kernel(axis, p_ref, out_ref, mine, theirs, in_dx, in_dy, in_x, in_y, load, send, recv):
+    me, other, along_x, along_y = neighbours(axis)
+    rows = out_ref.shape[0]
+    half = rows // 2
+    diagonal = along_x + along_y - me
+    greet(axis, (other, along_x, along_y))
+    goals = (diagonal, along_x, along_y, me)
+    shift = other - me
+    loads, swaps, copies = [], [], []
+
+    def shard(index, part=None):
+        if part is None:
+            return p_ref.at[pl.ds(pl.multiple_of(index * rows, rows), rows), :]
+        return p_ref.at[pl.ds(pl.multiple_of(index * rows + part * half, half), half), :]
+
+    for r, goal in enumerate(goals):
+        for part in range(2):
+            slot = 2 * r + part
+            at = pl.ds(part * half, half)
+            swap = copy_to(
+                shard(goal + shift, part), theirs.at[r, at, :], send.at[slot], recv.at[slot], axis, other
+            )
+            swap.start()
+            swaps.append(swap)
+            copy = pltpu.make_async_copy(shard(goal, part), mine.at[r, at, :], load.at[slot])
+            copy.start()
+            loads.append(copy)
+
+    def pair_sum(r, part):
+        loads[2 * r + part].wait()
+        swaps[2 * r + part].wait_recv()
+        at = pl.ds(part * half, half)
+        mine[r, at, :] = (mine[r, at, :].astype(f32) + theirs[r, at, :].astype(f32)).astype(bf16)
+
+    def begin(src, dst, target):
+        index = 8 + len(copies)
+        copy = copy_to(src, dst, send.at[index], recv.at[index], axis, target)
+        copy.start()
+        copies.append(copy)
+        return copy
+
+    first, second = pl.ds(0, half), pl.ds(half, half)
+    pair_sum(0, 0)
+    far_x = begin(mine.at[0, first, :], in_dx, along_x)
+    pair_sum(0, 1)
+    far_y = begin(mine.at[0, second, :], in_dy, along_y)
+    pair_sum(1, 0)
+    near_x0 = begin(mine.at[1, first, :], in_x.at[first, :], along_x)
+    pair_sum(2, 1)
+    near_y1 = begin(mine.at[2, second, :], in_y.at[second, :], along_y)
+    pair_sum(1, 1)
+    pair_sum(2, 0)
+    far_x.wait_recv()
+    mine[2, first, :] = (mine[2, first, :].astype(f32) + in_dx[...].astype(f32)).astype(bf16)
+    near_y0 = begin(mine.at[2, first, :], in_y.at[first, :], along_y)
+    far_y.wait_recv()
+    mine[1, second, :] = (mine[1, second, :].astype(f32) + in_dy[...].astype(f32)).astype(bf16)
+    near_x1 = begin(mine.at[1, second, :], in_x.at[second, :], along_x)
+    for part, at in ((0, first), (1, second)):
+        loads[6 + part].wait()
+        swaps[6 + part].wait_recv()
+        out_ref[at, :] = mine[3, at, :].astype(f32) + theirs[3, at, :].astype(f32)
+    near_x0.wait_recv()
+    out_ref[first, :] += in_x[first, :].astype(f32)
+    near_y1.wait_recv()
+    out_ref[second, :] += in_y[second, :].astype(f32)
+    near_y0.wait_recv()
+    out_ref[first, :] += in_y[first, :].astype(f32)
+    near_x1.wait_recv()
+    out_ref[second, :] += in_x[second, :].astype(f32)
+    for copy in swaps + copies:
+        copy.wait_send()
+
+
+def scatter_rows(partial, identity, sizes):
+    if identity is None or not square(sizes):
+        return lax.psum_scatter(partial, "tensor", scatter_dimension=0, tiled=True).astype(f32)
+    height, width = partial.shape
+    rows = height // 8
+    vmem = pl.BlockSpec(memory_space=pltpu.VMEM)
+    return pl.pallas_call(
+        functools.partial(scatter_kernel, "tensor"),
+        out_shape=jax.ShapeDtypeStruct((rows, width), f32),
+        in_specs=[pl.BlockSpec(memory_space=pl.ANY)],
+        out_specs=vmem,
+        scratch_shapes=[
+            pltpu.VMEM((4, rows, width), bf16),
+            pltpu.VMEM((4, rows, width), bf16),
+            pltpu.VMEM((rows // 2, width), bf16),
+            pltpu.VMEM((rows // 2, width), bf16),
+            pltpu.VMEM((rows, width), bf16),
+            pltpu.VMEM((rows, width), bf16),
+            pltpu.SemaphoreType.DMA((8,)),
+            pltpu.SemaphoreType.DMA((14,)),
+            pltpu.SemaphoreType.DMA((14,)),
+        ],
+        compiler_params=pltpu.CompilerParams(
+            collective_id=identity, has_side_effects=True, vmem_limit_bytes=32 * 1024 * 1024
+        ),
+        cost_estimate=pl.CostEstimate(flops=0, bytes_accessed=1_000_000, transcendentals=0),
+        name="scatter_rows",
+    )(partial)
+
+
+CHUNK = 64
+
+
+def line_kernel(axis, widths, *refs):
+    count = len(widths)
+    g_refs, out_refs = refs[:count], refs[count : 2 * count]
+    scratch = refs[2 * count :]
+    z = lax.axis_index(axis)
+    near = z + 1 - 2 * (z % 2)
+    across = 3 - z
+    inner = (z * (3 - z)) > 0
+    barrier = pltpu.get_barrier_semaphore()
+    pl.semaphore_signal(barrier, inc=1, device_id={axis: near}, device_id_type=pl.DeviceIdType.MESH)
+
+    @pl.when(inner)
+    def _():
+        pl.semaphore_signal(
+            barrier, inc=1, device_id={axis: across}, device_id_type=pl.DeviceIdType.MESH
+        )
+        pl.semaphore_wait(barrier, 2)
+
+    @pl.when(jnp.logical_not(inner))
+    def _():
+        pl.semaphore_wait(barrier, 1)
+
+    groups = []
+    for i in range(count):
+        own, from_out, from_in, total, sems = scratch[5 * i : 5 * i + 5]
+        g_ref, out_ref = g_refs[i], out_refs[i]
+        chunks, chunk = own.shape[0], own.shape[1]
+
+        def rows_of(ref, c, width=widths[i], chunk=chunk):
+            return ref.at[pl.ds(pl.multiple_of(c * chunk, chunk), chunk), pl.ds(0, width)]
+
+        def load(c, g_ref=g_ref, own=own, sems=sems, rows_of=rows_of):
+            return pltpu.make_async_copy(rows_of(g_ref, c), own.at[c], sems.at[0, c])
+
+        def inward(c, g_ref=g_ref, from_out=from_out, sems=sems, rows_of=rows_of):
+            return copy_to(rows_of(g_ref, c), from_out.at[c], sems.at[1, c], sems.at[2, c], axis, near)
+
+        def middle(c, own=own, from_in=from_in, sems=sems):
+            return copy_to(own.at[c], from_in.at[c], sems.at[3, c], sems.at[4, c], axis, across)
+
+        def outward(c, total=total, out_ref=out_ref, sems=sems, rows_of=rows_of):
+            return copy_to(total.at[c], rows_of(out_ref, c), sems.at[5, c], sems.at[6, c], axis, near)
+
+        def keep(c, total=total, out_ref=out_ref, sems=sems, rows_of=rows_of):
+            return pltpu.make_async_copy(total.at[c], rows_of(out_ref, c), sems.at[7, c])
+
+        groups.append((chunks, own, from_out, from_in, total, load, inward, middle, outward, keep))
+
+    def each(chunks, body):
+        def step(c, carry):
+            body(c)
+            return carry
+
+        lax.fori_loop(0, chunks, step, 0)
+
+    @pl.when(jnp.logical_not(inner))
+    def _():
+        for chunks, _, _, _, _, _, inward, _, _, _ in groups:
+            each(chunks, lambda c: inward(c).start())
+        for chunks, _, _, _, _, _, inward, _, outward, _ in groups:
+            each(chunks, lambda c: outward(c).wait_recv())
+            each(chunks, lambda c: inward(c).wait_send())
+
+    @pl.when(inner)
+    def _():
+        for chunks, _, _, _, _, load, _, _, _, _ in groups:
+            each(chunks, lambda c: load(c).start())
+        for chunks, own, from_out, from_in, total, load, inward, middle, outward, keep in groups:
+
+            def first(c):
+                load(c).wait()
+                inward(c).wait_recv()
+                own[c] = (own[c].astype(f32) + from_out[c].astype(f32)).astype(bf16)
+                middle(c).start()
+
+            def second(c):
+                middle(c).wait_recv()
+                total[c] = (own[c].astype(f32) + from_in[c].astype(f32)).astype(bf16)
+                outward(c).start()
+                keep(c).start()
+
+            first(0)
+
+            def both(c):
+                first(c + 1)
+                second(c)
+
+            each(chunks - 1, both)
+            second(chunks - 1)
+        for chunks, _, _, _, _, _, _, middle, outward, keep in groups:
+            def settle(c):
+                middle(c).wait_send()
+                outward(c).wait_send()
+                keep(c).wait()
+
+            each(chunks, settle)
+
+
+def sum_over_line(arrays, widths, identity, sizes):
+    if not square(sizes):
+        return lax.psum(tuple(a[:, :w] for a, w in zip(arrays, widths)), "dp")
+    scratch = []
+    for a, w in zip(arrays, widths):
+        chunks = a.shape[0] // CHUNK
+        scratch += [pltpu.VMEM((chunks, CHUNK, w), bf16)] * 4
+        scratch.append(pltpu.SemaphoreType.DMA((8, chunks)))
+    anywhere = pl.BlockSpec(memory_space=pl.ANY)
+    total = sum(a.shape[0] * w for a, w in zip(arrays, widths))
+    return pl.pallas_call(
+        functools.partial(line_kernel, "dp", tuple(widths)),
+        out_shape=tuple(jax.ShapeDtypeStruct((a.shape[0], w), bf16) for a, w in zip(arrays, widths)),
+        in_specs=[anywhere] * len(arrays),
+        out_specs=(anywhere,) * len(arrays),
+        scratch_shapes=scratch,
+        compiler_params=pltpu.CompilerParams(
+            collective_id=identity, has_side_effects=True, vmem_limit_bytes=56 * 1024 * 1024
+        ),
+        cost_estimate=pl.CostEstimate(flops=0, bytes_accessed=total, transcendentals=0),
+        name="sum_over_line",
+    )(*arrays)
+
+
 def rms_factor(matrix):
     return lax.rsqrt(jnp.mean(matrix * matrix, -1, keepdims=True) + norm_eps)
 
@@ -569,15 +905,12 @@
     return factor * (weighted - scaled * jnp.mean(weighted * scaled, -1, keepdims=True))
 
 
-def scatter_rows(partial):
-    return lax.psum_scatter(partial.astype(bf16), "tensor", scatter_dimension=0, tiled=True).astype(f32)
-
-
-def gather_rows(rows):
-    return lax.all_gather(rows, "tensor", axis=0, tiled=True)
+def sum_small(vector, axes):
+    return jnp.sum(lax.all_gather(vector, axes, axis=0, tiled=False), 0)
 
 
 def shards(
+    sizes,
     tokens,
     start_state,
     gain_attn,
@@ -602,14 +935,16 @@
 ):
     inputs = tokens[0].astype(f32)
     heads = decay_log.shape[0]
+    width = inputs.shape[1]
     factor_attn = rms_factor(inputs)
     scaled_attn = inputs * factor_attn
     gain_first = gain_attn.astype(f32)
     gain_second = gain_ffn.astype(f32)
     normed = (scaled_attn * gain_first).astype(bf16)
-    gathered = gather_rows(normed)
+    gathered = gather_rows(normed, 0, sizes)
     padding = jnp.zeros((w_alpha.shape[0], EXTRA - 2 * heads), bf16)
     w_in = jnp.concatenate([w_query, w_key, w_value, w_gate_out, w_alpha, w_beta, padding], axis=1)
+    main = w_in.shape[1] - EXTRA
     projected = jnp.dot(gathered, w_in, preferred_element_type=f32)
     extras = (
         conv_query.astype(f32),
@@ -620,66 +955,92 @@
         out_gain.astype(f32),
     )
     mixed, final, states, inverse, update, raw = mixer_forward(projected, *extras, start_state[0])
-    grad_out_rows = cotangent[0]
-    grad_gathered = gather_rows(grad_out_rows)
-    attended = scatter_rows(jnp.dot(mixed, w_out, preferred_element_type=f32))
+    grad_out_rows, gathered = lax.optimization_barrier((cotangent[0], gathered))
+    grad_gathered = lax.all_gather(grad_out_rows, "tensor", axis=0, tiled=True)
+    attended = scatter_rows(
+        jnp.dot(mixed, w_out, preferred_element_type=f32).astype(bf16), 1, sizes
+    )
     hidden = inputs + attended
     factor_ffn = rms_factor(hidden)
     scaled_ffn = hidden * factor_ffn
     normed_ffn = (scaled_ffn * gain_second).astype(bf16)
-    gathered_ffn = gather_rows(normed_ffn)
+    gathered_ffn = gather_rows(normed_ffn, 2, sizes)
     gate_proj = jnp.dot(gathered_ffn, w_ffn_gate, preferred_element_type=f32)
     up_proj = jnp.dot(gathered_ffn, w_ffn_up, preferred_element_type=f32)
     sigmoid_gate = jax.nn.sigmoid(gate_proj)
     activated = gate_proj * sigmoid_gate
     inner = (activated * up_proj).astype(bf16)
-    ffn_out = scatter_rows(jnp.dot(inner, w_ffn_down, preferred_element_type=f32))
-    output = (hidden + ffn_out).astype(bf16)
     grad_inner = times_transposed(grad_gathered, w_ffn_down)
     grad_gate_rows = (
         grad_inner * up_proj * sigmoid_gate * (1.0 + gate_proj * (1.0 - sigmoid_gate))
     ).astype(bf16)
     grad_up_rows = (grad_inner * activated).astype(bf16)
-    grad_normed_ffn = scatter_rows(
+    grad_down = cross_rows(inner, grad_gathered).astype(bf16)
+    grad_gate_weight = cross_rows(gathered_ffn, grad_gate_rows).astype(bf16)
+    grad_up_weight = cross_rows(gathered_ffn, grad_up_rows).astype(bf16)
+    grad_down_summed, grad_gate_summed = lax.psum((grad_down, grad_gate_weight), "dp")
+    part_normed_ffn = (
         times_transposed(grad_gate_rows, w_ffn_gate) + times_transposed(grad_up_rows, w_ffn_up)
-    )
+    ).astype(bf16)
+    part_normed_ffn, grad_down, grad_gate_weight = lax.optimization_barrier(
+        (part_normed_ffn, grad_down, grad_gate_weight)
+    )
+    grad_normed_ffn = scatter_rows(part_normed_ffn, 3, sizes)
     part_gain_ffn = jnp.sum(grad_normed_ffn * scaled_ffn, 0)
     grad_hidden = grad_out_rows.astype(f32) + norm_backward(
         grad_normed_ffn, scaled_ffn, factor_ffn, gain_second
     )
-    grad_attended = gather_rows(grad_hidden.astype(bf16))
-    early = (
-        cross_rows(gathered_ffn, grad_gate_rows).astype(bf16),
-        cross_rows(gathered_ffn, grad_up_rows).astype(bf16),
-        cross_rows(inner, grad_gathered).astype(bf16),
-    )
-    early = lax.psum(early, "dp")
+    grad_attended = gather_rows(grad_hidden.astype(bf16), 4, sizes)
     grad_mixed = times_transposed(grad_attended, w_out)
-    middle = cross_rows(mixed, grad_attended).astype(bf16)
+    ffn_part = jnp.dot(inner, w_ffn_down, preferred_element_type=f32).astype(bf16)
+    grad_out_weight = cross_rows(mixed, grad_attended).astype(bf16)
     grad_projected, grad_tq, grad_tk, grad_tv, grad_dl, grad_db, grad_gain = mixer_backward(
         projected, *extras, states, inverse, update, raw, grad_mixed
     )
+    part_normed = times_transposed(grad_projected, w_in).astype(bf16)
     grad_in = cross_rows(gathered, grad_projected).astype(bf16)
-    grad_in, early = lax.optimization_barrier((grad_in, early))
-    grad_in, middle = lax.psum((grad_in, middle), "dp")
-    grad_normed = scatter_rows(times_transposed(grad_projected, w_in))
-    part_gain_attn = jnp.sum(grad_normed * scaled_attn, 0)
+    (
+        grad_in,
+        grad_out_weight,
+        grad_up_weight,
+        part_normed,
+        ffn_part,
+        grad_down_summed,
+        grad_gate_summed,
+    ) = lax.optimization_barrier(
+        (
+            grad_in,
+            grad_out_weight,
+            grad_up_weight,
+            part_normed,
+            ffn_part,
+            grad_down_summed,
+            grad_gate_summed,
+        )
+    )
+    grad_normed = scatter_rows(part_normed, None, sizes)
+    ffn_out = scatter_rows(ffn_part, None, sizes)
+    output = (hidden + ffn_out).astype(bf16)
+    part_gain_attn = jnp.sum(grad_in.astype(f32) * w_in.astype(f32), 1) / gain_first
+    gain_grads = sum_small(
+        jnp.concatenate([part_gain_attn, part_gain_ffn, grad_gain[0]]), ("dp", "tensor")
+    )
+    grad_ab = grad_in[:, main : main + 2 * heads].astype(f32).T
+    smalls = (grad_tq, grad_tk, grad_tv, grad_dl[0], grad_db[0], grad_ab)
+    small = sum_small(jnp.concatenate([a.reshape(-1) for a in smalls]), "dp")
+    small_summed, at = [], 0
+    for a in smalls:
+        small_summed.append(small[at : at + a.size].reshape(a.shape))
+        at += a.size
+    grad_up_summed, grad_out_summed, grad_in_summed = sum_over_line(
+        (grad_up_weight, grad_out_weight, grad_in), (grad_up_weight.shape[1], width, main), 5, sizes
+    )
     grad_inputs = grad_hidden + norm_backward(grad_normed, scaled_attn, factor_attn, gain_first)
-    gain_grads = lax.psum(
-        jnp.concatenate([part_gain_attn, part_gain_ffn, grad_gain[0]]), ("dp", "tensor")
-    )
-    width = inputs.shape[1]
-    small = lax.psum(
-        jnp.concatenate([a.reshape(-1) for a in (grad_tq, grad_tk, grad_tv, grad_dl, grad_db)]), "dp"
-    )
-    smalls, at = [], 0
-    for a in (grad_tq, grad_tk, grad_tv, grad_dl[0], grad_db[0]):
-        smalls.append(small[at : at + a.size].reshape(a.shape))
-        at += a.size
     pieces, at = [], 0
-    for w in (w_query, w_key, w_value, w_gate_out, w_alpha, w_beta):
-        pieces.append(grad_in[:, at : at + w.shape[1]].astype(f32))
+    for w in (w_query, w_key, w_value, w_gate_out):
+        pieces.append(grad_in_summed[:, at : at + w.shape[1]].astype(f32))
         at += w.shape[1]
+    grad_ab = small_summed[5]
     return (
         output[None],
         final[None],
@@ -688,26 +1049,26 @@
         pieces[0],
         pieces[1],
         pieces[2],
-        pieces[4],
-        pieces[5],
+        grad_ab[:heads].T,
+        grad_ab[heads:].T,
         pieces[3],
-        smalls[0],
-        smalls[1],
-        smalls[2],
-        smalls[3],
-        smalls[4],
+        small_summed[0],
+        small_summed[1],
+        small_summed[2],
+        small_summed[3],
+        small_summed[4],
         gain_grads[2 * width :],
-        middle.astype(f32),
+        grad_out_summed.astype(f32),
         gain_grads[width : 2 * width],
-        early[0].astype(f32),
-        early[1].astype(f32),
-        early[2].astype(f32),
+        grad_gate_summed.astype(f32),
+        grad_up_summed.astype(f32),
+        grad_down_summed.astype(f32),
     )
 
 
 def solution(mesh):
     return jax.shard_map(
-        shards,
+        functools.partial(shards, dict(mesh.shape)),
         mesh=mesh,
         in_specs=(
             P("dp", "tensor", None),

time: 1320 us -> 934 us (0.71)
  waiting for transfers between devices: 831 us -> 1.13 us
  Pallas kernels: 138 us -> 606 us
  blocking collectives: 58.8 us -> 42.6 us
    pallas_call x0 -> x6, Pallas kernels: none -> 468 us  [the longest x1 269 us: sum_over_line(): pl.pallas_call(functools.partial(line_kernel, 'dp', tuple(widths)), out_s...]
    psum x2 -> x1, waiting for transfers between devices: 446 us -> 0.01 us  [shards(): lax.psum((grad_down, grad_gate_weight), 'dp')]
    reduce_scatter x4 -> x2, waiting for transfers between devices: 225 us -> 0.02 us  [scatter_rows(): lax.psum_scatter(partial, 'tensor', scatter_dimension=0, tiled=True)]
    all_gather x4 -> x1, waiting for transfers between devices: 160 us -> 0.01 us  [shards(): grad_gathered = lax.all_gather(grad_out_rows, 'tensor', axis=0, tiled=True)]
    psum x2 -> x0, blocking collectives: 58.8 us -> none  [the longest x1 39.8 us: shards(): lax.psum(jnp.concatenate([part_gain_attn, part_gain_ffn, grad_gain[0]]),...]
    all_gather x0 -> x1, blocking collectives: none -> 42.6 us  [sum_small(): return jnp.sum(lax.all_gather(vector, axes, axis=0, tiled=False), 0)]
    convert_element_type x8 -> x6, other arithmetic: 33.9 us -> 21.1 us  [the longest x2 6.88 us: shards(): pieces.append(grad_in_summed[:, at:at + w.shape[1]].astype(f32))]
  transfers between devices with their start and end apart: 10 -> 5, of which waited for: 10 -> 0; matrix products, arithmetic and copies ran while one was open for 13% -> 18% of each run, Pallas kernels for 5% -> 61%
where the time goes in v2:
time: 934 us; the launch traced here: 925 us
  Pallas kernels  606 us (65%)
  matrix products  181 us (19%)
  other arithmetic  44.6 us (5%)
  blocking collectives  42.6 us (5%)
  local copies, waits for them, and re-layouts  34.2 us (4%)
  between operations  15.4 us (2%)
    pallas_call x1, Pallas kernels, sum_over_line(): pl.pallas_call(functools.partial(line_kernel, 'dp', tuple(widths)), out_s...  269 us
    pallas_call x3, Pallas kernels, gather_rows(): pl.pallas_call(functools.partial(gather_kernel, 'tensor'), out_shape=jax....  119 us
    pallas_call x2, Pallas kernels, scatter_rows(): pl.pallas_call(functools.partial(scatter_kernel, 'tensor'), out_shape=jax...  79.8 us
    pallas_call x1, Pallas kernels, mixer_forward(): pl.pallas_call(functools.partial(forward_kernel, heads, key_dim, value_di...  75.8 us
    dot_general x5, matrix products, times_transposed(): lax.dot_general(left, right, (((1,), (1,)), ((), ())), preferred_element_...  66.7 us
    pallas_call x1, Pallas kernels, mixer_backward(): pl.pallas_call(functools.partial(backward_kernel, heads, key_dim, value_d...  62.7 us
    dot_general x5, matrix products, cross_rows(): lax.dot_general(left, right, (((0,), (0,)), ((), ())), preferred_element_...  56.3 us
    all_gather x1, blocking collectives, sum_small(): return jnp.sum(lax.all_gather(vector, axes, axis=0, tiled=False), 0)  42.6 us
  transfers between devices with their start and end apart: 5, of which 0 were waited for; matrix products, arithmetic and copies ran while one was open for 18% of the time, Pallas kernels for 61%

profile of v2, /device:TPU:0, one launch (start us, length us, event | category | flops | bytes accessed | tf_op | source)
XLA Modules:
  0.0 925.3 jit_solution(3322525171510257815)
XLA Ops:
  7.3 1.7 fusion.10
  8.9 0.7 convert_element_type.112
  9.6 0.6 copy-done.25
  10.2 2.5 fusion.4.x_ref
  12.8 41.3 %gather_rows.3 = bf16[2048,2048]{1,0:T(8,128)(2,1)} custom-call(bf16[256,2048]{1,0:T(8,128)(2,1)} %fusion.4.x_ref), custom_call_target="tpu_custom_call" | custom-call | bytes 1000000 | tf_op jit(solution)/shard_map/gather_rows/pallas_call | solution.py:646
  54.5 0.4 copy.68
  54.9 1.1 copy.69
  56.0 0.9 broadcast_in_dim.20
  56.8 11.3 %concatenate.9 = bf16[2048,1664]{1,0:T(8,128)(2,1)} concatenate(bf16[2048,256]{1,0:T(8,128)(2,1)} %param.24, bf16[2048,256]{1,0:T(8,128)(2,1)} %param.25, bf16[2048,512]{1,0:T(8,128)(2,1)} %param.26, bf16[2048,512]{1,0:T(8,128)(2,1)} %param.29, bf16[2048,2]{1,0:T(8,128)(2,1)S(1)} %copy.68, bf16[2048,2]{1,0:T(8,128)(2,1)} %copy.69, bf16[2048,124]{1,0:T(8,128)(2,1)} %broadcast_in_dim.20), dimensions={1} | concatenate | bytes 13631488 | tf_op jit(solution)/shard_map/concatenate | solution.py:946
  68.1 21.3 %fusion.17.proj_ref.eq_ref.ek_ref.ev_ref = f32[2048,1664]{1,0:T(8,128)} fusion(bf16[2048,2048]{1,0:T(8,128)(2,1)} %gather_rows.3, bf16[2048,1664]{1,0:T(8,128)(2,1)} %concatenate.9), kind=kOutput, calls=%fused_computation.52 | convolution fusion | flops 13958643712 | bytes 28835840 | tf_op jit(solution)/shard_map/dot_general | solution.py:948
  89.4 75.8 %mixer_forward.1 = (bf16[2048,512]{1,0:T(8,128)(2,1)S(1)}, f32[2,128,256]{2,1,0:T(8,128)}, bf16[8,2,128,256]{3,2,1,0:T(8,128)(2,1)S(1)}, bf16[8,2,256,256]{3,2,1...) custom-call(f32[2048,1664]{1,0:T(8,128)} %fusion.17.proj_ref.eq_ref.ek_ref.ev_ref, ...), custom_call_target="tpu_custom_call" | custom-call | bytes 200000000 | tf_op jit(solution)/shard_map/mixer_forward/pallas_call | solution.py:230
  165.3 4.7 convolution_convert_fusion.1.p_ref
  170.0 39.9 %scatter_rows.2 = f32[256,2048]{1,0:T(8,128)S(1)} custom-call(bf16[2048,2048]{1,0:T(8,128)(2,1)S(1)} %convolution_convert_fusion.1.p_ref), custom_call_target="tpu_custom_call" | custom-call | bytes 1000000 | tf_op jit(solution)/shard_map/scatter_rows/pallas_call | solution.py:742
  210.0 0.4 multiply_reduce_fusion.3
  210.4 1.3 copy-done.17
  211.7 1.2 multiply_convert_fusion.3.x_ref
  212.9 38.8 %gather_rows.4 = bf16[2048,2048]{1,0:T(8,128)(2,1)} custom-call(bf16[256,2048]{1,0:T(8,128)(2,1)} %multiply_convert_fusion.3.x_ref), custom_call_target="tpu_custom_call" | custom-call | bytes 1000000 | tf_op jit(solution)/shard_map/gather_rows/pallas_call | solution.py:646
  251.7 0.6 dynamic-slice
  252.9 10.9 %fusion.19 = f32[2048,688]{0,1:T(8,128)} fusion(bf16[2048,2048]{1,0:T(8,128)(2,1)} %gather_rows.4, bf16[2048,688]{0,1:T(8,128)(2,1)} %param.38), kind=kOutput, calls=%fused_computation.54 | convolution fusion | flops 5771362304 | bytes 16842752 | tf_op jit(solution)/shard_map/dot_general | solution.py:968
  263.8 11.0 %fusion.18 = f32[2048,688]{0,1:T(8,128)} fusion(bf16[2048,2048]{1,0:T(8,128)(2,1)} %all-gather.5.cloned.1.call-done, bf16[688,2048]{1,0:T(8,128)(2,1)} %param.40), kind=kOutput, calls=%fused_computation.53 | convolution fusion | flops 5771362304 | bytes 16842752 | tf_op jit(solution)/shard_map/dot_general | solution.py:900
  274.8 11.7 %multiply_convert_fusion = (bf16[2048,688]{0,1:T(8,128)(2,1)}, bf16[2048,688]{0,1:T(8,128)(2,1)S(1)}, bf16[2048,688]{0,1:T(8,128)(2,1)}) fusion(f32[2048,688]{0,1:T(8,128)S(1)} %copy-done.47, f32[2048,688]{0,1:T(8,128)} %fusion.18, bf16[2048,2048]{1,0:T(8,128)(2,1)S(1)} %copy-done.22, bf16[2048,688]{0,1:T(8,128)(2,1)S(1)} %copy-done), kind=kOutput, calls=%fused_computation.6 | convolution fusion | flops 5792497664 | bytes 30932992 | tf_op jit(solution)/shard_map/dot_general | solution.py:969
  286.6 7.7 convolution_convert_fusion.5
  294.3 10.3 %fusion.20 = f32[2048,2048]{1,0:T(8,128)} fusion(bf16[2048,688]{0,1:T(8,128)(2,1)S(1)} %get-tuple-element.164, bf16[2048,688]{0,1:T(8,128)(2,1)S(1)} %copy-done.42), kind=kOutput, calls=%fused_computation.55 | convolution fusion | flops 5771362304 | bytes 22413312 | tf_op jit(solution)/shard_map/dot_general | solution.py:900
  304.5 9.1 convolution_convert_fusion
  313.7 13.5 %add_convert_fusion.p_ref = bf16[2048,2048]{1,0:T(8,128)(2,1)} fusion(f32[2048,2048]{1,0:T(8,128)} %fusion.20, bf16[2048,688]{0,1:T(8,128)(2,1)} %get-tuple-element.165, bf16[2048,688]{0,1:T(8,128)(2,1)S(1)} %copy-done), kind=kOutput, calls=%fused_computation | convolution fusion | flops 5779750912 | bytes 30801920 | tf_op jit(solution)/shard_map/dot_general | solution.py:900
  327.2 10.7 %convolution_convert_fusion.6 = bf16[688,2048]{1,0:T(8,128)(2,1)} fusion(bf16[2048,688]{0,1:T(8,128)(2,1)S(1)} %copy-done.50, bf16[2048,2048]{1,0:T(8,128)(2,1)} %all-gather.5.cloned.1.call-done), kind=kOutput, calls=%fused_computation.13 | convolution fusion | flops 5772771328 | bytes 14024704 | tf_op jit(solution)/shard_map/dot_general | solution.py:896
  337.9 3.4 copy-done.3
  341.3 39.9 %scatter_rows.3 = f32[256,2048]{1,0:T(8,128)S(1)} custom-call(bf16[2048,2048]{1,0:T(8,128)(2,1)S(1)} %copy-done.3), custom_call_target="tpu_custom_call" | custom-call | bytes 1000000 | tf_op jit(solution)/shard_map/scatter_rows/pallas_call | solution.py:742
  381.2 0.6 multiply_reduce_fusion.1
  381.8 1.4 copy-done.21
  383.2 1.6 fusion.12.x_ref
  384.8 38.9 %gather_rows.5 = bf16[2048,2048]{1,0:T(8,128)(2,1)} custom-call(bf16[256,2048]{1,0:T(8,128)(2,1)} %fusion.12.x_ref), custom_call_target="tpu_custom_call" | custom-call | bytes 1000000 | tf_op jit(solution)/shard_map/gather_rows/pallas_call | solution.py:646
  423.7 10.6 %fusion.21.grad_ref = f32[2048,512]{1,0:T(8,128)} fusion(bf16[2048,2048]{1,0:T(8,128)(2,1)} %gather_rows.5, bf16[512,2048]{1,0:T(8,128)(2,1)} %param.36), kind=kOutput, calls=%fused_computation.56 | convolution fusion | flops 4294967296 | bytes 14680064 | tf_op jit(solution)/shard_map/dot_general | solution.py:900
  434.4 62.7 %mixer_backward.1 = (bf16[2048,1664]{1,0:T(8,128)(2,1)}, f32[4,256]{1,0:T(4,128)}, f32[4,256]{1,0:T(4,128)}, f32[4,512]{1,0:T(4,128)}, f32[1,2]{1,0:T(1,128)}, /*index=5*/f32[1,2]{1,0:T(1,128)}, f32[1,256]{1,0:T(1,128)}) custom-call(f32[2048,1664]{1,0:T(8,128)} %fusion.17.proj_ref.eq_ref.ek_ref.ev_ref, f32[2048,1664]{1,0:T(8,128)} %fusion.17.proj_ref.eq_ref.ek_ref.ev_ref, ...), custom_call_target="tpu_custom_call" | custom-call | bytes 200000000 | tf_op jit(solution)/shard_map/mixer_backward/pallas_call | solution.py:482
  497.1 21.3 %convolution_convert_fusion.2 = bf16[2048,2048]{1,0:T(8,128)(2,1)} fusion(bf16[2048,1664]{1,0:T(8,128)(2,1)} %get-tuple-element.55, bf16[2048,1664]{1,0:T(8,128)(2,1)} %concatenate.9), kind=kOutput, calls=%fused_computation.4 | convolution fusion | flops 13962838016 | bytes 22020096 | tf_op jit(solution)/shard_map/dot_general | solution.py:900
  518.4 9.3 %convolution_convert_fusion.7.refs_1_ = bf16[512,2048]{1,0:T(8,128)(2,1)} fusion(bf16[2048,512]{1,0:T(8,128)(2,1)S(1)} %copy-done.16, bf16[2048,2048]{1,0:T(8,128)(2,1)} %gather_rows.5), kind=kOutput, calls=%fused_computation.17 | convolution fusion | flops 4296015872 | bytes 12582912 | tf_op jit(solution)/shard_map/dot_general | solution.py:896
  527.8 10.8 %convolution_convert_fusion.4.refs_0_ = bf16[2048,688]{1,0:T(8,128)(2,1)} fusion(bf16[2048,2048]{1,0:T(8,128)(2,1)} %gather_rows.4, bf16[2048,688]{0,1:T(8,128)(2,1)S(1)} %copy-done.48), kind=kOutput, calls=%fused_computation.11 | convolution fusion | flops 5772771328 | bytes 14024704 | tf_op jit(solution)/shard_map/dot_general | solution.py:896
  538.6 17.9 %convolution_convert_fusion.3.refs_2_ = bf16[2048,1664]{1,0:T(8,128)(2,1)} fusion(bf16[2048,2048]{1,0:T(8,128)(2,1)S(1)} %bitcast.79, bf16[2048,1664]{1,0:T(8,128)(2,1)S(1)} %bitcast.96), kind=kOutput, calls=%fused_computation.5 | convolution fusion | flops 13962051584 | bytes 22020096 | tf_op jit(solution)/shard_map/dot_general | solution.py:896
  556.5 1.1 convert_bitcast_fusion
  557.6 0.3 copy.75
  558.1 0.7 dynamic-update-slice
  558.8 0.7 copy-done.24
  559.5 0.5 reduce-scatter.5.cloned.1.call-update
  560.1 0.5 reduce-scatter.3.cloned.1.call-update
  560.7 6.7 multiply_reduce_fusion
  567.5 42.6 %all-gather.2 = f32[32,1,4352]{2,1,0:T(1,128)S(1)} all-gather(f32[1,1,4352]{2,1,0:T(1,128)S(1)} %reshape.119), channel_id=2, replica_groups=mesh['dp'=4,'tensor'=8] {'dp','tensor'}, dimensions={0}, use_global_device_ids=true | all-gather | bytes 574464 | tf_op jit(solution)/shard_map/all_gather | solution.py:909
  610.4 0.6 slice.83
  611.0 269.2 %sum_over_line.1 = (bf16[2048,688]{1,0:T(8,128)(2,1)}, bf16[512,2048]{1,0:T(8,128)(2,1)}, bf16[2048,1536]{1,0:T(8,128)(2,1)}) custom-call(bf16[2048,688]{1,0:T(8,128)(2,1)} %convolution_convert_fusion.4.refs_0_, bf16[512,2048]{1,0:T(8,128)(2,1)} %convolution_convert_fusion.7.refs_1_, bf16[2048,1664]{1,0:T(8,128)(2,1)} %convolution_convert_fusion.3.refs_2_), custom_call_target="tpu_custom_call" | custom-call | bytes 5603328 | tf_op jit(solution)/shard_map/sum_over_line/pallas_call | solution.py:877
  880.1 4.1 convert_element_type.142
  884.3 5.2 copy.76
  889.4 5.2 convert_element_type.143
  894.6 3.2 convert_element_type.145
  897.9 0.6 fusion.16
  898.5 2.3 slice_convert_fusion.2
  900.8 4.6 slice_convert_fusion
  905.4 1.1 reshape.115
  906.6 0.6 reshape.108
  907.3 0.6 slice.66
  907.9 0.6 reshape.107
  908.5 0.6 reshape.106
  909.1 0.6 slice.64
  909.7 0.6 fusion.13
  910.3 1.8 fusion.5
  912.2 6.4 fusion.9
  (150 shorter events, 1.4 us)
Async XLA Ops:
  7.2 267.6 %copy-start = (bf16[2048,688]{0,1:T(8,128)(2,1)S(1)}, bf16[2048,688]{0,1:T(8,128)(2,1)}, u32[]{:S(2)}) copy-start(bf16[2048,688]{0,1:T(8,128)(2,1)} %param.39) | copy-start | bytes 8454148
  7.2 256.6 %all-gather.5.cloned.1.call-start = ((), (), s32[]{:S(2)}) async-start(), calls=%async_computation.2 | async-start | bytes 9437184 | tf_op jit(solution)/shard_map/all_gather | solution.py:959
  8.9 0.7 copy-start.28
  9.6 0.6 copy-start.25
  12.7 41.5 %copy-start.14 = (f32[2]{0:T(128)S(1)}, f32[2]{0:T(128)}, u32[]{:S(2)}) copy-start(f32[2]{0:T(128)} %param.34) | copy-start | bytes 28
  12.7 41.6 %copy-start.13 = (f32[2]{0:T(128)S(1)}, f32[2]{0:T(128)}, u32[]{:S(2)}) copy-start(f32[2]{0:T(128)} %param.33) | copy-start | bytes 28
  12.7 41.7 %copy-start.45 = (bf16[256]{0:T(256)(128)(2,1)S(1)}, bf16[256]{0:T(256)(128)(2,1)}, u32[]{:S(2)}) copy-start(bf16[256]{0:T(256)(128)(2,1)} %param.35) | copy-start | bytes 1540
  12.7 41.7 %copy-start.37 = (bf16[4,256]{1,0:T(4,128)(2,1)S(1)}, bf16[4,256]{1,0:T(4,128)(2,1)}, u32[]{:S(2)}) copy-start(bf16[4,256]{1,0:T(4,128)(2,1)} %param.30) | copy-start | bytes 6148
  12.7 41.7 %copy-start.38 = (bf16[4,256]{1,0:T(4,128)(2,1)S(1)}, bf16[4,256]{1,0:T(4,128)(2,1)}, u32[]{:S(2)}) copy-start(bf16[4,256]{1,0:T(4,128)(2,1)} %param.31) | copy-start | bytes 6148
  12.8 41.7 %copy-start.33 = (bf16[2048]{0:T(1024)(128)(2,1)S(1)}, bf16[2048]{0:T(1024)(128)(2,1)}, u32[]{:S(2)}) copy-start(bf16[2048]{0:T(1024)(128)(2,1)} %param.37) | copy-start | bytes 12292
  12.8 41.7 %copy-start.34 = (bf16[4,512]{1,0:T(4,128)(2,1)S(1)}, bf16[4,512]{1,0:T(4,128)(2,1)}, u32[]{:S(2)}) copy-start(bf16[4,512]{1,0:T(4,128)(2,1)} %param.32) | copy-start | bytes 12292
  12.8 41.7 %copy-start.30 = (bf16[2048,2]{0,1:T(2,128)(2,1)S(1)}, bf16[2048,2]{0,1:T(2,128)(2,1)}, u32[]{:S(2)}) copy-start(bf16[2048,2]{0,1:T(2,128)(2,1)} %param.27) | copy-start | bytes 24580
  12.8 42.1 %copy-start.31 = (bf16[2048,2]{0,1:T(2,128)(2,1)S(1)}, bf16[2048,2]{0,1:T(2,128)(2,1)}, u32[]{:S(2)}) copy-start(bf16[2048,2]{0,1:T(2,128)(2,1)} %param.28) | copy-start | bytes 24580
  54.1 502.4 %all-reduce.7.cloned.1.call-start = ((), (), s32[]{:S(2)}) async-start(), calls=%async_computation.6 | async-start | bytes 11272192 | tf_op jit(solution)/shard_map/psum | solution.py:981
  54.3 35.1 %copy-start.10 = (f32[2,1]{1,0:T(2,128)}, f32[2,1]{1,0:T(2,128)S(1)}, u32[]{:S(2)}) copy-start(f32[2,1]{1,0:T(2,128)S(1)} %copy.71.db_col_ref) | copy-start | bytes 28
  54.4 35.0 %copy-start.11 = (f32[2,1]{1,0:T(2,128)}, f32[2,1]{1,0:T(2,128)S(1)}, u32[]{:S(2)}) copy-start(f32[2,1]{1,0:T(2,128)S(1)} %copy.70.dl_col_ref) | copy-start | bytes 28
  54.4 35.0 %copy-start.12 = (f32[256]{0:T(256)}, f32[256]{0:T(256)S(1)}, u32[]{:S(2)}) copy-start(f32[256]{0:T(256)S(1)} %broadcast_in_dim.52) | copy-start | bytes 3076
  54.4 35.0 %copy-start.8 = (f32[4,256]{1,0:T(4,128)}, f32[4,256]{1,0:T(4,128)S(1)}, u32[]{:S(2)}) copy-start(f32[4,256]{1,0:T(4,128)S(1)} %convert_element_type.114.tq_ref) | copy-start | bytes 12292
  54.5 34.9 %copy-start.9 = (f32[4,256]{1,0:T(4,128)}, f32[4,256]{1,0:T(4,128)S(1)}, u32[]{:S(2)}) copy-start(f32[4,256]{1,0:T(4,128)S(1)} %convert_element_type.115.tk_ref) | copy-start | bytes 12292
  54.5 34.9 %copy-start.7 = (f32[4,512]{1,0:T(4,128)}, f32[4,512]{1,0:T(4,128)S(1)}, u32[]{:S(2)}) copy-start(f32[4,512]{1,0:T(4,128)S(1)} %convert_element_type.116.tv_ref) | copy-start | bytes 24580
  68.1 21.3 %copy-start.6 = (f32[1,2,128,256]{3,2,1,0:T(8,128)S(1)}, f32[1,2,128,256]{3,2,1,0:T(8,128)}, u32[]{:S(2)}) copy-start(f32[1,2,128,256]{3,2,1,0:T(8,128)} %param.22) | copy-start | bytes 786436
  89.4 75.8 %copy-start.44 = (bf16[512,2048]{1,0:T(8,128)(2,1)S(1)}, bf16[512,2048]{1,0:T(8,128)(2,1)}, u32[]{:S(2)}) copy-start(bf16[512,2048]{1,0:T(8,128)(2,1)} %param.36) | copy-start | bytes 6291460
  165.2 4.8 copy-start.4
  165.3 4.8 copy-start.5
  165.3 4.8 copy-start.15
  170.0 40.0 %copy-start.19 = (bf16[1,256,2048]{2,1,0:T(8,128)(2,1)S(1)}, bf16[1,256,2048]{2,1,0:T(8,128)(2,1)}, u32[]{:S(2)}) copy-start(bf16[1,256,2048]{2,1,0:T(8,128)(2,1)} %param.21) | copy-start | bytes 3145732
  210.4 1.3 copy-start.17
  212.9 38.8 %copy-start.46 = (u32[32]{0:T(128)S(1)}, u32[32]{0:T(128)}, u32[]{:S(2)}) copy-start(u32[32]{0:T(128)} %constant.23) | copy-start | bytes 388
  263.8 11.0 %copy-start.22 = (bf16[2048,2048]{1,0:T(8,128)(2,1)S(1)}, bf16[2048,2048]{1,0:T(8,128)(2,1)}, u32[]{:S(2)}) copy-start(bf16[2048,2048]{1,0:T(8,128)(2,1)} %gather_rows.4) | copy-start | bytes 25165828
  263.8 11.0 %copy-start.47 = (f32[2048,688]{0,1:T(8,128)S(1)}, f32[2048,688]{0,1:T(8,128)}, u32[]{:S(2)}) copy-start(f32[2048,688]{0,1:T(8,128)} %fusion.19) | copy-start | bytes 16908292
  286.6 7.7 copy-start.42
  294.3 10.3 %copy-start.43 = (bf16[688,2048]{1,0:T(8,128)(2,1)S(1)}, bf16[688,2048]{1,0:T(8,128)(2,1)}, u32[]{:S(2)}) copy-start(bf16[688,2048]{1,0:T(8,128)(2,1)} %param.40) | copy-start | bytes 8454148
  294.3 10.3 %copy-start.49 = (bf16[2048,688]{0,1:T(8,128)(2,1)S(1)}, bf16[2048,688]{0,1:T(8,128)(2,1)}, u32[]{:S(2)}) copy-start(bf16[2048,688]{0,1:T(8,128)(2,1)} %get-tuple-element.163) | copy-start | bytes 8454148
  313.7 13.5 %copy-start.50 = (bf16[2048,688]{0,1:T(8,128)(2,1)S(1)}, bf16[2048,688]{0,1:T(8,128)(2,1)}, u32[]{:S(2)}) copy-start(bf16[2048,688]{0,1:T(8,128)(2,1)} %get-tuple-element.163) | copy-start | bytes 8454148
  337.9 567.5 %all-reduce.5.cloned.1.call-start = ((), (), s32[]{:S(2)}) async-start(), calls=%async_computation.5 | async-start | bytes 401408
  337.9 3.4 copy-start.3
  341.3 39.9 %copy-start.18 = (f32[256,2048]{1,0:T(8,128)S(1)}, f32[256,2048]{1,0:T(8,128)}, u32[]{:S(2)}) copy-start(f32[256,2048]{1,0:T(8,128)} %copy-done.17) | copy-start | bytes 6291460
  381.2 3.6 copy-start.2
  381.2 2.0 copy-start.21
  497.1 21.3 %copy-start.16 = (bf16[2048,512]{1,0:T(8,128)(2,1)S(1)}, bf16[2048,512]{1,0:T(8,128)(2,1)}, u32[]{:S(2)}) copy-start(bf16[2048,512]{1,0:T(8,128)(2,1)} %copy-done.15) | copy-start | bytes 6291460
  518.4 9.3 %copy-start.36 = (f32[4,256]{1,0:T(4,128)S(1)}, f32[4,256]{1,0:T(4,128)}, u32[]{:S(2)}) copy-start(f32[4,256]{1,0:T(4,128)} %get-tuple-element.64) | copy-start | bytes 12292
  518.4 9.3 %copy-start.35 = (f32[4,256]{1,0:T(4,128)S(1)}, f32[4,256]{1,0:T(4,128)}, u32[]{:S(2)}) copy-start(f32[4,256]{1,0:T(4,128)} %get-tuple-element.65) | copy-start | bytes 12292
  518.4 9.3 %copy-start.32 = (f32[4,512]{1,0:T(4,128)S(1)}, f32[4,512]{1,0:T(4,128)}, u32[]{:S(2)}) copy-start(f32[4,512]{1,0:T(4,128)} %get-tuple-element.66) | copy-start | bytes 24580
  518.4 9.3 %copy-start.48 = (bf16[2048,688]{0,1:T(8,128)(2,1)S(1)}, bf16[2048,688]{0,1:T(8,128)(2,1)}, u32[]{:S(2)}) copy-start(bf16[2048,688]{0,1:T(8,128)(2,1)} %get-tuple-element.165) | copy-start | bytes 8454148
  518.4 20.1 %slice-start = ((s8[8388608]{0:T(1024)(128)(4,1)}), s8[4194304]{0:T(1024)(128)(4,1)S(1)}, s32[]{:S(2)}) async-start(s8[8388608]{0:T(1024)(128)(4,1)} %bitcast.78), calls=%async_computation.7 | async-start | bytes 8388608
  518.4 20.1 %slice-start.4 = ((s8[6815744]{0:T(1024)(128)(4,1)}), s8[4194304]{0:T(1024)(128)(4,1)S(1)}, s32[]{:S(2)}) async-start(s8[6815744]{0:T(1024)(128)(4,1)} %bitcast.95), calls=%async_computation.11 | async-start | bytes 8388608
  527.7 10.8 %slice-start.1 = ((s8[8388608]{0:T(1024)(128)(4,1)}), s8[4194304]{0:T(1024)(128)(4,1)S(1)}, s32[]{:S(2)}) async-start(s8[8388608]{0:T(1024)(128)(4,1)} %bitcast.78), calls=%async_computation.8 | async-start | bytes 8388608
  527.7 10.8 %slice-start.5 = ((s8[6815744]{0:T(1024)(128)(4,1)}), s8[2621440]{0:T(1024)(128)(4,1)S(1)}, s32[]{:S(2)}) async-start(s8[6815744]{0:T(1024)(128)(4,1)} %bitcast.95), calls=%async_computation.12 | async-start | bytes 5242880
  538.5 19.4 %copy-start.40 = (f32[1,2]{1,0:T(1,128)S(1)}, f32[1,2]{1,0:T(1,128)}, u32[]{:S(2)}) copy-start(f32[1,2]{1,0:T(1,128)} %get-tuple-element.67) | copy-start | bytes 28
  538.6 19.4 %copy-start.41 = (f32[1,2]{1,0:T(1,128)S(1)}, f32[1,2]{1,0:T(1,128)}, u32[]{:S(2)}) copy-start(f32[1,2]{1,0:T(1,128)} %get-tuple-element.68) | copy-start | bytes 28
  558.8 0.7 copy-start.24
  559.5 350.8 %reduce-scatter.5.cloned.1.call-start = ((), (), s32[]{:S(2)}) async-start(), calls=%async_computation.4 | async-start | bytes 9437184 | tf_op jit(solution)/shard_map/reduce_scatter | solution.py:738
  560.1 352.1 %reduce-scatter.3.cloned.1.call-start = ((), (), s32[]{:S(2)}) async-start(), calls=%async_computation.3 | async-start | bytes 9437184 | tf_op jit(solution)/shard_map/reduce_scatter | solution.py:738
  560.7 6.8 copy-start.27
  560.7 6.8 copy-start.39
  889.4 5.2 copy-start.23
  889.4 9.0 slice-start.2
  894.6 3.9 slice-start.3
  900.8 9.6 %copy-start.20 = (bf16[1,256,2048]{2,1,0:T(8,128)(2,1)S(1)}, bf16[1,256,2048]{2,1,0:T(8,128)(2,1)}, u32[]{:S(2)}) copy-start(bf16[1,256,2048]{2,1,0:T(8,128)(2,1)} %param.21) | copy-start | bytes 3145732
  900.8 9.6 %copy-start.26 = (f32[2048]{0:T(1024)S(1)}, f32[2048]{0:T(1024)}, u32[]{:S(2)}) copy-start(f32[2048]{0:T(1024)} %copy-done.25) | copy-start | bytes 24580
  900.8 9.6 %copy-start.29 = (f32[256]{0:T(256)S(1)}, f32[256]{0:T(256)}, u32[]{:S(2)}) copy-start(f32[256]{0:T(256)} %copy-done.28) | copy-start | bytes 3076
  912.1 6.4 copy-start.1
Sparse Core Ops, SparseCore 0:
  54.3 54.8 all-gather.4
  338.0 202.3 all-reduce.6
  559.6 34.8 all-reduce.4
  598.2 71.3 reduce-scatter.4
  672.9 71.2 reduce-scatter.2

commit v3 on v2

--- a/solution.py
+++ b/solution.py
@@ -766,27 +766,57 @@
 CHUNK = 64
 
 
-def line_kernel(axis, widths, *refs):
+def chunk_rows(rows):
+    return next((c for c in range(CHUNK, 0, -16) if rows % c == 0), rows)
+
+
+def line_kernel(axis, cross, widths, *refs):
     count = len(widths)
     g_refs, out_refs = refs[:count], refs[count : 2 * count]
-    scratch = refs[2 * count :]
+    both_ref, parts, part_sems = refs[2 * count], refs[2 * count + 1], refs[2 * count + 2]
+    scratch = refs[2 * count + 3 :]
+    peers = parts.shape[0]
+    me = lax.axis_index(cross)
     z = lax.axis_index(axis)
     near = z + 1 - 2 * (z % 2)
     across = 3 - z
     inner = (z * (3 - z)) > 0
     barrier = pltpu.get_barrier_semaphore()
     pl.semaphore_signal(barrier, inc=1, device_id={axis: near}, device_id_type=pl.DeviceIdType.MESH)
+    for k in range(1, peers):
+        pl.semaphore_signal(
+            barrier, inc=1, device_id={cross: (me + k) % peers}, device_id_type=pl.DeviceIdType.MESH
+        )
 
     @pl.when(inner)
     def _():
         pl.semaphore_signal(
             barrier, inc=1, device_id={axis: across}, device_id_type=pl.DeviceIdType.MESH
         )
-        pl.semaphore_wait(barrier, 2)
+        pl.semaphore_wait(barrier, peers + 1)
 
     @pl.when(jnp.logical_not(inner))
     def _():
-        pl.semaphore_wait(barrier, 1)
+        pl.semaphore_wait(barrier, peers)
+
+    def spread(k):
+        return copy_to(
+            out_refs[0].at[pl.ds(0, parts.shape[1]), :],
+            parts.at[k],
+            part_sems.at[0, k],
+            part_sems.at[1, k],
+            cross,
+            (me + k) % peers,
+        )
+
+    own_part = pltpu.make_async_copy(
+        out_refs[0].at[pl.ds(0, parts.shape[1]), :], parts.at[0], part_sems.at[0, 0]
+    )
+
+    def spread_all():
+        own_part.start()
+        for k in range(1, peers):
+            spread(k).start()
 
     groups = []
     for i in range(count):
@@ -825,25 +855,28 @@
     def _():
         for chunks, _, _, _, _, _, inward, _, _, _ in groups:
             each(chunks, lambda c: inward(c).start())
-        for chunks, _, _, _, _, _, inward, _, outward, _ in groups:
+        for i, (chunks, _, _, _, _, _, inward, _, outward, _) in enumerate(groups):
             each(chunks, lambda c: outward(c).wait_recv())
             each(chunks, lambda c: inward(c).wait_send())
+            if i == 0:
+                spread_all()
 
     @pl.when(inner)
     def _():
         for chunks, _, _, _, _, load, _, _, _, _ in groups:
             each(chunks, lambda c: load(c).start())
-        for chunks, own, from_out, from_in, total, load, inward, middle, outward, keep in groups:
+        for i, group in enumerate(groups):
+            chunks, own, from_out, from_in, total, load, inward, middle, outward, keep = group
 
             def first(c):
                 load(c).wait()
                 inward(c).wait_recv()
-                own[c] = (own[c].astype(f32) + from_out[c].astype(f32)).astype(bf16)
+                own[c] = (own[c].astype(f32) + from_out[c].astype(f32)).astype(own.dtype)
                 middle(c).start()
 
             def second(c):
                 middle(c).wait_recv()
-                total[c] = (own[c].astype(f32) + from_in[c].astype(f32)).astype(bf16)
+                total[c] = (own[c].astype(f32) + from_in[c].astype(f32)).astype(total.dtype)
                 outward(c).start()
                 keep(c).start()
 
@@ -853,37 +886,56 @@
                 first(c + 1)
                 second(c)
 
-            each(chunks - 1, both)
+            if chunks > 1:
+                each(chunks - 1, both)
             second(chunks - 1)
-        for chunks, _, _, _, _, _, _, middle, outward, keep in groups:
+            if i == 0:
+                each(chunks, lambda c: keep(c).wait())
+                spread_all()
+        for i, (chunks, _, _, _, _, _, _, middle, outward, keep) in enumerate(groups):
+
             def settle(c):
                 middle(c).wait_send()
                 outward(c).wait_send()
-                keep(c).wait()
+                if i > 0:
+                    keep(c).wait()
 
             each(chunks, settle)
 
-
-def sum_over_line(arrays, widths, identity, sizes):
+    own_part.wait()
+    total = parts[0]
+    for k in range(1, peers):
+        spread(k).wait_recv()
+        total = total + parts[k]
+    both_ref[...] = total
+    for k in range(1, peers):
+        spread(k).wait_send()
+
+
+def sum_over_line(arrays, widths, both, identity, sizes):
     if not square(sizes):
-        return lax.psum(tuple(a[:, :w] for a, w in zip(arrays, widths)), "dp")
-    scratch = []
+        summed = lax.psum(tuple(a[:, :w] for a, w in zip(arrays, widths)), "dp")
+        return summed + (lax.psum(summed[0][:both], "tensor"),)
+    peers = sizes["tensor"]
+    scratch = [pltpu.VMEM((peers, both, widths[0]), arrays[0].dtype), pltpu.SemaphoreType.DMA((2, peers))]
     for a, w in zip(arrays, widths):
-        chunks = a.shape[0] // CHUNK
-        scratch += [pltpu.VMEM((chunks, CHUNK, w), bf16)] * 4
+        chunk = chunk_rows(a.shape[0])
+        chunks = a.shape[0] // chunk
+        scratch += [pltpu.VMEM((chunks, chunk, w), a.dtype)] * 4
         scratch.append(pltpu.SemaphoreType.DMA((8, chunks)))
     anywhere = pl.BlockSpec(memory_space=pl.ANY)
     total = sum(a.shape[0] * w for a, w in zip(arrays, widths))
     return pl.pallas_call(
-        functools.partial(line_kernel, "dp", tuple(widths)),
-        out_shape=tuple(jax.ShapeDtypeStruct((a.shape[0], w), bf16) for a, w in zip(arrays, widths)),
+        functools.partial(line_kernel, "dp", "tensor", tuple(widths)),
+        out_shape=tuple(jax.ShapeDtypeStruct((a.shape[0], w), a.dtype) for a, w in zip(arrays, widths))
+        + (jax.ShapeDtypeStruct((both, widths[0]), arrays[0].dtype),),
         in_specs=[anywhere] * len(arrays),
-        out_specs=(anywhere,) * len(arrays),
+        out_specs=(anywhere,) * len(arrays) + (pl.BlockSpec(memory_space=pltpu.VMEM),),
         scratch_shapes=scratch,
         compiler_params=pltpu.CompilerParams(
             collective_id=identity, has_side_effects=True, vmem_limit_bytes=56 * 1024 * 1024
         ),
-        cost_estimate=pl.CostEstimate(flops=0, bytes_accessed=total, transcendentals=0),
+        cost_estimate=pl.CostEstimate(flops=0, bytes_accessed=200 * total, transcendentals=0),
         name="sum_over_line",
     )(*arrays)
 
@@ -903,10 +955,6 @@
 def norm_backward(grad_normed, scaled, factor, gain_value):
     weighted = grad_normed * gain_value
     return factor * (weighted - scaled * jnp.mean(weighted * scaled, -1, keepdims=True))
-
-
-def sum_small(vector, axes):
-    return jnp.sum(lax.all_gather(vector, axes, axis=0, tiled=False), 0)
 
 
 def shards(
@@ -970,77 +1018,90 @@
     sigmoid_gate = jax.nn.sigmoid(gate_proj)
     activated = gate_proj * sigmoid_gate
     inner = (activated * up_proj).astype(bf16)
+    grad_down = cross_rows(inner, grad_gathered).astype(bf16)
+    grad_gathered, grad_down = lax.optimization_barrier((grad_gathered, grad_down))
+    grad_down_summed = lax.psum(grad_down, "dp")
     grad_inner = times_transposed(grad_gathered, w_ffn_down)
     grad_gate_rows = (
         grad_inner * up_proj * sigmoid_gate * (1.0 + gate_proj * (1.0 - sigmoid_gate))
     ).astype(bf16)
     grad_up_rows = (grad_inner * activated).astype(bf16)
-    grad_down = cross_rows(inner, grad_gathered).astype(bf16)
-    grad_gate_weight = cross_rows(gathered_ffn, grad_gate_rows).astype(bf16)
-    grad_up_weight = cross_rows(gathered_ffn, grad_up_rows).astype(bf16)
-    grad_down_summed, grad_gate_summed = lax.psum((grad_down, grad_gate_weight), "dp")
     part_normed_ffn = (
         times_transposed(grad_gate_rows, w_ffn_gate) + times_transposed(grad_up_rows, w_ffn_up)
     ).astype(bf16)
-    part_normed_ffn, grad_down, grad_gate_weight = lax.optimization_barrier(
-        (part_normed_ffn, grad_down, grad_gate_weight)
-    )
+    grad_gate_weight = cross_rows(grad_gate_rows, gathered_ffn).astype(bf16)
+    part_normed_ffn, grad_gate_weight = lax.optimization_barrier((part_normed_ffn, grad_gate_weight))
+    grad_gate_weight, grad_down_summed = lax.optimization_barrier((grad_gate_weight, grad_down_summed))
+    grad_gate_summed = lax.psum(grad_gate_weight, "dp")
     grad_normed_ffn = scatter_rows(part_normed_ffn, 3, sizes)
     part_gain_ffn = jnp.sum(grad_normed_ffn * scaled_ffn, 0)
     grad_hidden = grad_out_rows.astype(f32) + norm_backward(
         grad_normed_ffn, scaled_ffn, factor_ffn, gain_second
     )
     grad_attended = gather_rows(grad_hidden.astype(bf16), 4, sizes)
+    grad_attended, grad_down_summed = lax.optimization_barrier((grad_attended, grad_down_summed))
     grad_mixed = times_transposed(grad_attended, w_out)
+    grad_up_weight = cross_rows(grad_up_rows, gathered_ffn).astype(bf16)
     ffn_part = jnp.dot(inner, w_ffn_down, preferred_element_type=f32).astype(bf16)
-    grad_out_weight = cross_rows(mixed, grad_attended).astype(bf16)
     grad_projected, grad_tq, grad_tk, grad_tv, grad_dl, grad_db, grad_gain = mixer_backward(
         projected, *extras, states, inverse, update, raw, grad_mixed
     )
+    grad_projected, grad_gate_summed = lax.optimization_barrier((grad_projected, grad_gate_summed))
+    grad_out_weight = cross_rows(mixed, grad_attended).astype(bf16)
+    grad_out_weight, grad_gate_summed = lax.optimization_barrier((grad_out_weight, grad_gate_summed))
+    grad_out_summed = lax.psum(grad_out_weight, "dp")
     part_normed = times_transposed(grad_projected, w_in).astype(bf16)
     grad_in = cross_rows(gathered, grad_projected).astype(bf16)
+    part_gain_attn = jnp.sum(grad_in.astype(f32) * w_in.astype(f32), 1) / gain_first
+    grad_ab = grad_in[:, main : main + 2 * heads].astype(f32).T
+    smalls = (part_gain_attn, part_gain_ffn, grad_gain[0], grad_tq, grad_tk, grad_tv, grad_dl[0], grad_db[0], grad_ab)
+    used = sum(a.size for a in smalls)
+    smalls_rows = -(-used // (16 * 128)) * 16
+    small = jnp.concatenate([a.reshape(-1) for a in smalls] + [jnp.zeros((smalls_rows * 128 - used,), f32)])
     (
         grad_in,
-        grad_out_weight,
         grad_up_weight,
+        small,
         part_normed,
         ffn_part,
         grad_down_summed,
         grad_gate_summed,
+        grad_out_summed,
     ) = lax.optimization_barrier(
         (
             grad_in,
-            grad_out_weight,
             grad_up_weight,
+            small,
             part_normed,
             ffn_part,
             grad_down_summed,
             grad_gate_summed,
+            grad_out_summed,
         )
     )
     grad_normed = scatter_rows(part_normed, None, sizes)
     ffn_out = scatter_rows(ffn_part, None, sizes)
     output = (hidden + ffn_out).astype(bf16)
-    part_gain_attn = jnp.sum(grad_in.astype(f32) * w_in.astype(f32), 1) / gain_first
-    gain_grads = sum_small(
-        jnp.concatenate([part_gain_attn, part_gain_ffn, grad_gain[0]]), ("dp", "tensor")
-    )
-    grad_ab = grad_in[:, main : main + 2 * heads].astype(f32).T
-    smalls = (grad_tq, grad_tk, grad_tv, grad_dl[0], grad_db[0], grad_ab)
-    small = sum_small(jnp.concatenate([a.reshape(-1) for a in smalls]), "dp")
-    small_summed, at = [], 0
-    for a in smalls:
-        small_summed.append(small[at : at + a.size].reshape(a.shape))
+    gains = 2 * width + out_gain.shape[0]
+    small_summed, grad_up_summed, grad_in_summed, gain_grads = sum_over_line(
+        (small.reshape(smalls_rows, 128), grad_up_weight, grad_in),
+        (128, width, main),
+        -(-gains // (16 * 128)) * 16,
+        5,
+        sizes,
+    )
+    small_summed = small_summed.reshape(-1)
+    gain_grads = gain_grads.reshape(-1)
+    small_parts, at = [], gains
+    for a in smalls[3:]:
+        small_parts.append(small_summed[at : at + a.size].reshape(a.shape))
         at += a.size
-    grad_up_summed, grad_out_summed, grad_in_summed = sum_over_line(
-        (grad_up_weight, grad_out_weight, grad_in), (grad_up_weight.shape[1], width, main), 5, sizes
-    )
     grad_inputs = grad_hidden + norm_backward(grad_normed, scaled_attn, factor_attn, gain_first)
     pieces, at = [], 0
     for w in (w_query, w_key, w_value, w_gate_out):
         pieces.append(grad_in_summed[:, at : at + w.shape[1]].astype(f32))
         at += w.shape[1]
-    grad_ab = small_summed[5]
+    grad_ab = small_parts[5]
     return (
         output[None],
         final[None],
@@ -1052,16 +1113,16 @@
         grad_ab[:heads].T,
         grad_ab[heads:].T,
         pieces[3],
-        small_summed[0],
-        small_summed[1],
-        small_summed[2],
-        small_summed[3],
-        small_summed[4],
-        gain_grads[2 * width :],
+        small_parts[0],
+        small_parts[1],
+        small_parts[2],
+        small_parts[3],
+        small_parts[4],
+        gain_grads[2 * width : gains],
         grad_out_summed.astype(f32),
         gain_grads[width : 2 * width],
-        grad_gate_summed.astype(f32),
-        grad_up_summed.astype(f32),
+        grad_gate_summed.astype(f32).T,
+        grad_up_summed.astype(f32).T,
         grad_down_summed.astype(f32),
     )
 

time: 934 us -> 949 us (1.016)
  waiting for transfers between devices: 1.13 us -> 90.8 us
  blocking collectives: 42.6 us -> 0 us
  Pallas kernels: 606 us -> 570 us
    psum x1 -> x3, waiting for transfers between devices: 0.01 us -> 90.2 us  [the longest x1 62.7 us: shards(): grad_out_summed = lax.psum(grad_out_weight, 'dp')]
    all_gather x1 -> x0, blocking collectives: 42.6 us -> none  [sum_small(): return jnp.sum(lax.all_gather(vector, axes, axis=0, tiled=False), 0)]
    pallas_call x1, Pallas kernels: 269 us -> 232 us  [sum_over_line(): pl.pallas_call(functools.partial(line_kernel, 'dp', 'tensor', tuple(width...]
  transfers between devices with their start and end apart: 5 -> 6, of which waited for: 0 -> 2; matrix products, arithmetic and copies ran while one was open for 18% -> 19% of each run, Pallas kernels for 61% -> 56%
where the time goes in v3:
time: 949 us; the launch traced here: 940 us
  Pallas kernels  570 us (60%)
  matrix products  184 us (19%)
  waiting for transfers between devices  90.8 us (10%)
  local copies, waits for them, and re-layouts  39.9 us (4%)
  other arithmetic  39 us (4%)
  between operations  15.2 us (2%)
    pallas_call x1, Pallas kernels, sum_over_line(): pl.pallas_call(functools.partial(line_kernel, 'dp', 'tensor', tuple(width...  232 us
    pallas_call x3, Pallas kernels, gather_rows(): pl.pallas_call(functools.partial(gather_kernel, 'tensor'), out_shape=jax....  120 us
    pallas_call x2, Pallas kernels, scatter_rows(): pl.pallas_call(functools.partial(scatter_kernel, 'tensor'), out_shape=jax...  79.8 us
    pallas_call x1, Pallas kernels, mixer_forward(): pl.pallas_call(functools.partial(forward_kernel, heads, key_dim, value_di...  75.8 us
    dot_general x5, matrix products, times_transposed(): lax.dot_general(left, right, (((1,), (1,)), ((), ())), preferred_element_...  69.6 us
    psum x1, waiting for transfers between devices, shards(): grad_out_summed = lax.psum(grad_out_weight, 'dp')  62.7 us
    pallas_call x1, Pallas kernels, mixer_backward(): pl.pallas_call(functools.partial(backward_kernel, heads, key_dim, value_d...  62.4 us
    dot_general x5, matrix products, cross_rows(): lax.dot_general(left, right, (((0,), (0,)), ((), ())), preferred_element_...  62 us
  transfers between devices with their start and end apart: 6, of which 2 were waited for; matrix products, arithmetic and copies ran while one was open for 19% of the time, Pallas kernels for 56%

profile of v3, /device:TPU:0, one launch (start us, length us, event | category | flops | bytes accessed | tf_op | source)
XLA Modules:
  0.0 939.7 jit_solution(17938393408744292223)
XLA Ops:
  7.3 0.8 convert_element_type.108
  8.1 1.5 fusion.10
  9.6 0.6 copy-done.29
  10.2 2.5 fusion.4.x_ref
  12.8 41.3 %gather_rows.3 = bf16[2048,2048]{1,0:T(8,128)(2,1)} custom-call(bf16[256,2048]{1,0:T(8,128)(2,1)} %fusion.4.x_ref), custom_call_target="tpu_custom_call" | custom-call | bytes 1000000 | tf_op jit(solution)/shard_map/gather_rows/pallas_call | solution.py:646
  54.5 1.1 copy.50
  55.9 0.9 broadcast_in_dim.22
  56.8 11.3 %concatenate.6 = bf16[2048,1664]{1,0:T(8,128)(2,1)} concatenate(bf16[2048,256]{1,0:T(8,128)(2,1)} %param.24, bf16[2048,256]{1,0:T(8,128)(2,1)} %param.25, bf16[2048,512]{1,0:T(8,128)(2,1)} %param.26, bf16[2048,512]{1,0:T(8,128)(2,1)} %param.29, bf16[2048,2]{1,0:T(8,128)(2,1)S(1)} %copy.49, bf16[2048,2]{1,0:T(8,128)(2,1)} %copy.50, bf16[2048,124]{1,0:T(8,128)(2,1)} %broadcast_in_dim.22), dimensions={1} | concatenate | bytes 13631488 | tf_op jit(solution)/shard_map/concatenate | solution.py:994
  68.1 21.3 %fusion.16.proj_ref.eq_ref.ek_ref.ev_ref = f32[2048,1664]{1,0:T(8,128)} fusion(bf16[2048,2048]{1,0:T(8,128)(2,1)} %gather_rows.3, bf16[2048,1664]{1,0:T(8,128)(2,1)} %concatenate.6), kind=kOutput, calls=%fused_computation.55 | convolution fusion | flops 13958643712 | bytes 28835840 | tf_op jit(solution)/shard_map/dot_general | solution.py:996
  89.4 75.8 %mixer_forward.1 = (bf16[2048,512]{1,0:T(8,128)(2,1)S(1)}, f32[2,128,256]{2,1,0:T(8,128)}, bf16[8,2,128,256]{3,2,1,0:T(8,128)(2,1)S(1)}, bf16[8,2,256,256]{3,2,1...) custom-call(f32[2048,1664]{1,0:T(8,128)} %fusion.16.proj_ref.eq_ref.ek_ref.ev_ref, ...), custom_call_target="tpu_custom_call" | custom-call | bytes 200000000 | tf_op jit(solution)/shard_map/mixer_forward/pallas_call | solution.py:230
  165.2 4.7 convolution_convert_fusion.1.p_ref
  170.0 39.9 %scatter_rows.2 = f32[256,2048]{1,0:T(8,128)S(1)} custom-call(bf16[2048,2048]{1,0:T(8,128)(2,1)S(1)} %convolution_convert_fusion.1.p_ref), custom_call_target="tpu_custom_call" | custom-call | bytes 1000000 | tf_op jit(solution)/shard_map/scatter_rows/pallas_call | solution.py:742
  210.4 1.3 copy-done.17
  211.7 1.2 multiply_convert_fusion.3.x_ref
  212.9 38.8 %gather_rows.4 = bf16[2048,2048]{1,0:T(8,128)(2,1)} custom-call(bf16[256,2048]{1,0:T(8,128)(2,1)} %multiply_convert_fusion.3.x_ref), custom_call_target="tpu_custom_call" | custom-call | bytes 1000000 | tf_op jit(solution)/shard_map/gather_rows/pallas_call | solution.py:646
  251.7 9.5 %fusion.17 = f32[2048,688]{0,1:T(8,128)S(1)} fusion(bf16[2048,2048]{1,0:T(8,128)(2,1)} %gather_rows.4, bf16[2048,688]{0,1:T(8,128)(2,1)} %param.38), kind=kOutput, calls=%fused_computation.56 | convolution fusion | flops 5771362304 | bytes 16842752 | tf_op jit(solution)/shard_map/dot_general | solution.py:1016
  261.2 8.2 multiply_convert_fusion.2
  269.4 1.6 copy-done.51
  271.0 9.1 convolution_convert_fusion
  280.1 10.5 %convolution_convert_fusion.6 = bf16[688,2048]{1,0:T(8,128)(2,1)} fusion(bf16[2048,688]{0,1:T(8,128)(2,1)} %copy-done.51, bf16[2048,2048]{1,0:T(8,128)(2,1)} %all-gather.2.cloned.1.call-done), kind=kOutput, calls=%fused_computation.15 | convolution fusion | flops 5772771328 | bytes 14024704 | tf_op jit(solution)/shard_map/dot_general | solution.py:948
  290.6 13.8 %multiply_convert_fusion = (bf16[2048,688]{0,1:T(8,128)(2,1)}, bf16[2048,688]{0,1:T(8,128)(2,1)S(1)}) fusion(f32[2048,688]{0,1:T(8,128)} %copy-done.47, f32[2048,688]{0,1:T(8,128)} %get-tuple-element.120, bf16[2048,2048]{1,0:T(8,128)(2,1)} %all-gather.2.cloned.1.call-done, bf16[688,2048]{1,0:T(8,128)(2,1)S(1)} %copy-done), kind=kOutput, calls=%fused_computation.8 | convolution fusion | flops 5789679616 | bytes 28114944 | tf_op jit(solution)/shard_map/dot_general | solution.py:952
  304.4 1.6 copy-done.49
  306.0 10.3 %fusion.18 = f32[2048,2048]{1,0:T(8,128)} fusion(bf16[2048,688]{0,1:T(8,128)(2,1)S(1)} %get-tuple-element.104, bf16[2048,688]{0,1:T(8,128)(2,1)S(1)} %copy-done.41), kind=kOutput, calls=%fused_computation.57 | convolution fusion | flops 5771362304 | bytes 22413312 | tf_op jit(solution)/shard_map/dot_general | solution.py:952
  316.3 1.7 copy-done.43
  318.1 14.3 %add_convert_fusion.p_ref = bf16[2048,2048]{1,0:T(8,128)(2,1)} fusion(f32[2048,2048]{1,0:T(8,128)} %fusion.18, bf16[2048,688]{0,1:T(8,128)(2,1)} %get-tuple-element.103, bf16[2048,688]{0,1:T(8,128)(2,1)S(1)} %copy-done.43), kind=kOutput, calls=%fused_computation | convolution fusion | flops 5779750912 | bytes 30801920 | tf_op jit(solution)/shard_map/dot_general | solution.py:952
  332.4 10.8 %convolution_convert_fusion.5 = bf16[688,2048]{1,0:T(8,128)(2,1)} fusion(bf16[2048,688]{0,1:T(8,128)(2,1)S(1)} %copy-done.50, bf16[2048,2048]{1,0:T(8,128)(2,1)} %gather_rows.4), kind=kOutput, calls=%fused_computation.14 | convolution fusion | flops 5772771328 | bytes 14024704 | tf_op jit(solution)/shard_map/dot_general | solution.py:948
  343.1 3.4 copy-done.3
  346.6 39.9 %scatter_rows.3 = f32[256,2048]{1,0:T(8,128)S(1)} custom-call(bf16[2048,2048]{1,0:T(8,128)(2,1)S(1)} %copy-done.3), custom_call_target="tpu_custom_call" | custom-call | bytes 1000000 | tf_op jit(solution)/shard_map/scatter_rows/pallas_call | solution.py:742
  386.5 0.6 multiply_reduce_fusion.1
  387.1 2.0 copy-done.48
  389.1 10.7 %convolution_convert_fusion.4.refs_1_ = bf16[688,2048]{1,0:T(8,128)(2,1)} fusion(bf16[2048,688]{0,1:T(8,128)(2,1)S(1)} %copy-done.48, bf16[2048,2048]{1,0:T(8,128)(2,1)} %gather_rows.4), kind=kOutput, calls=%fused_computation.13 | convolution fusion | flops 5772771328 | bytes 14024704 | tf_op jit(solution)/shard_map/dot_general | solution.py:948
  399.7 27.5 %all-reduce.4.cloned.1.call-done = bf16[688,2048]{1,0:T(8,128)(2,1)} async-done(((bf16[688,2048]{1,0:T(8,128)(2,1)}), bf16[688,2048]{1,0:T(8,128)(2,1)}) %all-reduce.4.cloned.1.call-update) | async-done | bytes 2818064 | tf_op jit(solution)/shard_map/psum | solution.py:1023
  427.3 3.4 fusion.12.x_ref
  430.7 39.7 %gather_rows.5 = bf16[2048,2048]{1,0:T(8,128)(2,1)} custom-call(bf16[256,2048]{1,0:T(8,128)(2,1)} %fusion.12.x_ref), custom_call_target="tpu_custom_call" | custom-call | bytes 1000000 | tf_op jit(solution)/shard_map/gather_rows/pallas_call | solution.py:646
  470.5 9.7 %fusion.19.grad_ref = f32[2048,512]{1,0:T(8,128)} fusion(bf16[2048,2048]{1,0:T(8,128)(2,1)} %gather_rows.5, bf16[512,2048]{1,0:T(8,128)(2,1)S(1)} %copy-done.45), kind=kOutput, calls=%fused_computation.58 | convolution fusion | flops 4294967296 | bytes 14680064 | tf_op jit(solution)/shard_map/dot_general | solution.py:952
  480.2 62.4 %mixer_backward.1 = (bf16[2048,1664]{1,0:T(8,128)(2,1)}, f32[4,256]{1,0:T(4,128)}, f32[4,256]{1,0:T(4,128)}, f32[4,512]{1,0:T(4,128)}, f32[1,2]{1,0:T(1,128)}, /*index=5*/f32[1,2]{1,0:T(1,128)}, f32[1,256]{1,0:T(1,128)}) custom-call(f32[2048,1664]{1,0:T(8,128)} %fusion.16.proj_ref.eq_ref.ek_ref.ev_ref, f32[2048,1664]{1,0:T(8,128)} %fusion.16.proj_ref.eq_ref.ek_ref.ev_ref, ...), custom_call_target="tpu_custom_call" | custom-call | bytes 200000000 | tf_op jit(solution)/shard_map/mixer_backward/pallas_call | solution.py:482
  542.6 0.7 copy.58
  543.3 0.7 copy.59
  544.0 0.7 copy.60
  544.7 9.1 convolution_convert_fusion.7
  553.8 20.9 %multiply_reduce_fusion = (f32[2048]{0:T(1024)S(1)}, bf16[2048,1664]{1,0:T(8,128)(2,1)S(1)}) fusion(bf16[2048,1664]{1,0:T(8,128)(2,1)} %concatenate.6, bf16[2048,2048]{1,0:T(8,128)(2,1)} %gather_rows.3, bf16[2048,1664]{1,0:T(8,128)(2,1)} %get-tuple-element.75), kind=kOutput, calls=%fused_computation.1 | convolution fusion | flops 13975681024 | bytes 28844032 | tf_op jit(solution)/shard_map/dot_general | solution.py:948
  574.8 2.7 copy-done.22
  578.1 0.7 concatenate.7
  578.8 21.4 %convolution_convert_fusion.2 = bf16[2048,2048]{1,0:T(8,128)(2,1)} fusion(bf16[2048,1664]{1,0:T(8,128)(2,1)} %get-tuple-element.75, bf16[2048,1664]{1,0:T(8,128)(2,1)} %concatenate.6), kind=kOutput, calls=%fused_computation.4 | convolution fusion | flops 13962838016 | bytes 22020096 | tf_op jit(solution)/shard_map/dot_general | solution.py:952
  600.2 62.7 %all-reduce.8.cloned.1.call-done = bf16[512,2048]{1,0:T(8,128)(2,1)} async-done(((bf16[512,2048]{1,0:T(8,128)(2,1)}), bf16[512,2048]{1,0:T(8,128)(2,1)}) %all-reduce.8.cloned.1.call-update) | async-done | bytes 2097168 | tf_op jit(solution)/shard_map/psum | solution.py:1052
  663.6 232.4 %sum_over_line.1 = (f32[144,128]{1,0:T(8,128)}, bf16[688,2048]{1,0:T(8,128)(2,1)}, bf16[2048,1536]{1,0:T(8,128)(2,1)}, f32[48,128]{1,0:T(8,128)}) custom-call(f32[144,128]{1,0:T(8,128)} %bitcast.91, bf16[688,2048]{1,0:T(8,128)(2,1)} %convolution_convert_fusion.4.refs_1_, bf16[2048,1664]{1,0:T(8,128)(2,1)} %copy-done.22), custom_call_target="tpu_custom_call" | custom-call | bytes 914636800 | tf_op jit(solution)/shard_map/sum_over_line/pallas_call | solution.py:928
  895.9 0.7 slice.83
  896.7 0.9 fusion.15
  897.5 0.6 slice.77
  898.2 0.6 slice.79
  898.8 0.8 fusion.14
  899.5 0.6 reshape.124
  900.1 0.6 reshape.125
  900.7 0.6 reshape.126
  901.4 4.3 convert_element_type.138
  905.6 3.2 convert_element_type.139
  908.9 1.3 fusion.13
  910.2 0.6 slice_bitcast_fusion.2
  910.8 0.6 slice_bitcast_fusion
  911.4 2.3 slice_convert_fusion.2
  913.7 4.6 slice_convert_fusion
  918.3 5.9 convert_bitcast_fusion
  924.2 1.8 fusion.5
  926.0 6.4 fusion.9
  (135 shorter events, 2.5 us)
Async XLA Ops:
  7.2 263.8 %copy-start = (bf16[688,2048]{1,0:T(8,128)(2,1)S(1)}, bf16[688,2048]{1,0:T(8,128)(2,1)}, u32[]{:S(2)}) copy-start(bf16[688,2048]{1,0:T(8,128)(2,1)} %param.40) | copy-start | bytes 8454148
  7.2 272.9 %all-gather.2.cloned.1.call-start = ((), (), s32[]{:S(2)}) async-start(), calls=%async_computation.2 | async-start | bytes 9437184 | tf_op jit(solution)/shard_map/all_gather | solution.py:1007
  8.1 1.5 copy-start.26
  9.6 0.6 copy-start.29
  12.7 41.4 %copy-start.32 = (bf16[2048,2]{0,1:T(2,128)(2,1)S(1)}, bf16[2048,2]{0,1:T(2,128)(2,1)}, u32[]{:S(2)}) copy-start(bf16[2048,2]{0,1:T(2,128)(2,1)} %param.27) | copy-start | bytes 24580
  12.7 41.8 %copy-start.33 = (bf16[2048,2]{0,1:T(2,128)(2,1)S(1)}, bf16[2048,2]{0,1:T(2,128)(2,1)}, u32[]{:S(2)}) copy-start(bf16[2048,2]{0,1:T(2,128)(2,1)} %param.28) | copy-start | bytes 24580
  12.7 42.9 %copy-start.36 = (bf16[4,256]{1,0:T(4,128)(2,1)S(1)}, bf16[4,256]{1,0:T(4,128)(2,1)}, u32[]{:S(2)}) copy-start(bf16[4,256]{1,0:T(4,128)(2,1)} %param.30) | copy-start | bytes 6148
  12.7 42.9 %copy-start.37 = (bf16[4,256]{1,0:T(4,128)(2,1)S(1)}, bf16[4,256]{1,0:T(4,128)(2,1)}, u32[]{:S(2)}) copy-start(bf16[4,256]{1,0:T(4,128)(2,1)} %param.31) | copy-start | bytes 6148
  12.7 42.9 %copy-start.34 = (bf16[4,512]{1,0:T(4,128)(2,1)S(1)}, bf16[4,512]{1,0:T(4,128)(2,1)}, u32[]{:S(2)}) copy-start(bf16[4,512]{1,0:T(4,128)(2,1)} %param.32) | copy-start | bytes 12292
  12.7 43.0 %copy-start.13 = (f32[2]{0:T(128)S(1)}, f32[2]{0:T(128)}, u32[]{:S(2)}) copy-start(f32[2]{0:T(128)} %param.33) | copy-start | bytes 28
  12.8 43.0 %copy-start.14 = (f32[2]{0:T(128)S(1)}, f32[2]{0:T(128)}, u32[]{:S(2)}) copy-start(f32[2]{0:T(128)} %param.34) | copy-start | bytes 28
  12.8 43.1 %copy-start.46 = (bf16[256]{0:T(256)(128)(2,1)S(1)}, bf16[256]{0:T(256)(128)(2,1)}, u32[]{:S(2)}) copy-start(bf16[256]{0:T(256)(128)(2,1)} %param.35) | copy-start | bytes 1540
  54.1 373.1 %all-reduce.4.cloned.1.call-start = ((), (), s32[]{:S(2)}) async-start(), calls=%async_computation.3 | async-start | bytes 5636096 | tf_op jit(solution)/shard_map/psum | solution.py:1023
  55.6 33.7 %copy-start.8 = (f32[4,256]{1,0:T(4,128)}, f32[4,256]{1,0:T(4,128)S(1)}, u32[]{:S(2)}) copy-start(f32[4,256]{1,0:T(4,128)S(1)} %convert_element_type.110.tq_ref) | copy-start | bytes 12292
  55.7 33.7 %copy-start.9 = (f32[4,256]{1,0:T(4,128)}, f32[4,256]{1,0:T(4,128)S(1)}, u32[]{:S(2)}) copy-start(f32[4,256]{1,0:T(4,128)S(1)} %convert_element_type.111.tk_ref) | copy-start | bytes 12292
  55.7 33.7 %copy-start.7 = (f32[4,512]{1,0:T(4,128)}, f32[4,512]{1,0:T(4,128)S(1)}, u32[]{:S(2)}) copy-start(f32[4,512]{1,0:T(4,128)S(1)} %convert_element_type.112.tv_ref) | copy-start | bytes 24580
  55.8 33.6 %copy-start.10 = (f32[2,1]{1,0:T(2,128)}, f32[2,1]{1,0:T(2,128)S(1)}, u32[]{:S(2)}) copy-start(f32[2,1]{1,0:T(2,128)S(1)} %copy.51.dl_col_ref) | copy-start | bytes 28
  55.9 33.5 %copy-start.11 = (f32[2,1]{1,0:T(2,128)}, f32[2,1]{1,0:T(2,128)S(1)}, u32[]{:S(2)}) copy-start(f32[2,1]{1,0:T(2,128)S(1)} %copy.52.db_col_ref) | copy-start | bytes 28
  55.9 33.5 %copy-start.12 = (f32[256]{0:T(256)}, f32[256]{0:T(256)S(1)}, u32[]{:S(2)}) copy-start(f32[256]{0:T(256)S(1)} %broadcast_in_dim.56) | copy-start | bytes 3076
  68.1 21.3 %copy-start.6 = (f32[1,2,128,256]{3,2,1,0:T(8,128)S(1)}, f32[1,2,128,256]{3,2,1,0:T(8,128)}, u32[]{:S(2)}) copy-start(f32[1,2,128,256]{3,2,1,0:T(8,128)} %param.22) | copy-start | bytes 786436
  89.4 75.8 %copy-start.44 = (bf16[512,2048]{1,0:T(8,128)(2,1)S(1)}, bf16[512,2048]{1,0:T(8,128)(2,1)}, u32[]{:S(2)}) copy-start(bf16[512,2048]{1,0:T(8,128)(2,1)} %param.36) | copy-start | bytes 6291460
  165.2 4.8 copy-start.4
  165.2 4.8 copy-start.5
  165.2 4.8 copy-start.15
  170.0 39.9 %copy-start.35 = (bf16[2048]{0:T(1024)(128)(2,1)S(1)}, bf16[2048]{0:T(1024)(128)(2,1)}, u32[]{:S(2)}) copy-start(bf16[2048]{0:T(1024)(128)(2,1)} %param.37) | copy-start | bytes 12292
  170.0 40.0 %copy-start.19 = (bf16[1,256,2048]{2,1,0:T(8,128)(2,1)S(1)}, bf16[1,256,2048]{2,1,0:T(8,128)(2,1)}, u32[]{:S(2)}) copy-start(bf16[1,256,2048]{2,1,0:T(8,128)(2,1)} %param.21) | copy-start | bytes 3145732
  210.3 1.3 copy-start.17
  251.6 9.5 %copy-start.21 = (bf16[2048,2048]{1,0:T(8,128)(2,1)S(1)}, bf16[2048,2048]{1,0:T(8,128)(2,1)}, u32[]{:S(2)}) copy-start(bf16[2048,2048]{1,0:T(8,128)(2,1)} %gather_rows.4) | copy-start | bytes 25165828
  251.7 9.5 %copy-start.42 = (bf16[2048,688]{0,1:T(8,128)(2,1)S(1)}, bf16[2048,688]{0,1:T(8,128)(2,1)}, u32[]{:S(2)}) copy-start(bf16[2048,688]{0,1:T(8,128)(2,1)} %param.39) | copy-start | bytes 8454148
  261.1 8.2 copy-start.47
  269.4 1.6 copy-start.51
  290.6 15.4 %copy-start.41 = (bf16[2048,688]{0,1:T(8,128)(2,1)S(1)}, bf16[2048,688]{0,1:T(8,128)(2,1)}, u32[]{:S(2)}) copy-start(bf16[2048,688]{0,1:T(8,128)(2,1)} %param.38) | copy-start | bytes 8454148
  304.4 1.6 copy-start.49
  316.3 1.8 copy-start.43
  316.3 237.5 %all-reduce.6.cloned.1.call-start = ((), (), s32[]{:S(2)}) async-start(), calls=%async_computation.4 | async-start | bytes 5636096 | tf_op jit(solution)/shard_map/psum | solution.py:1035
  318.1 14.3 %copy-start.50 = (bf16[2048,688]{0,1:T(8,128)(2,1)S(1)}, bf16[2048,688]{0,1:T(8,128)(2,1)}, u32[]{:S(2)}) copy-start(bf16[2048,688]{0,1:T(8,128)(2,1)} %copy-done.49) | copy-start | bytes 8454148
  343.1 3.4 copy-start.3
  346.6 39.9 %copy-start.18 = (f32[256,2048]{1,0:T(8,128)S(1)}, f32[256,2048]{1,0:T(8,128)}, u32[]{:S(2)}) copy-start(f32[256,2048]{1,0:T(8,128)} %copy-done.17) | copy-start | bytes 6291460
  386.5 40.8 %copy-start.2 = (f32[256,2048]{1,0:T(8,128)}, f32[256,2048]{1,0:T(8,128)S(1)}, u32[]{:S(2)}) copy-start(f32[256,2048]{1,0:T(8,128)S(1)} %scatter_rows.3) | copy-start | bytes 6291460
  386.5 2.6 copy-start.48
  427.3 235.7 %all-reduce.8.cloned.1.call-start = ((), (), s32[]{:S(2)}) async-start(), calls=%async_computation.5 | async-start | bytes 4194304 | tf_op jit(solution)/shard_map/psum | solution.py:1052
  430.7 39.7 %copy-start.45 = (bf16[512,2048]{1,0:T(8,128)(2,1)S(1)}, bf16[512,2048]{1,0:T(8,128)(2,1)}, u32[]{:S(2)}) copy-start(bf16[512,2048]{1,0:T(8,128)(2,1)} %param.36) | copy-start | bytes 6291460
  480.2 64.5 %copy-start.16 = (bf16[2048,512]{1,0:T(8,128)(2,1)S(1)}, bf16[2048,512]{1,0:T(8,128)(2,1)}, u32[]{:S(2)}) copy-start(bf16[2048,512]{1,0:T(8,128)(2,1)} %copy-done.15) | copy-start | bytes 6291460
  553.8 21.0 %copy-start.28 = (bf16[2048]{0:T(1024)(128)(2,1)S(1)}, bf16[2048]{0:T(1024)(128)(2,1)}, u32[]{:S(2)}) copy-start(bf16[2048]{0:T(1024)(128)(2,1)} %param.23) | copy-start | bytes 12292
  574.7 2.8 copy-start.22
  574.8 3.3 copy-start.38
  574.8 3.3 copy-start.39
  574.8 3.3 copy-start.40
  578.0 346.2 %reduce-scatter.5.cloned.1.call-start = ((), (), s32[]{:S(2)}) async-start(), calls=%async_computation.7 | async-start | bytes 9437184 | tf_op jit(solution)/shard_map/reduce_scatter | solution.py:738
  663.0 263.0 %reduce-scatter.3.cloned.1.call-start = ((), (), s32[]{:S(2)}) async-start(), calls=%async_computation.6 | async-start | bytes 9437184 | tf_op jit(solution)/shard_map/reduce_scatter | solution.py:738
  663.5 242.1 %copy-start.23 = (bf16[688,2048]{1,0:T(8,128)(2,1)S(1)}, bf16[688,2048]{1,0:T(8,128)(2,1)}, u32[]{:S(2)}) copy-start(bf16[688,2048]{1,0:T(8,128)(2,1)} %all-reduce.4.cloned.1.call-done) | copy-start | bytes 8454148
  901.4 10.0 %slice-start = ((s8[6291456]{0:T(1024)(128)(4,1)}), s8[4194304]{0:T(1024)(128)(4,1)S(1)}, s32[]{:S(2)}) async-start(s8[6291456]{0:T(1024)(128)(4,1)} %bitcast.89), calls=%async_computation.8 | async-start | bytes 8388608
  905.6 4.6 copy-start.31
  905.6 5.8 slice-start.1
  913.7 4.6 copy-start.24
  913.7 4.6 copy-start.25
  918.3 5.9 copy-start.20
  918.3 5.9 copy-start.27
  918.3 5.9 copy-start.30
  926.0 6.4 copy-start.1
Sparse Core Ops, SparseCore 0:
  54.2 54.8 all-gather.1
  316.4 110.7 all-reduce.3
  430.3 109.4 all-reduce.5
  578.1 84.7 all-reduce.7
  666.6 70.2 reduce-scatter.4
  740.2 71.2 reduce-scatter.2

commit v4 on v3

--- a/solution.py
+++ b/solution.py
@@ -14,6 +14,8 @@
 EDGE = 8
 HALF = 128
 EXTRA = 128
+FORWARD_GROUP = 2
+BACKWARD_GROUP = 2
 
 f32 = jnp.float32
 bf16 = jnp.bfloat16
@@ -44,7 +46,7 @@
 
 
 def sigmoid(x):
-    return 1.0 / (1.0 + jnp.exp(-x))
+    return 0.5 * jnp.tanh(0.5 * x) + 0.5
 
 
 def softplus(x):
@@ -55,40 +57,47 @@
     return lax.broadcasted_iota(jnp.int32, shape, axis)
 
 
-def unit_lower_inverse(lower):
-    size = lower.shape[0]
+def unit_lower_inverses(lowers):
+    size = lowers[0].shape[0]
     half = min(size, HALF)
-
-    def small(part):
-        rows, cols = iota((half, half), 0), iota((half, half), 1)
-        eye = jnp.where(rows == cols, 1.0, 0.0)
-        differ = rows ^ cols
-        inverse = eye - jnp.where(differ == 1, part, 0.0)
-        step = 2
-        while step < half:
-            level = jnp.where((differ >= step) & (differ < 2 * step), part, 0.0)
-            inverse = inverse - dot_nn(inverse, dot_nn(level, inverse))
-            step *= 2
-        return inverse
-
-    blocks = [small(lower[i : i + half, i : i + half]) for i in range(0, size, half)]
-    if len(blocks) == 1:
-        return blocks[0]
-    first, second = blocks
-    corner = -dot_nn(second, dot_nn(lower[half:, :half], first))
-    top = jnp.concatenate([first, jnp.zeros((half, half), f32)], axis=1)
-    return jnp.concatenate([top, jnp.concatenate([corner, second], axis=1)], axis=0)
-
-
-def refined_inverse(lower):
-    size = lower.shape[0]
-    rough = unit_lower_inverse(lower).astype(bf16)
-    high = lower.astype(bf16)
-    low = (lower - high.astype(f32)).astype(bf16)
+    rows, cols = iota((half, half), 0), iota((half, half), 1)
+    eye = jnp.where(rows == cols, 1.0, 0.0)
+    differ = rows ^ cols
+    parts = [low[i : i + half, i : i + half] for low in lowers for i in range(0, size, half)]
+    found = [eye - jnp.where(differ == 1, part, 0.0) for part in parts]
+    step = 2
+    while step < half:
+        mask = (differ >= step) & (differ < 2 * step)
+        levels = [jnp.where(mask, part, 0.0).astype(bf16) for part in parts]
+        narrow = [x.astype(bf16) for x in found]
+        middle = [dot_nn(level, x).astype(bf16) for level, x in zip(levels, narrow)]
+        found = [x - dot_nn(n, m) for x, n, m in zip(found, narrow, middle)]
+        step *= 2
+    if size == half:
+        return found
+    firsts, seconds = found[0::2], found[1::2]
+    middle = [dot_nn(low[half:, :half], first) for low, first in zip(lowers, firsts)]
+    corners = [-dot_nn(second, m) for second, m in zip(seconds, middle)]
+    empty = jnp.zeros((half, half), f32)
+    return [
+        jnp.concatenate(
+            [jnp.concatenate([x, empty], axis=1), jnp.concatenate([c, y], axis=1)], axis=0
+        )
+        for x, c, y in zip(firsts, corners, seconds)
+    ]
+
+
+def refined_inverses(lowers):
+    size = lowers[0].shape[0]
+    rough = [x.astype(bf16) for x in unit_lower_inverses(lowers)]
+    highs = [low.astype(bf16) for low in lowers]
+    rests = [(low - high.astype(f32)).astype(bf16) for low, high in zip(lowers, highs)]
     eye = jnp.where(iota((size, size), 0) == iota((size, size), 1), 1.0, 0.0)
-    rough32 = rough.astype(f32)
-    rest = eye - rough32 - dot_nn(high, rough) - dot_nn(low, rough)
-    return rough32 + dot_nn(rough, rest)
+    errors = [
+        eye - x.astype(f32) - dot_nn(high, x) - dot_nn(rest, x)
+        for x, high, rest in zip(rough, highs, rests)
+    ]
+    return [(x.astype(f32) + dot_nn(x, error)).astype(bf16) for x, error in zip(rough, errors)]
 
 
 def conv_from(ext_ref, taps, size):
@@ -121,14 +130,15 @@
     cum_col = dot_exact(tril, ld_col)
     cum_row = dot_exact(ld_row, triu)
     beta_col = sigmoid(ab_col[:, heads:])
-    return incl, rows > cols, alpha_col, ld_col, cum_col, cum_row, beta_col
+    return alpha_col, ld_col, cum_col, cum_row, beta_col
 
 
 def forward_kernel(
     heads,
     key_dim,
     value_dim,
-    blocks,
+    steps,
+    block,
     proj_ref,
     tq_ref,
     tk_ref,
@@ -171,43 +181,77 @@
     values = conv_v * sigmoid(conv_v)
     gate = pg_ref[...]
     gate = gate * sigmoid(gate)
-    incl, strict, _, _, cum_col, cum_row, beta_col = decay_parts(
-        ab_ref[...], dl_row_ref[...], db_row_ref[...], dl_col_ref[...], db_col_ref[...], heads, size
-    )
     gain = gain_ref[...]
-    for h in range(heads):
-        keys = slice(h * key_dim, (h + 1) * key_dim)
-        vals = slice(h * value_dim, (h + 1) * value_dim)
-        q = act_q[:, keys]
-        q = q * (lax.rsqrt(jnp.sum(q * q, -1, keepdims=True) + unit_eps) * key_dim**-0.5)
-        k = act_k[:, keys]
-        k = k * lax.rsqrt(jnp.sum(k * k, -1, keepdims=True) + unit_eps)
-        v = values[:, vals]
-        beta = beta_col[:, h : h + 1]
-        cum = cum_col[:, h : h + 1]
-        last = cum_row[h : h + 1, size - 1 : size]
-        growth = jnp.exp(cum)
-        tail = jnp.exp(last - cum)
-        within = jnp.exp(jnp.where(incl, cum - cum_row[h : h + 1, :], -1e30))
-        kb = k.astype(bf16)
-        lower = jnp.where(strict, dot_nt(kb, kb) * within * beta, 0.0)
-        inverse = refined_inverse(lower).astype(bf16)
-        attend = dot_nt(q, kb) * within
-        current = state[h]
-        current_low = current.astype(bf16)
-        rhs = beta * (v - growth * dot_nn(kb, current_low))
-        update = dot_nn(inverse, rhs)
-        update_low = update.astype(bf16)
-        out = growth * dot_nn(q, current_low) + dot_nn(attend, update_low)
-        state[h] = jnp.exp(last) * current + dot_tn(tail * k, update_low)
-        states_ref[0, h] = current_low
-        inverse_ref[0, h] = inverse
-        update_ref[:, vals] = update_low
-        raw_ref[:, vals] = out.astype(raw_ref.dtype)
+    incl = iota((block, block), 0) >= iota((block, block), 1)
+    strict = iota((block, block), 0) > iota((block, block), 1)
+    ab = ab_ref[...]
+    units = [(g, h) for g in range(size // block) for h in range(heads)]
+    parts = [
+        decay_parts(
+            ab[g * block : (g + 1) * block],
+            dl_row_ref[...],
+            db_row_ref[...],
+            dl_col_ref[...],
+            db_col_ref[...],
+            heads,
+            block,
+        )
+        for g in range(size // block)
+    ]
+
+    def cut(array, unit, dim):
+        g, h = unit
+        return array[g * block : (g + 1) * block, h * dim : (h + 1) * dim]
+
+    qs = [cut(act_q, u, key_dim) for u in units]
+    qs = [q * (lax.rsqrt(jnp.sum(q * q, -1, keepdims=True) + unit_eps) * key_dim**-0.5) for q in qs]
+    qs = [q.astype(bf16) for q in qs]
+    ks = [cut(act_k, u, key_dim) for u in units]
+    ks = [k * lax.rsqrt(jnp.sum(k * k, -1, keepdims=True) + unit_eps) for k in ks]
+    kbs = [k.astype(bf16) for k in ks]
+    grams = [dot_nt(k, k) for k in kbs]
+    attends = [dot_nt(q, k) for q, k in zip(qs, kbs)]
+    betas = [parts[g][4][:, h : h + 1] for g, h in units]
+    cums = [parts[g][2][:, h : h + 1] for g, h in units]
+    cum_rows = [parts[g][3][h : h + 1, :] for g, h in units]
+    lasts = [row[:, block - 1 :] for row in cum_rows]
+    withins = [jnp.exp(jnp.where(incl, c - r, -1e30)) for c, r in zip(cums, cum_rows)]
+    lowers = [
+        jnp.where(strict, gram * w * beta, 0.0) for gram, w, beta in zip(grams, withins, betas)
+    ]
+    attends = [(a * w).astype(bf16) for a, w in zip(attends, withins)]
+    inverses = refined_inverses(lowers)
+    growths = [jnp.exp(c) for c in cums]
+    tails = [(jnp.exp(last - c) * k).astype(bf16) for last, c, k in zip(lasts, cums, ks)]
+    outs = []
+    for g in range(size // block):
+        mine = [i for i, u in enumerate(units) if u[0] == g]
+        states = [state[h] for h in range(heads)]
+        lows = [x.astype(bf16) for x in states]
+        seen = [dot_nn(kbs[i], low) for i, low in zip(mine, lows)]
+        rhs = [
+            (betas[i] * (cut(values, units[i], value_dim) - growths[i] * x)).astype(bf16)
+            for i, x in zip(mine, seen)
+        ]
+        updates = [dot_nn(inverses[i], x).astype(bf16) for i, x in zip(mine, rhs)]
+        news = [dot_tn(tails[i], x) for i, x in zip(mine, updates)]
+        for h, i in enumerate(mine):
+            state[h] = jnp.exp(lasts[i]) * states[h] + news[h]
+        reads = [dot_nn(qs[i], low) for i, low in zip(mine, lows)]
+        spreads = [dot_nn(attends[i], x) for i, x in zip(mine, updates)]
+        outs += [growths[i] * x + y for i, x, y in zip(mine, reads, spreads)]
+        for h, i in enumerate(mine):
+            at = (slice(g * block, (g + 1) * block), slice(h * value_dim, (h + 1) * value_dim))
+            states_ref[g, h] = lows[h]
+            inverse_ref[g, h] = inverses[i]
+            update_ref[at] = updates[h]
+    for (g, h), out in zip(units, outs):
+        at = (slice(g * block, (g + 1) * block), slice(h * value_dim, (h + 1) * value_dim))
+        raw_ref[at] = out.astype(raw_ref.dtype)
         scale = lax.rsqrt(jnp.mean(out * out, -1, keepdims=True) + norm_eps)
-        gated_ref[:, vals] = (out * scale * gain * gate[:, vals]).astype(bf16)
-
-    @pl.when(step == blocks - 1)
+        gated_ref[at] = (out * scale * gain * cut(gate, (g, h), value_dim)).astype(bf16)
+
+    @pl.when(step == steps - 1)
     def _():
         final_ref[...] = state[...]
 
@@ -219,22 +263,26 @@
 def mixer_forward(proj, tq, tk, tv, decay_log, decay_bias, gain, start):
     heads, key_dim, value_dim = start.shape
     length, width = proj.shape
-    size = min(BLOCK, length)
-    blocks = length // size
+    block = min(BLOCK, length)
+    blocks = length // block
+    group = FORWARD_GROUP if blocks % FORWARD_GROUP == 0 else 1
+    size, steps = group * block, blocks // group
     kw, vw = heads * key_dim, heads * value_dim
 
     def rows(width):
         return pl.BlockSpec((size, width), lambda i: (i, 0))
 
-    per_block = lambda *dims: pl.BlockSpec((1,) + dims, lambda i: (i,) + (0,) * len(dims))
+    def per_block(*dims):
+        return pl.BlockSpec((group,) + dims, lambda i: (i,) + (0,) * len(dims))
+
     return pl.pallas_call(
-        functools.partial(forward_kernel, heads, key_dim, value_dim, blocks),
-        grid=(blocks,),
+        functools.partial(forward_kernel, heads, key_dim, value_dim, steps, block),
+        grid=(steps,),
         out_shape=(
             jax.ShapeDtypeStruct((length, vw), bf16),
             jax.ShapeDtypeStruct((heads, key_dim, value_dim), f32),
             jax.ShapeDtypeStruct((blocks, heads, key_dim, value_dim), bf16),
-            jax.ShapeDtypeStruct((blocks, heads, size, size), bf16),
+            jax.ShapeDtypeStruct((blocks, heads, block, block), bf16),
             jax.ShapeDtypeStruct((length, vw), bf16),
             jax.ShapeDtypeStruct((length, vw), f32),
         ),
@@ -254,7 +302,7 @@
             rows(vw),
             full_spec(start.shape),
             per_block(heads, key_dim, value_dim),
-            per_block(heads, size, size),
+            per_block(heads, block, block),
             rows(vw),
             rows(vw),
         ),
@@ -267,7 +315,7 @@
         compiler_params=pltpu.CompilerParams(
             dimension_semantics=("arbitrary",), vmem_limit_bytes=48 * 1024 * 1024
         ),
-        cost_estimate=pl.CostEstimate(flops=0, bytes_accessed=200_000_000, transcendentals=0),
+        cost_estimate=pl.CostEstimate(flops=0, bytes_accessed=100_000_000, transcendentals=0),
         name="mixer_forward",
     )(
         proj,
@@ -287,7 +335,8 @@
     heads,
     key_dim,
     value_dim,
-    blocks,
+    steps,
+    block,
     proj_ref,
     eq_ref,
     ek_ref,
@@ -335,7 +384,7 @@
         for out in (dtq_ref, dtk_ref, dtv_ref, ddl_ref, ddb_ref, dgain_ref):
             out[...] = jnp.zeros_like(out)
 
-    is_first = step == blocks - 1
+    is_first = step == steps - 1
     convs = []
     for ext, src, edge, taps in (
         (ext_q, pq_ref, eq_ref, tq_ref),
@@ -352,96 +401,152 @@
     gate_sig = sigmoid(gate_in)
     gate = gate_in * gate_sig
     gate_slope = gate_sig * (1.0 + gate_in * (1.0 - gate_sig))
-    incl, strict, alpha_col, ld_col, cum_col, cum_row, beta_col = decay_parts(
-        ab_ref[...], dl_row_ref[...], db_row_ref[...], dl_col_ref[...], db_col_ref[...], heads, size
-    )
     gain = gain_ref[...]
-    cum_cols, cum_rows, lasts, dbetas = [], [], [], []
+    incl = iota((block, block), 0) >= iota((block, block), 1)
+    strict = iota((block, block), 0) > iota((block, block), 1)
+    late = jnp.where(iota((block, block), 0) <= iota((block, block), 1), 1.0, 0.0)
+    ab = ab_ref[...]
+    units = [(g, h) for g in range(size // block) for h in range(heads)]
+    parts = [
+        decay_parts(
+            ab[g * block : (g + 1) * block],
+            dl_row_ref[...],
+            db_row_ref[...],
+            dl_col_ref[...],
+            db_col_ref[...],
+            heads,
+            block,
+        )
+        for g in range(size // block)
+    ]
+
+    def place(unit, dim):
+        g, h = unit
+        return (slice(g * block, (g + 1) * block), slice(h * dim, (h + 1) * dim))
+
+    def cut(array, unit, dim):
+        return array[place(unit, dim)]
+
+    dos = []
     grad_gain = jnp.zeros((1, value_dim), f32)
-    for h in range(heads):
-        keys = slice(h * key_dim, (h + 1) * key_dim)
-        vals = slice(h * value_dim, (h + 1) * value_dim)
-        out = raw_ref[:, vals].astype(f32)
-        grad = grad_ref[:, vals].astype(f32)
+    for u in units:
+        at = place(u, value_dim)
+        out = raw_ref[at].astype(f32)
+        grad = grad_ref[at].astype(f32)
         scale = lax.rsqrt(jnp.mean(out * out, -1, keepdims=True) + norm_eps)
         unit = out * scale
-        dpg_ref[:, vals] = (grad * unit * gain * gate_slope[:, vals]).astype(bf16)
-        dn = grad * gate[:, vals]
+        dpg_ref[at] = (grad * unit * gain * cut(gate_slope, u, value_dim)).astype(bf16)
+        dn = grad * cut(gate, u, value_dim)
         grad_gain = grad_gain + jnp.sum(dn * unit, 0, keepdims=True)
         e = dn * gain
-        do = scale * (e - unit * jnp.mean(e * unit, -1, keepdims=True))
-        do = do.astype(bf16)
-        aq = acts[0][:, keys]
-        rq = lax.rsqrt(jnp.sum(aq * aq, -1, keepdims=True) + unit_eps)
-        uq = aq * rq
-        q = uq * key_dim**-0.5
-        ak = acts[1][:, keys]
-        rk = lax.rsqrt(jnp.sum(ak * ak, -1, keepdims=True) + unit_eps)
-        k = ak * rk
-        v = acts[2][:, vals]
-        beta = beta_col[:, h : h + 1]
-        cum = cum_col[:, h : h + 1]
-        last = cum_row[h : h + 1, size - 1 : size]
-        growth = jnp.exp(cum)
-        tail = jnp.exp(last - cum)
-        dec = jnp.exp(last)
-        within = jnp.exp(jnp.where(incl, cum - cum_row[h : h + 1, :], -1e30))
-        within_strict = jnp.where(strict, within, 0.0)
-        qb, kb = q.astype(bf16), k.astype(bf16)
-        attend = dot_nt(qb, kb) * within
-        gram = dot_nt(kb, kb) * within_strict
-        state = states_ref[0, h]
-        update = update_ref[:, vals]
-        ds = dstate[h]
-        dsb = ds.astype(bf16)
-        du = dot_tn(attend, do) + dot_nn(tail * k, dsb)
-        db = dot_tn(inverse_ref[0, h], du)
-        dbb = db.astype(bf16)
-        dstate[h] = dec * ds + dot_tn(growth * q, do) - dot_tn(beta * growth * k, dbb)
-        dqg = dot_nt(do, state)
-        dkb = -dot_nt(dbb, state)
-        da = dot_nt(do, update)
-        dl = -dot_nt(dbb, update)
-        dkt = dot_nt(update, dsb)
-        dgq = (da * within).astype(bf16)
-        dl_gram = dl * gram
-        dgk = (dl * within_strict * beta).astype(bf16)
-        dq = dot_nn(dgq, kb) + growth * dqg
-        bg = beta * growth
-        dk = dot_tn(dgq, qb) + dot_nn(dgk, kb) + dot_tn(dgk, kb) + tail * dkt + bg * dkb
-        dv = beta * db
-        sum_bk = jnp.sum(dkb * k, -1, keepdims=True)
-        row_gram = jnp.sum(dl_gram, -1, keepdims=True)
-        dbetas.append(jnp.sum(db * v, -1, keepdims=True) + growth * sum_bk + row_gram)
-        mix = da * attend + dl_gram * beta
-        tail_sum = tail * jnp.sum(dkt * k, -1, keepdims=True)
-        cum_cols.append(
-            jnp.sum(mix, -1, keepdims=True) + growth * jnp.sum(dqg * q, -1, keepdims=True) + bg * sum_bk - tail_sum
+        dos.append((scale * (e - unit * jnp.mean(e * unit, -1, keepdims=True))).astype(bf16))
+    dgain_ref[...] += grad_gain
+    aqs = [cut(acts[0], u, key_dim) for u in units]
+    rqs = [lax.rsqrt(jnp.sum(a * a, -1, keepdims=True) + unit_eps) for a in aqs]
+    uqs = [a * r for a, r in zip(aqs, rqs)]
+    qs = [u * key_dim**-0.5 for u in uqs]
+    aks = [cut(acts[1], u, key_dim) for u in units]
+    rks = [lax.rsqrt(jnp.sum(a * a, -1, keepdims=True) + unit_eps) for a in aks]
+    ks = [a * r for a, r in zip(aks, rks)]
+    qbs, kbs = [q.astype(bf16) for q in qs], [k.astype(bf16) for k in ks]
+    attends = [dot_nt(q, k) for q, k in zip(qbs, kbs)]
+    grams = [dot_nt(k, k) for k in kbs]
+    betas = [parts[g][4][:, h : h + 1] for g, h in units]
+    cums = [parts[g][2][:, h : h + 1] for g, h in units]
+    rows_of = [parts[g][3][h : h + 1, :] for g, h in units]
+    lasts = [row[:, block - 1 :] for row in rows_of]
+    growths = [jnp.exp(c) for c in cums]
+    tails = [jnp.exp(last - c) for last, c in zip(lasts, cums)]
+    decs = [jnp.exp(last) for last in lasts]
+    bgs = [b * g for b, g in zip(betas, growths)]
+    withins = [jnp.exp(jnp.where(incl, c - r, -1e30)) for c, r in zip(cums, rows_of)]
+    stricts = [jnp.where(strict, w, 0.0) for w in withins]
+    attends = [a * w for a, w in zip(attends, withins)]
+    grams = [a * w for a, w in zip(grams, stricts)]
+    from_out = [dot_tn(a, do) for a, do in zip(attends, dos)]
+    into_state = [dot_tn(g * q, do) for g, q, do in zip(growths, qs, dos)]
+    tail_keys = [(t * k).astype(bf16) for t, k in zip(tails, ks)]
+    bg_keys = [(b * k).astype(bf16) for b, k in zip(bgs, ks)]
+    dss, dsbs, dbs, dbbs = {}, {}, {}, {}
+    for g in reversed(range(size // block)):
+        mine = [i for i, u in enumerate(units) if u[0] == g]
+        for h, i in enumerate(mine):
+            dss[i] = dstate[h]
+            dsbs[i] = dss[i].astype(bf16)
+        dus = [(from_out[i] + dot_nn(tail_keys[i], dsbs[i])).astype(bf16) for i in mine]
+        for h, i in enumerate(mine):
+            dbs[i] = dot_tn(inverse_ref[g, h], dus[h])
+            dbbs[i] = dbs[i].astype(bf16)
+        backs_in = [dot_tn(bg_keys[i], dbbs[i]) for i in mine]
+        for h, i in enumerate(mine):
+            dstate[h] = decs[i] * dss[i] + into_state[i] - backs_in[h]
+    index = range(len(units))
+    states = [states_ref[g, h] for g, h in units]
+    updates = [update_ref[place(u, value_dim)] for u in units]
+    das = [dot_nt(do, x) for do, x in zip(dos, updates)]
+    dls = [-dot_nt(dbbs[i], updates[i]) for i in index]
+    dqgs = [dot_nt(do, x) for do, x in zip(dos, states)]
+    dkbs = [-dot_nt(dbbs[i], states[i]) for i in index]
+    dkts = [dot_nt(updates[i], dsbs[i]) for i in index]
+    dgqs = [(x * w).astype(bf16) for x, w in zip(das, withins)]
+    dl_grams = [x * y for x, y in zip(dls, grams)]
+    dgks = [(x * w * b).astype(bf16) for x, w, b in zip(dls, stricts, betas)]
+    dqs = [dot_nn(x, k) for x, k in zip(dgqs, kbs)]
+    dks = [dot_tn(x, q) for x, q in zip(dgqs, qbs)]
+    dks = [y + dot_nn(x, k) for y, x, k in zip(dks, dgks, kbs)]
+    dks = [y + dot_tn(x, k) for y, x, k in zip(dks, dgks, kbs)]
+    mixes = [da * a + x * b for da, a, x, b in zip(das, attends, dl_grams, betas)]
+    sum_bks = [jnp.sum(x * k, -1, keepdims=True) for x, k in zip(dkbs, ks)]
+    sum_qgs = [jnp.sum(x * q, -1, keepdims=True) for x, q in zip(dqgs, qs)]
+    tail_sums = [t * jnp.sum(x * k, -1, keepdims=True) for t, x, k in zip(tails, dkts, ks)]
+    dbetas = [
+        jnp.sum(dbs[i] * cut(acts[2], units[i], value_dim), -1, keepdims=True)
+        + growths[i] * sum_bks[i]
+        + jnp.sum(dl_grams[i], -1, keepdims=True)
+        for i in index
+    ]
+    cum_cols = [
+        jnp.sum(mixes[i], -1, keepdims=True)
+        + growths[i] * sum_qgs[i]
+        + bgs[i] * sum_bks[i]
+        - tail_sums[i]
+        for i in index
+    ]
+    cum_rows = [jnp.sum(x, 0, keepdims=True) for x in mixes]
+    ends = [
+        jnp.sum(tail_sums[i], 0, keepdims=True)
+        + decs[i]
+        * jnp.sum(jnp.sum(states[i].astype(f32) * dss[i], -1, keepdims=True), 0, keepdims=True)
+        for i in index
+    ]
+    dqs = [(x + g * y) * (key_dim**-0.5) for x, g, y in zip(dqs, growths, dqgs)]
+    dks = [x + t * y + b * z for x, t, y, b, z in zip(dks, tails, dkts, bgs, dkbs)]
+    for i, u in enumerate(units):
+        keys, vals = place(u, key_dim), place(u, value_dim)
+        back_q[keys] = (
+            rqs[i] * (dqs[i] - uqs[i] * jnp.sum(dqs[i] * uqs[i], -1, keepdims=True)) * slopes[0][keys]
         )
-        cum_rows.append(jnp.sum(mix, 0, keepdims=True))
-        lasts.append(
-            jnp.sum(tail_sum, 0, keepdims=True)
-            + dec * jnp.sum(jnp.sum(state.astype(f32) * ds, -1, keepdims=True), 0, keepdims=True)
+        back_k[keys] = (
+            rks[i] * (dks[i] - ks[i] * jnp.sum(dks[i] * ks[i], -1, keepdims=True)) * slopes[1][keys]
         )
-        dq = dq * (key_dim**-0.5)
-        back_q[0:size, keys] = rq * (dq - uq * jnp.sum(dq * uq, -1, keepdims=True)) * slopes[0][:, keys]
-        back_k[0:size, keys] = rk * (dk - k * jnp.sum(dk * k, -1, keepdims=True)) * slopes[1][:, keys]
-        back_v[0:size, vals] = dv * slopes[2][:, vals]
-
-    dgain_ref[...] += grad_gain
-    rows, cols = iota((size, size), 0), iota((size, size), 1)
-    late = jnp.where(rows <= cols, 1.0, 0.0)
-    cum_all = jnp.concatenate(cum_cols, axis=1)
-    row_all = jnp.concatenate(cum_rows + [jnp.zeros((EDGE - heads, size), f32)], axis=0)
-    cum_all = cum_all - jnp.transpose(row_all)[:, :heads]
-    dld = dot_exact(late, cum_all) + jnp.concatenate(lasts, axis=1)
-    dalpha = dld * (-jnp.exp(dl_row_ref[...])) * sigmoid(alpha_col)
-    ddb_ref[...] += jnp.sum(dalpha, 0, keepdims=True)
-    ddl_ref[...] += jnp.sum(dld * ld_col, 0, keepdims=True)
-    dbeta = jnp.concatenate(dbetas, axis=1) * beta_col * (1.0 - beta_col)
-    dab_ref[...] = jnp.concatenate(
-        [dalpha, dbeta, jnp.zeros((size, EXTRA - 2 * heads), f32)], axis=1
-    ).astype(bf16)
+        back_v[vals] = betas[i] * dbs[i] * slopes[2][vals]
+
+    for g in range(size // block):
+        alpha_col, ld_col, _, _, beta_col = parts[g]
+        mine = [i for i, u in enumerate(units) if u[0] == g]
+        cum_all = jnp.concatenate([cum_cols[i] for i in mine], axis=1)
+        row_all = jnp.concatenate(
+            [cum_rows[i] for i in mine] + [jnp.zeros((EDGE - heads, block), f32)], axis=0
+        )
+        cum_all = cum_all - jnp.transpose(row_all)[:, :heads]
+        dld = dot_exact(late, cum_all) + jnp.concatenate([ends[i] for i in mine], axis=1)
+        dalpha = dld * (-jnp.exp(dl_row_ref[...])) * sigmoid(alpha_col)
+        ddb_ref[...] += jnp.sum(dalpha, 0, keepdims=True)
+        ddl_ref[...] += jnp.sum(dld * ld_col, 0, keepdims=True)
+        dbeta = jnp.concatenate([dbetas[i] for i in mine], axis=1) * beta_col * (1.0 - beta_col)
+        dab_ref[g * block : (g + 1) * block, :] = jnp.concatenate(
+            [dalpha, dbeta, jnp.zeros((block, EXTRA - 2 * heads), f32)], axis=1
+        ).astype(bf16)
     for ext, back, taps_ref, dp_ref, dt_ref in (
         (ext_q, back_q, tq_ref, dpq_ref, dtq_ref),
         (ext_k, back_k, tk_ref, dpk_ref, dtk_ref),
@@ -465,12 +570,14 @@
 ):
     blocks, heads, key_dim, value_dim = states.shape
     length, width = proj.shape
-    size = inverse.shape[-1]
+    block = inverse.shape[-1]
+    group = BACKWARD_GROUP if blocks % BACKWARD_GROUP == 0 else 1
+    size, steps = group * block, blocks // group
     kw, vw = heads * key_dim, heads * value_dim
     per_edge = size // EDGE
 
     def at(i):
-        return blocks - 1 - i
+        return steps - 1 - i
 
     def rows(width):
         return pl.BlockSpec((size, width), lambda i: (at(i), 0))
@@ -478,10 +585,12 @@
     def edge(width, column):
         return pl.BlockSpec((EDGE, width), lambda i: (jnp.maximum(at(i) * per_edge - 1, 0), column))
 
-    per_block = lambda *dims: pl.BlockSpec((1,) + dims, lambda i: (at(i),) + (0,) * len(dims))
+    def per_block(*dims):
+        return pl.BlockSpec((group,) + dims, lambda i: (at(i),) + (0,) * len(dims))
+
     return pl.pallas_call(
-        functools.partial(backward_kernel, heads, key_dim, value_dim, blocks),
-        grid=(blocks,),
+        functools.partial(backward_kernel, heads, key_dim, value_dim, steps, block),
+        grid=(steps,),
         out_shape=(
             jax.ShapeDtypeStruct((length, width), bf16),
             jax.ShapeDtypeStruct(tq.shape, f32),
@@ -505,7 +614,7 @@
             full_spec((heads, 1)),
             full_spec((1, value_dim)),
             per_block(heads, key_dim, value_dim),
-            per_block(heads, size, size),
+            per_block(heads, block, block),
             rows(vw),
             rows(vw),
             rows(vw),
@@ -531,7 +640,7 @@
         compiler_params=pltpu.CompilerParams(
             dimension_semantics=("arbitrary",), vmem_limit_bytes=56 * 1024 * 1024
         ),
-        cost_estimate=pl.CostEstimate(flops=0, bytes_accessed=200_000_000, transcendentals=0),
+        cost_estimate=pl.CostEstimate(flops=0, bytes_accessed=100_000_000, transcendentals=0),
         name="mixer_backward",
     )(
         proj,
@@ -1018,38 +1127,33 @@
     sigmoid_gate = jax.nn.sigmoid(gate_proj)
     activated = gate_proj * sigmoid_gate
     inner = (activated * up_proj).astype(bf16)
-    grad_down = cross_rows(inner, grad_gathered).astype(bf16)
-    grad_gathered, grad_down = lax.optimization_barrier((grad_gathered, grad_down))
-    grad_down_summed = lax.psum(grad_down, "dp")
     grad_inner = times_transposed(grad_gathered, w_ffn_down)
     grad_gate_rows = (
         grad_inner * up_proj * sigmoid_gate * (1.0 + gate_proj * (1.0 - sigmoid_gate))
     ).astype(bf16)
     grad_up_rows = (grad_inner * activated).astype(bf16)
+    grad_down = cross_rows(inner, grad_gathered).astype(bf16)
+    grad_gate_weight = cross_rows(grad_gate_rows, gathered_ffn).astype(bf16)
+    grad_down_summed, grad_gate_summed = lax.psum((grad_down, grad_gate_weight), "dp")
+    grad_gate_rows, grad_up_rows, grad_down, grad_gate_weight = lax.optimization_barrier(
+        (grad_gate_rows, grad_up_rows, grad_down, grad_gate_weight)
+    )
     part_normed_ffn = (
         times_transposed(grad_gate_rows, w_ffn_gate) + times_transposed(grad_up_rows, w_ffn_up)
     ).astype(bf16)
-    grad_gate_weight = cross_rows(grad_gate_rows, gathered_ffn).astype(bf16)
-    part_normed_ffn, grad_gate_weight = lax.optimization_barrier((part_normed_ffn, grad_gate_weight))
-    grad_gate_weight, grad_down_summed = lax.optimization_barrier((grad_gate_weight, grad_down_summed))
-    grad_gate_summed = lax.psum(grad_gate_weight, "dp")
     grad_normed_ffn = scatter_rows(part_normed_ffn, 3, sizes)
     part_gain_ffn = jnp.sum(grad_normed_ffn * scaled_ffn, 0)
     grad_hidden = grad_out_rows.astype(f32) + norm_backward(
         grad_normed_ffn, scaled_ffn, factor_ffn, gain_second
     )
     grad_attended = gather_rows(grad_hidden.astype(bf16), 4, sizes)
-    grad_attended, grad_down_summed = lax.optimization_barrier((grad_attended, grad_down_summed))
     grad_mixed = times_transposed(grad_attended, w_out)
     grad_up_weight = cross_rows(grad_up_rows, gathered_ffn).astype(bf16)
+    grad_out_weight = cross_rows(mixed, grad_attended).astype(bf16)
     ffn_part = jnp.dot(inner, w_ffn_down, preferred_element_type=f32).astype(bf16)
     grad_projected, grad_tq, grad_tk, grad_tv, grad_dl, grad_db, grad_gain = mixer_backward(
         projected, *extras, states, inverse, update, raw, grad_mixed
     )
-    grad_projected, grad_gate_summed = lax.optimization_barrier((grad_projected, grad_gate_summed))
-    grad_out_weight = cross_rows(mixed, grad_attended).astype(bf16)
-    grad_out_weight, grad_gate_summed = lax.optimization_barrier((grad_out_weight, grad_gate_summed))
-    grad_out_summed = lax.psum(grad_out_weight, "dp")
     part_normed = times_transposed(grad_projected, w_in).astype(bf16)
     grad_in = cross_rows(gathered, grad_projected).astype(bf16)
     part_gain_attn = jnp.sum(grad_in.astype(f32) * w_in.astype(f32), 1) / gain_first
@@ -1066,7 +1170,7 @@
         ffn_part,
         grad_down_summed,
         grad_gate_summed,
-        grad_out_summed,
+        grad_out_weight,
     ) = lax.optimization_barrier(
         (
             grad_in,
@@ -1076,16 +1180,16 @@
             ffn_part,
             grad_down_summed,
             grad_gate_summed,
-            grad_out_summed,
+            grad_out_weight,
         )
     )
     grad_normed = scatter_rows(part_normed, None, sizes)
     ffn_out = scatter_rows(ffn_part, None, sizes)
     output = (hidden + ffn_out).astype(bf16)
     gains = 2 * width + out_gain.shape[0]
-    small_summed, grad_up_summed, grad_in_summed, gain_grads = sum_over_line(
-        (small.reshape(smalls_rows, 128), grad_up_weight, grad_in),
-        (128, width, main),
+    small_summed, grad_up_summed, grad_out_summed, grad_in_summed, gain_grads = sum_over_line(
+        (small.reshape(smalls_rows, 128), grad_up_weight, grad_out_weight, grad_in),
+        (128, width, width, main),
         -(-gains // (16 * 128)) * 16,
         5,
         sizes,

time: 949 us -> 830 us (0.87)
  waiting for transfers between devices: 90.8 us -> 0.6 us
  Pallas kernels: 570 us -> 557 us
    psum x3 -> x1, waiting for transfers between devices: 90.2 us -> 0.01 us  [shards(): lax.psum((grad_down, grad_gate_weight), 'dp')]
    pallas_call x1, Pallas kernels: 232 us -> 279 us  [sum_over_line(): pl.pallas_call(functools.partial(line_kernel, 'dp', 'tensor', tuple(width...]
    pallas_call x1, Pallas kernels: 75.8 us -> 30 us  [mixer_forward(): pl.pallas_call(functools.partial(forward_kernel, heads, key_dim, value_di...]
    pallas_call x1, Pallas kernels: 62.4 us -> 48.9 us  [mixer_backward(): pl.pallas_call(functools.partial(backward_kernel, heads, key_dim, value_d...]
  transfers between devices with their start and end apart: 6 -> 4, of which waited for: 2 -> 0; matrix products, arithmetic and copies ran while one was open for 19% -> 22% of each run, Pallas kernels for 56% -> 63%
where the time goes in v4:
time: 830 us; the launch traced here: 820 us
  Pallas kernels  557 us (67%)
  matrix products  180 us (22%)
  other arithmetic  37.2 us (4%)
  local copies, waits for them, and re-layouts  31 us (4%)
  between operations  14.6 us (2%)
    pallas_call x1, Pallas kernels, sum_over_line(): pl.pallas_call(functools.partial(line_kernel, 'dp', 'tensor', tuple(width...  279 us
    pallas_call x3, Pallas kernels, gather_rows(): pl.pallas_call(functools.partial(gather_kernel, 'tensor'), out_shape=jax....  119 us
    pallas_call x2, Pallas kernels, scatter_rows(): pl.pallas_call(functools.partial(scatter_kernel, 'tensor'), out_shape=jax...  79.8 us
    dot_general x5, matrix products, times_transposed(): lax.dot_general(left, right, (((1,), (1,)), ((), ())), preferred_element_...  67.3 us
    dot_general x5, matrix products, cross_rows(): lax.dot_general(left, right, (((0,), (0,)), ((), ())), preferred_element_...  55.1 us
    pallas_call x1, Pallas kernels, mixer_backward(): pl.pallas_call(functools.partial(backward_kernel, heads, key_dim, value_d...  48.9 us
    pallas_call x1, Pallas kernels, mixer_forward(): pl.pallas_call(functools.partial(forward_kernel, heads, key_dim, value_di...  30 us
    dot_general x1, matrix products, shards(): projected = jnp.dot(gathered, w_in, preferred_element_type=f32)  21.3 us
  transfers between devices with their start and end apart: 4, of which 0 were waited for; matrix products, arithmetic and copies ran while one was open for 22% of the time, Pallas kernels for 63%

profile of v4, /device:TPU:0, one launch (start us, length us, event | category | flops | bytes accessed | tf_op | source)
XLA Modules:
  0.0 820.2 jit_solution(3770450223134310691)
XLA Ops:
  7.3 0.8 convert_element_type.108
  8.1 1.5 fusion.10
  9.6 0.5 copy-done.30
  10.2 2.5 fusion.4.x_ref
  12.7 41.3 %gather_rows.3 = bf16[2048,2048]{1,0:T(8,128)(2,1)} custom-call(bf16[256,2048]{1,0:T(8,128)(2,1)} %fusion.4.x_ref), custom_call_target="tpu_custom_call" | custom-call | bytes 1000000 | tf_op jit(solution)/shard_map/gather_rows/pallas_call | solution.py:755
  54.1 0.4 copy.49
  54.5 1.1 copy.50
  55.7 0.1 copy.51.dl_col_ref
  55.8 0.1 copy.52.db_col_ref
  55.9 0.9 broadcast_in_dim.22
  56.7 11.3 %concatenate.6 = bf16[2048,1664]{1,0:T(8,128)(2,1)} concatenate(bf16[2048,256]{1,0:T(8,128)(2,1)} %param.24, bf16[2048,256]{1,0:T(8,128)(2,1)} %param.25, bf16[2048,512]{1,0:T(8,128)(2,1)} %param.26, bf16[2048,512]{1,0:T(8,128)(2,1)} %param.29, bf16[2048,2]{1,0:T(8,128)(2,1)S(1)} %copy.49, bf16[2048,2]{1,0:T(8,128)(2,1)} %copy.50, bf16[2048,124]{1,0:T(8,128)(2,1)} %broadcast_in_dim.22), dimensions={1} | concatenate | bytes 13631488 | tf_op jit(solution)/shard_map/concatenate | solution.py:1103
  68.0 21.3 %fusion.16.proj_ref.eq_ref.ek_ref.ev_ref = f32[2048,1664]{1,0:T(8,128)} fusion(bf16[2048,2048]{1,0:T(8,128)(2,1)} %gather_rows.3, bf16[2048,1664]{1,0:T(8,128)(2,1)} %concatenate.6), kind=kOutput, calls=%fused_computation.55 | convolution fusion | flops 13958643712 | bytes 28835840 | tf_op jit(solution)/shard_map/dot_general | solution.py:1105
  89.4 30.0 %mixer_forward.1 = (bf16[2048,512]{1,0:T(8,128)(2,1)S(1)}, f32[2,128,256]{2,1,0:T(8,128)}, bf16[8,2,128,256]{3,2,1,0:T(8,128)(2,1)S(1)}, bf16[8,2,256,256]{3,2,1...) custom-call(f32[2048,1664]{1,0:T(8,128)} %fusion.16.proj_ref.eq_ref.ek_ref.ev_ref, ...), custom_call_target="tpu_custom_call" | custom-call | bytes 100000000 | tf_op jit(solution)/shard_map/mixer_forward/pallas_call | solution.py:278
  119.4 4.7 convolution_convert_fusion.1.p_ref
  124.2 39.9 %scatter_rows.2 = f32[256,2048]{1,0:T(8,128)S(1)} custom-call(bf16[2048,2048]{1,0:T(8,128)(2,1)S(1)} %convolution_convert_fusion.1.p_ref), custom_call_target="tpu_custom_call" | custom-call | bytes 1000000 | tf_op jit(solution)/shard_map/scatter_rows/pallas_call | solution.py:851
  164.1 0.4 multiply_reduce_fusion.3
  164.5 1.3 copy-done.16
  165.8 1.2 multiply_convert_fusion.3.x_ref
  167.0 38.8 %gather_rows.4 = bf16[2048,2048]{1,0:T(8,128)(2,1)} custom-call(bf16[256,2048]{1,0:T(8,128)(2,1)} %multiply_convert_fusion.3.x_ref), custom_call_target="tpu_custom_call" | custom-call | bytes 1000000 | tf_op jit(solution)/shard_map/gather_rows/pallas_call | solution.py:755
  205.8 10.9 %fusion.18 = f32[2048,688]{0,1:T(8,128)} fusion(bf16[2048,2048]{1,0:T(8,128)(2,1)} %gather_rows.4, bf16[2048,688]{0,1:T(8,128)(2,1)} %param.38), kind=kOutput, calls=%fused_computation.57 | convolution fusion | flops 5771362304 | bytes 16842752 | tf_op jit(solution)/shard_map/dot_general | solution.py:1125
  216.7 11.0 %fusion.17 = f32[2048,688]{0,1:T(8,128)} fusion(bf16[2048,2048]{1,0:T(8,128)(2,1)} %all-gather.2.cloned.1.call-done, bf16[688,2048]{1,0:T(8,128)(2,1)} %param.40), kind=kOutput, calls=%fused_computation.56 | convolution fusion | flops 5771362304 | bytes 16842752 | tf_op jit(solution)/shard_map/dot_general | solution.py:1061
  227.7 11.7 %multiply_convert_fusion = (bf16[2048,688]{0,1:T(8,128)(2,1)}, bf16[2048,688]{0,1:T(8,128)(2,1)S(1)}, bf16[2048,688]{0,1:T(8,128)(2,1)}) fusion(f32[2048,688]{0,1:T(8,128)S(1)} %copy-done.45, f32[2048,688]{0,1:T(8,128)} %fusion.17, bf16[2048,2048]{1,0:T(8,128)(2,1)S(1)} %copy-done.21, bf16[2048,688]{0,1:T(8,128)(2,1)S(1)} %copy-done), kind=kOutput, calls=%fused_computation.8 | convolution fusion | flops 5792497664 | bytes 30932992 | tf_op jit(solution)/shard_map/dot_general | solution.py:1126
  239.5 7.7 convolution_convert_fusion.5
  247.2 9.1 %convolution_convert_fusion = bf16[2048,2048]{1,0:T(8,128)(2,1)} fusion(bf16[2048,688]{0,1:T(8,128)(2,1)S(1)} %copy-done.48, bf16[688,2048]{1,0:T(8,128)(2,1)S(1)} %copy-done.42), kind=kOutput, calls=%fused_computation.2 | convolution fusion | flops 5775556608 | bytes 14024704 | tf_op jit(solution)/shard_map/dot_general | solution.py:1153
  256.3 10.3 %convolution_convert_fusion.6 = bf16[688,2048]{1,0:T(8,128)(2,1)} fusion(bf16[2048,688]{0,1:T(8,128)(2,1)} %get-tuple-element.87, bf16[2048,2048]{1,0:T(8,128)(2,1)} %all-gather.2.cloned.1.call-done), kind=kOutput, calls=%fused_computation.15 | convolution fusion | flops 5772771328 | bytes 14024704 | tf_op jit(solution)/shard_map/dot_general | solution.py:1057
  266.8 12.8 %fusion.19 = f32[2048,2048]{1,0:T(8,128)} fusion(bf16[2048,688]{0,1:T(8,128)(2,1)} %copy-done.47, bf16[2048,688]{0,1:T(8,128)(2,1)} %param.38), kind=kOutput, calls=%fused_computation.58 | convolution fusion | flops 5771362304 | bytes 22413312 | tf_op jit(solution)/shard_map/dot_general | solution.py:1061
  279.5 10.5 %add_convert_fusion.p_ref = bf16[2048,2048]{1,0:T(8,128)(2,1)S(1)} fusion(f32[2048,2048]{1,0:T(8,128)} %fusion.19, bf16[2048,688]{0,1:T(8,128)(2,1)S(1)} %copy-done.46, bf16[2048,688]{0,1:T(8,128)(2,1)S(1)} %copy-done), kind=kOutput, calls=%fused_computation | convolution fusion | flops 5779750912 | bytes 30801920 | tf_op jit(solution)/shard_map/dot_general | solution.py:1061
  290.1 39.9 %scatter_rows.3 = f32[256,2048]{1,0:T(8,128)S(1)} custom-call(bf16[2048,2048]{1,0:T(8,128)(2,1)S(1)} %add_convert_fusion.p_ref), custom_call_target="tpu_custom_call" | custom-call | bytes 1000000 | tf_op jit(solution)/shard_map/scatter_rows/pallas_call | solution.py:851
  330.0 0.6 multiply_reduce_fusion.1
  330.6 1.4 copy-done.20
  332.0 1.6 fusion.12.x_ref
  333.6 38.9 %gather_rows.5 = bf16[2048,2048]{1,0:T(8,128)(2,1)} custom-call(bf16[256,2048]{1,0:T(8,128)(2,1)} %fusion.12.x_ref), custom_call_target="tpu_custom_call" | custom-call | bytes 1000000 | tf_op jit(solution)/shard_map/gather_rows/pallas_call | solution.py:755
  372.5 11.9 %fusion.20.grad_ref = f32[2048,512]{1,0:T(8,128)} fusion(bf16[2048,2048]{1,0:T(8,128)(2,1)} %gather_rows.5, bf16[512,2048]{1,0:T(8,128)(2,1)} %param.36), kind=kOutput, calls=%fused_computation.59 | convolution fusion | flops 4294967296 | bytes 14680064 | tf_op jit(solution)/shard_map/dot_general | solution.py:1061
  384.4 5.8 convolution_convert_fusion.7.refs_2_
  390.3 48.9 %mixer_backward.1 = (bf16[2048,1664]{1,0:T(8,128)(2,1)}, f32[4,256]{1,0:T(4,128)}, f32[4,256]{1,0:T(4,128)}, f32[4,512]{1,0:T(4,128)}, f32[1,2]{1,0:T(1,128)}, /*index=5*/f32[1,2]{1,0:T(1,128)}, f32[1,256]{1,0:T(1,128)}) custom-call(f32[2048,1664]{1,0:T(8,128)} %fusion.16.proj_ref.eq_ref.ek_ref.ev_ref, f32[2048,1664]{1,0:T(8,128)} %fusion.16.proj_ref.eq_ref.ek_ref.ev_ref, ...), custom_call_target="tpu_custom_call" | custom-call | bytes 100000000 | tf_op jit(solution)/shard_map/mixer_backward/pallas_call | solution.py:591
  439.2 0.7 copy.58
  439.8 0.7 copy.59
  440.5 0.7 copy.60
  441.3 20.9 %multiply_reduce_fusion = (f32[2048]{0:T(1024)S(1)}, bf16[2048,1664]{1,0:T(8,128)(2,1)S(1)}) fusion(bf16[2048,1664]{1,0:T(8,128)(2,1)} %concatenate.6, bf16[2048,2048]{1,0:T(8,128)(2,1)} %gather_rows.3, bf16[2048,1664]{1,0:T(8,128)(2,1)} %get-tuple-element.60), kind=kOutput, calls=%fused_computation.1 | convolution fusion | flops 13975681024 | bytes 28844032 | tf_op jit(solution)/shard_map/dot_general | solution.py:1057
  462.2 2.7 copy-done.23
  465.0 0.3 copy.56
  465.4 0.7 concatenate.7
  466.1 10.3 %convolution_convert_fusion.4.refs_1_ = bf16[688,2048]{1,0:T(8,128)(2,1)} fusion(bf16[2048,688]{0,1:T(8,128)(2,1)} %get-tuple-element.59, bf16[2048,2048]{1,0:T(8,128)(2,1)} %gather_rows.4), kind=kOutput, calls=%fused_computation.13 | convolution fusion | flops 5772771328 | bytes 14024704 | tf_op jit(solution)/shard_map/dot_general | solution.py:1057
  476.4 21.1 %convolution_convert_fusion.2 = bf16[2048,2048]{1,0:T(8,128)(2,1)} fusion(bf16[2048,1664]{1,0:T(8,128)(2,1)} %get-tuple-element.60, bf16[2048,1664]{1,0:T(8,128)(2,1)} %concatenate.6), kind=kOutput, calls=%fused_computation.4 | convolution fusion | flops 13962838016 | bytes 22020096 | tf_op jit(solution)/shard_map/dot_general | solution.py:1061
  497.6 0.5 reduce-scatter.3.cloned.1.call-update
  498.1 278.8 %sum_over_line.1 = (f32[144,128]{1,0:T(8,128)}, bf16[688,2048]{1,0:T(8,128)(2,1)}, bf16[512,2048]{1,0:T(8,128)(2,1)}, bf16[2048,1536]{1,0:T(8,128)(2,1)}, f32[48,128]{1,0:T(8,128)}) custom-call(f32[144,128]{1,0:T(8,128)} %bitcast.91, bf16[688,2048]{1,0:T(8,128)(2,1)} %convolution_convert_fusion.4.refs_1_, ...), custom_call_target="tpu_custom_call" | custom-call | bytes 1124352000 | tf_op jit(solution)/shard_map/sum_over_line/pallas_call | solution.py:1037
  777.0 0.7 slice.83
  777.7 0.9 fusion.15
  778.5 0.6 slice.77
  779.2 0.6 slice.79
  779.8 0.8 fusion.14
  780.6 0.6 reshape.124
  781.2 0.6 reshape.125
  781.8 0.6 reshape.126
  782.4 4.3 convert_element_type.138
  786.7 3.2 convert_element_type.139
  789.9 1.3 fusion.13
  791.2 0.6 slice_bitcast_fusion.2
  791.8 0.6 slice_bitcast_fusion
  792.4 2.3 slice_convert_fusion.2
  794.7 4.6 slice_convert_fusion
  799.3 5.9 convert_bitcast_fusion
  805.2 1.8 fusion.5
  807.0 6.4 fusion.9
  (123 shorter events, 0.6 us)
Async XLA Ops:
  7.2 220.5 %copy-start = (bf16[2048,688]{0,1:T(8,128)(2,1)S(1)}, bf16[2048,688]{0,1:T(8,128)(2,1)}, u32[]{:S(2)}) copy-start(bf16[2048,688]{0,1:T(8,128)(2,1)} %param.39) | copy-start | bytes 8454148
  7.2 209.5 %all-gather.2.cloned.1.call-start = ((), (), s32[]{:S(2)}) async-start(), calls=%async_computation.2 | async-start | bytes 9437184 | tf_op jit(solution)/shard_map/all_gather | solution.py:1116
  8.1 1.5 copy-start.27
  9.6 0.5 copy-start.30
  12.7 41.4 %copy-start.33 = (bf16[2048,2]{0,1:T(2,128)(2,1)S(1)}, bf16[2048,2]{0,1:T(2,128)(2,1)}, u32[]{:S(2)}) copy-start(bf16[2048,2]{0,1:T(2,128)(2,1)} %param.27) | copy-start | bytes 24580
  12.7 41.8 %copy-start.34 = (bf16[2048,2]{0,1:T(2,128)(2,1)S(1)}, bf16[2048,2]{0,1:T(2,128)(2,1)}, u32[]{:S(2)}) copy-start(bf16[2048,2]{0,1:T(2,128)(2,1)} %param.28) | copy-start | bytes 24580
  12.7 42.9 %copy-start.37 = (bf16[4,256]{1,0:T(4,128)(2,1)S(1)}, bf16[4,256]{1,0:T(4,128)(2,1)}, u32[]{:S(2)}) copy-start(bf16[4,256]{1,0:T(4,128)(2,1)} %param.30) | copy-start | bytes 6148
  12.7 42.9 %copy-start.38 = (bf16[4,256]{1,0:T(4,128)(2,1)S(1)}, bf16[4,256]{1,0:T(4,128)(2,1)}, u32[]{:S(2)}) copy-start(bf16[4,256]{1,0:T(4,128)(2,1)} %param.31) | copy-start | bytes 6148
  12.7 42.9 %copy-start.35 = (bf16[4,512]{1,0:T(4,128)(2,1)S(1)}, bf16[4,512]{1,0:T(4,128)(2,1)}, u32[]{:S(2)}) copy-start(bf16[4,512]{1,0:T(4,128)(2,1)} %param.32) | copy-start | bytes 12292
  12.7 43.0 %copy-start.12 = (f32[2]{0:T(128)S(1)}, f32[2]{0:T(128)}, u32[]{:S(2)}) copy-start(f32[2]{0:T(128)} %param.33) | copy-start | bytes 28
  12.7 43.0 %copy-start.13 = (f32[2]{0:T(128)S(1)}, f32[2]{0:T(128)}, u32[]{:S(2)}) copy-start(f32[2]{0:T(128)} %param.34) | copy-start | bytes 28
  12.7 43.1 %copy-start.44 = (bf16[256]{0:T(256)(128)(2,1)S(1)}, bf16[256]{0:T(256)(128)(2,1)}, u32[]{:S(2)}) copy-start(bf16[256]{0:T(256)(128)(2,1)} %param.35) | copy-start | bytes 1540
  54.1 443.4 %all-reduce.3.cloned.1.call-start = ((), (), s32[]{:S(2)}) async-start(), calls=%async_computation.5 | async-start | bytes 11272192 | tf_op jit(solution)/shard_map/psum | solution.py:1137
  55.6 33.7 %copy-start.7 = (f32[4,256]{1,0:T(4,128)}, f32[4,256]{1,0:T(4,128)S(1)}, u32[]{:S(2)}) copy-start(f32[4,256]{1,0:T(4,128)S(1)} %convert_element_type.110.tq_ref) | copy-start | bytes 12292
  55.6 33.7 %copy-start.8 = (f32[4,256]{1,0:T(4,128)}, f32[4,256]{1,0:T(4,128)S(1)}, u32[]{:S(2)}) copy-start(f32[4,256]{1,0:T(4,128)S(1)} %convert_element_type.111.tk_ref) | copy-start | bytes 12292
  55.6 33.7 %copy-start.6 = (f32[4,512]{1,0:T(4,128)}, f32[4,512]{1,0:T(4,128)S(1)}, u32[]{:S(2)}) copy-start(f32[4,512]{1,0:T(4,128)S(1)} %convert_element_type.112.tv_ref) | copy-start | bytes 24580
  55.7 33.6 %copy-start.9 = (f32[2,1]{1,0:T(2,128)}, f32[2,1]{1,0:T(2,128)S(1)}, u32[]{:S(2)}) copy-start(f32[2,1]{1,0:T(2,128)S(1)} %copy.51.dl_col_ref) | copy-start | bytes 28
  55.8 33.5 %copy-start.10 = (f32[2,1]{1,0:T(2,128)}, f32[2,1]{1,0:T(2,128)S(1)}, u32[]{:S(2)}) copy-start(f32[2,1]{1,0:T(2,128)S(1)} %copy.52.db_col_ref) | copy-start | bytes 28
  55.9 33.5 %copy-start.11 = (f32[256]{0:T(256)}, f32[256]{0:T(256)S(1)}, u32[]{:S(2)}) copy-start(f32[256]{0:T(256)S(1)} %broadcast_in_dim.56) | copy-start | bytes 3076
  68.0 21.3 %copy-start.5 = (f32[1,2,128,256]{3,2,1,0:T(8,128)S(1)}, f32[1,2,128,256]{3,2,1,0:T(8,128)}, u32[]{:S(2)}) copy-start(f32[1,2,128,256]{3,2,1,0:T(8,128)} %param.22) | copy-start | bytes 786436
  89.3 30.0 %copy-start.43 = (bf16[512,2048]{1,0:T(8,128)(2,1)S(1)}, bf16[512,2048]{1,0:T(8,128)(2,1)}, u32[]{:S(2)}) copy-start(bf16[512,2048]{1,0:T(8,128)(2,1)} %param.36) | copy-start | bytes 6291460
  119.4 4.8 copy-start.3
  119.4 4.8 copy-start.4
  119.4 4.8 copy-start.14
  124.2 40.0 %copy-start.36 = (bf16[2048]{0:T(1024)(128)(2,1)S(1)}, bf16[2048]{0:T(1024)(128)(2,1)}, u32[]{:S(2)}) copy-start(bf16[2048]{0:T(1024)(128)(2,1)} %param.37) | copy-start | bytes 12292
  124.2 40.0 %copy-start.18 = (bf16[1,256,2048]{2,1,0:T(8,128)(2,1)S(1)}, bf16[1,256,2048]{2,1,0:T(8,128)(2,1)}, u32[]{:S(2)}) copy-start(bf16[1,256,2048]{2,1,0:T(8,128)(2,1)} %param.21) | copy-start | bytes 3145732
  164.5 1.3 copy-start.16
  216.7 11.0 %copy-start.21 = (bf16[2048,2048]{1,0:T(8,128)(2,1)S(1)}, bf16[2048,2048]{1,0:T(8,128)(2,1)}, u32[]{:S(2)}) copy-start(bf16[2048,2048]{1,0:T(8,128)(2,1)} %gather_rows.4) | copy-start | bytes 25165828
  216.7 11.0 %copy-start.45 = (f32[2048,688]{0,1:T(8,128)S(1)}, f32[2048,688]{0,1:T(8,128)}, u32[]{:S(2)}) copy-start(f32[2048,688]{0,1:T(8,128)} %fusion.18) | copy-start | bytes 16908292
  239.5 7.7 copy-start.47
  239.5 7.7 copy-start.42
  239.5 7.7 copy-start.48
  266.7 538.5 %reduce-scatter.5.cloned.1.call-start = ((), (), s32[]{:S(2)}) async-start(), calls=%async_computation.4 | async-start | bytes 9437184 | tf_op jit(solution)/shard_map/reduce_scatter | solution.py:847
  266.7 12.8 %copy-start.46 = (bf16[2048,688]{0,1:T(8,128)(2,1)S(1)}, bf16[2048,688]{0,1:T(8,128)(2,1)}, u32[]{:S(2)}) copy-start(bf16[2048,688]{0,1:T(8,128)(2,1)} %get-tuple-element.59) | copy-start | bytes 8454148
  290.0 39.9 %copy-start.17 = (f32[256,2048]{1,0:T(8,128)S(1)}, f32[256,2048]{1,0:T(8,128)}, u32[]{:S(2)}) copy-start(f32[256,2048]{1,0:T(8,128)} %copy-done.16) | copy-start | bytes 6291460
  330.0 3.6 copy-start.2
  330.0 2.0 copy-start.20
  372.5 11.9 %copy-start.15 = (bf16[2048,512]{1,0:T(8,128)(2,1)S(1)}, bf16[2048,512]{1,0:T(8,128)(2,1)}, u32[]{:S(2)}) copy-start(bf16[2048,512]{1,0:T(8,128)(2,1)} %copy-done.14) | copy-start | bytes 6291460
  372.5 11.9 %copy-start.22 = (bf16[2048,2048]{1,0:T(8,128)(2,1)S(1)}, bf16[2048,2048]{1,0:T(8,128)(2,1)}, u32[]{:S(2)}) copy-start(bf16[2048,2048]{1,0:T(8,128)(2,1)} %gather_rows.5) | copy-start | bytes 25165828
  441.2 24.1 %copy-start.29 = (bf16[2048]{0:T(1024)(128)(2,1)S(1)}, bf16[2048]{0:T(1024)(128)(2,1)}, u32[]{:S(2)}) copy-start(bf16[2048]{0:T(1024)(128)(2,1)} %param.23) | copy-start | bytes 12292
  441.2 24.1 %copy-start.39 = (f32[1,256]{1,0:T(1,128)S(1)}, f32[1,256]{1,0:T(1,128)}, u32[]{:S(2)}) copy-start(f32[1,256]{1,0:T(1,128)} %get-tuple-element.61) | copy-start | bytes 3076
  441.2 24.1 %copy-start.40 = (f32[1,2]{1,0:T(1,128)S(1)}, f32[1,2]{1,0:T(1,128)}, u32[]{:S(2)}) copy-start(f32[1,2]{1,0:T(1,128)} %get-tuple-element.65) | copy-start | bytes 28
  441.2 24.1 %copy-start.41 = (f32[1,2]{1,0:T(1,128)S(1)}, f32[1,2]{1,0:T(1,128)}, u32[]{:S(2)}) copy-start(f32[1,2]{1,0:T(1,128)} %get-tuple-element.66) | copy-start | bytes 28
  462.2 2.7 copy-start.23
  497.5 309.5 %reduce-scatter.3.cloned.1.call-start = ((), (), s32[]{:S(2)}) async-start(), calls=%async_computation.3 | async-start | bytes 9437184 | tf_op jit(solution)/shard_map/reduce_scatter | solution.py:847
  498.1 288.5 %copy-start.24 = (bf16[688,2048]{1,0:T(8,128)(2,1)S(1)}, bf16[688,2048]{1,0:T(8,128)(2,1)}, u32[]{:S(2)}) copy-start(bf16[688,2048]{1,0:T(8,128)(2,1)} %get-tuple-element.80) | copy-start | bytes 8454148
  782.4 10.0 %slice-start = ((s8[6291456]{0:T(1024)(128)(4,1)}), s8[4194304]{0:T(1024)(128)(4,1)S(1)}, s32[]{:S(2)}) async-start(s8[6291456]{0:T(1024)(128)(4,1)} %bitcast.89), calls=%async_computation.6 | async-start | bytes 8388608
  786.7 4.6 copy-start.32
  786.7 5.8 slice-start.1
  794.7 4.6 copy-start.25
  794.7 4.6 copy-start.26
  799.3 5.9 copy-start.19
  799.3 5.9 copy-start.28
  799.3 5.9 copy-start.31
  807.0 6.4 copy-start.1
Sparse Core Ops, SparseCore 0:
  54.2 54.7 all-gather.1
  266.8 202.5 all-reduce.2
  497.7 71.8 reduce-scatter.4
  573.2 71.2 reduce-scatter.2

commit v5 on v4

--- a/solution.py
+++ b/solution.py
@@ -663,6 +663,23 @@
     )
 
 
+def rms_factor(matrix):
+    return lax.rsqrt(jnp.mean(matrix * matrix, -1, keepdims=True) + norm_eps)
+
+
+def cross_rows(left, right):
+    return lax.dot_general(left, right, (((0,), (0,)), ((), ())), preferred_element_type=f32)
+
+
+def times_transposed(left, right):
+    return lax.dot_general(left, right, (((1,), (1,)), ((), ())), preferred_element_type=f32)
+
+
+def norm_backward(grad_normed, scaled, factor, gain_value):
+    weighted = grad_normed * gain_value
+    return factor * (weighted - scaled * jnp.mean(weighted * scaled, -1, keepdims=True))
+
+
 def copy_to(src, dst, send, recv, axis, index):
     return pltpu.make_async_remote_copy(
         src_ref=src,
@@ -694,17 +711,23 @@
 PIECES = 4
 
 
-def gather_kernel(axis, x_ref, out_ref, send, recv, local):
+def square(axis_sizes):
+    return axis_sizes["tensor"] == 8 and axis_sizes["dp"] == 4
+
+
+def gather_parts(axis, x_ref, held, send, recv, local):
     me, other, along_x, along_y = neighbours(axis)
     rows = x_ref.shape[0]
     part = rows // PIECES
     diagonal = along_x + along_y - me
+    shift = other - me
+    order = (me, other, along_x, along_y, along_x + shift, along_y + shift, diagonal, diagonal + shift)
     greet(axis, (other, along_x, along_y))
 
     def place(shard, j):
-        return out_ref.at[pl.ds(pl.multiple_of(shard * rows + j * part, part), part), :]
-
-    own = pltpu.make_async_copy(x_ref, out_ref.at[pl.ds(pl.multiple_of(me * rows, rows), rows), :], local)
+        return held.at[pl.ds(pl.multiple_of(shard * rows + j * part, part), part), :]
+
+    own = pltpu.make_async_copy(x_ref, held.at[pl.ds(pl.multiple_of(me * rows, rows), rows), :], local)
     own.start()
     copies = {}
 
@@ -714,162 +737,518 @@
         copies[kind, j] = copy_to(src, place(shard, j), send.at[index], recv.at[index], axis, target)
         copies[kind, j].start()
 
+    half = PIECES // 2
     for j in range(PIECES):
         begin("ox", j, along_x, me)
-        begin("oy", (j + PIECES // 2) % PIECES, along_y, me)
-    for j in range(PIECES):
+        begin("oy", (j + half) % PIECES, along_y, me)
         begin("oc", j, other, me)
-    for j in range(PIECES):
+
+    def hop(j):
+        k = (j + half) % PIECES
         copies["ox", j].wait_recv()
-        if j < PIECES // 2:
+        if j < half:
             begin("xy", j, along_y, along_x)
         begin("xc", j, other, along_x)
-        k = (j + PIECES // 2) % PIECES
         copies["oy", k].wait_recv()
-        if k >= PIECES // 2:
+        if k >= half:
             begin("yx", k, along_x, along_y)
         begin("yc", k, other, along_y)
-    for j in range(PIECES // 2):
-        copies["xy", j].wait_recv()
-        begin("dc", j, other, diagonal)
-        k = j + PIECES // 2
-        copies["yx", k].wait_recv()
-        begin("dc", k, other, diagonal)
-    for j in range(PIECES):
-        for kind in ("oc", "xc", "yc", "dc"):
-            copies[kind, j].wait_recv()
-    for copy in copies.values():
-        copy.wait_send()
-    own.wait()
-
-
-def square(axis_sizes):
-    return axis_sizes["tensor"] == 8 and axis_sizes["dp"] == 4
-
-
-def gather_rows(rows, identity, sizes):
+
+    def ready(i):
+        if i == 0:
+            own.wait()
+        elif i == 2:
+            for j in range(PIECES):
+                hop(j)
+        elif i == 6:
+            for j in range(half):
+                copies["xy", j].wait_recv()
+                begin("dc", j, other, diagonal)
+                copies["yx", j + half].wait_recv()
+                begin("dc", j + half, other, diagonal)
+        elif i != 3:
+            kind = {1: "oc", 4: "xc", 5: "yc", 7: "dc"}[i]
+            for j in range(PIECES):
+                copies[kind, j].wait_recv()
+        return order[i]
+
+    def finish():
+        for copy in copies.values():
+            copy.wait_send()
+
+    return ready, finish
+
+
+def rows_at(ref, shard, rows):
+    return ref.at[pl.ds(pl.multiple_of(shard * rows, rows), rows), :]
+
+
+def columns_at(ref, shard, rows):
+    return ref.at[:, pl.ds(pl.multiple_of(shard * rows, rows), rows)]
+
+
+def gather_project_kernel(
+    axis,
+    x_ref,
+    alpha_ref,
+    beta_ref,
+    wq_ref,
+    wk_ref,
+    wv_ref,
+    wg_ref,
+    all_ref,
+    w_ref,
+    y_ref,
+    held,
+    weights,
+    stage,
+    send,
+    recv,
+    local,
+    keep,
+    load,
+    out,
+):
+    rows = x_ref.shape[0]
+    ready, finish = gather_parts(axis, x_ref, held, send, recv, local)
+    loads, at = [], 0
+    for i, ref in enumerate((wq_ref, wk_ref, wv_ref, wg_ref)):
+        width = ref.shape[1]
+        loads.append(pltpu.make_async_copy(ref, weights.at[:, pl.ds(at, width)], load.at[i]))
+        loads[-1].start()
+        at += width
+    main = at
+    heads, depth = alpha_ref.shape
+    thin = jnp.concatenate(
+        [
+            alpha_ref[...].astype(f32),
+            beta_ref[...].astype(f32),
+            jnp.zeros((EXTRA - 2 * heads, depth), f32),
+        ],
+        axis=0,
+    )
+    weights[:, main:] = jnp.transpose(thin).astype(bf16)
+    for copy in loads:
+        copy.wait()
+    save = pltpu.make_async_copy(weights, w_ref, load.at[4])
+    save.start()
+    tile = main // 3
+    keeps, outs = [], []
+    for i in range(8):
+        shard = ready(i)
+        keeps.append(pltpu.make_async_copy(rows_at(held, shard, rows), rows_at(all_ref, shard, rows), keep.at[i]))
+        keeps[-1].start()
+        if i >= 2:
+            outs[i - 2].wait()
+        slot = i % 2
+
+        def column(t, carry):
+            here = pl.ds(pl.multiple_of(t * tile, 128), tile)
+            stage[slot, :, here] = dot_nn(rows_at(held, shard, rows)[...], weights[:, here])
+            return carry
+
+        lax.fori_loop(0, 3, column, 0)
+        stage[slot, :, main:] = dot_nn(rows_at(held, shard, rows)[...], weights[:, main:])
+        outs.append(pltpu.make_async_copy(stage.at[slot], rows_at(y_ref, shard, rows), out.at[i]))
+        outs[-1].start()
+    for copy in keeps + outs[6:] + [save]:
+        copy.wait()
+    finish()
+
+
+def gather_scratch(rows, width):
+    count = 7 * PIECES
+    return [
+        pltpu.SemaphoreType.DMA((count,)),
+        pltpu.SemaphoreType.DMA((count,)),
+        pltpu.SemaphoreType.DMA,
+        pltpu.SemaphoreType.DMA((8,)),
+    ]
+
+
+ANYWHERE = pl.BlockSpec(memory_space=pl.ANY)
+IN_VMEM = pl.BlockSpec(memory_space=pltpu.VMEM)
+
+
+def gather_project(x, w_query, w_key, w_value, w_gate_out, w_alpha, w_beta, identity, sizes):
+    heads = w_alpha.shape[1]
+    rows, depth = x.shape
+    mains = (w_query, w_key, w_value, w_gate_out)
+    width = sum(w.shape[1] for w in mains) + EXTRA
     if not square(sizes):
-        return lax.all_gather(rows, "tensor", axis=0, tiled=True)
-    height, width = rows.shape
-    count = 7 * PIECES
+        padding = jnp.zeros((depth, EXTRA - 2 * heads), bf16)
+        w_in = jnp.concatenate(mains + (w_alpha, w_beta, padding), axis=1)
+        gathered = lax.all_gather(x, "tensor", axis=0, tiled=True)
+        return gathered, w_in, jnp.dot(gathered, w_in, preferred_element_type=f32)
     return pl.pallas_call(
-        functools.partial(gather_kernel, "tensor"),
-        out_shape=jax.ShapeDtypeStruct((8 * height, width), rows.dtype),
-        in_specs=[pl.BlockSpec(memory_space=pl.ANY)],
-        out_specs=pl.BlockSpec(memory_space=pl.ANY),
+        functools.partial(gather_project_kernel, "tensor"),
+        out_shape=(
+            jax.ShapeDtypeStruct((8 * rows, depth), bf16),
+            jax.ShapeDtypeStruct((depth, width), bf16),
+            jax.ShapeDtypeStruct((8 * rows, width), f32),
+        ),
+        in_specs=[ANYWHERE, IN_VMEM, IN_VMEM] + [ANYWHERE] * 4,
+        out_specs=(ANYWHERE,) * 3,
         scratch_shapes=[
-            pltpu.SemaphoreType.DMA((count,)),
-            pltpu.SemaphoreType.DMA((count,)),
-            pltpu.SemaphoreType.DMA,
-        ],
-        compiler_params=pltpu.CompilerParams(collective_id=identity, has_side_effects=True),
+            pltpu.VMEM((8 * rows, depth), bf16),
+            pltpu.VMEM((depth, width), bf16),
+            pltpu.VMEM((2, rows, width), f32),
+        ]
+        + gather_scratch(rows, depth)
+        + [pltpu.SemaphoreType.DMA((5,)), pltpu.SemaphoreType.DMA((8,))],
+        compiler_params=pltpu.CompilerParams(
+            collective_id=identity, has_side_effects=True, vmem_limit_bytes=40 * 1024 * 1024
+        ),
         cost_estimate=pl.CostEstimate(flops=0, bytes_accessed=1_000_000, transcendentals=0),
-        name="gather_rows",
-    )(rows)
-
-
-def scatter_kernel(axis, p_ref, out_ref, mine, theirs, in_dx, in_dy, in_x, in_y, load, send, recv):
+        name="gather_project",
+    )(x, w_alpha.T, w_beta.T, *mains)
+
+
+def gather_expand_kernel(
+    axis,
+    x_ref,
+    wg_ref,
+    wu_ref,
+    all_ref,
+    gate_ref,
+    up_ref,
+    inner_ref,
+    held,
+    w_gate,
+    w_up,
+    gates,
+    ups,
+    inners,
+    send,
+    recv,
+    local,
+    keep,
+    load,
+    out,
+):
+    rows = x_ref.shape[0]
+    ready, finish = gather_parts(axis, x_ref, held, send, recv, local)
+    loads = [
+        pltpu.make_async_copy(wg_ref, w_gate, load.at[0]),
+        pltpu.make_async_copy(wu_ref, w_up, load.at[1]),
+    ]
+    for copy in loads:
+        copy.start()
+    for copy in loads:
+        copy.wait()
+    keeps, outs = [], []
+    for i in range(8):
+        shard = ready(i)
+        keeps.append(pltpu.make_async_copy(rows_at(held, shard, rows), rows_at(all_ref, shard, rows), keep.at[i]))
+        keeps[-1].start()
+        if i >= 2:
+            for copy in outs[i - 2]:
+                copy.wait()
+        slot = i % 2
+        x = rows_at(held, shard, rows)[...]
+        gate = dot_nt(w_gate[...], x)
+        gates[slot] = gate
+        up = dot_nt(w_up[...], x)
+        ups[slot] = up
+        inners[slot] = (gate * sigmoid(gate) * up).astype(bf16)
+        moves = []
+        for k, (src, dst) in enumerate(((gates, gate_ref), (ups, up_ref), (inners, inner_ref))):
+            moves.append(pltpu.make_async_copy(src.at[slot], columns_at(dst, shard, rows), out.at[k, i]))
+            moves[-1].start()
+        outs.append(moves)
+    for copy in keeps + outs[6] + outs[7]:
+        copy.wait()
+    finish()
+
+
+def gather_expand(x, gate_rows, up_rows, identity, sizes):
+    rows, depth = x.shape
+    units = gate_rows.shape[0]
+    if not square(sizes):
+        gathered = lax.all_gather(x, "tensor", axis=0, tiled=True)
+        gate, up = times_transposed(gate_rows, gathered), times_transposed(up_rows, gathered)
+        return gathered, gate, up, (gate * sigmoid(gate) * up).astype(bf16)
+    return pl.pallas_call(
+        functools.partial(gather_expand_kernel, "tensor"),
+        out_shape=(
+            jax.ShapeDtypeStruct((8 * rows, depth), bf16),
+            jax.ShapeDtypeStruct((units, 8 * rows), f32),
+            jax.ShapeDtypeStruct((units, 8 * rows), f32),
+            jax.ShapeDtypeStruct((units, 8 * rows), bf16),
+        ),
+        in_specs=[ANYWHERE] * 3,
+        out_specs=(ANYWHERE,) * 4,
+        scratch_shapes=[
+            pltpu.VMEM((8 * rows, depth), bf16),
+            pltpu.VMEM((units, depth), bf16),
+            pltpu.VMEM((units, depth), bf16),
+            pltpu.VMEM((2, units, rows), f32),
+            pltpu.VMEM((2, units, rows), f32),
+            pltpu.VMEM((2, units, rows), bf16),
+        ]
+        + gather_scratch(rows, depth)
+        + [pltpu.SemaphoreType.DMA((2,)), pltpu.SemaphoreType.DMA((3, 8))],
+        compiler_params=pltpu.CompilerParams(
+            collective_id=identity, has_side_effects=True, vmem_limit_bytes=40 * 1024 * 1024
+        ),
+        cost_estimate=pl.CostEstimate(flops=0, bytes_accessed=1_000_000, transcendentals=0),
+        name="gather_expand",
+    )(x, gate_rows, up_rows)
+
+
+def gather_back_kernel(axis, x_ref, w_ref, all_ref, y_ref, held, weights, stage, send, recv, local, keep, load, out):
+    rows = x_ref.shape[0]
+    ready, finish = gather_parts(axis, x_ref, held, send, recv, local)
+    copy = pltpu.make_async_copy(w_ref, weights, load)
+    copy.start()
+    copy.wait()
+    keeps, outs = [], []
+    for i in range(8):
+        shard = ready(i)
+        keeps.append(pltpu.make_async_copy(rows_at(held, shard, rows), rows_at(all_ref, shard, rows), keep.at[i]))
+        keeps[-1].start()
+        if i >= 2:
+            outs[i - 2].wait()
+        slot = i % 2
+        stage[slot] = dot_nt(rows_at(held, shard, rows)[...], weights[...])
+        outs.append(pltpu.make_async_copy(stage.at[slot], rows_at(y_ref, shard, rows), out.at[i]))
+        outs[-1].start()
+    for copy in keeps + outs[6:]:
+        copy.wait()
+    finish()
+
+
+def gather_back(x, w, identity, sizes):
+    rows, depth = x.shape
+    width = w.shape[0]
+    if not square(sizes):
+        gathered = lax.all_gather(x, "tensor", axis=0, tiled=True)
+        return gathered, times_transposed(gathered, w)
+    return pl.pallas_call(
+        functools.partial(gather_back_kernel, "tensor"),
+        out_shape=(
+            jax.ShapeDtypeStruct((8 * rows, depth), bf16),
+            jax.ShapeDtypeStruct((8 * rows, width), f32),
+        ),
+        in_specs=[ANYWHERE] * 2,
+        out_specs=(ANYWHERE,) * 2,
+        scratch_shapes=[
+            pltpu.VMEM((8 * rows, depth), bf16),
+            pltpu.VMEM((width, depth), bf16),
+            pltpu.VMEM((2, rows, width), f32),
+        ]
+        + gather_scratch(rows, depth)
+        + [pltpu.SemaphoreType.DMA, pltpu.SemaphoreType.DMA((8,))],
+        compiler_params=pltpu.CompilerParams(
+            collective_id=identity, has_side_effects=True, vmem_limit_bytes=40 * 1024 * 1024
+        ),
+        cost_estimate=pl.CostEstimate(flops=0, bytes_accessed=1_000_000, transcendentals=0),
+        name="gather_back",
+    )(x, w)
+
+
+def scatter_parts(axis, product, finish, mine, theirs, leaving, in_dx, in_dy, in_x, in_y, send, recv):
     me, other, along_x, along_y = neighbours(axis)
-    rows = out_ref.shape[0]
+    rows = in_x.shape[0]
     half = rows // 2
     diagonal = along_x + along_y - me
     greet(axis, (other, along_x, along_y))
+    shift = other - me
+    first, second = pl.ds(0, half), pl.ds(half, half)
     goals = (diagonal, along_x, along_y, me)
-    shift = other - me
-    loads, swaps, copies = [], [], []
-
-    def shard(index, part=None):
-        if part is None:
-            return p_ref.at[pl.ds(pl.multiple_of(index * rows, rows), rows), :]
-        return p_ref.at[pl.ds(pl.multiple_of(index * rows + part * half, half), half), :]
-
-    for r, goal in enumerate(goals):
-        for part in range(2):
-            slot = 2 * r + part
-            at = pl.ds(part * half, half)
-            swap = copy_to(
-                shard(goal + shift, part), theirs.at[r, at, :], send.at[slot], recv.at[slot], axis, other
-            )
-            swap.start()
-            swaps.append(swap)
-            copy = pltpu.make_async_copy(shard(goal, part), mine.at[r, at, :], load.at[slot])
-            copy.start()
-            loads.append(copy)
-
-    def pair_sum(r, part):
-        loads[2 * r + part].wait()
-        swaps[2 * r + part].wait_recv()
-        at = pl.ds(part * half, half)
-        mine[r, at, :] = (mine[r, at, :].astype(f32) + theirs[r, at, :].astype(f32)).astype(bf16)
+    swaps, copies = [], []
 
     def begin(src, dst, target):
-        index = 8 + len(copies)
+        index = 4 + len(copies)
         copy = copy_to(src, dst, send.at[index], recv.at[index], axis, target)
         copy.start()
         copies.append(copy)
         return copy
 
-    first, second = pl.ds(0, half), pl.ds(half, half)
-    pair_sum(0, 0)
+    def theirs_of(r):
+        product(goals[r] + shift, leaving.at[r])
+        swap = copy_to(leaving.at[r], theirs.at[r], send.at[r], recv.at[r], axis, other)
+        swap.start()
+        swaps.append(swap)
+
+    def pair_sum(r):
+        swaps[r].wait_recv()
+        mine[r] = (mine[r].astype(f32) + theirs[r].astype(f32)).astype(bf16)
+
+    theirs_of(0)
+    product(goals[0], mine.at[0])
+    pair_sum(0)
     far_x = begin(mine.at[0, first, :], in_dx, along_x)
-    pair_sum(0, 1)
     far_y = begin(mine.at[0, second, :], in_dy, along_y)
-    pair_sum(1, 0)
+    theirs_of(1)
+    product(goals[1], mine.at[1])
+    theirs_of(2)
+    pair_sum(1)
     near_x0 = begin(mine.at[1, first, :], in_x.at[first, :], along_x)
-    pair_sum(2, 1)
+    product(goals[2], mine.at[2])
+    pair_sum(2)
     near_y1 = begin(mine.at[2, second, :], in_y.at[second, :], along_y)
-    pair_sum(1, 1)
-    pair_sum(2, 0)
+    theirs_of(3)
     far_x.wait_recv()
     mine[2, first, :] = (mine[2, first, :].astype(f32) + in_dx[...].astype(f32)).astype(bf16)
     near_y0 = begin(mine.at[2, first, :], in_y.at[first, :], along_y)
     far_y.wait_recv()
     mine[1, second, :] = (mine[1, second, :].astype(f32) + in_dy[...].astype(f32)).astype(bf16)
     near_x1 = begin(mine.at[1, second, :], in_x.at[second, :], along_x)
-    for part, at in ((0, first), (1, second)):
-        loads[6 + part].wait()
-        swaps[6 + part].wait_recv()
-        out_ref[at, :] = mine[3, at, :].astype(f32) + theirs[3, at, :].astype(f32)
-    near_x0.wait_recv()
-    out_ref[first, :] += in_x[first, :].astype(f32)
-    near_y1.wait_recv()
-    out_ref[second, :] += in_y[second, :].astype(f32)
-    near_y0.wait_recv()
-    out_ref[first, :] += in_y[first, :].astype(f32)
-    near_x1.wait_recv()
-    out_ref[second, :] += in_x[second, :].astype(f32)
+    product(goals[3], mine.at[3])
+    swaps[3].wait_recv()
+    for at, near_x, near_y in ((first, near_x0, near_y0), (second, near_x1, near_y1)):
+        near_x.wait_recv()
+        near_y.wait_recv()
+        finish(
+            at,
+            mine[3, at, :].astype(f32)
+            + theirs[3, at, :].astype(f32)
+            + in_x[at, :].astype(f32)
+            + in_y[at, :].astype(f32),
+        )
     for copy in swaps + copies:
         copy.wait_send()
 
 
-def scatter_rows(partial, identity, sizes):
-    if identity is None or not square(sizes):
-        return lax.psum_scatter(partial, "tensor", scatter_dimension=0, tiled=True).astype(f32)
-    height, width = partial.shape
-    rows = height // 8
-    vmem = pl.BlockSpec(memory_space=pltpu.VMEM)
+def scatter_scratch(rows, width):
+    return [
+        pltpu.VMEM((4, rows, width), bf16),
+        pltpu.VMEM((4, rows, width), bf16),
+        pltpu.VMEM((4, rows, width), bf16),
+        pltpu.VMEM((rows // 2, width), bf16),
+        pltpu.VMEM((rows // 2, width), bf16),
+        pltpu.VMEM((rows, width), bf16),
+        pltpu.VMEM((rows, width), bf16),
+        pltpu.SemaphoreType.DMA((10,)),
+        pltpu.SemaphoreType.DMA((10,)),
+    ]
+
+
+def in_columns(width, tile, body):
+    def step(t, carry):
+        body(pl.ds(pl.multiple_of(t * tile, tile), tile))
+        return carry
+
+    lax.fori_loop(0, width // tile, step, 0)
+
+
+def attend_kernel(axis, mixed_ref, w_ref, tokens_ref, gain_ref, hidden_ref, normed_ref, *scratch):
+    rows, width = hidden_ref.shape
+
+    def product(shard, ref):
+        left = mixed_ref.at[pl.ds(pl.multiple_of(shard * rows, rows), rows), :]
+
+        def tile(here):
+            ref[:, here] = dot_nn(left[...], w_ref[:, here]).astype(bf16)
+
+        in_columns(width, 512, tile)
+
+    def finish(at, value):
+        hidden = tokens_ref[at, :].astype(f32) + value
+        hidden_ref[at, :] = hidden
+        factor = lax.rsqrt(jnp.mean(hidden * hidden, -1, keepdims=True) + norm_eps)
+        normed_ref[at, :] = (hidden * factor * gain_ref[...]).astype(bf16)
+
+    scatter_parts(axis, product, finish, *scratch)
+
+
+def attend(mixed, w_out, tokens, gain, identity, sizes):
+    rows, width = tokens.shape
+    if not square(sizes):
+        part = jnp.dot(mixed, w_out, preferred_element_type=f32).astype(bf16)
+        hidden = tokens.astype(f32) + scatter_rows(part)
+        return hidden, (hidden * rms_factor(hidden) * gain).astype(bf16)
     return pl.pallas_call(
-        functools.partial(scatter_kernel, "tensor"),
-        out_shape=jax.ShapeDtypeStruct((rows, width), f32),
-        in_specs=[pl.BlockSpec(memory_space=pl.ANY)],
-        out_specs=vmem,
-        scratch_shapes=[
-            pltpu.VMEM((4, rows, width), bf16),
-            pltpu.VMEM((4, rows, width), bf16),
-            pltpu.VMEM((rows // 2, width), bf16),
-            pltpu.VMEM((rows // 2, width), bf16),
-            pltpu.VMEM((rows, width), bf16),
-            pltpu.VMEM((rows, width), bf16),
-            pltpu.SemaphoreType.DMA((8,)),
-            pltpu.SemaphoreType.DMA((14,)),
-            pltpu.SemaphoreType.DMA((14,)),
-        ],
+        functools.partial(attend_kernel, "tensor"),
+        out_shape=(jax.ShapeDtypeStruct((rows, width), f32), jax.ShapeDtypeStruct((rows, width), bf16)),
+        in_specs=[IN_VMEM] * 4,
+        out_specs=(IN_VMEM,) * 2,
+        scratch_shapes=scatter_scratch(rows, width),
         compiler_params=pltpu.CompilerParams(
-            collective_id=identity, has_side_effects=True, vmem_limit_bytes=32 * 1024 * 1024
+            collective_id=identity, has_side_effects=True, vmem_limit_bytes=40 * 1024 * 1024
         ),
         cost_estimate=pl.CostEstimate(flops=0, bytes_accessed=1_000_000, transcendentals=0),
-        name="scatter_rows",
-    )(partial)
+        name="attend",
+    )(mixed, w_out, tokens, gain[None, :])
+
+
+def return_kernel(
+    axis,
+    dgate_ref,
+    dup_ref,
+    wg_ref,
+    wu_ref,
+    hidden_ref,
+    cotangent_ref,
+    gain_ref,
+    grad_ref,
+    low_ref,
+    dgain_ref,
+    turned,
+    *scratch,
+):
+    rows, width = hidden_ref.shape
+
+    def product(shard, ref):
+        at = pl.ds(pl.multiple_of(shard * rows, rows), rows)
+        turned[0] = jnp.transpose(dgate_ref[:, at])
+        turned[1] = jnp.transpose(dup_ref[:, at])
+
+        def tile(here):
+            ref[:, here] = (
+                dot_nn(turned[0], wg_ref[:, here]) + dot_nn(turned[1], wu_ref[:, here])
+            ).astype(bf16)
+
+        in_columns(width, 512, tile)
+
+    dgain_ref[...] = jnp.zeros_like(dgain_ref)
+
+    def finish(at, value):
+        hidden = hidden_ref[at, :]
+        factor = lax.rsqrt(jnp.mean(hidden * hidden, -1, keepdims=True) + norm_eps)
+        scaled = hidden * factor
+        dgain_ref[...] += jnp.sum(value * scaled, 0, keepdims=True)
+        weighted = value * gain_ref[...]
+        grad = cotangent_ref[at, :].astype(f32) + factor * (
+            weighted - scaled * jnp.mean(weighted * scaled, -1, keepdims=True)
+        )
+        grad_ref[at, :] = grad
+        low_ref[at, :] = grad.astype(bf16)
+
+    scatter_parts(axis, product, finish, *scratch)
+
+
+def return_hidden(dgate, dup, gate_rows, up_rows, hidden, cotangent, gain, identity, sizes):
+    rows, width = hidden.shape
+    if not square(sizes):
+        part = (cross_rows(dgate, gate_rows) + cross_rows(dup, up_rows)).astype(bf16)
+        grad_normed = scatter_rows(part)
+        factor = rms_factor(hidden)
+        scaled = hidden * factor
+        grad = cotangent.astype(f32) + norm_backward(grad_normed, scaled, factor, gain)
+        return grad, grad.astype(bf16), jnp.sum(grad_normed * scaled, 0)
+    grad, low, dgain = pl.pallas_call(
+        functools.partial(return_kernel, "tensor"),
+        out_shape=(
+            jax.ShapeDtypeStruct((rows, width), f32),
+            jax.ShapeDtypeStruct((rows, width), bf16),
+            jax.ShapeDtypeStruct((1, width), f32),
+        ),
+        in_specs=[IN_VMEM] * 7,
+        out_specs=(IN_VMEM,) * 3,
+        scratch_shapes=[pltpu.VMEM((2, rows, dgate.shape[0]), bf16)] + scatter_scratch(rows, width),
+        compiler_params=pltpu.CompilerParams(
+            collective_id=identity, has_side_effects=True, vmem_limit_bytes=52 * 1024 * 1024
+        ),
+        cost_estimate=pl.CostEstimate(flops=0, bytes_accessed=1_000_000, transcendentals=0),
+        name="return_hidden",
+    )(dgate, dup, gate_rows, up_rows, hidden, cotangent, gain[None, :])
+    return grad, low, dgain[0]
+
+
+def scatter_rows(partial):
+    return lax.psum_scatter(partial, "tensor", scatter_dimension=0, tiled=True).astype(f32)
 
 
 CHUNK = 64
@@ -1047,23 +1426,6 @@
         cost_estimate=pl.CostEstimate(flops=0, bytes_accessed=200 * total, transcendentals=0),
         name="sum_over_line",
     )(*arrays)
-
-
-def rms_factor(matrix):
-    return lax.rsqrt(jnp.mean(matrix * matrix, -1, keepdims=True) + norm_eps)
-
-
-def cross_rows(left, right):
-    return lax.dot_general(left, right, (((0,), (0,)), ((), ())), preferred_element_type=f32)
-
-
-def times_transposed(left, right):
-    return lax.dot_general(left, right, (((1,), (1,)), ((), ())), preferred_element_type=f32)
-
-
-def norm_backward(grad_normed, scaled, factor, gain_value):
-    weighted = grad_normed * gain_value
-    return factor * (weighted - scaled * jnp.mean(weighted * scaled, -1, keepdims=True))
 
 
 def shards(
@@ -1098,11 +1460,10 @@
     gain_first = gain_attn.astype(f32)
     gain_second = gain_ffn.astype(f32)
     normed = (scaled_attn * gain_first).astype(bf16)
-    gathered = gather_rows(normed, 0, sizes)
-    padding = jnp.zeros((w_alpha.shape[0], EXTRA - 2 * heads), bf16)
-    w_in = jnp.concatenate([w_query, w_key, w_value, w_gate_out, w_alpha, w_beta, padding], axis=1)
+    gathered, w_in, projected = gather_project(
+        normed, w_query, w_key, w_value, w_gate_out, w_alpha, w_beta, 0, sizes
+    )
     main = w_in.shape[1] - EXTRA
-    projected = jnp.dot(gathered, w_in, preferred_element_type=f32)
     extras = (
         conv_query.astype(f32),
         conv_key.astype(f32),
@@ -1114,43 +1475,28 @@
     mixed, final, states, inverse, update, raw = mixer_forward(projected, *extras, start_state[0])
     grad_out_rows, gathered = lax.optimization_barrier((cotangent[0], gathered))
     grad_gathered = lax.all_gather(grad_out_rows, "tensor", axis=0, tiled=True)
-    attended = scatter_rows(
-        jnp.dot(mixed, w_out, preferred_element_type=f32).astype(bf16), 1, sizes
-    )
-    hidden = inputs + attended
-    factor_ffn = rms_factor(hidden)
-    scaled_ffn = hidden * factor_ffn
-    normed_ffn = (scaled_ffn * gain_second).astype(bf16)
-    gathered_ffn = gather_rows(normed_ffn, 2, sizes)
-    gate_proj = jnp.dot(gathered_ffn, w_ffn_gate, preferred_element_type=f32)
-    up_proj = jnp.dot(gathered_ffn, w_ffn_up, preferred_element_type=f32)
+    hidden, normed_ffn = attend(mixed, w_out, tokens[0], gain_second, 1, sizes)
+    gate_rows, up_rows = w_ffn_gate.T, w_ffn_up.T
+    gathered_ffn, gate_proj, up_proj, inner = gather_expand(normed_ffn, gate_rows, up_rows, 2, sizes)
     sigmoid_gate = jax.nn.sigmoid(gate_proj)
-    activated = gate_proj * sigmoid_gate
-    inner = (activated * up_proj).astype(bf16)
-    grad_inner = times_transposed(grad_gathered, w_ffn_down)
+    grad_inner = times_transposed(w_ffn_down, grad_gathered)
     grad_gate_rows = (
         grad_inner * up_proj * sigmoid_gate * (1.0 + gate_proj * (1.0 - sigmoid_gate))
     ).astype(bf16)
-    grad_up_rows = (grad_inner * activated).astype(bf16)
-    grad_down = cross_rows(inner, grad_gathered).astype(bf16)
-    grad_gate_weight = cross_rows(grad_gate_rows, gathered_ffn).astype(bf16)
+    grad_up_rows = (grad_inner * gate_proj * sigmoid_gate).astype(bf16)
+    grad_down = jnp.dot(inner, grad_gathered, preferred_element_type=f32).astype(bf16)
+    grad_gate_weight = jnp.dot(grad_gate_rows, gathered_ffn, preferred_element_type=f32).astype(bf16)
     grad_down_summed, grad_gate_summed = lax.psum((grad_down, grad_gate_weight), "dp")
-    grad_gate_rows, grad_up_rows, grad_down, grad_gate_weight = lax.optimization_barrier(
-        (grad_gate_rows, grad_up_rows, grad_down, grad_gate_weight)
-    )
-    part_normed_ffn = (
-        times_transposed(grad_gate_rows, w_ffn_gate) + times_transposed(grad_up_rows, w_ffn_up)
-    ).astype(bf16)
-    grad_normed_ffn = scatter_rows(part_normed_ffn, 3, sizes)
-    part_gain_ffn = jnp.sum(grad_normed_ffn * scaled_ffn, 0)
-    grad_hidden = grad_out_rows.astype(f32) + norm_backward(
-        grad_normed_ffn, scaled_ffn, factor_ffn, gain_second
-    )
-    grad_attended = gather_rows(grad_hidden.astype(bf16), 4, sizes)
-    grad_mixed = times_transposed(grad_attended, w_out)
-    grad_up_weight = cross_rows(grad_up_rows, gathered_ffn).astype(bf16)
+    grad_gate_rows, grad_up_rows, inner, grad_down, grad_gate_weight = lax.optimization_barrier(
+        (grad_gate_rows, grad_up_rows, inner, grad_down, grad_gate_weight)
+    )
+    grad_hidden, grad_attended, part_gain_ffn = return_hidden(
+        grad_gate_rows, grad_up_rows, gate_rows, up_rows, hidden, grad_out_rows, gain_second, 3, sizes
+    )
+    grad_attended, grad_mixed = gather_back(grad_attended, w_out, 4, sizes)
+    grad_up_weight = jnp.dot(grad_up_rows, gathered_ffn, preferred_element_type=f32).astype(bf16)
     grad_out_weight = cross_rows(mixed, grad_attended).astype(bf16)
-    ffn_part = jnp.dot(inner, w_ffn_down, preferred_element_type=f32).astype(bf16)
+    ffn_part = cross_rows(inner, w_ffn_down).astype(bf16)
     grad_projected, grad_tq, grad_tk, grad_tv, grad_dl, grad_db, grad_gain = mixer_backward(
         projected, *extras, states, inverse, update, raw, grad_mixed
     )
@@ -1183,8 +1529,8 @@
             grad_out_weight,
         )
     )
-    grad_normed = scatter_rows(part_normed, None, sizes)
-    ffn_out = scatter_rows(ffn_part, None, sizes)
+    grad_normed = scatter_rows(part_normed)
+    ffn_out = scatter_rows(ffn_part)
     output = (hidden + ffn_out).astype(bf16)
     gains = 2 * width + out_gain.shape[0]
     small_summed, grad_up_summed, grad_out_summed, grad_in_summed, gain_grads = sum_over_line(

time: 830 us -> 767 us (0.924)
  matrix products: 180 us -> 101 us
  Pallas kernels: 557 us -> 593 us
  local copies, waits for them, and re-layouts: 31 us -> 17.6 us
    pallas_call x5, Pallas kernels: 199 us -> 235 us  [the longest x1 57.1 us: attend(): pl.pallas_call(functools.partial(attend_kernel, 'tensor'), out_shape=(jax...]
    dot_general x5 -> x3, matrix products: 57.7 us -> 24.9 us  [the longest x1 10.3 us: shards(): jnp.dot(grad_up_rows, gathered_ffn, preferred_element_type=f32).astype(bf16)]
    dot_general x5 -> x2, matrix products: 67.3 us -> 35 us  [times_transposed(): lax.dot_general(left, right, (((1,), (1,)), ((), ())), preferred_element_...]
    dot_general x5 -> x3, matrix products: 55.1 us -> 40.8 us  [cross_rows(): lax.dot_general(left, right, (((0,), (0,)), ((), ())), preferred_element_...]
    concatenate x1 -> x0, local copies, waits for them, and re-layouts: 11.3 us -> none  [shards(): jnp.concatenate([w_query, w_key, w_value, w_gate_out, w_alpha, w_beta, pa...]
  transfers between devices with their start and end apart: 4 -> 4, of which waited for: 0 -> 0; matrix products, arithmetic and copies ran while one was open for 22% -> 13% of each run, Pallas kernels for 63% -> 72%
where the time goes in v5:
time: 767 us; the launch traced here: 761 us
  Pallas kernels  593 us (77%)
  matrix products  101 us (13%)
  other arithmetic  33.8 us (4%)
  local copies, waits for them, and re-layouts  17.6 us (2%)
  between operations  14.8 us (2%)
    pallas_call x1, Pallas kernels, sum_over_line(): pl.pallas_call(functools.partial(line_kernel, 'dp', 'tensor', tuple(width...  279 us
    pallas_call x1, Pallas kernels, attend(): pl.pallas_call(functools.partial(attend_kernel, 'tensor'), out_shape=(jax...  57.1 us
    pallas_call x1, Pallas kernels, return_hidden(): pl.pallas_call(functools.partial(return_kernel, 'tensor'), out_shape=(jax...  51.7 us
    pallas_call x1, Pallas kernels, mixer_backward(): pl.pallas_call(functools.partial(backward_kernel, heads, key_dim, value_d...  48.5 us
    pallas_call x1, Pallas kernels, gather_project(): pl.pallas_call(functools.partial(gather_project_kernel, 'tensor'), out_sh...  45.6 us
    pallas_call x1, Pallas kernels, gather_expand(): pl.pallas_call(functools.partial(gather_expand_kernel, 'tensor'), out_sha...  42 us
    dot_general x3, matrix products, cross_rows(): lax.dot_general(left, right, (((0,), (0,)), ((), ())), preferred_element_...  40.8 us
    pallas_call x1, Pallas kernels, gather_back(): pl.pallas_call(functools.partial(gather_back_kernel, 'tensor'), out_shape...  39 us
  transfers between devices with their start and end apart: 4, of which 0 were waited for; matrix products, arithmetic and copies ran while one was open for 13% of the time, Pallas kernels for 72%

profile of v5, /device:TPU:0, one launch (start us, length us, event | category | flops | bytes accessed | tf_op | source)
XLA Modules:
  0.0 761.0 jit_solution(191152286893467964)
XLA Ops:
  7.2 0.0 copy-start
  7.2 0.0 all-gather.2.cloned.1.call-start
  7.3 0.8 convert_element_type.84
  8.1 1.7 fusion.14
  9.9 1.5 fusion.8.x_ref
  11.5 0.0 copy-start.11
  11.5 1.6 copy-done.11
  13.1 1.2 copy-done.17
  14.3 0.0 copy-start.28
  14.3 0.0 copy-start.49
  14.4 45.6 %gather_project.1 = (bf16[2048,2048]{1,0:T(8,128)(2,1)}, bf16[2048,1664]{1,0:T(8,128)(2,1)S(1)}, f32[2048,1664]{1,0:T(8,128)}) custom-call(bf16[256,2048]{1,0:T(8,128)(2,1)S(1)} %fusion.8.x_ref, bf16[2,2048]{1,0:T(2,128)(2,1)S(1)} %bitcast.87, bf16[2,2048]{1,0:T(2,128)(2,1)S(1)} %bitcast.88, bf16[2048,256]{1,0:T(8,128)(2,1)S(1)} %copy-done.16, ...), custom_call_target="tpu_custom_call" | custom-call | bytes 1000000 | tf_op jit(solution)/shard_map/gather_project/pallas_call | solution.py:883
  60.0 2.8 copy-done.29
  62.8 0.0 all-gather.2.cloned.1.call-update
  62.8 0.0 all-reduce.3.cloned.1.call-start
  62.9 0.0 copy-start.19
  63.0 0.1 copy.47.dl_col_ref
  63.1 0.1 copy.48.db_col_ref
  63.2 0.0 copy-start.2
  63.2 0.0 copy-start.6
  63.2 30.2 %mixer_forward.1 = (bf16[2048,512]{1,0:T(8,128)(2,1)S(1)}, f32[2,128,256]{2,1,0:T(8,128)}, bf16[8,2,128,256]{3,2,1,0:T(8,128)(2,1)S(1)}, bf16[8,2,256,256]{3,2,1...) custom-call(f32[2048,1664]{1,0:T(8,128)} %get-tuple-element.66.proj_ref.eq_ref.ek_ref.ev_ref, ...), custom_call_target="tpu_custom_call" | custom-call | bytes 100000000 | tf_op jit(solution)/shard_map/mixer_forward/pallas_call | solution.py:278
  93.5 0.0 copy-start.12
  93.6 57.1 %attend.1 = (f32[256,2048]{1,0:T(8,128)S(1)}, bf16[256,2048]{1,0:T(8,128)(2,1)S(1)}) custom-call(bf16[2048,512]{1,0:T(8,128)(2,1)S(1)} %get-tuple-element.67.mixed_ref, bf16[512,2048]{1,0:T(8,128)(2,1)S(1)} %copy-done.6, bf16[256,2048]{1,0:T(8,128)(2,1)S(1)} %bitcast.79, f32[1,2048]{1,0:T(1,128)S(1)} %bitcast.85), custom_call_target="tpu_custom_call" | custom-call | bytes 1000000 | tf_op jit(solution)/shard_map/attend/pallas_call | solution.py:1162
  150.6 1.3 copy-done.8
  152.0 42.0 %gather_expand.1 = (bf16[2048,2048]{1,0:T(8,128)(2,1)}, f32[688,2048]{1,0:T(8,128)}, f32[688,2048]{1,0:T(8,128)}, bf16[688,2048]{1,0:T(8,128)(2,1)S(1)}) custom-call(bf16[256,2048]{1,0:T(8,128)(2,1)S(1)} %get-tuple-element.76.x_ref, bf16[688,2048]{1,0:T(8,128)(2,1)S(1)} %bitcast.81, bf16[688,2048]{1,0:T(8,128)(2,1)S(1)} %bitcast.83), custom_call_target="tpu_custom_call" | custom-call | bytes 1000000 | tf_op jit(solution)/shard_map/gather_expand/pallas_call | solution.py:971
  194.0 1.5 copy-done.30
  195.5 13.9 %fusion.4 = (bf16[688,2048]{1,0:T(8,128)(2,1)}, bf16[688,2048]{1,0:T(8,128)(2,1)S(1)}) fusion(f32[688,2048]{1,0:T(8,128)} %get-tuple-element.78, f32[688,2048]{1,0:T(8,128)} %get-tuple-element.77, bf16[2048,2048]{1,0:T(8,128)(2,1)} %all-gather.2.cloned.1.call-done, bf16[688,2048]{1,0:T(8,128)(2,1)S(1)} %copy-done), kind=kOutput, calls=%fused_computation.10 | convolution fusion | flops 5789679616 | bytes 28114944 | tf_op jit(solution)/shard_map/dot_general | solution.py:675
  209.5 7.3 convolution_convert_fusion.4
  216.8 7.3 convolution_convert_fusion.5
  224.1 0.0 all-reduce.3.cloned.1.call-update
  224.1 0.0 reduce-scatter.5.cloned.1.call-start
  224.2 51.7 %return_hidden.1 = (f32[256,2048]{1,0:T(8,128)}, bf16[256,2048]{1,0:T(8,128)(2,1)S(1)}, f32[1,2048]{1,0:T(1,128)S(1)}) custom-call(bf16[688,2048]{1,0:T(8,128)(2,1)} %copy-done.39, bf16[688,2048]{1,0:T(8,128)(2,1)} %get-tuple-element.82.dup_ref, bf16[688,2048]{1,0:T(8,128)(2,1)} %bitcast.80, bf16[688,2048]{1,0:T(8,128)(2,1)} %bitcast.82, ...), custom_call_target="tpu_custom_call" | custom-call | bytes 1000000 | tf_op jit(solution)/shard_map/return_hidden/pallas_call | solution.py:1231
  275.9 39.0 %gather_back.1 = (bf16[2048,2048]{1,0:T(8,128)(2,1)}, f32[2048,512]{1,0:T(8,128)S(1)}) custom-call(bf16[256,2048]{1,0:T(8,128)(2,1)S(1)} %get-tuple-element.83.x_ref, bf16[512,2048]{1,0:T(8,128)(2,1)S(1)} %copy-done.7), custom_call_target="tpu_custom_call" | custom-call | bytes 1000000 | tf_op jit(solution)/shard_map/gather_back/pallas_call | solution.py:1027
  315.0 10.8 %convolution_convert_fusion.6.refs_2_ = bf16[512,2048]{1,0:T(8,128)(2,1)} fusion(bf16[2048,512]{1,0:T(8,128)(2,1)S(1)} %copy-done.14, bf16[2048,2048]{1,0:T(8,128)(2,1)} %get-tuple-element.95), kind=kOutput, calls=%fused_computation.17 | convolution fusion | flops 4296015872 | bytes 12582912 | tf_op jit(solution)/shard_map/dot_general | solution.py:671
  325.7 9.1 %convolution_convert_fusion = bf16[2048,2048]{1,0:T(8,128)(2,1)} fusion(bf16[688,2048]{1,0:T(8,128)(2,1)S(1)} %copy-done.32, bf16[688,2048]{1,0:T(8,128)(2,1)S(1)} %copy-done), kind=kOutput, calls=%fused_computation.1 | convolution fusion | flops 5775556608 | bytes 14024704 | tf_op jit(solution)/shard_map/dot_general | solution.py:671
  334.9 48.5 %mixer_backward.1 = (bf16[2048,1664]{1,0:T(8,128)(2,1)}, f32[4,256]{1,0:T(4,128)}, f32[4,256]{1,0:T(4,128)}, f32[4,512]{1,0:T(4,128)}, f32[1,2]{1,0:T(1,128)}, /*index=5*/f32[1,2]{1,0:T(1,128)}, f32[1,256]{1,0:T(1,128)}) custom-call(f32[2048,1664]{1,0:T(8,128)} %get-tuple-element.66.proj_ref.eq_ref.ek_ref.ev_ref, ...), custom_call_target="tpu_custom_call" | custom-call | bytes 100000000 | tf_op jit(solution)/shard_map/mixer_backward/pallas_call | solution.py:591
  383.4 21.0 %multiply_reduce_fusion = (f32[2048]{0:T(1024)S(1)}, bf16[2048,1664]{1,0:T(8,128)(2,1)S(1)}) fusion(bf16[2048,1664]{1,0:T(8,128)(2,1)} %copy-done.29, bf16[2048,2048]{1,0:T(8,128)(2,1)} %get-tuple-element.70, bf16[2048,1664]{1,0:T(8,128)(2,1)} %get-tuple-element.85), kind=kOutput, calls=%fused_computation | convolution fusion | flops 13975681024 | bytes 28844032 | tf_op jit(solution)/shard_map/dot_general | solution.py:671
  404.4 2.8 copy-done.33
  407.2 0.1 convert_bitcast_fusion.2
  407.3 0.3 copy.52
  407.7 0.7 concatenate.3
  408.4 10.3 %convolution_convert_fusion.3.refs_1_ = bf16[688,2048]{1,0:T(8,128)(2,1)} fusion(bf16[688,2048]{1,0:T(8,128)(2,1)} %get-tuple-element.82.dup_ref, bf16[2048,2048]{1,0:T(8,128)(2,1)} %get-tuple-element.80), kind=kOutput, calls=%fused_computation.14 | convolution fusion | flops 5772771328 | bytes 14024704 | tf_op jit(solution)/shard_map/dot_general | solution.py:1497
  418.8 21.1 %convolution_convert_fusion.1 = bf16[2048,2048]{1,0:T(8,128)(2,1)} fusion(bf16[2048,1664]{1,0:T(8,128)(2,1)} %get-tuple-element.85, bf16[2048,1664]{1,0:T(8,128)(2,1)} %copy-done.29), kind=kOutput, calls=%fused_computation.2 | convolution fusion | flops 13962838016 | bytes 22020096 | tf_op jit(solution)/shard_map/dot_general | solution.py:675
  439.9 0.0 reduce-scatter.5.cloned.1.call-update
  439.9 0.0 reduce-scatter.3.cloned.1.call-start
  439.9 0.5 reduce-scatter.3.cloned.1.call-update
  440.5 279.2 %sum_over_line.1 = (f32[144,128]{1,0:T(8,128)}, bf16[688,2048]{1,0:T(8,128)(2,1)}, bf16[512,2048]{1,0:T(8,128)(2,1)}, bf16[2048,1536]{1,0:T(8,128)(2,1)}, f32[48,128]{1,0:T(8,128)}) custom-call(f32[144,128]{1,0:T(8,128)} %bitcast.100, bf16[688,2048]{1,0:T(8,128)(2,1)} %convolution_convert_fusion.3.refs_1_, ...), custom_call_target="tpu_custom_call" | custom-call | bytes 1124352000 | tf_op jit(solution)/shard_map/sum_over_line/pallas_call | solution.py:1416
  719.7 4.3 convert_element_type.107
  724.0 0.1 fusion.18
  724.1 0.6 slice.77
  724.7 0.6 slice.79
  725.3 0.6 reshape.111
  725.9 0.6 reshape.109
  726.5 0.6 reshape.110
  727.1 3.6 convert_element_type.108
  730.8 0.6 fusion.16
  731.3 0.6 slice_bitcast_fusion.2
  731.9 0.6 slice_bitcast_fusion
  732.5 2.3 slice_convert_fusion.2
  734.8 4.6 slice_convert_fusion
  739.4 5.9 convert_bitcast_fusion
  745.3 1.8 fusion.9
  747.1 0.0 reduce-scatter.3.cloned.1.call-done
  747.1 3.2 fusion.15
  750.3 3.9 fusion.13
  (124 shorter events, 0.3 us)
Async XLA Ops:
  7.2 188.3 %copy-start = (bf16[688,2048]{1,0:T(8,128)(2,1)S(1)}, bf16[688,2048]{1,0:T(8,128)(2,1)}, u32[]{:S(2)}) copy-start(bf16[688,2048]{1,0:T(8,128)(2,1)} %param.40) | copy-start | bytes 8454148
  7.2 4.2 copy-start.22
  7.2 4.2 copy-start.23
  7.2 188.3 %all-gather.2.cloned.1.call-start = ((), (), s32[]{:S(2)}) async-start(), calls=%async_computation.2 | async-start | bytes 9437184 | tf_op jit(solution)/shard_map/all_gather | solution.py:1477
  7.3 4.2 copy-start.10
  7.3 4.2 copy-start.16
  8.1 3.3 copy-start.40
  9.9 1.6 copy-start.43
  11.5 1.6 copy-start.11
  13.1 1.2 copy-start.17
  14.3 48.5 %copy-start.48 = (bf16[4,512]{1,0:T(4,128)(2,1)S(1)}, bf16[4,512]{1,0:T(4,128)(2,1)}, u32[]{:S(2)}) copy-start(bf16[4,512]{1,0:T(4,128)(2,1)} %param.32) | copy-start | bytes 12292
  14.3 48.6 %copy-start.52 = (bf16[4,256]{1,0:T(4,128)(2,1)S(1)}, bf16[4,256]{1,0:T(4,128)(2,1)}, u32[]{:S(2)}) copy-start(bf16[4,256]{1,0:T(4,128)(2,1)} %param.30) | copy-start | bytes 6148
  14.3 48.6 %copy-start.53 = (bf16[4,256]{1,0:T(4,128)(2,1)S(1)}, bf16[4,256]{1,0:T(4,128)(2,1)}, u32[]{:S(2)}) copy-start(bf16[4,256]{1,0:T(4,128)(2,1)} %param.31) | copy-start | bytes 6148
  14.3 48.6 %copy-start.59 = (bf16[256]{0:T(256)(128)(2,1)S(1)}, bf16[256]{0:T(256)(128)(2,1)}, u32[]{:S(2)}) copy-start(bf16[256]{0:T(256)(128)(2,1)} %param.35) | copy-start | bytes 1540
  14.3 48.7 %copy-start.27 = (f32[2]{0:T(128)S(1)}, f32[2]{0:T(128)}, u32[]{:S(2)}) copy-start(f32[2]{0:T(128)} %param.33) | copy-start | bytes 28
  14.3 48.8 %copy-start.28 = (f32[2]{0:T(128)S(1)}, f32[2]{0:T(128)}, u32[]{:S(2)}) copy-start(f32[2]{0:T(128)} %param.34) | copy-start | bytes 28
  14.3 48.8 %copy-start.49 = (bf16[2048]{0:T(1024)(128)(2,1)S(1)}, bf16[2048]{0:T(1024)(128)(2,1)}, u32[]{:S(2)}) copy-start(bf16[2048]{0:T(1024)(128)(2,1)} %param.37) | copy-start | bytes 12292
  14.4 48.8 %copy-start.18 = (f32[1,2,128,256]{3,2,1,0:T(8,128)S(1)}, f32[1,2,128,256]{3,2,1,0:T(8,128)}, u32[]{:S(2)}) copy-start(f32[1,2,128,256]{3,2,1,0:T(8,128)} %param.22) | copy-start | bytes 786436
  60.0 2.8 copy-start.29
  62.8 377.1 %all-reduce.3.cloned.1.call-start = ((), (), s32[]{:S(2)}) async-start(), calls=%async_computation.5 | async-start | bytes 11272192 | tf_op jit(solution)/shard_map/psum | solution.py:1489
  62.9 30.6 %copy-start.19 = (f32[4,512]{1,0:T(4,128)}, f32[4,512]{1,0:T(4,128)S(1)}, u32[]{:S(2)}) copy-start(f32[4,512]{1,0:T(4,128)S(1)} %convert_element_type.88.tv_ref) | copy-start | bytes 24580
  62.9 30.5 %copy-start.20 = (f32[4,256]{1,0:T(4,128)}, f32[4,256]{1,0:T(4,128)S(1)}, u32[]{:S(2)}) copy-start(f32[4,256]{1,0:T(4,128)S(1)} %convert_element_type.86.tq_ref) | copy-start | bytes 12292
  63.0 30.5 %copy-start.21 = (f32[4,256]{1,0:T(4,128)}, f32[4,256]{1,0:T(4,128)S(1)}, u32[]{:S(2)}) copy-start(f32[4,256]{1,0:T(4,128)S(1)} %convert_element_type.87.tk_ref) | copy-start | bytes 12292
  63.0 30.5 %copy-start.24 = (f32[256]{0:T(256)}, f32[256]{0:T(256)S(1)}, u32[]{:S(2)}) copy-start(f32[256]{0:T(256)S(1)} %broadcast_in_dim.56) | copy-start | bytes 3076
  63.1 30.4 %copy-start.25 = (f32[2,1]{1,0:T(2,128)}, f32[2,1]{1,0:T(2,128)S(1)}, u32[]{:S(2)}) copy-start(f32[2,1]{1,0:T(2,128)S(1)} %copy.47.dl_col_ref) | copy-start | bytes 28
  63.2 30.3 %copy-start.26 = (f32[2,1]{1,0:T(2,128)}, f32[2,1]{1,0:T(2,128)S(1)}, u32[]{:S(2)}) copy-start(f32[2,1]{1,0:T(2,128)S(1)} %copy.48.db_col_ref) | copy-start | bytes 28
  63.2 30.3 %copy-start.2 = (bf16[1,256,2048]{2,1,0:T(8,128)(2,1)S(1)}, bf16[1,256,2048]{2,1,0:T(8,128)(2,1)}, u32[]{:S(2)}) copy-start(bf16[1,256,2048]{2,1,0:T(8,128)(2,1)} %param.21) | copy-start | bytes 3145732
  63.2 30.3 %copy-start.6 = (bf16[512,2048]{1,0:T(8,128)(2,1)S(1)}, bf16[512,2048]{1,0:T(8,128)(2,1)}, u32[]{:S(2)}) copy-start(bf16[512,2048]{1,0:T(8,128)(2,1)} %w_ref.3) | copy-start | bytes 6291460
  63.2 88.7 %copy-start.5 = (bf16[2048,688]{0,1:T(8,128)(2,1)S(1)}, bf16[2048,688]{0,1:T(8,128)(2,1)}, u32[]{:S(2)}) copy-start(bf16[2048,688]{0,1:T(8,128)(2,1)} %param.39) | copy-start | bytes 8454148
  93.5 57.1 %copy-start.12 = (bf16[8,2,256,256]{3,2,1,0:T(8,128)(2,1)}, bf16[8,2,256,256]{3,2,1,0:T(8,128)(2,1)S(1)}, u32[]{:S(2)}) copy-start(bf16[8,2,256,256]{3,2,1,0:T(8,128)(2,1)S(1)} %get-tuple-element.72.inverse_ref) | copy-start | bytes 6291460
  93.5 58.5 %copy-start.13 = (bf16[2048,512]{1,0:T(8,128)(2,1)}, bf16[2048,512]{1,0:T(8,128)(2,1)S(1)}, u32[]{:S(2)}) copy-start(bf16[2048,512]{1,0:T(8,128)(2,1)S(1)} %get-tuple-element.67.mixed_ref) | copy-start | bytes 6291460
  93.5 58.4 %copy-start.15 = (bf16[8,2,128,256]{3,2,1,0:T(8,128)(2,1)}, bf16[8,2,128,256]{3,2,1,0:T(8,128)(2,1)S(1)}, u32[]{:S(2)}) copy-start(bf16[8,2,128,256]{3,2,1,0:T(8,128)(2,1)S(1)} %get-tuple-element.71.states_ref) | copy-start | bytes 3145732
  93.5 58.4 %copy-start.4 = (bf16[2048,688]{0,1:T(8,128)(2,1)S(1)}, bf16[2048,688]{0,1:T(8,128)(2,1)}, u32[]{:S(2)}) copy-start(bf16[2048,688]{0,1:T(8,128)(2,1)} %param.38) | copy-start | bytes 8454148
  150.6 1.3 copy-start.8
  194.0 1.6 copy-start.30
  195.5 13.9 %copy-start.57 = (bf16[2048,2048]{1,0:T(8,128)(2,1)S(1)}, bf16[2048,2048]{1,0:T(8,128)(2,1)}, u32[]{:S(2)}) copy-start(bf16[2048,2048]{1,0:T(8,128)(2,1)} %get-tuple-element.80) | copy-start | bytes 25165828
  209.5 7.4 copy-start.39
  209.5 7.3 copy-start.31
  209.5 7.3 copy-start.58
  224.1 521.2 %reduce-scatter.5.cloned.1.call-start = ((), (), s32[]{:S(2)}) async-start(), calls=%async_computation.4 | async-start | bytes 9437184 | tf_op jit(solution)/shard_map/reduce_scatter | solution.py:1251
  224.2 51.7 %copy-start.7 = (bf16[512,2048]{1,0:T(8,128)(2,1)S(1)}, bf16[512,2048]{1,0:T(8,128)(2,1)}, u32[]{:S(2)}) copy-start(bf16[512,2048]{1,0:T(8,128)(2,1)} %w_ref.3) | copy-start | bytes 6291460
  275.9 39.1 %copy-start.14 = (bf16[2048,512]{1,0:T(8,128)(2,1)S(1)}, bf16[2048,512]{1,0:T(8,128)(2,1)}, u32[]{:S(2)}) copy-start(bf16[2048,512]{1,0:T(8,128)(2,1)} %copy-done.13) | copy-start | bytes 6291460
  314.9 10.8 %copy-start.9 = (f32[2048,512]{1,0:T(8,128)}, f32[2048,512]{1,0:T(8,128)S(1)}, u32[]{:S(2)}) copy-start(f32[2048,512]{1,0:T(8,128)S(1)} %get-tuple-element.84.grad_ref) | copy-start | bytes 12582916
  315.0 10.8 %copy-start.32 = (bf16[688,2048]{1,0:T(8,128)(2,1)S(1)}, bf16[688,2048]{1,0:T(8,128)(2,1)}, u32[]{:S(2)}) copy-start(bf16[688,2048]{1,0:T(8,128)(2,1)} %copy-done.30) | copy-start | bytes 8454148
  383.4 24.2 %copy-start.47 = (f32[4,512]{1,0:T(4,128)S(1)}, f32[4,512]{1,0:T(4,128)}, u32[]{:S(2)}) copy-start(f32[4,512]{1,0:T(4,128)} %get-tuple-element.91) | copy-start | bytes 24580
  383.4 24.2 %copy-start.51 = (f32[4,256]{1,0:T(4,128)S(1)}, f32[4,256]{1,0:T(4,128)}, u32[]{:S(2)}) copy-start(f32[4,256]{1,0:T(4,128)} %get-tuple-element.89) | copy-start | bytes 12292
  383.4 24.2 %copy-start.50 = (f32[4,256]{1,0:T(4,128)S(1)}, f32[4,256]{1,0:T(4,128)}, u32[]{:S(2)}) copy-start(f32[4,256]{1,0:T(4,128)} %get-tuple-element.90) | copy-start | bytes 12292
  383.4 24.3 %copy-start.45 = (bf16[2048]{0:T(1024)(128)(2,1)S(1)}, bf16[2048]{0:T(1024)(128)(2,1)}, u32[]{:S(2)}) copy-start(bf16[2048]{0:T(1024)(128)(2,1)} %param.23) | copy-start | bytes 12292
  404.4 2.8 copy-start.33
  404.4 3.3 copy-start.54
  404.4 3.3 copy-start.55
  404.4 3.3 copy-start.56
  439.9 307.2 %reduce-scatter.3.cloned.1.call-start = ((), (), s32[]{:S(2)}) async-start(), calls=%async_computation.3 | async-start | bytes 9437184 | tf_op jit(solution)/shard_map/reduce_scatter | solution.py:1251
  719.7 4.3 copy-start.42
  719.7 7.4 copy-start.36
  727.1 4.2 copy-start.46
  727.1 5.4 copy-start.34
  734.8 4.6 copy-start.37
  734.8 4.6 copy-start.38
  739.4 5.9 copy-start.3
  739.4 5.9 copy-start.41
  739.4 5.9 copy-start.44
  747.1 3.2 copy-start.35
  750.3 4.0 copy-start.1
Sparse Core Ops, SparseCore 0:
  62.9 69.7 all-gather.1
  224.2 201.9 all-reduce.2
  440.0 71.9 reduce-scatter.4
  515.7 71.2 reduce-scatter.2

commit v6 on v5

--- a/solution.py
+++ b/solution.py
@@ -43,6 +43,17 @@
     return lax.dot_general(
         left, right, (((1,), (0,)), ((), ())), precision=lax.Precision.HIGHEST, preferred_element_type=f32
     )
+
+
+def split(x):
+    high = x.astype(bf16)
+    return high, (x - high.astype(f32)).astype(bf16)
+
+
+def wide(dot, left, right):
+    left_high, left_low = split(left)
+    right_high, right_low = split(right)
+    return dot(left_high, right_high) + dot(left_low, right_high) + dot(left_high, right_low)
 
 
 def sigmoid(x):
@@ -97,7 +108,7 @@
         eye - x.astype(f32) - dot_nn(high, x) - dot_nn(rest, x)
         for x, high, rest in zip(rough, highs, rests)
     ]
-    return [(x.astype(f32) + dot_nn(x, error)).astype(bf16) for x, error in zip(rough, errors)]
+    return [x.astype(f32) + dot_nn(x, error) for x, error in zip(rough, errors)]
 
 
 def conv_from(ext_ref, taps, size):
@@ -205,12 +216,10 @@
 
     qs = [cut(act_q, u, key_dim) for u in units]
     qs = [q * (lax.rsqrt(jnp.sum(q * q, -1, keepdims=True) + unit_eps) * key_dim**-0.5) for q in qs]
-    qs = [q.astype(bf16) for q in qs]
     ks = [cut(act_k, u, key_dim) for u in units]
     ks = [k * lax.rsqrt(jnp.sum(k * k, -1, keepdims=True) + unit_eps) for k in ks]
-    kbs = [k.astype(bf16) for k in ks]
-    grams = [dot_nt(k, k) for k in kbs]
-    attends = [dot_nt(q, k) for q, k in zip(qs, kbs)]
+    grams = [wide(dot_nt, k, k) for k in ks]
+    attends = [wide(dot_nt, q, k) for q, k in zip(qs, ks)]
     betas = [parts[g][4][:, h : h + 1] for g, h in units]
     cums = [parts[g][2][:, h : h + 1] for g, h in units]
     cum_rows = [parts[g][3][h : h + 1, :] for g, h in units]
@@ -219,30 +228,29 @@
     lowers = [
         jnp.where(strict, gram * w * beta, 0.0) for gram, w, beta in zip(grams, withins, betas)
     ]
-    attends = [(a * w).astype(bf16) for a, w in zip(attends, withins)]
+    attends = [a * w for a, w in zip(attends, withins)]
     inverses = refined_inverses(lowers)
     growths = [jnp.exp(c) for c in cums]
-    tails = [(jnp.exp(last - c) * k).astype(bf16) for last, c, k in zip(lasts, cums, ks)]
+    tails = [(jnp.exp(last - c) * k) for last, c, k in zip(lasts, cums, ks)]
     outs = []
     for g in range(size // block):
         mine = [i for i, u in enumerate(units) if u[0] == g]
         states = [state[h] for h in range(heads)]
-        lows = [x.astype(bf16) for x in states]
-        seen = [dot_nn(kbs[i], low) for i, low in zip(mine, lows)]
+        seen = [wide(dot_nn, ks[i], x) for i, x in zip(mine, states)]
         rhs = [
-            (betas[i] * (cut(values, units[i], value_dim) - growths[i] * x)).astype(bf16)
+            betas[i] * (cut(values, units[i], value_dim) - growths[i] * x)
             for i, x in zip(mine, seen)
         ]
-        updates = [dot_nn(inverses[i], x).astype(bf16) for i, x in zip(mine, rhs)]
-        news = [dot_tn(tails[i], x) for i, x in zip(mine, updates)]
+        updates = [wide(dot_nn, inverses[i], x) for i, x in zip(mine, rhs)]
+        news = [wide(dot_tn, tails[i], x) for i, x in zip(mine, updates)]
         for h, i in enumerate(mine):
             state[h] = jnp.exp(lasts[i]) * states[h] + news[h]
-        reads = [dot_nn(qs[i], low) for i, low in zip(mine, lows)]
-        spreads = [dot_nn(attends[i], x) for i, x in zip(mine, updates)]
+        reads = [wide(dot_nn, qs[i], x) for i, x in zip(mine, states)]
+        spreads = [wide(dot_nn, attends[i], x) for i, x in zip(mine, updates)]
         outs += [growths[i] * x + y for i, x, y in zip(mine, reads, spreads)]
         for h, i in enumerate(mine):
             at = (slice(g * block, (g + 1) * block), slice(h * value_dim, (h + 1) * value_dim))
-            states_ref[g, h] = lows[h]
+            states_ref[g, h] = states[h]
             inverse_ref[g, h] = inverses[i]
             update_ref[at] = updates[h]
     for (g, h), out in zip(units, outs):
@@ -281,9 +289,9 @@
         out_shape=(
             jax.ShapeDtypeStruct((length, vw), bf16),
             jax.ShapeDtypeStruct((heads, key_dim, value_dim), f32),
-            jax.ShapeDtypeStruct((blocks, heads, key_dim, value_dim), bf16),
-            jax.ShapeDtypeStruct((blocks, heads, block, block), bf16),
-            jax.ShapeDtypeStruct((length, vw), bf16),
+            jax.ShapeDtypeStruct((blocks, heads, key_dim, value_dim), f32),
+            jax.ShapeDtypeStruct((blocks, heads, block, block), f32),
+            jax.ShapeDtypeStruct((length, vw), f32),
             jax.ShapeDtypeStruct((length, vw), f32),
         ),
         in_specs=[
@@ -439,7 +447,7 @@
         dn = grad * cut(gate, u, value_dim)
         grad_gain = grad_gain + jnp.sum(dn * unit, 0, keepdims=True)
         e = dn * gain
-        dos.append((scale * (e - unit * jnp.mean(e * unit, -1, keepdims=True))).astype(bf16))
+        dos.append(scale * (e - unit * jnp.mean(e * unit, -1, keepdims=True)))
     dgain_ref[...] += grad_gain
     aqs = [cut(acts[0], u, key_dim) for u in units]
     rqs = [lax.rsqrt(jnp.sum(a * a, -1, keepdims=True) + unit_eps) for a in aqs]
@@ -448,9 +456,8 @@
     aks = [cut(acts[1], u, key_dim) for u in units]
     rks = [lax.rsqrt(jnp.sum(a * a, -1, keepdims=True) + unit_eps) for a in aks]
     ks = [a * r for a, r in zip(aks, rks)]
-    qbs, kbs = [q.astype(bf16) for q in qs], [k.astype(bf16) for k in ks]
-    attends = [dot_nt(q, k) for q, k in zip(qbs, kbs)]
-    grams = [dot_nt(k, k) for k in kbs]
+    attends = [wide(dot_nt, q, k) for q, k in zip(qs, ks)]
+    grams = [wide(dot_nt, k, k) for k in ks]
     betas = [parts[g][4][:, h : h + 1] for g, h in units]
     cums = [parts[g][2][:, h : h + 1] for g, h in units]
     rows_of = [parts[g][3][h : h + 1, :] for g, h in units]
@@ -463,31 +470,30 @@
     stricts = [jnp.where(strict, w, 0.0) for w in withins]
     attends = [a * w for a, w in zip(attends, withins)]
     grams = [a * w for a, w in zip(grams, stricts)]
-    from_out = [dot_tn(a, do) for a, do in zip(attends, dos)]
-    into_state = [dot_tn(g * q, do) for g, q, do in zip(growths, qs, dos)]
-    tail_keys = [(t * k).astype(bf16) for t, k in zip(tails, ks)]
-    bg_keys = [(b * k).astype(bf16) for b, k in zip(bgs, ks)]
-    dss, dsbs, dbs, dbbs = {}, {}, {}, {}
+    from_out = [wide(dot_tn, a, do) for a, do in zip(attends, dos)]
+    into_state = [wide(dot_tn, g * q, do) for g, q, do in zip(growths, qs, dos)]
+    tail_keys = [t * k for t, k in zip(tails, ks)]
+    bg_keys = [b * k for b, k in zip(bgs, ks)]
+    dss, dbs = {}, {}
     for g in reversed(range(size // block)):
         mine = [i for i, u in enumerate(units) if u[0] == g]
         for h, i in enumerate(mine):
             dss[i] = dstate[h]
-            dsbs[i] = dss[i].astype(bf16)
-        dus = [(from_out[i] + dot_nn(tail_keys[i], dsbs[i])).astype(bf16) for i in mine]
+        dus = [from_out[i] + wide(dot_nn, tail_keys[i], dss[i]) for i in mine]
         for h, i in enumerate(mine):
-            dbs[i] = dot_tn(inverse_ref[g, h], dus[h])
-            dbbs[i] = dbs[i].astype(bf16)
-        backs_in = [dot_tn(bg_keys[i], dbbs[i]) for i in mine]
+            dbs[i] = wide(dot_tn, inverse_ref[g, h], dus[h])
+        backs_in = [wide(dot_tn, bg_keys[i], dbs[i]) for i in mine]
         for h, i in enumerate(mine):
             dstate[h] = decs[i] * dss[i] + into_state[i] - backs_in[h]
     index = range(len(units))
     states = [states_ref[g, h] for g, h in units]
     updates = [update_ref[place(u, value_dim)] for u in units]
-    das = [dot_nt(do, x) for do, x in zip(dos, updates)]
-    dls = [-dot_nt(dbbs[i], updates[i]) for i in index]
-    dqgs = [dot_nt(do, x) for do, x in zip(dos, states)]
-    dkbs = [-dot_nt(dbbs[i], states[i]) for i in index]
-    dkts = [dot_nt(updates[i], dsbs[i]) for i in index]
+    das = [wide(dot_nt, do, x) for do, x in zip(dos, updates)]
+    dls = [-wide(dot_nt, dbs[i], updates[i]) for i in index]
+    dqgs = [wide(dot_nt, do, x) for do, x in zip(dos, states)]
+    dkbs = [-wide(dot_nt, dbs[i], states[i]) for i in index]
+    dkts = [wide(dot_nt, updates[i], dss[i]) for i in index]
+    qbs, kbs = [q.astype(bf16) for q in qs], [k.astype(bf16) for k in ks]
     dgqs = [(x * w).astype(bf16) for x, w in zip(das, withins)]
     dl_grams = [x * y for x, y in zip(dls, grams)]
     dgks = [(x * w * b).astype(bf16) for x, w, b in zip(dls, stricts, betas)]
@@ -516,7 +522,7 @@
     ends = [
         jnp.sum(tail_sums[i], 0, keepdims=True)
         + decs[i]
-        * jnp.sum(jnp.sum(states[i].astype(f32) * dss[i], -1, keepdims=True), 0, keepdims=True)
+        * jnp.sum(jnp.sum(states[i] * dss[i], -1, keepdims=True), 0, keepdims=True)
         for i in index
     ]
     dqs = [(x + g * y) * (key_dim**-0.5) for x, g, y in zip(dqs, growths, dqgs)]
@@ -776,7 +782,7 @@
         for copy in copies.values():
             copy.wait_send()
 
-    return ready, finish
+    return ready, finish, order
 
 
 def rows_at(ref, shard, rows):
@@ -810,7 +816,7 @@
     out,
 ):
     rows = x_ref.shape[0]
-    ready, finish = gather_parts(axis, x_ref, held, send, recv, local)
+    ready, finish, _ = gather_parts(axis, x_ref, held, send, recv, local)
     loads, at = [], 0
     for i, ref in enumerate((wq_ref, wk_ref, wv_ref, wg_ref)):
         width = ref.shape[1]
@@ -907,37 +913,52 @@
 def gather_expand_kernel(
     axis,
     x_ref,
+    cot_ref,
     wg_ref,
     wu_ref,
+    wd_ref,
     all_ref,
-    gate_ref,
-    up_ref,
     inner_ref,
+    dgate_ref,
+    dup_ref,
     held,
     w_gate,
     w_up,
-    gates,
-    ups,
+    w_down,
+    cots,
+    dinners,
     inners,
+    dgates,
+    dups,
     send,
     recv,
     local,
     keep,
     load,
+    fetch,
     out,
 ):
     rows = x_ref.shape[0]
-    ready, finish = gather_parts(axis, x_ref, held, send, recv, local)
+    ready, finish, order = gather_parts(axis, x_ref, held, send, recv, local)
     loads = [
-        pltpu.make_async_copy(wg_ref, w_gate, load.at[0]),
-        pltpu.make_async_copy(wu_ref, w_up, load.at[1]),
+        pltpu.make_async_copy(src, dst, load.at[k])
+        for k, (src, dst) in enumerate(((wg_ref, w_gate), (wu_ref, w_up), (wd_ref, w_down)))
     ]
-    for copy in loads:
+    fetches = [
+        pltpu.make_async_copy(rows_at(cot_ref, order[i], rows), cots.at[i % 2], fetch.at[i])
+        for i in range(8)
+    ]
+    for copy in (loads[2], fetches[0], loads[0], loads[1]):
         copy.start()
-    for copy in loads:
-        copy.wait()
     keeps, outs = [], []
-    for i in range(8):
+
+    def backward(i):
+        if i + 1 < 8:
+            fetches[i + 1].start()
+        fetches[i].wait()
+        dinners[i] = dot_nt(w_down[...], cots[i % 2])
+
+    def forward(i):
         shard = ready(i)
         keeps.append(pltpu.make_async_copy(rows_at(held, shard, rows), rows_at(all_ref, shard, rows), keep.at[i]))
         keeps[-1].start()
@@ -947,63 +968,118 @@
         slot = i % 2
         x = rows_at(held, shard, rows)[...]
         gate = dot_nt(w_gate[...], x)
-        gates[slot] = gate
         up = dot_nt(w_up[...], x)
-        ups[slot] = up
-        inners[slot] = (gate * sigmoid(gate) * up).astype(bf16)
+        dinner = dinners[i]
+        sig = sigmoid(gate)
+        act = gate * sig
+        inners[slot] = (act * up).astype(bf16)
+        dups[slot] = (dinner * act).astype(bf16)
+        dgates[slot] = (dinner * up * sig * (1.0 + gate * (1.0 - sig))).astype(bf16)
         moves = []
-        for k, (src, dst) in enumerate(((gates, gate_ref), (ups, up_ref), (inners, inner_ref))):
+        for k, (src, dst) in enumerate(((inners, inner_ref), (dgates, dgate_ref), (dups, dup_ref))):
             moves.append(pltpu.make_async_copy(src.at[slot], columns_at(dst, shard, rows), out.at[k, i]))
             moves[-1].start()
         outs.append(moves)
+
+    loads[2].wait()
+    backward(0)
+    loads[0].wait()
+    loads[1].wait()
+    forward(0)
+    backward(1)
+    forward(1)
+    for i in range(2, 8):
+        backward(i)
+    for i in range(2, 8):
+        forward(i)
     for copy in keeps + outs[6] + outs[7]:
         copy.wait()
     finish()
 
 
-def gather_expand(x, gate_rows, up_rows, identity, sizes):
+def gather_expand(x, cotangent, gate_rows, up_rows, down_rows, identity, sizes):
     rows, depth = x.shape
     units = gate_rows.shape[0]
     if not square(sizes):
         gathered = lax.all_gather(x, "tensor", axis=0, tiled=True)
         gate, up = times_transposed(gate_rows, gathered), times_transposed(up_rows, gathered)
-        return gathered, gate, up, (gate * sigmoid(gate) * up).astype(bf16)
+        dinner = times_transposed(down_rows, cotangent)
+        sig = sigmoid(gate)
+        dgate = dinner * up * sig * (1.0 + gate * (1.0 - sig))
+        return gathered, (gate * sig * up).astype(bf16), dgate.astype(bf16), (dinner * gate * sig).astype(bf16)
+    by_token = jax.ShapeDtypeStruct((units, 8 * rows), bf16)
     return pl.pallas_call(
         functools.partial(gather_expand_kernel, "tensor"),
-        out_shape=(
-            jax.ShapeDtypeStruct((8 * rows, depth), bf16),
-            jax.ShapeDtypeStruct((units, 8 * rows), f32),
-            jax.ShapeDtypeStruct((units, 8 * rows), f32),
-            jax.ShapeDtypeStruct((units, 8 * rows), bf16),
-        ),
-        in_specs=[ANYWHERE] * 3,
+        out_shape=(jax.ShapeDtypeStruct((8 * rows, depth), bf16), by_token, by_token, by_token),
+        in_specs=[ANYWHERE] * 5,
         out_specs=(ANYWHERE,) * 4,
         scratch_shapes=[
             pltpu.VMEM((8 * rows, depth), bf16),
             pltpu.VMEM((units, depth), bf16),
             pltpu.VMEM((units, depth), bf16),
-            pltpu.VMEM((2, units, rows), f32),
-            pltpu.VMEM((2, units, rows), f32),
+            pltpu.VMEM((units, depth), bf16),
+            pltpu.VMEM((2, rows, depth), bf16),
+            pltpu.VMEM((8, units, rows), f32),
+            pltpu.VMEM((2, units, rows), bf16),
+            pltpu.VMEM((2, units, rows), bf16),
             pltpu.VMEM((2, units, rows), bf16),
         ]
         + gather_scratch(rows, depth)
-        + [pltpu.SemaphoreType.DMA((2,)), pltpu.SemaphoreType.DMA((3, 8))],
+        + [pltpu.SemaphoreType.DMA((3,)), pltpu.SemaphoreType.DMA((8,)), pltpu.SemaphoreType.DMA((3, 8))],
         compiler_params=pltpu.CompilerParams(
-            collective_id=identity, has_side_effects=True, vmem_limit_bytes=40 * 1024 * 1024
+            collective_id=identity, has_side_effects=True, vmem_limit_bytes=48 * 1024 * 1024
         ),
         cost_estimate=pl.CostEstimate(flops=0, bytes_accessed=1_000_000, transcendentals=0),
         name="gather_expand",
-    )(x, gate_rows, up_rows)
-
-
-def gather_back_kernel(axis, x_ref, w_ref, all_ref, y_ref, held, weights, stage, send, recv, local, keep, load, out):
-    rows = x_ref.shape[0]
-    ready, finish = gather_parts(axis, x_ref, held, send, recv, local)
-    copy = pltpu.make_async_copy(w_ref, weights, load)
-    copy.start()
-    copy.wait()
-    keeps, outs = [], []
-    for i in range(8):
+    )(x, cotangent, gate_rows, up_rows, down_rows)
+
+
+def gather_back_kernel(
+    axis,
+    x_ref,
+    w_ref,
+    inner_ref,
+    down_ref,
+    dup_ref,
+    normed_ref,
+    all_ref,
+    y_ref,
+    part_ref,
+    dw_ref,
+    held,
+    weights,
+    stage,
+    inner,
+    down,
+    dup,
+    normed,
+    parts,
+    dws,
+    send,
+    recv,
+    local,
+    keep,
+    load,
+    fetch,
+    out,
+):
+    rows, depth = x_ref.shape
+    ready, finish, _ = gather_parts(axis, x_ref, held, send, recv, local)
+    loads = [
+        pltpu.make_async_copy(src, dst, load.at[k])
+        for k, (src, dst) in enumerate(((w_ref, weights), (inner_ref, inner), (down_ref, down), (dup_ref, dup)))
+    ]
+    for copy in loads:
+        copy.start()
+    wide = depth // 8
+    fetches = [
+        pltpu.make_async_copy(normed_ref.at[:, pl.ds(i * wide, wide)], normed.at[i % 2], fetch.at[i])
+        for i in range(8)
+    ]
+    fetches[0].start()
+    keeps, outs, moves = [], [], []
+
+    def project(i):
         shard = ready(i)
         keeps.append(pltpu.make_async_copy(rows_at(held, shard, rows), rows_at(all_ref, shard, rows), keep.at[i]))
         keeps[-1].start()
@@ -1011,40 +1087,89 @@
             outs[i - 2].wait()
         slot = i % 2
         stage[slot] = dot_nt(rows_at(held, shard, rows)[...], weights[...])
-        outs.append(pltpu.make_async_copy(stage.at[slot], rows_at(y_ref, shard, rows), out.at[i]))
+        outs.append(pltpu.make_async_copy(stage.at[slot], rows_at(y_ref, shard, rows), out.at[0, i]))
         outs[-1].start()
-    for copy in keeps + outs[6:]:
+
+    def aside(i):
+        slot = i % 2
+        if i + 1 < 8:
+            fetches[i + 1].start()
+        if i >= 2:
+            for copy in moves[i - 2]:
+                copy.wait()
+        turned = jnp.transpose(inner[:, i * rows : (i + 1) * rows])
+
+        def tile(here):
+            parts[slot, :, here] = dot_nn(turned, down[:, here]).astype(bf16)
+
+        in_columns(depth, 512, tile)
+        fetches[i].wait()
+        dws[slot] = dot_nn(dup[...], normed[slot]).astype(bf16)
+        pair = (
+            pltpu.make_async_copy(parts.at[slot], part_ref.at[pl.ds(i * rows, rows), :], out.at[1, i]),
+            pltpu.make_async_copy(dws.at[slot], dw_ref.at[:, pl.ds(i * wide, wide)], out.at[2, i]),
+        )
+        for copy in pair:
+            copy.start()
+        moves.append(pair)
+
+    loads[0].wait()
+    project(0)
+    for copy in loads[1:]:
+        copy.wait()
+    for i in range(3):
+        aside(i)
+    project(1)
+    aside(3)
+    aside(4)
+    for i in range(2, 6):
+        project(i)
+    for i in range(5, 8):
+        aside(i)
+    project(6)
+    project(7)
+    for copy in keeps + outs[6:] + list(moves[6]) + list(moves[7]):
         copy.wait()
     finish()
 
 
-def gather_back(x, w, identity, sizes):
+def gather_back(x, w, inner, down, dup, normed, identity, sizes):
     rows, depth = x.shape
-    width = w.shape[0]
+    width, units = w.shape[0], inner.shape[0]
     if not square(sizes):
         gathered = lax.all_gather(x, "tensor", axis=0, tiled=True)
-        return gathered, times_transposed(gathered, w)
+        part = cross_rows(inner, down).astype(bf16)
+        dw = jnp.dot(dup, normed, preferred_element_type=f32).astype(bf16)
+        return gathered, times_transposed(gathered, w), part, dw
     return pl.pallas_call(
         functools.partial(gather_back_kernel, "tensor"),
         out_shape=(
             jax.ShapeDtypeStruct((8 * rows, depth), bf16),
             jax.ShapeDtypeStruct((8 * rows, width), f32),
+            jax.ShapeDtypeStruct((8 * rows, depth), bf16),
+            jax.ShapeDtypeStruct((units, depth), bf16),
         ),
-        in_specs=[ANYWHERE] * 2,
-        out_specs=(ANYWHERE,) * 2,
+        in_specs=[ANYWHERE] * 6,
+        out_specs=(ANYWHERE,) * 4,
         scratch_shapes=[
             pltpu.VMEM((8 * rows, depth), bf16),
             pltpu.VMEM((width, depth), bf16),
             pltpu.VMEM((2, rows, width), f32),
+            pltpu.VMEM((units, 8 * rows), bf16),
+            pltpu.VMEM((units, depth), bf16),
+            pltpu.VMEM((units, 8 * rows), bf16),
+            pltpu.VMEM((2, 8 * rows, depth // 8), bf16),
+            pltpu.VMEM((2, rows, depth), bf16),
+            pltpu.VMEM((2, units, depth // 8), bf16),
         ]
         + gather_scratch(rows, depth)
-        + [pltpu.SemaphoreType.DMA, pltpu.SemaphoreType.DMA((8,))],
+        + [pltpu.SemaphoreType.DMA((4,)), pltpu.SemaphoreType.DMA((8,)), pltpu.SemaphoreType.DMA((3, 8))],
         compiler_params=pltpu.CompilerParams(
-            collective_id=identity, has_side_effects=True, vmem_limit_bytes=40 * 1024 * 1024
+            collective_id=identity, has_side_effects=True, vmem_limit_bytes=48 * 1024 * 1024
         ),
         cost_estimate=pl.CostEstimate(flops=0, bytes_accessed=1_000_000, transcendentals=0),
         name="gather_back",
-    )(x, w)
+    )(x, w, inner, down, dup, normed)
 
 
 def scatter_parts(axis, product, finish, mine, theirs, leaving, in_dx, in_dy, in_x, in_y, send, recv):
@@ -1254,11 +1379,20 @@
 CHUNK = 64
 
 
-def chunk_rows(rows):
-    return next((c for c in range(CHUNK, 0, -16) if rows % c == 0), rows)
-
-
-def line_kernel(axis, cross, widths, *refs):
+def row_groups(arrays):
+    groups = []
+    for i, a in enumerate(arrays):
+        whole = a.shape[0] // CHUNK
+        if i > 0 and whole > 0:
+            groups.append((i, 0, CHUNK, whole))
+            if a.shape[0] % CHUNK:
+                groups.append((i, whole * CHUNK, a.shape[0] % CHUNK, 1))
+        else:
+            groups.append((i, 0, a.shape[0], 1))
+    return groups
+
+
+def line_kernel(axis, cross, widths, spans, *refs):
     count = len(widths)
     g_refs, out_refs = refs[:count], refs[count : 2 * count]
     both_ref, parts, part_sems = refs[2 * count], refs[2 * count + 1], refs[2 * count + 2]
@@ -1307,13 +1441,12 @@
             spread(k).start()
 
     groups = []
-    for i in range(count):
-        own, from_out, from_in, total, sems = scratch[5 * i : 5 * i + 5]
+    for k, (i, start, chunk, chunks) in enumerate(spans):
+        own, from_out, from_in, total, sems = scratch[5 * k : 5 * k + 5]
         g_ref, out_ref = g_refs[i], out_refs[i]
-        chunks, chunk = own.shape[0], own.shape[1]
-
-        def rows_of(ref, c, width=widths[i], chunk=chunk):
-            return ref.at[pl.ds(pl.multiple_of(c * chunk, chunk), chunk), pl.ds(0, width)]
+
+        def rows_of(ref, c, start=start, width=widths[i], chunk=chunk):
+            return ref.at[pl.ds(pl.multiple_of(start + c * chunk, 16), chunk), pl.ds(0, width)]
 
         def load(c, g_ref=g_ref, own=own, sems=sems, rows_of=rows_of):
             return pltpu.make_async_copy(rows_of(g_ref, c), own.at[c], sems.at[0, c])
@@ -1406,15 +1539,14 @@
         return summed + (lax.psum(summed[0][:both], "tensor"),)
     peers = sizes["tensor"]
     scratch = [pltpu.VMEM((peers, both, widths[0]), arrays[0].dtype), pltpu.SemaphoreType.DMA((2, peers))]
-    for a, w in zip(arrays, widths):
-        chunk = chunk_rows(a.shape[0])
-        chunks = a.shape[0] // chunk
-        scratch += [pltpu.VMEM((chunks, chunk, w), a.dtype)] * 4
+    spans = row_groups(arrays)
+    for i, _, chunk, chunks in spans:
+        scratch += [pltpu.VMEM((chunks, chunk, widths[i]), arrays[i].dtype)] * 4
         scratch.append(pltpu.SemaphoreType.DMA((8, chunks)))
     anywhere = pl.BlockSpec(memory_space=pl.ANY)
     total = sum(a.shape[0] * w for a, w in zip(arrays, widths))
     return pl.pallas_call(
-        functools.partial(line_kernel, "dp", "tensor", tuple(widths)),
+        functools.partial(line_kernel, "dp", "tensor", tuple(widths), tuple(spans)),
         out_shape=tuple(jax.ShapeDtypeStruct((a.shape[0], w), a.dtype) for a, w in zip(arrays, widths))
         + (jax.ShapeDtypeStruct((both, widths[0]), arrays[0].dtype),),
         in_specs=[anywhere] * len(arrays),
@@ -1477,13 +1609,9 @@
     grad_gathered = lax.all_gather(grad_out_rows, "tensor", axis=0, tiled=True)
     hidden, normed_ffn = attend(mixed, w_out, tokens[0], gain_second, 1, sizes)
     gate_rows, up_rows = w_ffn_gate.T, w_ffn_up.T
-    gathered_ffn, gate_proj, up_proj, inner = gather_expand(normed_ffn, gate_rows, up_rows, 2, sizes)
-    sigmoid_gate = jax.nn.sigmoid(gate_proj)
-    grad_inner = times_transposed(w_ffn_down, grad_gathered)
-    grad_gate_rows = (
-        grad_inner * up_proj * sigmoid_gate * (1.0 + gate_proj * (1.0 - sigmoid_gate))
-    ).astype(bf16)
-    grad_up_rows = (grad_inner * gate_proj * sigmoid_gate).astype(bf16)
+    gathered_ffn, inner, grad_gate_rows, grad_up_rows = gather_expand(
+        normed_ffn, grad_gathered, gate_rows, up_rows, w_ffn_down, 2, sizes
+    )
     grad_down = jnp.dot(inner, grad_gathered, preferred_element_type=f32).astype(bf16)
     grad_gate_weight = jnp.dot(grad_gate_rows, gathered_ffn, preferred_element_type=f32).astype(bf16)
     grad_down_summed, grad_gate_summed = lax.psum((grad_down, grad_gate_weight), "dp")
@@ -1493,10 +1621,10 @@
     grad_hidden, grad_attended, part_gain_ffn = return_hidden(
         grad_gate_rows, grad_up_rows, gate_rows, up_rows, hidden, grad_out_rows, gain_second, 3, sizes
     )
-    grad_attended, grad_mixed = gather_back(grad_attended, w_out, 4, sizes)
-    grad_up_weight = jnp.dot(grad_up_rows, gathered_ffn, preferred_element_type=f32).astype(bf16)
+    grad_attended, grad_mixed, ffn_part, grad_up_weight = gather_back(
+        grad_attended, w_out, inner, w_ffn_down, grad_up_rows, gathered_ffn, 4, sizes
+    )
     grad_out_weight = cross_rows(mixed, grad_attended).astype(bf16)
-    ffn_part = cross_rows(inner, w_ffn_down).astype(bf16)
     grad_projected, grad_tq, grad_tk, grad_tv, grad_dl, grad_db, grad_gain = mixer_backward(
         projected, *extras, states, inverse, update, raw, grad_mixed
     )

time: 767 us -> 747 us (0.974)
  matrix products: 101 us -> 69.6 us
  local copies, waits for them, and re-layouts: 17.6 us -> 26.8 us
    dot_general x2 -> x1, matrix products: 35 us -> 21.1 us  [times_transposed(): lax.dot_general(left, right, (((1,), (1,)), ((), ())), preferred_element_...]
    pallas_call x1, Pallas kernels: 279 us -> 268 us  [sum_over_line(): pl.pallas_call(functools.partial(line_kernel, 'dp', 'tensor', tuple(width...]
    dot_general x3 -> x2, matrix products: 40.8 us -> 29.9 us  [cross_rows(): lax.dot_general(left, right, (((0,), (0,)), ((), ())), preferred_element_...]
    dot_general x1 -> x0, matrix products: 10.3 us -> none  [shards(): jnp.dot(grad_up_rows, gathered_ffn, preferred_element_type=f32).astype(bf16)]
    pallas_call x1, Pallas kernels: 48.5 us -> 58.8 us  [mixer_backward(): pl.pallas_call(functools.partial(backward_kernel, heads, key_dim, value_d...]
    unnamed x124 -> x110, local copies, waits for them, and re-layouts: 11.5 us -> 16.5 us
  transfers between devices with their start and end apart: 4 -> 4, of which waited for: 0 -> 0; matrix products, arithmetic and copies ran while one was open for 13% -> 12% of each run, Pallas kernels for 72% -> 68%
where the time goes in v6:
time: 747 us; the launch traced here: 740 us
  Pallas kernels  594 us (80%)
  matrix products  69.6 us (9%)
  other arithmetic  33.8 us (5%)
  local copies, waits for them, and re-layouts  26.8 us (4%)
  between operations  14.9 us (2%)
    pallas_call x1, Pallas kernels, sum_over_line(): pl.pallas_call(functools.partial(line_kernel, 'dp', 'tensor', tuple(width...  268 us
    pallas_call x1, Pallas kernels, mixer_backward(): pl.pallas_call(functools.partial(backward_kernel, heads, key_dim, value_d...  58.8 us
    pallas_call x1, Pallas kernels, return_hidden(): pl.pallas_call(functools.partial(return_kernel, 'tensor'), out_shape=(jax...  51.6 us
    pallas_call x1, Pallas kernels, attend(): pl.pallas_call(functools.partial(attend_kernel, 'tensor'), out_shape=(jax...  49.5 us
    pallas_call x1, Pallas kernels, gather_project(): pl.pallas_call(functools.partial(gather_project_kernel, 'tensor'), out_sh...  45.6 us
    pallas_call x1, Pallas kernels, gather_expand(): pl.pallas_call(functools.partial(gather_expand_kernel, 'tensor'), out_sha...  42.6 us
    pallas_call x1, Pallas kernels, gather_back(): pl.pallas_call(functools.partial(gather_back_kernel, 'tensor'), out_shape...  42.1 us
    pallas_call x1, Pallas kernels, mixer_forward(): pl.pallas_call(functools.partial(forward_kernel, heads, key_dim, value_di...  36.3 us
  transfers between devices with their start and end apart: 4, of which 0 were waited for; matrix products, arithmetic and copies ran while one was open for 12% of the time, Pallas kernels for 68%

profile of v6, /device:TPU:0, one launch (start us, length us, event | category | flops | bytes accessed | tf_op | source)
XLA Modules:
  0.0 740.5 jit_solution(13434682083383436221)
XLA Ops:
  7.2 0.0 all-gather.2.cloned.1.call-start
  7.3 0.8 convert_element_type.72
  8.1 1.6 fusion.9
  9.7 1.5 fusion.3.x_ref
  11.3 1.6 copy-done.7
  12.9 1.2 copy-done.12
  14.2 0.0 copy-start.40
  14.2 0.0 copy-start.15
  14.2 45.6 %gather_project.1 = (bf16[2048,2048]{1,0:T(8,128)(2,1)}, bf16[2048,1664]{1,0:T(8,128)(2,1)S(1)}, f32[2048,1664]{1,0:T(8,128)}) custom-call(bf16[256,2048]{1,0:T(8,128)(2,1)S(1)} %fusion.3.x_ref, bf16[2,2048]{1,0:T(2,128)(2,1)S(1)} %bitcast.64, bf16[2,2048]{1,0:T(2,128)(2,1)S(1)} %bitcast.65, bf16[2048,256]{1,0:T(8,128)(2,1)S(1)} %copy-done.11, ...), custom_call_target="tpu_custom_call" | custom-call | bytes 1000000 | tf_op jit(solution)/shard_map/gather_project/pallas_call | solution.py:889
  59.9 2.8 copy-done.26
  62.7 0.0 all-gather.2.cloned.1.call-update
  62.7 0.3 all-reduce.3.cloned.1.call-start
  63.0 0.0 copy-start.17
  63.1 0.1 copy.47.dl_col_ref
  63.2 0.1 copy.48.db_col_ref
  63.3 0.0 copy-start
  63.3 0.0 copy-start.1
  63.3 36.3 %mixer_forward.1 = (bf16[2048,512]{1,0:T(8,128)(2,1)S(1)}, f32[2,128,256]{2,1,0:T(8,128)}, f32[8,2,128,256]{3,2,1,0:T(8,128)S(1)}, f32[8,2,256,256]{3,2,1,0:T(8,...) custom-call(f32[2048,1664]{1,0:T(8,128)} %get-tuple-element.68.proj_ref.eq_ref.ek_ref.ev_ref, ...), custom_call_target="tpu_custom_call" | custom-call | bytes 100000000 | tf_op jit(solution)/shard_map/mixer_forward/pallas_call | solution.py:286
  99.7 1.3 copy-done.10
  101.0 49.5 %attend.1 = (f32[256,2048]{1,0:T(8,128)S(1)}, bf16[256,2048]{1,0:T(8,128)(2,1)S(1)}) custom-call(bf16[2048,512]{1,0:T(8,128)(2,1)S(1)} %get-tuple-element.69.mixed_ref, bf16[512,2048]{1,0:T(8,128)(2,1)S(1)} %copy-done.1, bf16[256,2048]{1,0:T(8,128)(2,1)S(1)} %bitcast.60, f32[1,2048]{1,0:T(1,128)S(1)} %bitcast.62), custom_call_target="tpu_custom_call" | custom-call | bytes 1000000 | tf_op jit(solution)/shard_map/attend/pallas_call | solution.py:1287
  150.5 1.3 copy-done.2
  151.8 1.3 copy-done.8
  153.2 1.0 copy-done.13
  154.1 1.2 copy-done.14
  155.4 42.6 %gather_expand.1 = (bf16[2048,2048]{1,0:T(8,128)(2,1)}, bf16[688,2048]{1,0:T(8,128)(2,1)S(1)}, bf16[688,2048]{1,0:T(8,128)(2,1)}, bf16[688,2048]{1,0:T(8,128)(2,1)}) custom-call(bf16[256,2048]{1,0:T(8,128)(2,1)S(1)} %copy-done.14, bf16[2048,2048]{1,0:T(8,128)(2,1)} %all-gather.2.cloned.1.call-done.cot_ref, bf16[688,2048]{1,0:T(8,128)(2,1)} %bitcast.75, ...), custom_call_target="tpu_custom_call" | custom-call | bytes 1000000 | tf_op jit(solution)/shard_map/gather_expand/pallas_call | solution.py:1011
  198.0 11.4 %convolution_convert_fusion.2 = bf16[688,2048]{1,0:T(8,128)(2,1)} fusion(bf16[688,2048]{1,0:T(8,128)(2,1)} %get-tuple-element.83.dgate_ref, bf16[2048,2048]{1,0:T(8,128)(2,1)} %get-tuple-element.82.normed_ref), kind=kOutput, calls=%fused_computation.5 | convolution fusion | flops 5772771328 | bytes 14024704 | tf_op jit(solution)/shard_map/dot_general | solution.py:1616
  209.4 7.3 convolution_convert_fusion.3
  216.6 0.0 all-reduce.3.cloned.1.call-update
  216.7 0.0 reduce-scatter.5.cloned.1.call-start
  216.7 51.6 %return_hidden.1 = (f32[256,2048]{1,0:T(8,128)}, bf16[256,2048]{1,0:T(8,128)(2,1)S(1)}, f32[1,2048]{1,0:T(1,128)S(1)}) custom-call(bf16[688,2048]{1,0:T(8,128)(2,1)} %get-tuple-element.83.dgate_ref, bf16[688,2048]{1,0:T(8,128)(2,1)} %get-tuple-element.84.dup_ref, bf16[688,2048]{1,0:T(8,128)(2,1)} %bitcast.76, bf16[688,2048]{1,0:T(8,128)(2,1)} %bitcast.78, ...), custom_call_target="tpu_custom_call" | custom-call | bytes 1000000 | tf_op jit(solution)/shard_map/return_hidden/pallas_call | solution.py:1356
  268.3 42.1 %gather_back.1 = (bf16[2048,2048]{1,0:T(8,128)(2,1)}, f32[2048,512]{1,0:T(8,128)}, bf16[2048,2048]{1,0:T(8,128)(2,1)}, bf16[688,2048]{1,0:T(8,128)(2,1)S(1)}) custom-call(bf16[256,2048]{1,0:T(8,128)(2,1)S(1)} %get-tuple-element.85.x_ref, bf16[512,2048]{1,0:T(8,128)(2,1)S(1)} %copy-done.1, bf16[688,2048]{1,0:T(8,128)(2,1)} %copy-done.4, ...), custom_call_target="tpu_custom_call" | custom-call | bytes 1000000 | tf_op jit(solution)/shard_map/gather_back/pallas_call | solution.py:1144
  310.5 1.5 copy-done.5
  312.0 58.8 %mixer_backward.1 = (bf16[2048,1664]{1,0:T(8,128)(2,1)}, f32[4,256]{1,0:T(4,128)}, f32[4,256]{1,0:T(4,128)}, f32[4,512]{1,0:T(4,128)}, f32[1,2]{1,0:T(1,128)}, /*index=5*/f32[1,2]{1,0:T(1,128)}, f32[1,256]{1,0:T(1,128)}) custom-call(f32[2048,1664]{1,0:T(8,128)} %get-tuple-element.68.proj_ref.eq_ref.ek_ref.ev_ref, ...), custom_call_target="tpu_custom_call" | custom-call | bytes 100000000 | tf_op jit(solution)/shard_map/mixer_backward/pallas_call | solution.py:597
  370.9 20.8 %multiply_reduce_fusion = (f32[2048]{0:T(1024)S(1)}, bf16[2048,1664]{1,0:T(8,128)(2,1)S(1)}) fusion(bf16[2048,1664]{1,0:T(8,128)(2,1)} %copy-done.26, bf16[2048,2048]{1,0:T(8,128)(2,1)} %get-tuple-element.72, bf16[2048,1664]{1,0:T(8,128)(2,1)} %get-tuple-element.88), kind=kOutput, calls=%fused_computation | convolution fusion | flops 13975681024 | bytes 28844032 | tf_op jit(solution)/shard_map/dot_general | solution.py:677
  391.8 3.0 copy-done.27
  394.7 1.0 convert_bitcast_fusion.2
  395.8 1.6 copy.52
  397.4 0.7 concatenate.3
  398.1 9.1 %convolution_convert_fusion.4.refs_2_ = bf16[512,2048]{1,0:T(8,128)(2,1)} fusion(bf16[2048,512]{1,0:T(8,128)(2,1)S(1)} %copy-done.9, bf16[2048,2048]{1,0:T(8,128)(2,1)} %get-tuple-element.99), kind=kOutput, calls=%fused_computation.7 | convolution fusion | flops 4296015872 | bytes 12582912 | tf_op jit(solution)/shard_map/dot_general | solution.py:677
  407.2 21.1 %convolution_convert_fusion = bf16[2048,2048]{1,0:T(8,128)(2,1)} fusion(bf16[2048,1664]{1,0:T(8,128)(2,1)} %get-tuple-element.88, bf16[2048,1664]{1,0:T(8,128)(2,1)} %copy-done.26), kind=kOutput, calls=%fused_computation.1 | convolution fusion | flops 13962838016 | bytes 22020096 | tf_op jit(solution)/shard_map/dot_general | solution.py:681
  428.3 0.0 reduce-scatter.5.cloned.1.call-update
  428.3 0.0 reduce-scatter.3.cloned.1.call-start
  428.4 0.5 reduce-scatter.3.cloned.1.call-update
  428.9 267.9 %sum_over_line.1 = (f32[144,128]{1,0:T(8,128)}, bf16[688,2048]{1,0:T(8,128)(2,1)}, bf16[512,2048]{1,0:T(8,128)(2,1)}, bf16[2048,1536]{1,0:T(8,128)(2,1)}, f32[48,128]{1,0:T(8,128)}) custom-call(f32[144,128]{1,0:T(8,128)} %bitcast.85, bf16[688,2048]{1,0:T(8,128)(2,1)} %copy-done.5, bf16[512,2048]{1,0:T(8,128)(2,1)} %convolution_convert_fusion.4.refs_2_, ...), custom_call_target="tpu_custom_call" | custom-call | bytes 1124352000 | tf_op jit(solution)/shard_map/sum_over_line/pallas_call | solution.py:1548
  696.8 0.7 slice.83
  697.5 0.9 fusion.13
  698.3 0.6 slice.77
  699.0 0.6 slice.79
  699.6 0.8 fusion.12
  700.4 0.6 reshape.109
  701.0 0.6 reshape.110
  701.6 0.6 reshape.111
  702.2 4.3 convert_element_type.91
  706.5 5.2 convert_element_type.92
  711.6 1.3 fusion.11
  713.0 0.6 slice_bitcast_fusion.2
  713.5 0.6 slice_bitcast_fusion
  714.1 2.3 slice_convert_fusion.2
  716.4 4.6 slice_convert_fusion
  721.0 5.9 convert_bitcast_fusion
  726.9 1.9 fusion.4
  728.9 0.0 reduce-scatter.3.cloned.1.call-done
  728.9 2.6 fusion.10
  731.6 2.0 fusion.8
  (109 shorter events, 0.3 us)
Async XLA Ops:
  7.2 4.1 copy-start.19
  7.2 4.1 copy-start.20
  7.2 4.1 copy-start.11
  7.2 4.1 copy-start.6
  7.2 146.9 %all-gather.2.cloned.1.call-start = ((), (), s32[]{:S(2)}) async-start(), calls=%async_computation.2 | async-start | bytes 9437184 | tf_op jit(solution)/shard_map/all_gather | solution.py:1609
  8.1 3.1 copy-start.32
  9.7 1.6 copy-start.34
  11.3 1.6 copy-start.7
  12.9 1.2 copy-start.12
  14.1 48.8 %copy-start.43 = (bf16[4,256]{1,0:T(4,128)(2,1)S(1)}, bf16[4,256]{1,0:T(4,128)(2,1)}, u32[]{:S(2)}) copy-start(bf16[4,256]{1,0:T(4,128)(2,1)} %param.30) | copy-start | bytes 6148
  14.1 48.8 %copy-start.44 = (bf16[4,256]{1,0:T(4,128)(2,1)S(1)}, bf16[4,256]{1,0:T(4,128)(2,1)}, u32[]{:S(2)}) copy-start(bf16[4,256]{1,0:T(4,128)(2,1)} %param.31) | copy-start | bytes 6148
  14.1 48.9 %copy-start.39 = (bf16[4,512]{1,0:T(4,128)(2,1)S(1)}, bf16[4,512]{1,0:T(4,128)(2,1)}, u32[]{:S(2)}) copy-start(bf16[4,512]{1,0:T(4,128)(2,1)} %param.32) | copy-start | bytes 12292
  14.1 48.9 %copy-start.24 = (f32[2]{0:T(128)S(1)}, f32[2]{0:T(128)}, u32[]{:S(2)}) copy-start(f32[2]{0:T(128)} %param.33) | copy-start | bytes 28
  14.1 49.0 %copy-start.25 = (f32[2]{0:T(128)S(1)}, f32[2]{0:T(128)}, u32[]{:S(2)}) copy-start(f32[2]{0:T(128)} %param.34) | copy-start | bytes 28
  14.2 49.1 %copy-start.48 = (bf16[256]{0:T(256)(128)(2,1)S(1)}, bf16[256]{0:T(256)(128)(2,1)}, u32[]{:S(2)}) copy-start(bf16[256]{0:T(256)(128)(2,1)} %param.35) | copy-start | bytes 1540
  14.2 49.1 %copy-start.40 = (bf16[2048]{0:T(1024)(128)(2,1)S(1)}, bf16[2048]{0:T(1024)(128)(2,1)}, u32[]{:S(2)}) copy-start(bf16[2048]{0:T(1024)(128)(2,1)} %param.37) | copy-start | bytes 12292
  14.2 49.1 %copy-start.15 = (f32[1,2,128,256]{3,2,1,0:T(8,128)S(1)}, f32[1,2,128,256]{3,2,1,0:T(8,128)}, u32[]{:S(2)}) copy-start(f32[1,2,128,256]{3,2,1,0:T(8,128)} %param.22) | copy-start | bytes 786436
  59.8 2.8 copy-start.26
  62.7 365.6 %all-reduce.3.cloned.1.call-start = ((), (), s32[]{:S(2)}) async-start(), calls=%async_computation.5 | async-start | bytes 11272192 | tf_op jit(solution)/shard_map/psum | solution.py:1617
  63.0 36.7 %copy-start.17 = (f32[4,256]{1,0:T(4,128)}, f32[4,256]{1,0:T(4,128)S(1)}, u32[]{:S(2)}) copy-start(f32[4,256]{1,0:T(4,128)S(1)} %convert_element_type.74.tq_ref) | copy-start | bytes 12292
  63.0 36.7 %copy-start.18 = (f32[4,256]{1,0:T(4,128)}, f32[4,256]{1,0:T(4,128)S(1)}, u32[]{:S(2)}) copy-start(f32[4,256]{1,0:T(4,128)S(1)} %convert_element_type.75.tk_ref) | copy-start | bytes 12292
  63.0 36.6 %copy-start.16 = (f32[4,512]{1,0:T(4,128)}, f32[4,512]{1,0:T(4,128)S(1)}, u32[]{:S(2)}) copy-start(f32[4,512]{1,0:T(4,128)S(1)} %convert_element_type.76.tv_ref) | copy-start | bytes 24580
  63.1 36.5 %copy-start.21 = (f32[2,1]{1,0:T(2,128)}, f32[2,1]{1,0:T(2,128)S(1)}, u32[]{:S(2)}) copy-start(f32[2,1]{1,0:T(2,128)S(1)} %copy.47.dl_col_ref) | copy-start | bytes 28
  63.2 36.4 %copy-start.22 = (f32[2,1]{1,0:T(2,128)}, f32[2,1]{1,0:T(2,128)S(1)}, u32[]{:S(2)}) copy-start(f32[2,1]{1,0:T(2,128)S(1)} %copy.48.db_col_ref) | copy-start | bytes 28
  63.3 36.4 %copy-start.23 = (f32[256]{0:T(256)}, f32[256]{0:T(256)S(1)}, u32[]{:S(2)}) copy-start(f32[256]{0:T(256)S(1)} %broadcast_in_dim.56) | copy-start | bytes 3076
  63.3 37.7 %copy-start = (bf16[1,256,2048]{2,1,0:T(8,128)(2,1)S(1)}, bf16[1,256,2048]{2,1,0:T(8,128)(2,1)}, u32[]{:S(2)}) copy-start(bf16[1,256,2048]{2,1,0:T(8,128)(2,1)} %param.21) | copy-start | bytes 3145732
  63.3 37.7 %copy-start.1 = (bf16[512,2048]{1,0:T(8,128)(2,1)S(1)}, bf16[512,2048]{1,0:T(8,128)(2,1)}, u32[]{:S(2)}) copy-start(bf16[512,2048]{1,0:T(8,128)(2,1)} %w_ref.3) | copy-start | bytes 6291460
  99.7 1.3 copy-start.10
  150.5 1.3 copy-start.2
  151.8 1.3 copy-start.8
  153.2 1.0 copy-start.13
  154.1 1.2 copy-start.14
  155.4 54.0 %slice-start = ((s8[8388608]{0:T(1024)(128)(4,1)}), s8[4194304]{0:T(1024)(128)(4,1)S(1)}, s32[]{:S(2)}) async-start(s8[8388608]{0:T(1024)(128)(4,1)} %bitcast.79), calls=%async_computation.6 | async-start | bytes 8388608
  198.0 11.4 %copy-start.4 = (bf16[688,2048]{1,0:T(8,128)(2,1)}, bf16[688,2048]{1,0:T(8,128)(2,1)S(1)}, u32[]{:S(2)}) copy-start(bf16[688,2048]{1,0:T(8,128)(2,1)S(1)} %get-tuple-element.86.inner_ref) | copy-start | bytes 8454148
  198.0 11.4 %slice-start.1 = ((s8[8388608]{0:T(1024)(128)(4,1)}), s8[4194304]{0:T(1024)(128)(4,1)S(1)}, s32[]{:S(2)}) async-start(s8[8388608]{0:T(1024)(128)(4,1)} %bitcast.79), calls=%async_computation.7 | async-start | bytes 8388608
  216.7 510.3 %reduce-scatter.5.cloned.1.call-start = ((), (), s32[]{:S(2)}) async-start(), calls=%async_computation.4 | async-start | bytes 9437184 | tf_op jit(solution)/shard_map/reduce_scatter | solution.py:1376
  310.5 1.6 copy-start.5
  370.8 20.9 %copy-start.42 = (f32[4,256]{1,0:T(4,128)S(1)}, f32[4,256]{1,0:T(4,128)}, u32[]{:S(2)}) copy-start(f32[4,256]{1,0:T(4,128)} %get-tuple-element.93) | copy-start | bytes 12292
  370.8 20.9 %copy-start.41 = (f32[4,256]{1,0:T(4,128)S(1)}, f32[4,256]{1,0:T(4,128)}, u32[]{:S(2)}) copy-start(f32[4,256]{1,0:T(4,128)} %get-tuple-element.94) | copy-start | bytes 12292
  370.9 20.9 %copy-start.38 = (f32[4,512]{1,0:T(4,128)S(1)}, f32[4,512]{1,0:T(4,128)}, u32[]{:S(2)}) copy-start(f32[4,512]{1,0:T(4,128)} %get-tuple-element.95) | copy-start | bytes 24580
  370.9 26.5 %copy-start.36 = (bf16[2048]{0:T(1024)(128)(2,1)S(1)}, bf16[2048]{0:T(1024)(128)(2,1)}, u32[]{:S(2)}) copy-start(bf16[2048]{0:T(1024)(128)(2,1)} %param.23) | copy-start | bytes 12292
  391.6 3.1 copy-start.27
  391.7 5.7 copy-start.45
  391.7 5.7 copy-start.46
  391.7 5.7 copy-start.47
  391.7 6.4 copy-start.9
  428.3 300.6 %reduce-scatter.3.cloned.1.call-start = ((), (), s32[]{:S(2)}) async-start(), calls=%async_computation.3 | async-start | bytes 9437184 | tf_op jit(solution)/shard_map/reduce_scatter | solution.py:1376
  702.2 12.0 %slice-start.2 = ((s8[6291456]{0:T(1024)(128)(4,1)}), s8[4194304]{0:T(1024)(128)(4,1)S(1)}, s32[]{:S(2)}) async-start(s8[6291456]{0:T(1024)(128)(4,1)} %bitcast.81), calls=%async_computation.8 | async-start | bytes 8388608
  706.5 6.5 copy-start.37
  706.5 7.7 %slice-start.3 = ((s8[6291456]{0:T(1024)(128)(4,1)}), s8[2097152]{0:T(1024)(128)(4,1)S(1)}, s32[]{:S(2)}) async-start(s8[6291456]{0:T(1024)(128)(4,1)} %bitcast.81), calls=%async_computation.9 | async-start | bytes 4194304
  716.4 4.6 copy-start.29
  716.4 4.6 copy-start.30
  721.0 5.9 copy-start.33
  721.0 5.9 copy-start.35
  726.9 2.0 copy-start.3
  728.9 2.7 copy-start.28
  728.9 2.6 copy-start.31
Sparse Core Ops, SparseCore 0:
  62.8 62.3 all-gather.1
  216.8 201.9 all-reduce.2
  428.4 71.9 reduce-scatter.4
  504.2 71.2 reduce-scatter.2

commit v7 on v6

--- a/solution.py
+++ b/solution.py
@@ -14,7 +14,7 @@
 EDGE = 8
 HALF = 128
 EXTRA = 128
-FORWARD_GROUP = 2
+FORWARD_GROUP = 4
 BACKWARD_GROUP = 2
 
 f32 = jnp.float32
@@ -321,7 +321,7 @@
             pltpu.VMEM((size + EDGE, vw), f32),
         ],
         compiler_params=pltpu.CompilerParams(
-            dimension_semantics=("arbitrary",), vmem_limit_bytes=48 * 1024 * 1024
+            dimension_semantics=("arbitrary",), vmem_limit_bytes=32 * 1024 * 1024
         ),
         cost_estimate=pl.CostEstimate(flops=0, bytes_accessed=100_000_000, transcendentals=0),
         name="mixer_forward",
@@ -644,7 +644,7 @@
             pltpu.VMEM((size + EDGE, vw), f32),
         ],
         compiler_params=pltpu.CompilerParams(
-            dimension_semantics=("arbitrary",), vmem_limit_bytes=56 * 1024 * 1024
+            dimension_semantics=("arbitrary",), vmem_limit_bytes=40 * 1024 * 1024
         ),
         cost_estimate=pl.CostEstimate(flops=0, bytes_accessed=100_000_000, transcendentals=0),
         name="mixer_backward",
@@ -795,7 +795,8 @@
 
 def gather_project_kernel(
     axis,
-    x_ref,
+    tokens_ref,
+    gain_ref,
     alpha_ref,
     beta_ref,
     wq_ref,
@@ -805,6 +806,7 @@
     all_ref,
     w_ref,
     y_ref,
+    normed,
     held,
     weights,
     stage,
@@ -815,14 +817,17 @@
     load,
     out,
 ):
-    rows = x_ref.shape[0]
-    ready, finish, _ = gather_parts(axis, x_ref, held, send, recv, local)
+    rows = tokens_ref.shape[0]
     loads, at = [], 0
     for i, ref in enumerate((wq_ref, wk_ref, wv_ref, wg_ref)):
         width = ref.shape[1]
         loads.append(pltpu.make_async_copy(ref, weights.at[:, pl.ds(at, width)], load.at[i]))
         loads[-1].start()
         at += width
+    tokens = tokens_ref[...].astype(f32)
+    factor = lax.rsqrt(jnp.mean(tokens * tokens, -1, keepdims=True) + norm_eps)
+    normed[...] = (tokens * factor * gain_ref[...]).astype(bf16)
+    ready, finish, _ = gather_parts(axis, normed, held, send, recv, local)
     main = at
     heads, depth = alpha_ref.shape
     thin = jnp.concatenate(
@@ -876,15 +881,17 @@
 IN_VMEM = pl.BlockSpec(memory_space=pltpu.VMEM)
 
 
-def gather_project(x, w_query, w_key, w_value, w_gate_out, w_alpha, w_beta, identity, sizes):
+def gather_project(tokens, gain, w_query, w_key, w_value, w_gate_out, w_alpha, w_beta, identity, sizes):
     heads = w_alpha.shape[1]
-    rows, depth = x.shape
+    rows, depth = tokens.shape
     mains = (w_query, w_key, w_value, w_gate_out)
     width = sum(w.shape[1] for w in mains) + EXTRA
     if not square(sizes):
         padding = jnp.zeros((depth, EXTRA - 2 * heads), bf16)
         w_in = jnp.concatenate(mains + (w_alpha, w_beta, padding), axis=1)
-        gathered = lax.all_gather(x, "tensor", axis=0, tiled=True)
+        inputs = tokens.astype(f32)
+        normed = (inputs * rms_factor(inputs) * gain).astype(bf16)
+        gathered = lax.all_gather(normed, "tensor", axis=0, tiled=True)
         return gathered, w_in, jnp.dot(gathered, w_in, preferred_element_type=f32)
     return pl.pallas_call(
         functools.partial(gather_project_kernel, "tensor"),
@@ -893,9 +900,10 @@
             jax.ShapeDtypeStruct((depth, width), bf16),
             jax.ShapeDtypeStruct((8 * rows, width), f32),
         ),
-        in_specs=[ANYWHERE, IN_VMEM, IN_VMEM] + [ANYWHERE] * 4,
+        in_specs=[IN_VMEM] * 4 + [ANYWHERE] * 4,
         out_specs=(ANYWHERE,) * 3,
         scratch_shapes=[
+            pltpu.VMEM((rows, depth), bf16),
             pltpu.VMEM((8 * rows, depth), bf16),
             pltpu.VMEM((depth, width), bf16),
             pltpu.VMEM((2, rows, width), f32),
@@ -903,11 +911,11 @@
         + gather_scratch(rows, depth)
         + [pltpu.SemaphoreType.DMA((5,)), pltpu.SemaphoreType.DMA((8,))],
         compiler_params=pltpu.CompilerParams(
-            collective_id=identity, has_side_effects=True, vmem_limit_bytes=40 * 1024 * 1024
+            collective_id=identity, has_side_effects=True, vmem_limit_bytes=26 * 1024 * 1024
         ),
         cost_estimate=pl.CostEstimate(flops=0, bytes_accessed=1_000_000, transcendentals=0),
         name="gather_project",
-    )(x, w_alpha.T, w_beta.T, *mains)
+    )(tokens, gain[None, :], w_alpha.T, w_beta.T, *mains)
 
 
 def gather_expand_kernel(
@@ -1027,7 +1035,7 @@
         + gather_scratch(rows, depth)
         + [pltpu.SemaphoreType.DMA((3,)), pltpu.SemaphoreType.DMA((8,)), pltpu.SemaphoreType.DMA((3, 8))],
         compiler_params=pltpu.CompilerParams(
-            collective_id=identity, has_side_effects=True, vmem_limit_bytes=48 * 1024 * 1024
+            collective_id=identity, has_side_effects=True, vmem_limit_bytes=36 * 1024 * 1024
         ),
         cost_estimate=pl.CostEstimate(flops=0, bytes_accessed=1_000_000, transcendentals=0),
         name="gather_expand",
@@ -1165,7 +1173,7 @@
         + gather_scratch(rows, depth)
         + [pltpu.SemaphoreType.DMA((4,)), pltpu.SemaphoreType.DMA((8,)), pltpu.SemaphoreType.DMA((3, 8))],
         compiler_params=pltpu.CompilerParams(
-            collective_id=identity, has_side_effects=True, vmem_limit_bytes=48 * 1024 * 1024
+            collective_id=identity, has_side_effects=True, vmem_limit_bytes=34 * 1024 * 1024
         ),
         cost_estimate=pl.CostEstimate(flops=0, bytes_accessed=1_000_000, transcendentals=0),
         name="gather_back",
@@ -1291,7 +1299,7 @@
         out_specs=(IN_VMEM,) * 2,
         scratch_shapes=scatter_scratch(rows, width),
         compiler_params=pltpu.CompilerParams(
-            collective_id=identity, has_side_effects=True, vmem_limit_bytes=40 * 1024 * 1024
+            collective_id=identity, has_side_effects=True, vmem_limit_bytes=28 * 1024 * 1024
         ),
         cost_estimate=pl.CostEstimate(flops=0, bytes_accessed=1_000_000, transcendentals=0),
         name="attend",
@@ -1364,7 +1372,7 @@
         out_specs=(IN_VMEM,) * 3,
         scratch_shapes=[pltpu.VMEM((2, rows, dgate.shape[0]), bf16)] + scatter_scratch(rows, width),
         compiler_params=pltpu.CompilerParams(
-            collective_id=identity, has_side_effects=True, vmem_limit_bytes=52 * 1024 * 1024
+            collective_id=identity, has_side_effects=True, vmem_limit_bytes=44 * 1024 * 1024
         ),
         cost_estimate=pl.CostEstimate(flops=0, bytes_accessed=1_000_000, transcendentals=0),
         name="return_hidden",
@@ -1591,9 +1599,8 @@
     scaled_attn = inputs * factor_attn
     gain_first = gain_attn.astype(f32)
     gain_second = gain_ffn.astype(f32)
-    normed = (scaled_attn * gain_first).astype(bf16)
     gathered, w_in, projected = gather_project(
-        normed, w_query, w_key, w_value, w_gate_out, w_alpha, w_beta, 0, sizes
+        tokens[0], gain_first, w_query, w_key, w_value, w_gate_out, w_alpha, w_beta, 0, sizes
     )
     main = w_in.shape[1] - EXTRA
     extras = (
@@ -1631,11 +1638,15 @@
     part_normed = times_transposed(grad_projected, w_in).astype(bf16)
     grad_in = cross_rows(gathered, grad_projected).astype(bf16)
     part_gain_attn = jnp.sum(grad_in.astype(f32) * w_in.astype(f32), 1) / gain_first
+    def in_rows(*parts):
+        joined = jnp.concatenate(parts, axis=1)
+        return jnp.pad(joined, ((0, 0), (0, width - joined.shape[1])))
+
     grad_ab = grad_in[:, main : main + 2 * heads].astype(f32).T
-    smalls = (part_gain_attn, part_gain_ffn, grad_gain[0], grad_tq, grad_tk, grad_tv, grad_dl[0], grad_db[0], grad_ab)
-    used = sum(a.size for a in smalls)
-    smalls_rows = -(-used // (16 * 128)) * 16
-    small = jnp.concatenate([a.reshape(-1) for a in smalls] + [jnp.zeros((smalls_rows * 128 - used,), f32)])
+    rows = [part_gain_attn[None], part_gain_ffn[None], in_rows(grad_gain), in_rows(grad_dl, grad_db)]
+    rows += [jnp.zeros((4, width), f32), in_rows(grad_tq, grad_tk, grad_tv), grad_ab]
+    used = sum(a.shape[0] for a in rows)
+    small = jnp.concatenate(rows + [jnp.zeros((-used % 8, width), f32)], axis=0)
     (
         grad_in,
         grad_up_weight,
@@ -1660,45 +1671,39 @@
     grad_normed = scatter_rows(part_normed)
     ffn_out = scatter_rows(ffn_part)
     output = (hidden + ffn_out).astype(bf16)
-    gains = 2 * width + out_gain.shape[0]
     small_summed, grad_up_summed, grad_out_summed, grad_in_summed, gain_grads = sum_over_line(
-        (small.reshape(smalls_rows, 128), grad_up_weight, grad_out_weight, grad_in),
-        (128, width, width, main),
-        -(-gains // (16 * 128)) * 16,
-        5,
-        sizes,
-    )
-    small_summed = small_summed.reshape(-1)
-    gain_grads = gain_grads.reshape(-1)
-    small_parts, at = [], gains
-    for a in smalls[3:]:
-        small_parts.append(small_summed[at : at + a.size].reshape(a.shape))
-        at += a.size
+        (small, grad_up_weight, grad_out_weight, grad_in), (width, width, width, main), 8, 5, sizes
+    )
+    taps = grad_tq.shape[0]
+    conv_grads, at = [], 0
+    for a in (grad_tq, grad_tk, grad_tv):
+        conv_grads.append(small_summed[8 : 8 + taps, at : at + a.shape[1]])
+        at += a.shape[1]
+    grad_ab = small_summed[8 + taps : 8 + taps + 2 * heads]
     grad_inputs = grad_hidden + norm_backward(grad_normed, scaled_attn, factor_attn, gain_first)
     pieces, at = [], 0
     for w in (w_query, w_key, w_value, w_gate_out):
         pieces.append(grad_in_summed[:, at : at + w.shape[1]].astype(f32))
         at += w.shape[1]
-    grad_ab = small_parts[5]
     return (
         output[None],
         final[None],
         grad_inputs[None],
-        gain_grads[:width],
+        gain_grads[0],
         pieces[0],
         pieces[1],
         pieces[2],
         grad_ab[:heads].T,
         grad_ab[heads:].T,
         pieces[3],
-        small_parts[0],
-        small_parts[1],
-        small_parts[2],
-        small_parts[3],
-        small_parts[4],
-        gain_grads[2 * width : gains],
+        conv_grads[0],
+        conv_grads[1],
+        conv_grads[2],
+        small_summed[3, :heads],
+        small_summed[3, heads : 2 * heads],
+        gain_grads[2, : out_gain.shape[0]],
         grad_out_summed.astype(f32),
-        gain_grads[width : 2 * width],
+        gain_grads[1],
         grad_gate_summed.astype(f32).T,
         grad_up_summed.astype(f32).T,
         grad_down_summed.astype(f32),

time: 747 us -> 773 us (1.035)
  local copies, waits for them, and re-layouts: 26.8 us -> 59.6 us
    unnamed x110 -> x122, local copies, waits for them, and re-layouts: 16.5 us -> 48.2 us
  transfers between devices with their start and end apart: 4 -> 4, of which waited for: 0 -> 0; matrix products, arithmetic and copies ran while one was open for 12% -> 11% of each run, Pallas kernels for 68% -> 65%
where the time goes in v7:
time: 773 us; the launch traced here: 766 us
  Pallas kernels  588 us (76%)
  matrix products  72.6 us (9%)
  local copies, waits for them, and re-layouts  59.6 us (8%)
  other arithmetic  30.2 us (4%)
  between operations  14.4 us (2%)
    pallas_call x1, Pallas kernels, sum_over_line(): pl.pallas_call(functools.partial(line_kernel, 'dp', 'tensor', tuple(width...  269 us
    pallas_call x1, Pallas kernels, mixer_backward(): pl.pallas_call(functools.partial(backward_kernel, heads, key_dim, value_d...  58.6 us
    pallas_call x1, Pallas kernels, return_hidden(): pl.pallas_call(functools.partial(return_kernel, 'tensor'), out_shape=(jax...  50 us
    unnamed x122, local copies, waits for them, and re-layouts  48.2 us
    pallas_call x1, Pallas kernels, attend(): pl.pallas_call(functools.partial(attend_kernel, 'tensor'), out_shape=(jax...  46.9 us
    pallas_call x1, Pallas kernels, gather_project(): pl.pallas_call(functools.partial(gather_project_kernel, 'tensor'), out_sh...  46.8 us
    pallas_call x1, Pallas kernels, gather_expand(): pl.pallas_call(functools.partial(gather_expand_kernel, 'tensor'), out_sha...  41.8 us
    pallas_call x1, Pallas kernels, gather_back(): pl.pallas_call(functools.partial(gather_back_kernel, 'tensor'), out_shape...  41.6 us
  transfers between devices with their start and end apart: 4, of which 0 were waited for; matrix products, arithmetic and copies ran while one was open for 11% of the time, Pallas kernels for 65%

profile of v7, /device:TPU:0, one launch (start us, length us, event | category | flops | bytes accessed | tf_op | source)
XLA Modules:
  0.0 765.7 jit_solution(8372782062364646908)
XLA Ops:
  7.2 0.7 convert_element_type.74
  7.9 1.2 copy-done
  9.2 1.6 copy-done.28
  10.8 1.6 copy-done.29
  12.3 1.2 copy-done.34
  13.6 1.2 copy-done.35
  14.8 0.7 copy-done.39
  15.5 0.7 copy-done.40
  16.2 46.8 %gather_project.1 = (bf16[2048,2048]{1,0:T(8,128)(2,1)S(1)}, bf16[2048,1664]{1,0:T(8,128)(2,1)S(1)}, f32[2048,1664]{1,0:T(8,128)}) custom-call(bf16[256,2048]{1,0:T(8,128)(2,1)S(1)} %bitcast.50, f32[1,2048]{1,0:T(1,128)S(1)} %bitcast.59, bf16[2,2048]{1,0:T(2,128)(2,1)S(1)} %bitcast.62, bf16[2,2048]{1,0:T(2,128)(2,1)S(1)} %bitcast.63, ...), custom_call_target="tpu_custom_call" | custom-call | bytes 1000000 | tf_op jit(solution)/shard_map/gather_project/pallas_call | solution.py:896
  63.1 3.3 copy-done.43
  66.4 2.8 copy-done.44
  69.4 0.1 copy.69.dl_col_ref
  69.5 0.1 copy.70.db_col_ref
  69.7 33.2 %mixer_forward.1 = (bf16[2048,512]{1,0:T(8,128)(2,1)S(1)}, f32[2,128,256]{2,1,0:T(8,128)}, f32[8,2,128,256]{3,2,1,0:T(8,128)S(1)}, f32[8,2,256,256]{3,2,1,0:T(8,...) custom-call(f32[2048,1664]{1,0:T(8,128)} %get-tuple-element.68.proj_ref.eq_ref.ek_ref.ev_ref, ...), custom_call_target="tpu_custom_call" | custom-call | bytes 100000000 | tf_op jit(solution)/shard_map/mixer_forward/pallas_call | solution.py:286
  102.8 2.0 copy-done.13
  104.8 2.0 copy-done.15
  106.9 2.0 copy-done.17
  108.9 1.3 copy-done.30
  110.2 46.9 %attend.1 = (f32[256,2048]{1,0:T(8,128)S(1)}, bf16[256,2048]{1,0:T(8,128)(2,1)S(1)}) custom-call(bf16[2048,512]{1,0:T(8,128)(2,1)S(1)} %get-tuple-element.69.mixed_ref, bf16[512,2048]{1,0:T(8,128)(2,1)S(1)} %copy-done.8, bf16[256,2048]{1,0:T(8,128)(2,1)S(1)} %bitcast.51, f32[1,2048]{1,0:T(1,128)S(1)} %bitcast.60), custom_call_target="tpu_custom_call" | custom-call | bytes 1000000 | tf_op jit(solution)/shard_map/attend/pallas_call | solution.py:1295
  157.1 1.3 copy-done.9
  158.4 1.3 copy-done.26
  159.8 1.0 copy-done.32
  160.7 1.8 copy-done.2
  162.5 1.8 copy-done.6
  164.3 1.8 copy-done.7
  166.1 1.2 copy-done.33
  167.3 41.8 %gather_expand.1 = (bf16[2048,2048]{1,0:T(8,128)(2,1)}, bf16[688,2048]{1,0:T(8,128)(2,1)S(1)}, bf16[688,2048]{1,0:T(8,128)(2,1)S(1)}, bf16[688,2048]{1,0:T(8,128)(2,1)S(1)}) custom-call(bf16[256,2048]{1,0:T(8,128)(2,1)S(1)} %copy-done.33, bf16[2048,2048]{1,0:T(8,128)(2,1)} %all-gather.2.cloned.1.call-done.cot_ref, bf16[688,2048]{1,0:T(8,128)(2,1)S(1)} %bitcast.53, ...), custom_call_target="tpu_custom_call" | custom-call | bytes 1000000 | tf_op jit(solution)/shard_map/gather_expand/pallas_call | solution.py:1019
  209.2 13.6 %convolution_convert_fusion.2 = bf16[688,2048]{1,0:T(8,128)(2,1)} fusion(bf16[688,2048]{1,0:T(8,128)(2,1)S(1)} %get-tuple-element.83.dgate_ref, bf16[2048,2048]{1,0:T(8,128)(2,1)} %get-tuple-element.82.normed_ref), kind=kOutput, calls=%fused_computation.5 | convolution fusion | flops 5772771328 | bytes 14024704 | tf_op jit(solution)/shard_map/dot_general | solution.py:1623
  222.8 7.3 convolution_convert_fusion.3
  230.2 1.6 copy-done.10
  231.8 1.2 copy-done.12
  233.0 1.8 copy-done.23
  234.8 50.0 %return_hidden.1 = (f32[256,2048]{1,0:T(8,128)S(1)}, bf16[256,2048]{1,0:T(8,128)(2,1)S(1)}, f32[1,2048]{1,0:T(1,128)S(1)}) custom-call(bf16[688,2048]{1,0:T(8,128)(2,1)S(1)} %copy-done.23, bf16[688,2048]{1,0:T(8,128)(2,1)} %copy-done.4, bf16[688,2048]{1,0:T(8,128)(2,1)} %bitcast.52, bf16[688,2048]{1,0:T(8,128)(2,1)} %bitcast.54, f32[256,2048]{1,0:T(8,128)S(1)} %copy-done.10, ...), custom_call_target="tpu_custom_call" | custom-call | bytes 1000000 | tf_op jit(solution)/shard_map/return_hidden/pallas_call | solution.py:1364
  284.8 1.3 copy-done.24
  286.2 1.8 copy-done.20
  288.0 41.6 %gather_back.1 = (bf16[2048,2048]{1,0:T(8,128)(2,1)}, f32[2048,512]{1,0:T(8,128)S(1)}, bf16[2048,2048]{1,0:T(8,128)(2,1)}, bf16[688,2048]{1,0:T(8,128)(2,1)S(1)}) custom-call(bf16[256,2048]{1,0:T(8,128)(2,1)S(1)} %get-tuple-element.85.x_ref, bf16[512,2048]{1,0:T(8,128)(2,1)S(1)} %copy-done.8, bf16[688,2048]{1,0:T(8,128)(2,1)S(1)} %copy-done.20, ...), custom_call_target="tpu_custom_call" | custom-call | bytes 1000000 | tf_op jit(solution)/shard_map/gather_back/pallas_call | solution.py:1152
  329.7 2.0 copy-done.18
  331.7 1.6 copy-done.21
  333.2 2.2 copy-done.14
  335.4 2.6 copy-done.16
  338.0 58.6 %mixer_backward.1 = (bf16[2048,1664]{1,0:T(8,128)(2,1)}, f32[4,256]{1,0:T(4,128)S(1)}, f32[4,256]{1,0:T(4,128)S(1)}, f32[4,512]{1,0:T(4,128)S(1)}, f32[1,2]{1,0:...) custom-call(f32[2048,1664]{1,0:T(8,128)} %get-tuple-element.68.proj_ref.eq_ref.ek_ref.ev_ref, ...), custom_call_target="tpu_custom_call" | custom-call | bytes 100000000 | tf_op jit(solution)/shard_map/mixer_backward/pallas_call | solution.py:597
  396.7 21.5 %multiply_reduce_fusion = (f32[2048]{0:T(1024)S(1)}, bf16[2048,1664]{1,0:T(8,128)(2,1)}) fusion(bf16[2048,1664]{1,0:T(8,128)(2,1)} %copy-done.44, bf16[2048,2048]{1,0:T(8,128)(2,1)S(1)} %bitcast.73, bf16[2048,1664]{1,0:T(8,128)(2,1)} %get-tuple-element.88), kind=kOutput, calls=%fused_computation | convolution fusion | flops 13975681024 | bytes 28844032 | tf_op jit(solution)/shard_map/dot_general | solution.py:677
  418.2 2.2 convert_bitcast_fusion.2
  420.4 1.6 copy.74
  422.1 1.3 concatenate.11.refs_0_
  423.4 9.1 %convolution_convert_fusion.4.refs_2_ = bf16[512,2048]{1,0:T(8,128)(2,1)} fusion(bf16[2048,512]{1,0:T(8,128)(2,1)S(1)} %copy-done.27, bf16[2048,2048]{1,0:T(8,128)(2,1)} %get-tuple-element.99), kind=kOutput, calls=%fused_computation.7 | convolution fusion | flops 4296015872 | bytes 12582912 | tf_op jit(solution)/shard_map/dot_general | solution.py:677
  432.5 21.1 %convolution_convert_fusion = bf16[2048,2048]{1,0:T(8,128)(2,1)} fusion(bf16[2048,1664]{1,0:T(8,128)(2,1)} %get-tuple-element.88, bf16[2048,1664]{1,0:T(8,128)(2,1)} %copy-done.44), kind=kOutput, calls=%fused_computation.1 | convolution fusion | flops 13962838016 | bytes 22020096 | tf_op jit(solution)/shard_map/dot_general | solution.py:681
  453.7 0.5 reduce-scatter.3.cloned.1.call-update
  454.2 0.3 fusion.7
  454.5 269.2 %sum_over_line.1 = (f32[16,2048]{1,0:T(8,128)}, bf16[688,2048]{1,0:T(8,128)(2,1)}, bf16[512,2048]{1,0:T(8,128)(2,1)}, bf16[2048,1536]{1,0:T(8,128)(2,1)}, f32[8,2048]{1,0:T(8,128)}) custom-call(f32[16,2048]{1,0:T(8,128)} %concatenate.11.refs_0_, bf16[688,2048]{1,0:T(8,128)(2,1)} %copy-done.21, bf16[512,2048]{1,0:T(8,128)(2,1)} %convolution_convert_fusion.4.refs_2_, ...), custom_call_target="tpu_custom_call" | custom-call | bytes 1127219200 | tf_op jit(solution)/shard_map/sum_over_line/pallas_call | solution.py:1556
  723.8 1.3 slice.58
  725.1 1.3 slice.61
  726.4 4.3 convert_element_type.93
  730.6 3.2 convert_element_type.94
  733.9 1.3 slice_bitcast_fusion.2
  735.2 1.3 fusion.10
  736.5 1.5 fusion.11
  738.1 1.5 slice_bitcast_fusion
  739.6 2.3 slice_convert_fusion.2
  741.9 4.6 slice_convert_fusion
  746.5 5.9 convert_bitcast_fusion
  752.4 1.9 fusion.2
  754.4 2.7 fusion.8
  757.1 2.0 fusion.6
  (119 shorter events, 0.6 us)
Async XLA Ops:
  7.2 153.5 %all-gather.2.cloned.1.call-start = ((), (), s32[]{:S(2)}) async-start(), calls=%async_computation.2 | async-start | bytes 9437184 | tf_op jit(solution)/shard_map/all_gather | solution.py:1616
  7.9 55.2 %copy-start.37 = (f32[2048]{0:T(1024)}, f32[2048]{0:T(1024)S(1)}, u32[]{:S(2)}) copy-start(f32[2048]{0:T(1024)S(1)} %convert_element_type.74) | copy-start | bytes 24580
  7.9 1.2 copy-start
  9.2 1.6 copy-start.28
  10.8 1.6 copy-start.29
  12.3 1.2 copy-start.34
  13.6 1.2 copy-start.35
  14.8 0.7 copy-start.39
  16.2 53.2 %copy-start.52 = (bf16[4,256]{1,0:T(4,128)(2,1)S(1)}, bf16[4,256]{1,0:T(4,128)(2,1)}, u32[]{:S(2)}) copy-start(bf16[4,256]{1,0:T(4,128)(2,1)} %param.30) | copy-start | bytes 6148
  16.2 53.2 %copy-start.53 = (bf16[4,256]{1,0:T(4,128)(2,1)S(1)}, bf16[4,256]{1,0:T(4,128)(2,1)}, u32[]{:S(2)}) copy-start(bf16[4,256]{1,0:T(4,128)(2,1)} %param.31) | copy-start | bytes 6148
  16.2 53.2 %copy-start.50 = (bf16[4,512]{1,0:T(4,128)(2,1)S(1)}, bf16[4,512]{1,0:T(4,128)(2,1)}, u32[]{:S(2)}) copy-start(bf16[4,512]{1,0:T(4,128)(2,1)} %param.32) | copy-start | bytes 12292
  16.2 53.2 %copy-start.41 = (f32[2]{0:T(128)S(1)}, f32[2]{0:T(128)}, u32[]{:S(2)}) copy-start(f32[2]{0:T(128)} %param.33) | copy-start | bytes 28
  16.2 53.3 %copy-start.42 = (f32[2]{0:T(128)S(1)}, f32[2]{0:T(128)}, u32[]{:S(2)}) copy-start(f32[2]{0:T(128)} %param.34) | copy-start | bytes 28
  16.2 53.4 %copy-start.54 = (bf16[256]{0:T(256)(128)(2,1)S(1)}, bf16[256]{0:T(256)(128)(2,1)}, u32[]{:S(2)}) copy-start(bf16[256]{0:T(256)(128)(2,1)} %param.35) | copy-start | bytes 1540
  16.2 53.4 %copy-start.51 = (bf16[2048]{0:T(1024)(128)(2,1)S(1)}, bf16[2048]{0:T(1024)(128)(2,1)}, u32[]{:S(2)}) copy-start(bf16[2048]{0:T(1024)(128)(2,1)} %param.37) | copy-start | bytes 12292
  16.2 53.4 %copy-start.36 = (f32[1,2,128,256]{3,2,1,0:T(8,128)S(1)}, f32[1,2,128,256]{3,2,1,0:T(8,128)}, u32[]{:S(2)}) copy-start(f32[1,2,128,256]{3,2,1,0:T(8,128)} %param.22) | copy-start | bytes 786436
  63.1 3.3 copy-start.43
  66.4 2.8 copy-start.44
  69.3 384.3 %all-reduce.6.cloned.1.call-start = ((), (), s32[]{:S(2)}) async-start(), calls=%async_computation.5 | async-start | bytes 11272192 | tf_op jit(solution)/shard_map/psum | solution.py:1624
  69.6 40.6 %copy-start.1 = (bf16[1,256,2048]{2,1,0:T(8,128)(2,1)S(1)}, bf16[1,256,2048]{2,1,0:T(8,128)(2,1)}, u32[]{:S(2)}) copy-start(bf16[1,256,2048]{2,1,0:T(8,128)(2,1)} %param.21) | copy-start | bytes 3145732
  69.7 40.5 %copy-start.8 = (bf16[512,2048]{1,0:T(8,128)(2,1)S(1)}, bf16[512,2048]{1,0:T(8,128)(2,1)}, u32[]{:S(2)}) copy-start(bf16[512,2048]{1,0:T(8,128)(2,1)} %w_ref.3) | copy-start | bytes 6291460
  102.8 2.0 copy-start.13
  104.8 2.0 copy-start.15
  106.9 2.0 copy-start.17
  108.9 1.3 copy-start.30
  157.1 1.3 copy-start.9
  158.4 1.3 copy-start.26
  159.8 1.0 copy-start.32
  160.7 1.8 copy-start.2
  162.5 1.8 copy-start.6
  164.3 1.8 copy-start.7
  166.1 1.2 copy-start.33
  167.3 55.5 %slice-start.2 = ((s8[8388608]{0:T(1024)(128)(4,1)}), s8[4194304]{0:T(1024)(128)(4,1)S(1)}, s32[]{:S(2)}) async-start(s8[8388608]{0:T(1024)(128)(4,1)} %bitcast.74), calls=%async_computation.8 | async-start | bytes 8388608
  209.1 13.7 %copy-start.4 = (bf16[688,2048]{1,0:T(8,128)(2,1)}, bf16[688,2048]{1,0:T(8,128)(2,1)S(1)}, u32[]{:S(2)}) copy-start(bf16[688,2048]{1,0:T(8,128)(2,1)S(1)} %get-tuple-element.84.dup_ref) | copy-start | bytes 8454148
  209.1 13.7 %copy-start.22 = (bf16[688,2048]{1,0:T(8,128)(2,1)}, bf16[688,2048]{1,0:T(8,128)(2,1)S(1)}, u32[]{:S(2)}) copy-start(bf16[688,2048]{1,0:T(8,128)(2,1)S(1)} %get-tuple-element.83.dgate_ref) | copy-start | bytes 8454148
  209.1 13.7 %copy-start.19 = (bf16[688,2048]{1,0:T(8,128)(2,1)}, bf16[688,2048]{1,0:T(8,128)(2,1)S(1)}, u32[]{:S(2)}) copy-start(bf16[688,2048]{1,0:T(8,128)(2,1)S(1)} %get-tuple-element.86.inner_ref) | copy-start | bytes 8454148
  209.1 13.7 %slice-start.3 = ((s8[8388608]{0:T(1024)(128)(4,1)}), s8[4194304]{0:T(1024)(128)(4,1)S(1)}, s32[]{:S(2)}) async-start(s8[8388608]{0:T(1024)(128)(4,1)} %bitcast.74), calls=%async_computation.9 | async-start | bytes 8388608
  230.2 522.2 %reduce-scatter.5.cloned.1.call-start = ((), (), s32[]{:S(2)}) async-start(), calls=%async_computation.4 | async-start | bytes 9437184 | tf_op jit(solution)/shard_map/reduce_scatter | solution.py:1384
  230.2 1.6 copy-start.10
  231.8 1.2 copy-start.12
  233.0 1.8 copy-start.23
  234.8 51.4 %copy-start.3 = (bf16[688,2048]{1,0:T(8,128)(2,1)S(1)}, bf16[688,2048]{1,0:T(8,128)(2,1)}, u32[]{:S(2)}) copy-start(bf16[688,2048]{1,0:T(8,128)(2,1)} %down_ref.1) | copy-start | bytes 8454148
  234.8 51.4 %copy-start.5 = (bf16[688,2048]{1,0:T(8,128)(2,1)S(1)}, bf16[688,2048]{1,0:T(8,128)(2,1)}, u32[]{:S(2)}) copy-start(bf16[688,2048]{1,0:T(8,128)(2,1)} %copy-done.4) | copy-start | bytes 8454148
  284.8 1.4 copy-start.24
  286.2 1.8 copy-start.20
  288.0 45.2 %copy-start.31 = (f32[8,2,128,256]{3,2,1,0:T(8,128)S(1)}, f32[8,2,128,256]{3,2,1,0:T(8,128)}, u32[]{:S(2)}) copy-start(f32[8,2,128,256]{3,2,1,0:T(8,128)} %copy-done.30) | copy-start | bytes 6291460
  288.0 108.6 %slice-start = ((s8[8388608]{0:T(1024)(128)(4,1)}), s8[4194304]{0:T(1024)(128)(4,1)S(1)}, s32[]{:S(2)}) async-start(s8[8388608]{0:T(1024)(128)(4,1)} %bitcast.72), calls=%async_computation.6 | async-start | bytes 8388608
  329.6 2.0 copy-start.18
  331.7 1.6 copy-start.21
  333.2 2.2 copy-start.14
  335.4 2.6 copy-start.16
  338.0 58.6 %slice-start.1 = ((s8[8388608]{0:T(1024)(128)(4,1)}), s8[4194304]{0:T(1024)(128)(4,1)S(1)}, s32[]{:S(2)}) async-start(s8[8388608]{0:T(1024)(128)(4,1)} %bitcast.72), calls=%async_computation.7 | async-start | bytes 8388608
  396.7 25.4 %copy-start.49 = (bf16[2048]{0:T(1024)(128)(2,1)S(1)}, bf16[2048]{0:T(1024)(128)(2,1)}, u32[]{:S(2)}) copy-start(bf16[2048]{0:T(1024)(128)(2,1)} %param.23) | copy-start | bytes 12292
  418.2 5.3 copy-start.27
  453.7 300.7 %reduce-scatter.3.cloned.1.call-start = ((), (), s32[]{:S(2)}) async-start(), calls=%async_computation.3 | async-start | bytes 9437184 | tf_op jit(solution)/shard_map/reduce_scatter | solution.py:1384
  454.5 276.1 %copy-start.46 = (bf16[688,2048]{1,0:T(8,128)(2,1)S(1)}, bf16[688,2048]{1,0:T(8,128)(2,1)}, u32[]{:S(2)}) copy-start(bf16[688,2048]{1,0:T(8,128)(2,1)} %get-tuple-element.114) | copy-start | bytes 8454148
  726.4 13.2 %slice-start.4 = ((s8[6291456]{0:T(1024)(128)(4,1)}), s8[4194304]{0:T(1024)(128)(4,1)S(1)}, s32[]{:S(2)}) async-start(s8[6291456]{0:T(1024)(128)(4,1)} %bitcast.76), calls=%async_computation.10 | async-start | bytes 8388608
  730.6 9.0 %slice-start.5 = ((s8[6291456]{0:T(1024)(128)(4,1)}), s8[2097152]{0:T(1024)(128)(4,1)S(1)}, s32[]{:S(2)}) async-start(s8[6291456]{0:T(1024)(128)(4,1)} %bitcast.76), calls=%async_computation.11 | async-start | bytes 4194304
  741.9 4.6 copy-start.47
  741.9 4.6 copy-start.48
  746.5 5.9 copy-start.38
  752.4 2.0 copy-start.11
  754.3 2.7 copy-start.25
  754.4 2.7 copy-start.45
  (1 other events, 0.7 us)
Sparse Core Ops, SparseCore 0:
  69.4 59.7 all-gather.1
  230.3 201.9 all-reduce.5
  453.8 71.9 reduce-scatter.4
  529.5 71.2 reduce-scatter.2

commit v8 on v6

--- a/solution.py
+++ b/solution.py
@@ -14,7 +14,7 @@
 EDGE = 8
 HALF = 128
 EXTRA = 128
-FORWARD_GROUP = 2
+FORWARD_GROUP = 4
 BACKWARD_GROUP = 2
 
 f32 = jnp.float32
@@ -51,8 +51,8 @@
 
 
 def wide(dot, left, right):
-    left_high, left_low = split(left)
-    right_high, right_low = split(right)
+    left_high, left_low = left if isinstance(left, tuple) else split(left)
+    right_high, right_low = right if isinstance(right, tuple) else split(right)
     return dot(left_high, right_high) + dot(left_low, right_high) + dot(left_high, right_low)
 
 
@@ -218,8 +218,9 @@
     qs = [q * (lax.rsqrt(jnp.sum(q * q, -1, keepdims=True) + unit_eps) * key_dim**-0.5) for q in qs]
     ks = [cut(act_k, u, key_dim) for u in units]
     ks = [k * lax.rsqrt(jnp.sum(k * k, -1, keepdims=True) + unit_eps) for k in ks]
-    grams = [wide(dot_nt, k, k) for k in ks]
-    attends = [wide(dot_nt, q, k) for q, k in zip(qs, ks)]
+    ks2, qs2 = [split(k) for k in ks], [split(q) for q in qs]
+    grams = [wide(dot_nt, k, k) for k in ks2]
+    attends = [wide(dot_nt, q, k) for q, k in zip(qs2, ks2)]
     betas = [parts[g][4][:, h : h + 1] for g, h in units]
     cums = [parts[g][2][:, h : h + 1] for g, h in units]
     cum_rows = [parts[g][3][h : h + 1, :] for g, h in units]
@@ -236,17 +237,19 @@
     for g in range(size // block):
         mine = [i for i, u in enumerate(units) if u[0] == g]
         states = [state[h] for h in range(heads)]
-        seen = [wide(dot_nn, ks[i], x) for i, x in zip(mine, states)]
+        states2 = [split(x) for x in states]
+        seen = [wide(dot_nn, ks2[i], x) for i, x in zip(mine, states2)]
         rhs = [
             betas[i] * (cut(values, units[i], value_dim) - growths[i] * x)
             for i, x in zip(mine, seen)
         ]
         updates = [wide(dot_nn, inverses[i], x) for i, x in zip(mine, rhs)]
-        news = [wide(dot_tn, tails[i], x) for i, x in zip(mine, updates)]
+        updates2 = [split(x) for x in updates]
+        news = [wide(dot_tn, tails[i], x) for i, x in zip(mine, updates2)]
         for h, i in enumerate(mine):
             state[h] = jnp.exp(lasts[i]) * states[h] + news[h]
-        reads = [wide(dot_nn, qs[i], x) for i, x in zip(mine, states)]
-        spreads = [wide(dot_nn, attends[i], x) for i, x in zip(mine, updates)]
+        reads = [wide(dot_nn, qs2[i], x) for i, x in zip(mine, states2)]
+        spreads = [wide(dot_nn, attends[i], x) for i, x in zip(mine, updates2)]
         outs += [growths[i] * x + y for i, x, y in zip(mine, reads, spreads)]
         for h, i in enumerate(mine):
             at = (slice(g * block, (g + 1) * block), slice(h * value_dim, (h + 1) * value_dim))
@@ -321,7 +324,7 @@
             pltpu.VMEM((size + EDGE, vw), f32),
         ],
         compiler_params=pltpu.CompilerParams(
-            dimension_semantics=("arbitrary",), vmem_limit_bytes=48 * 1024 * 1024
+            dimension_semantics=("arbitrary",), vmem_limit_bytes=60 * 1024 * 1024
         ),
         cost_estimate=pl.CostEstimate(flops=0, bytes_accessed=100_000_000, transcendentals=0),
         name="mixer_forward",
@@ -456,8 +459,10 @@
     aks = [cut(acts[1], u, key_dim) for u in units]
     rks = [lax.rsqrt(jnp.sum(a * a, -1, keepdims=True) + unit_eps) for a in aks]
     ks = [a * r for a, r in zip(aks, rks)]
-    attends = [wide(dot_nt, q, k) for q, k in zip(qs, ks)]
-    grams = [wide(dot_nt, k, k) for k in ks]
+    ks2, qs2 = [split(k) for k in ks], [split(q) for q in qs]
+    dos2 = [split(do) for do in dos]
+    attends = [wide(dot_nt, q, k) for q, k in zip(qs2, ks2)]
+    grams = [wide(dot_nt, k, k) for k in ks2]
     betas = [parts[g][4][:, h : h + 1] for g, h in units]
     cums = [parts[g][2][:, h : h + 1] for g, h in units]
     rows_of = [parts[g][3][h : h + 1, :] for g, h in units]
@@ -470,30 +475,33 @@
     stricts = [jnp.where(strict, w, 0.0) for w in withins]
     attends = [a * w for a, w in zip(attends, withins)]
     grams = [a * w for a, w in zip(grams, stricts)]
-    from_out = [wide(dot_tn, a, do) for a, do in zip(attends, dos)]
-    into_state = [wide(dot_tn, g * q, do) for g, q, do in zip(growths, qs, dos)]
+    from_out = [wide(dot_tn, a, do) for a, do in zip(attends, dos2)]
+    into_state = [wide(dot_tn, g * q, do) for g, q, do in zip(growths, qs, dos2)]
     tail_keys = [t * k for t, k in zip(tails, ks)]
     bg_keys = [b * k for b, k in zip(bgs, ks)]
-    dss, dbs = {}, {}
+    dss, dbs, dss2, dbs2 = {}, {}, {}, {}
     for g in reversed(range(size // block)):
         mine = [i for i, u in enumerate(units) if u[0] == g]
         for h, i in enumerate(mine):
             dss[i] = dstate[h]
-        dus = [from_out[i] + wide(dot_nn, tail_keys[i], dss[i]) for i in mine]
+            dss2[i] = split(dss[i])
+        dus = [from_out[i] + wide(dot_nn, tail_keys[i], dss2[i]) for i in mine]
         for h, i in enumerate(mine):
             dbs[i] = wide(dot_tn, inverse_ref[g, h], dus[h])
-        backs_in = [wide(dot_tn, bg_keys[i], dbs[i]) for i in mine]
+            dbs2[i] = split(dbs[i])
+        backs_in = [wide(dot_tn, bg_keys[i], dbs2[i]) for i in mine]
         for h, i in enumerate(mine):
             dstate[h] = decs[i] * dss[i] + into_state[i] - backs_in[h]
     index = range(len(units))
     states = [states_ref[g, h] for g, h in units]
     updates = [update_ref[place(u, value_dim)] for u in units]
-    das = [wide(dot_nt, do, x) for do, x in zip(dos, updates)]
-    dls = [-wide(dot_nt, dbs[i], updates[i]) for i in index]
-    dqgs = [wide(dot_nt, do, x) for do, x in zip(dos, states)]
-    dkbs = [-wide(dot_nt, dbs[i], states[i]) for i in index]
-    dkts = [wide(dot_nt, updates[i], dss[i]) for i in index]
-    qbs, kbs = [q.astype(bf16) for q in qs], [k.astype(bf16) for k in ks]
+    updates2, states2 = [split(x) for x in updates], [split(x) for x in states]
+    das = [wide(dot_nt, do, x) for do, x in zip(dos2, updates2)]
+    dls = [-wide(dot_nt, dbs2[i], updates2[i]) for i in index]
+    dqgs = [wide(dot_nt, do, x) for do, x in zip(dos2, states2)]
+    dkbs = [-wide(dot_nt, dbs2[i], states2[i]) for i in index]
+    dkts = [wide(dot_nt, updates2[i], dss2[i]) for i in index]
+    qbs, kbs = [q[0] for q in qs2], [k[0] for k in ks2]
     dgqs = [(x * w).astype(bf16) for x, w in zip(das, withins)]
     dl_grams = [x * y for x, y in zip(dls, grams)]
     dgks = [(x * w * b).astype(bf16) for x, w, b in zip(dls, stricts, betas)]
@@ -644,7 +652,7 @@
             pltpu.VMEM((size + EDGE, vw), f32),
         ],
         compiler_params=pltpu.CompilerParams(
-            dimension_semantics=("arbitrary",), vmem_limit_bytes=56 * 1024 * 1024
+            dimension_semantics=("arbitrary",), vmem_limit_bytes=60 * 1024 * 1024
         ),
         cost_estimate=pl.CostEstimate(flops=0, bytes_accessed=100_000_000, transcendentals=0),
         name="mixer_backward",
@@ -795,7 +803,8 @@
 
 def gather_project_kernel(
     axis,
-    x_ref,
+    tokens_ref,
+    gain_ref,
     alpha_ref,
     beta_ref,
     wq_ref,
@@ -805,6 +814,7 @@
     all_ref,
     w_ref,
     y_ref,
+    normed,
     held,
     weights,
     stage,
@@ -815,14 +825,17 @@
     load,
     out,
 ):
-    rows = x_ref.shape[0]
-    ready, finish, _ = gather_parts(axis, x_ref, held, send, recv, local)
+    rows = tokens_ref.shape[0]
     loads, at = [], 0
     for i, ref in enumerate((wq_ref, wk_ref, wv_ref, wg_ref)):
         width = ref.shape[1]
         loads.append(pltpu.make_async_copy(ref, weights.at[:, pl.ds(at, width)], load.at[i]))
         loads[-1].start()
         at += width
+    tokens = tokens_ref[...].astype(f32)
+    factor = lax.rsqrt(jnp.mean(tokens * tokens, -1, keepdims=True) + norm_eps)
+    normed[...] = (tokens * factor * gain_ref[...]).astype(bf16)
+    ready, finish, _ = gather_parts(axis, normed, held, send, recv, local)
     main = at
     heads, depth = alpha_ref.shape
     thin = jnp.concatenate(
@@ -876,15 +889,17 @@
 IN_VMEM = pl.BlockSpec(memory_space=pltpu.VMEM)
 
 
-def gather_project(x, w_query, w_key, w_value, w_gate_out, w_alpha, w_beta, identity, sizes):
+def gather_project(tokens, gain, w_query, w_key, w_value, w_gate_out, w_alpha, w_beta, identity, sizes):
     heads = w_alpha.shape[1]
-    rows, depth = x.shape
+    rows, depth = tokens.shape
     mains = (w_query, w_key, w_value, w_gate_out)
     width = sum(w.shape[1] for w in mains) + EXTRA
     if not square(sizes):
         padding = jnp.zeros((depth, EXTRA - 2 * heads), bf16)
         w_in = jnp.concatenate(mains + (w_alpha, w_beta, padding), axis=1)
-        gathered = lax.all_gather(x, "tensor", axis=0, tiled=True)
+        inputs = tokens.astype(f32)
+        normed = (inputs * rms_factor(inputs) * gain).astype(bf16)
+        gathered = lax.all_gather(normed, "tensor", axis=0, tiled=True)
         return gathered, w_in, jnp.dot(gathered, w_in, preferred_element_type=f32)
     return pl.pallas_call(
         functools.partial(gather_project_kernel, "tensor"),
@@ -893,9 +908,10 @@
             jax.ShapeDtypeStruct((depth, width), bf16),
             jax.ShapeDtypeStruct((8 * rows, width), f32),
         ),
-        in_specs=[ANYWHERE, IN_VMEM, IN_VMEM] + [ANYWHERE] * 4,
+        in_specs=[IN_VMEM] * 4 + [ANYWHERE] * 4,
         out_specs=(ANYWHERE,) * 3,
         scratch_shapes=[
+            pltpu.VMEM((rows, depth), bf16),
             pltpu.VMEM((8 * rows, depth), bf16),
             pltpu.VMEM((depth, width), bf16),
             pltpu.VMEM((2, rows, width), f32),
@@ -903,11 +919,11 @@
         + gather_scratch(rows, depth)
         + [pltpu.SemaphoreType.DMA((5,)), pltpu.SemaphoreType.DMA((8,))],
         compiler_params=pltpu.CompilerParams(
-            collective_id=identity, has_side_effects=True, vmem_limit_bytes=40 * 1024 * 1024
+            collective_id=identity, has_side_effects=True, vmem_limit_bytes=60 * 1024 * 1024
         ),
         cost_estimate=pl.CostEstimate(flops=0, bytes_accessed=1_000_000, transcendentals=0),
         name="gather_project",
-    )(x, w_alpha.T, w_beta.T, *mains)
+    )(tokens, gain[None, :], w_alpha.T, w_beta.T, *mains)
 
 
 def gather_expand_kernel(
@@ -1027,7 +1043,7 @@
         + gather_scratch(rows, depth)
         + [pltpu.SemaphoreType.DMA((3,)), pltpu.SemaphoreType.DMA((8,)), pltpu.SemaphoreType.DMA((3, 8))],
         compiler_params=pltpu.CompilerParams(
-            collective_id=identity, has_side_effects=True, vmem_limit_bytes=48 * 1024 * 1024
+            collective_id=identity, has_side_effects=True, vmem_limit_bytes=60 * 1024 * 1024
         ),
         cost_estimate=pl.CostEstimate(flops=0, bytes_accessed=1_000_000, transcendentals=0),
         name="gather_expand",
@@ -1165,7 +1181,7 @@
         + gather_scratch(rows, depth)
         + [pltpu.SemaphoreType.DMA((4,)), pltpu.SemaphoreType.DMA((8,)), pltpu.SemaphoreType.DMA((3, 8))],
         compiler_params=pltpu.CompilerParams(
-            collective_id=identity, has_side_effects=True, vmem_limit_bytes=48 * 1024 * 1024
+            collective_id=identity, has_side_effects=True, vmem_limit_bytes=60 * 1024 * 1024
         ),
         cost_estimate=pl.CostEstimate(flops=0, bytes_accessed=1_000_000, transcendentals=0),
         name="gather_back",
@@ -1291,7 +1307,7 @@
         out_specs=(IN_VMEM,) * 2,
         scratch_shapes=scatter_scratch(rows, width),
         compiler_params=pltpu.CompilerParams(
-            collective_id=identity, has_side_effects=True, vmem_limit_bytes=40 * 1024 * 1024
+            collective_id=identity, has_side_effects=True, vmem_limit_bytes=60 * 1024 * 1024
         ),
         cost_estimate=pl.CostEstimate(flops=0, bytes_accessed=1_000_000, transcendentals=0),
         name="attend",
@@ -1364,7 +1380,7 @@
         out_specs=(IN_VMEM,) * 3,
         scratch_shapes=[pltpu.VMEM((2, rows, dgate.shape[0]), bf16)] + scatter_scratch(rows, width),
         compiler_params=pltpu.CompilerParams(
-            collective_id=identity, has_side_effects=True, vmem_limit_bytes=52 * 1024 * 1024
+            collective_id=identity, has_side_effects=True, vmem_limit_bytes=60 * 1024 * 1024
         ),
         cost_estimate=pl.CostEstimate(flops=0, bytes_accessed=1_000_000, transcendentals=0),
         name="return_hidden",
@@ -1553,7 +1569,7 @@
         out_specs=(anywhere,) * len(arrays) + (pl.BlockSpec(memory_space=pltpu.VMEM),),
         scratch_shapes=scratch,
         compiler_params=pltpu.CompilerParams(
-            collective_id=identity, has_side_effects=True, vmem_limit_bytes=56 * 1024 * 1024
+            collective_id=identity, has_side_effects=True, vmem_limit_bytes=60 * 1024 * 1024
         ),
         cost_estimate=pl.CostEstimate(flops=0, bytes_accessed=200 * total, transcendentals=0),
         name="sum_over_line",
@@ -1591,9 +1607,8 @@
     scaled_attn = inputs * factor_attn
     gain_first = gain_attn.astype(f32)
     gain_second = gain_ffn.astype(f32)
-    normed = (scaled_attn * gain_first).astype(bf16)
     gathered, w_in, projected = gather_project(
-        normed, w_query, w_key, w_value, w_gate_out, w_alpha, w_beta, 0, sizes
+        tokens[0], gain_first, w_query, w_key, w_value, w_gate_out, w_alpha, w_beta, 0, sizes
     )
     main = w_in.shape[1] - EXTRA
     extras = (

time: 747 us -> 733 us (0.981)
  local copies, waits for them, and re-layouts: 26.8 us -> 14 us
    unnamed x110 -> x62, local copies, waits for them, and re-layouts: 16.5 us -> 3.77 us
  transfers between devices with their start and end apart: 4 -> 4, of which waited for: 0 -> 0; matrix products, arithmetic and copies ran while one was open for 12% -> 12% of each run, Pallas kernels for 68% -> 70%
where the time goes in v8:
time: 733 us; the launch traced here: 727 us
  Pallas kernels  595 us (81%)
  matrix products  68.7 us (9%)
  other arithmetic  33.4 us (5%)
  between operations  14.6 us (2%)
  local copies, waits for them, and re-layouts  14 us (2%)
    pallas_call x1, Pallas kernels, sum_over_line(): pl.pallas_call(functools.partial(line_kernel, 'dp', 'tensor', tuple(width...  268 us
    pallas_call x1, Pallas kernels, mixer_backward(): pl.pallas_call(functools.partial(backward_kernel, heads, key_dim, value_d...  58.8 us
    pallas_call x1, Pallas kernels, return_hidden(): pl.pallas_call(functools.partial(return_kernel, 'tensor'), out_shape=(jax...  52 us
    pallas_call x1, Pallas kernels, attend(): pl.pallas_call(functools.partial(attend_kernel, 'tensor'), out_shape=(jax...  49.1 us
    pallas_call x1, Pallas kernels, gather_project(): pl.pallas_call(functools.partial(gather_project_kernel, 'tensor'), out_sh...  47.3 us
    pallas_call x1, Pallas kernels, gather_expand(): pl.pallas_call(functools.partial(gather_expand_kernel, 'tensor'), out_sha...  42.3 us
    pallas_call x1, Pallas kernels, gather_back(): pl.pallas_call(functools.partial(gather_back_kernel, 'tensor'), out_shape...  42.2 us
    pallas_call x1, Pallas kernels, mixer_forward(): pl.pallas_call(functools.partial(forward_kernel, heads, key_dim, value_di...  36 us
  transfers between devices with their start and end apart: 4, of which 0 were waited for; matrix products, arithmetic and copies ran while one was open for 12% of the time, Pallas kernels for 70%

profile of v8, /device:TPU:0, one launch (start us, length us, event | category | flops | bytes accessed | tf_op | source)
XLA Modules:
  0.0 727.0 jit_solution(6797442362800963854)
XLA Ops:
  7.2 0.0 all-gather.2.cloned.1.call-start
  7.2 1.3 convert_element_type.68
  8.5 0.0 copy-start.22
  8.5 0.0 copy-start.26
  8.6 0.0 copy-start.16
  8.6 47.3 %gather_project.1 = (bf16[2048,2048]{1,0:T(8,128)(2,1)}, bf16[2048,1664]{1,0:T(8,128)(2,1)}, f32[2048,1664]{1,0:T(8,128)}) custom-call(bf16[256,2048]{1,0:T(8,128)(2,1)} %bitcast.60, f32[1,2048]{1,0:T(1,128)} %bitcast.74, bf16[2,2048]{1,0:T(2,128)(2,1)} %bitcast.86, bf16[2,2048]{1,0:T(2,128)(2,1)} %bitcast.87, bf16[2048,256]{1,0:T(8,128)(2,1)} %wq_ref.1, ...), custom_call_target="tpu_custom_call" | custom-call | bytes 1000000 | tf_op jit(solution)/shard_map/gather_project/pallas_call | solution.py:904
  55.9 0.0 all-gather.2.cloned.1.call-update
  55.9 0.0 all-reduce.3.cloned.1.call-start
  56.0 0.6 convert_element_type.69.tq_ref
  56.6 0.6 convert_element_type.70.tk_ref
  57.2 0.6 convert_element_type.71.tv_ref
  57.8 0.6 copy.47.dl_col_ref
  58.4 0.6 copy.48.db_col_ref
  59.1 0.6 broadcast_in_dim.59
  59.7 0.6 broadcast_in_dim.60
  60.3 36.0 %mixer_forward.1 = (bf16[2048,512]{1,0:T(8,128)(2,1)}, f32[2,128,256]{2,1,0:T(8,128)}, f32[8,2,128,256]{3,2,1,0:T(8,128)}, f32[8,2,256,256]{3,2,1,0:T(8,128)}, f32[2048,512]{1,0:T(8,128)}, /*index=5*/f32[2048,512]{1,0:T(8,128)}) custom-call(f32[2048,1664]{1,0:T(8,128)} %get-tuple-element.68.proj_ref.eq_ref.ek_ref.ev_ref, ...), custom_call_target="tpu_custom_call" | custom-call | bytes 100000000 | tf_op jit(solution)/shard_map/mixer_forward/pallas_call | solution.py:289
  96.3 49.1 %attend.1 = (f32[256,2048]{1,0:T(8,128)}, bf16[256,2048]{1,0:T(8,128)(2,1)}) custom-call(bf16[2048,512]{1,0:T(8,128)(2,1)} %get-tuple-element.69.mixed_ref, bf16[512,2048]{1,0:T(8,128)(2,1)} %w_ref.3, bf16[256,2048]{1,0:T(8,128)(2,1)} %bitcast.61, f32[1,2048]{1,0:T(1,128)} %bitcast.75), custom_call_target="tpu_custom_call" | custom-call | bytes 1000000 | tf_op jit(solution)/shard_map/attend/pallas_call | solution.py:1303
  145.3 0.0 all-gather.2.cloned.1.call-done.cot_ref
  145.4 42.3 %gather_expand.1 = (bf16[2048,2048]{1,0:T(8,128)(2,1)}, bf16[688,2048]{1,0:T(8,128)(2,1)}, bf16[688,2048]{1,0:T(8,128)(2,1)}, bf16[688,2048]{1,0:T(8,128)(2,1)}) custom-call(bf16[256,2048]{1,0:T(8,128)(2,1)} %get-tuple-element.77.x_ref, bf16[2048,2048]{1,0:T(8,128)(2,1)} %all-gather.2.cloned.1.call-done.cot_ref, bf16[688,2048]{1,0:T(8,128)(2,1)} %bitcast.62, ...), custom_call_target="tpu_custom_call" | custom-call | bytes 1000000 | tf_op jit(solution)/shard_map/gather_expand/pallas_call | solution.py:1027
  187.7 10.5 %convolution_convert_fusion.2 = bf16[688,2048]{1,0:T(8,128)(2,1)} fusion(bf16[688,2048]{1,0:T(8,128)(2,1)} %get-tuple-element.83.dgate_ref, bf16[2048,2048]{1,0:T(8,128)(2,1)} %get-tuple-element.82.normed_ref), kind=kOutput, calls=%fused_computation.5 | convolution fusion | flops 5772771328 | bytes 14024704 | tf_op jit(solution)/shard_map/dot_general | solution.py:1631
  198.2 7.3 convolution_convert_fusion.3
  205.5 0.0 all-reduce.3.cloned.1.call-update
  205.5 0.0 reduce-scatter.5.cloned.1.call-start
  205.6 52.0 %return_hidden.1 = (f32[256,2048]{1,0:T(8,128)}, bf16[256,2048]{1,0:T(8,128)(2,1)}, f32[1,2048]{1,0:T(1,128)}) custom-call(bf16[688,2048]{1,0:T(8,128)(2,1)} %get-tuple-element.83.dgate_ref, bf16[688,2048]{1,0:T(8,128)(2,1)} %get-tuple-element.84.dup_ref, bf16[688,2048]{1,0:T(8,128)(2,1)} %bitcast.63, bf16[688,2048]{1,0:T(8,128)(2,1)} %bitcast.65, ...), custom_call_target="tpu_custom_call" | custom-call | bytes 1000000 | tf_op jit(solution)/shard_map/return_hidden/pallas_call | solution.py:1372
  257.6 42.2 %gather_back.1 = (bf16[2048,2048]{1,0:T(8,128)(2,1)}, f32[2048,512]{1,0:T(8,128)}, bf16[2048,2048]{1,0:T(8,128)(2,1)}, bf16[688,2048]{1,0:T(8,128)(2,1)}) custom-call(bf16[256,2048]{1,0:T(8,128)(2,1)} %get-tuple-element.85.x_ref, bf16[512,2048]{1,0:T(8,128)(2,1)} %w_ref.3, bf16[688,2048]{1,0:T(8,128)(2,1)} %get-tuple-element.86.inner_ref, ...), custom_call_target="tpu_custom_call" | custom-call | bytes 1000000 | tf_op jit(solution)/shard_map/gather_back/pallas_call | solution.py:1160
  299.8 58.8 %mixer_backward.1 = (bf16[2048,1664]{1,0:T(8,128)(2,1)}, f32[4,256]{1,0:T(4,128)}, f32[4,256]{1,0:T(4,128)}, f32[4,512]{1,0:T(4,128)}, f32[1,2]{1,0:T(1,128)}, /*index=5*/f32[1,2]{1,0:T(1,128)}, f32[1,256]{1,0:T(1,128)}) custom-call(f32[2048,1664]{1,0:T(8,128)} %get-tuple-element.68.proj_ref.eq_ref.ek_ref.ev_ref, ...), custom_call_target="tpu_custom_call" | custom-call | bytes 100000000 | tf_op jit(solution)/shard_map/mixer_backward/pallas_call | solution.py:605
  358.6 0.0 copy-start.18
  358.6 0.0 copy-start.17
  358.6 0.0 copy-start.14
  358.6 20.8 %multiply_reduce_fusion = (f32[2048]{0:T(1024)S(1)}, bf16[2048,1664]{1,0:T(8,128)(2,1)S(1)}) fusion(bf16[2048,1664]{1,0:T(8,128)(2,1)} %get-tuple-element.90, bf16[2048,2048]{1,0:T(8,128)(2,1)} %get-tuple-element.72, bf16[2048,1664]{1,0:T(8,128)(2,1)} %get-tuple-element.88), kind=kOutput, calls=%fused_computation | convolution fusion | flops 13975681024 | bytes 28844032 | tf_op jit(solution)/shard_map/dot_general | solution.py:685
  379.4 0.0 copy-start.23
  379.4 0.0 copy-start.9
  379.5 3.0 copy-done.3
  382.5 0.1 convert_bitcast_fusion.2
  382.6 0.3 copy.52
  383.0 0.7 concatenate.3
  383.7 9.1 %convolution_convert_fusion.4.refs_2_ = bf16[512,2048]{1,0:T(8,128)(2,1)} fusion(bf16[2048,512]{1,0:T(8,128)(2,1)S(1)} %copy-done.9, bf16[2048,2048]{1,0:T(8,128)(2,1)} %get-tuple-element.99), kind=kOutput, calls=%fused_computation.7 | convolution fusion | flops 4296015872 | bytes 12582912 | tf_op jit(solution)/shard_map/dot_general | solution.py:685
  392.8 21.1 %convolution_convert_fusion = bf16[2048,2048]{1,0:T(8,128)(2,1)} fusion(bf16[2048,1664]{1,0:T(8,128)(2,1)} %get-tuple-element.88, bf16[2048,1664]{1,0:T(8,128)(2,1)} %get-tuple-element.90), kind=kOutput, calls=%fused_computation.1 | convolution fusion | flops 13962838016 | bytes 22020096 | tf_op jit(solution)/shard_map/dot_general | solution.py:689
  413.9 0.0 reduce-scatter.5.cloned.1.call-update
  414.0 0.0 reduce-scatter.3.cloned.1.call-start
  414.0 0.5 reduce-scatter.3.cloned.1.call-update
  414.5 0.6 copy-done
  415.2 0.3 fusion.7
  415.5 267.8 %sum_over_line.1 = (f32[144,128]{1,0:T(8,128)}, bf16[688,2048]{1,0:T(8,128)(2,1)}, bf16[512,2048]{1,0:T(8,128)(2,1)}, bf16[2048,1536]{1,0:T(8,128)(2,1)}, f32[48,128]{1,0:T(8,128)}) custom-call(f32[144,128]{1,0:T(8,128)} %bitcast.70, bf16[688,2048]{1,0:T(8,128)(2,1)} %get-tuple-element.105.refs_1_, bf16[512,2048]{1,0:T(8,128)(2,1)} %convolution_convert_fusion.4.refs_2_, ...), custom_call_target="tpu_custom_call" | custom-call | bytes 1124352000 | tf_op jit(solution)/shard_map/sum_over_line/pallas_call | solution.py:1564
  683.3 0.7 slice.83
  684.0 0.9 fusion.11
  684.8 0.6 slice.77
  685.5 0.6 slice.79
  686.1 0.8 fusion.10
  686.9 0.6 reshape.109
  687.5 0.6 reshape.110
  688.1 0.6 reshape.111
  688.7 4.3 convert_element_type.87
  693.0 5.2 convert_element_type.88
  698.1 1.3 fusion.9
  699.5 0.6 slice_bitcast_fusion.2
  700.0 0.6 slice_bitcast_fusion
  700.6 2.3 slice_convert_fusion.2
  702.9 4.6 slice_convert_fusion
  707.5 5.9 convert_bitcast_fusion
  713.4 1.9 fusion.2
  715.4 0.0 reduce-scatter.3.cloned.1.call-done
  715.4 2.6 fusion.8
  718.1 2.0 fusion.6
  (59 shorter events, 0.2 us)
Async XLA Ops:
  7.2 138.2 %all-gather.2.cloned.1.call-start = ((), (), s32[]{:S(2)}) async-start(), calls=%async_computation.2 | async-start | bytes 9437184 | tf_op jit(solution)/shard_map/all_gather | solution.py:1624
  8.5 47.5 %copy-start.19 = (bf16[4,256]{1,0:T(4,128)(2,1)S(1)}, bf16[4,256]{1,0:T(4,128)(2,1)}, u32[]{:S(2)}) copy-start(bf16[4,256]{1,0:T(4,128)(2,1)} %param.30) | copy-start | bytes 6148
  8.5 48.1 %copy-start.20 = (bf16[4,256]{1,0:T(4,128)(2,1)S(1)}, bf16[4,256]{1,0:T(4,128)(2,1)}, u32[]{:S(2)}) copy-start(bf16[4,256]{1,0:T(4,128)(2,1)} %param.31) | copy-start | bytes 6148
  8.5 48.7 %copy-start.15 = (bf16[4,512]{1,0:T(4,128)(2,1)S(1)}, bf16[4,512]{1,0:T(4,128)(2,1)}, u32[]{:S(2)}) copy-start(bf16[4,512]{1,0:T(4,128)(2,1)} %param.32) | copy-start | bytes 12292
  8.5 49.3 %copy-start.21 = (f32[2]{0:T(128)S(1)}, f32[2]{0:T(128)}, u32[]{:S(2)}) copy-start(f32[2]{0:T(128)} %param.33) | copy-start | bytes 28
  8.5 49.9 %copy-start.22 = (f32[2]{0:T(128)S(1)}, f32[2]{0:T(128)}, u32[]{:S(2)}) copy-start(f32[2]{0:T(128)} %param.34) | copy-start | bytes 28
  8.5 50.5 %copy-start.26 = (bf16[256]{0:T(256)(128)(2,1)S(1)}, bf16[256]{0:T(256)(128)(2,1)}, u32[]{:S(2)}) copy-start(bf16[256]{0:T(256)(128)(2,1)} %param.35) | copy-start | bytes 1540
  8.6 51.1 %copy-start.16 = (bf16[2048]{0:T(1024)(128)(2,1)S(1)}, bf16[2048]{0:T(1024)(128)(2,1)}, u32[]{:S(2)}) copy-start(bf16[2048]{0:T(1024)(128)(2,1)} %param.37) | copy-start | bytes 12292
  55.9 358.0 %all-reduce.3.cloned.1.call-start = ((), (), s32[]{:S(2)}) async-start(), calls=%async_computation.5 | async-start | bytes 11272192 | tf_op jit(solution)/shard_map/psum | solution.py:1632
  187.7 10.5 %copy-start.2 = (bf16[2048,2048]{1,0:T(8,128)(2,1)S(1)}, bf16[2048,2048]{1,0:T(8,128)(2,1)}, u32[]{:S(2)}) copy-start(bf16[2048,2048]{1,0:T(8,128)(2,1)} %all-gather.2.cloned.1.call-done.cot_ref) | copy-start | bytes 25165828
  187.7 10.5 %copy-start.5 = (bf16[688,2048]{1,0:T(8,128)(2,1)S(1)}, bf16[688,2048]{1,0:T(8,128)(2,1)}, u32[]{:S(2)}) copy-start(bf16[688,2048]{1,0:T(8,128)(2,1)} %get-tuple-element.86.inner_ref) | copy-start | bytes 8454148
  205.5 507.9 %reduce-scatter.5.cloned.1.call-start = ((), (), s32[]{:S(2)}) async-start(), calls=%async_computation.4 | async-start | bytes 9437184 | tf_op jit(solution)/shard_map/reduce_scatter | solution.py:1392
  358.6 20.9 %copy-start.18 = (f32[4,256]{1,0:T(4,128)S(1)}, f32[4,256]{1,0:T(4,128)}, u32[]{:S(2)}) copy-start(f32[4,256]{1,0:T(4,128)} %get-tuple-element.93) | copy-start | bytes 12292
  358.6 20.9 %copy-start.17 = (f32[4,256]{1,0:T(4,128)S(1)}, f32[4,256]{1,0:T(4,128)}, u32[]{:S(2)}) copy-start(f32[4,256]{1,0:T(4,128)} %get-tuple-element.94) | copy-start | bytes 12292
  358.6 20.9 %copy-start.14 = (f32[4,512]{1,0:T(4,128)S(1)}, f32[4,512]{1,0:T(4,128)}, u32[]{:S(2)}) copy-start(f32[4,512]{1,0:T(4,128)} %get-tuple-element.95) | copy-start | bytes 24580
  358.6 24.3 %copy-start.11 = (bf16[2048]{0:T(1024)(128)(2,1)S(1)}, bf16[2048]{0:T(1024)(128)(2,1)}, u32[]{:S(2)}) copy-start(bf16[2048]{0:T(1024)(128)(2,1)} %param.23) | copy-start | bytes 12292
  379.4 3.1 copy-start.3
  379.4 3.5 copy-start.13
  379.4 3.5 copy-start.23
  379.4 3.5 copy-start.24
  379.4 3.5 copy-start.25
  379.4 4.3 copy-start.9
  413.9 1.2 copy-start
  414.0 301.4 %reduce-scatter.3.cloned.1.call-start = ((), (), s32[]{:S(2)}) async-start(), calls=%async_computation.3 | async-start | bytes 9437184 | tf_op jit(solution)/shard_map/reduce_scatter | solution.py:1392
  688.7 12.0 %slice-start = ((s8[6291456]{0:T(1024)(128)(4,1)}), s8[4194304]{0:T(1024)(128)(4,1)S(1)}, s32[]{:S(2)}) async-start(s8[6291456]{0:T(1024)(128)(4,1)} %bitcast.66), calls=%async_computation.6 | async-start | bytes 8388608
  692.9 6.5 copy-start.12
  693.0 7.7 %slice-start.1 = ((s8[6291456]{0:T(1024)(128)(4,1)}), s8[2097152]{0:T(1024)(128)(4,1)S(1)}, s32[]{:S(2)}) async-start(s8[6291456]{0:T(1024)(128)(4,1)} %bitcast.66), calls=%async_computation.7 | async-start | bytes 4194304
  702.9 4.6 copy-start.6
  702.9 4.6 copy-start.7
  707.5 5.9 copy-start.10
  713.4 2.0 copy-start.1
  715.4 2.7 copy-start.4
  715.4 2.6 copy-start.8
Sparse Core Ops, SparseCore 0:
  56.0 57.8 all-gather.1
  205.6 202.0 all-reduce.2
  414.1 72.0 reduce-scatter.4
  489.9 71.2 reduce-scatter.2

commit v9 on v8

--- a/solution.py
+++ b/solution.py
@@ -128,6 +128,23 @@
     return parts
 
 
+def pack_params(tq, tk, tv, decay_log, decay_bias, gain):
+    taps = jnp.concatenate([tq, tk, tv], axis=1)
+    width = taps.shape[1]
+    rows = [jnp.pad(row.astype(f32), (0, width - row.shape[0]))[None] for row in (gain, decay_log, decay_bias)]
+    return jnp.concatenate([taps.astype(f32)] + rows + [jnp.zeros((EDGE - TAPS - 3, width), f32)], axis=0)
+
+
+def split_params(ref, heads, key_dim, value_dim):
+    kw, vw = heads * key_dim, heads * value_dim
+    taps = [ref.at[0:TAPS, 0:kw], ref.at[0:TAPS, kw : 2 * kw], ref.at[0:TAPS, 2 * kw : 2 * kw + vw]]
+    rows = ref[TAPS + 1 : TAPS + 3, :][:, :heads]
+    here = iota((heads, heads), 0) == iota((heads, heads), 1)
+    row_of = [rows[i : i + 1] for i in range(2)]
+    column_of = [jnp.sum(jnp.where(here, row, 0.0), 1, keepdims=True) for row in row_of]
+    return (*taps, ref[TAPS : TAPS + 1, :][:, :value_dim], (*row_of, *column_of))
+
+
 def decay_parts(ab, dl_row, db_row, dl_col, db_col, heads, size):
     ab_row = jnp.transpose(ab)[: 2 * heads, :]
     ab_col = ab[:, : 2 * heads]
@@ -151,14 +168,7 @@
     steps,
     block,
     proj_ref,
-    tq_ref,
-    tk_ref,
-    tv_ref,
-    dl_row_ref,
-    db_row_ref,
-    dl_col_ref,
-    db_col_ref,
-    gain_ref,
+    param_ref,
     start_ref,
     gated_ref,
     final_ref,
@@ -174,6 +184,7 @@
     step = pl.program_id(0)
     size = proj_ref.shape[0]
     pq_ref, pk_ref, pv_ref, pg_ref, ab_ref = split_columns(proj_ref, heads, key_dim, value_dim)
+    tq_ref, tk_ref, tv_ref, gain, decays = split_params(param_ref, heads, key_dim, value_dim)
 
     @pl.when(step == 0)
     def _():
@@ -192,7 +203,6 @@
     values = conv_v * sigmoid(conv_v)
     gate = pg_ref[...]
     gate = gate * sigmoid(gate)
-    gain = gain_ref[...]
     incl = iota((block, block), 0) >= iota((block, block), 1)
     strict = iota((block, block), 0) > iota((block, block), 1)
     ab = ab_ref[...]
@@ -200,10 +210,7 @@
     parts = [
         decay_parts(
             ab[g * block : (g + 1) * block],
-            dl_row_ref[...],
-            db_row_ref[...],
-            dl_col_ref[...],
-            db_col_ref[...],
+            *decays,
             heads,
             block,
         )
@@ -271,7 +278,7 @@
     return pl.BlockSpec(shape, lambda i: (0,) * len(shape))
 
 
-def mixer_forward(proj, tq, tk, tv, decay_log, decay_bias, gain, start):
+def mixer_forward(proj, params, start):
     heads, key_dim, value_dim = start.shape
     length, width = proj.shape
     block = min(BLOCK, length)
@@ -299,14 +306,7 @@
         ),
         in_specs=[
             rows(width),
-            full_spec(tq.shape),
-            full_spec(tk.shape),
-            full_spec(tv.shape),
-            full_spec((1, heads)),
-            full_spec((1, heads)),
-            full_spec((heads, 1)),
-            full_spec((heads, 1)),
-            full_spec((1, value_dim)),
+            full_spec(params.shape),
             full_spec(start.shape),
         ],
         out_specs=(
@@ -330,14 +330,7 @@
         name="mixer_forward",
     )(
         proj,
-        tq,
-        tk,
-        tv,
-        decay_log[None, :],
-        decay_bias[None, :],
-        decay_log[:, None],
-        decay_bias[:, None],
-        gain[None, :],
+        params,
         start,
     )
 
@@ -352,14 +345,7 @@
     eq_ref,
     ek_ref,
     ev_ref,
-    tq_ref,
-    tk_ref,
-    tv_ref,
-    dl_row_ref,
-    db_row_ref,
-    dl_col_ref,
-    db_col_ref,
-    gain_ref,
+    param_ref,
     states_ref,
     inverse_ref,
     update_ref,
@@ -383,6 +369,7 @@
     step = pl.program_id(0)
     size = proj_ref.shape[0]
     pq_ref, pk_ref, pv_ref, pg_ref, ab_ref = split_columns(proj_ref, heads, key_dim, value_dim)
+    tq_ref, tk_ref, tv_ref, gain, decays = split_params(param_ref, heads, key_dim, value_dim)
     dpq_ref, dpk_ref, dpv_ref, dpg_ref, dab_ref = split_columns(dproj_ref, heads, key_dim, value_dim)
     exts = (ext_q, ext_k, ext_v)
     backs = (back_q, back_k, back_v)
@@ -412,7 +399,6 @@
     gate_sig = sigmoid(gate_in)
     gate = gate_in * gate_sig
     gate_slope = gate_sig * (1.0 + gate_in * (1.0 - gate_sig))
-    gain = gain_ref[...]
     incl = iota((block, block), 0) >= iota((block, block), 1)
     strict = iota((block, block), 0) > iota((block, block), 1)
     late = jnp.where(iota((block, block), 0) <= iota((block, block), 1), 1.0, 0.0)
@@ -421,10 +407,7 @@
     parts = [
         decay_parts(
             ab[g * block : (g + 1) * block],
-            dl_row_ref[...],
-            db_row_ref[...],
-            dl_col_ref[...],
-            db_col_ref[...],
+            *decays,
             heads,
             block,
         )
@@ -554,7 +537,7 @@
         )
         cum_all = cum_all - jnp.transpose(row_all)[:, :heads]
         dld = dot_exact(late, cum_all) + jnp.concatenate([ends[i] for i in mine], axis=1)
-        dalpha = dld * (-jnp.exp(dl_row_ref[...])) * sigmoid(alpha_col)
+        dalpha = dld * (-jnp.exp(decays[0])) * sigmoid(alpha_col)
         ddb_ref[...] += jnp.sum(dalpha, 0, keepdims=True)
         ddl_ref[...] += jnp.sum(dld * ld_col, 0, keepdims=True)
         dbeta = jnp.concatenate([dbetas[i] for i in mine], axis=1) * beta_col * (1.0 - beta_col)
@@ -580,7 +563,7 @@
 
 
 def mixer_backward(
-    proj, tq, tk, tv, decay_log, decay_bias, gain, states, inverse, update, raw, grad
+    proj, params, states, inverse, update, raw, grad
 ):
     blocks, heads, key_dim, value_dim = states.shape
     length, width = proj.shape
@@ -607,9 +590,9 @@
         grid=(steps,),
         out_shape=(
             jax.ShapeDtypeStruct((length, width), bf16),
-            jax.ShapeDtypeStruct(tq.shape, f32),
-            jax.ShapeDtypeStruct(tk.shape, f32),
-            jax.ShapeDtypeStruct(tv.shape, f32),
+            jax.ShapeDtypeStruct((TAPS, kw), f32),
+            jax.ShapeDtypeStruct((TAPS, kw), f32),
+            jax.ShapeDtypeStruct((TAPS, vw), f32),
             jax.ShapeDtypeStruct((1, heads), f32),
             jax.ShapeDtypeStruct((1, heads), f32),
             jax.ShapeDtypeStruct((1, value_dim), f32),
@@ -619,14 +602,7 @@
             edge(kw, 0),
             edge(kw, 1),
             edge(vw, 2 * kw // vw),
-            full_spec(tq.shape),
-            full_spec(tk.shape),
-            full_spec(tv.shape),
-            full_spec((1, heads)),
-            full_spec((1, heads)),
-            full_spec((heads, 1)),
-            full_spec((heads, 1)),
-            full_spec((1, value_dim)),
+            full_spec(params.shape),
             per_block(heads, key_dim, value_dim),
             per_block(heads, block, block),
             rows(vw),
@@ -635,9 +611,9 @@
         ],
         out_specs=(
             rows(width),
-            full_spec(tq.shape),
-            full_spec(tk.shape),
-            full_spec(tv.shape),
+            full_spec((TAPS, kw)),
+            full_spec((TAPS, kw)),
+            full_spec((TAPS, vw)),
             full_spec((1, heads)),
             full_spec((1, heads)),
             full_spec((1, value_dim)),
@@ -661,14 +637,7 @@
         proj,
         proj,
         proj,
-        tq,
-        tk,
-        tv,
-        decay_log[None, :],
-        decay_bias[None, :],
-        decay_log[:, None],
-        decay_bias[:, None],
-        gain[None, :],
+        params,
         states,
         inverse,
         update,
@@ -1395,24 +1364,32 @@
 CHUNK = 64
 
 
-def row_groups(arrays):
+def row_groups(heights, places):
     groups = []
-    for i, a in enumerate(arrays):
-        whole = a.shape[0] // CHUNK
-        if i > 0 and whole > 0:
-            groups.append((i, 0, CHUNK, whole))
-            if a.shape[0] % CHUNK:
-                groups.append((i, whole * CHUNK, a.shape[0] % CHUNK, 1))
-        else:
-            groups.append((i, 0, a.shape[0], 1))
+    for i, (height, (output, row)) in enumerate(zip(heights, places)):
+        whole = height // CHUNK if i > 0 else 0
+        if whole > 0:
+            groups.append((i, 0, CHUNK, whole, output, row))
+        rest = height - whole * CHUNK
+        if rest > 0:
+            groups.append((i, whole * CHUNK, rest, 1, output, row + whole * CHUNK))
     return groups
 
 
-def line_kernel(axis, cross, widths, spans, *refs):
+def line_kernel(axis, cross, widths, spans, results, copied, *refs):
     count = len(widths)
-    g_refs, out_refs = refs[:count], refs[count : 2 * count]
-    both_ref, parts, part_sems = refs[2 * count], refs[2 * count + 1], refs[2 * count + 2]
-    scratch = refs[2 * count + 3 :]
+    g_refs, more_refs, refs = refs[:count], refs[count : count + len(copied)], refs[count + len(copied) :]
+    out_refs, refs = refs[:results], refs[results:]
+    both_ref, parts, part_sems, more_sems = refs[:4]
+    scratch = refs[4:]
+    more = [
+        pltpu.make_async_copy(
+            ref, out_refs[output].at[pl.ds(row, ref.shape[0]), :], more_sems.at[k]
+        )
+        for k, (ref, (output, row)) in enumerate(zip(more_refs, copied))
+    ]
+    for copy in more:
+        copy.start()
     peers = parts.shape[0]
     me = lax.axis_index(cross)
     z = lax.axis_index(axis)
@@ -1457,13 +1434,16 @@
             spread(k).start()
 
     groups = []
-    for k, (i, start, chunk, chunks) in enumerate(spans):
+    for k, (i, start, chunk, chunks, output, row) in enumerate(spans):
         own, from_out, from_in, total, sems = scratch[5 * k : 5 * k + 5]
-        g_ref, out_ref = g_refs[i], out_refs[i]
+        g_ref, out_ref = g_refs[i], out_refs[output]
 
         def rows_of(ref, c, start=start, width=widths[i], chunk=chunk):
             return ref.at[pl.ds(pl.multiple_of(start + c * chunk, 16), chunk), pl.ds(0, width)]
 
+        def rows_to(ref, c, start=row, width=widths[i], chunk=chunk):
+            return ref.at[pl.ds(pl.multiple_of(start + c * chunk, 16), chunk), pl.ds(0, width)]
+
         def load(c, g_ref=g_ref, own=own, sems=sems, rows_of=rows_of):
             return pltpu.make_async_copy(rows_of(g_ref, c), own.at[c], sems.at[0, c])
 
@@ -1473,11 +1453,11 @@
         def middle(c, own=own, from_in=from_in, sems=sems):
             return copy_to(own.at[c], from_in.at[c], sems.at[3, c], sems.at[4, c], axis, across)
 
-        def outward(c, total=total, out_ref=out_ref, sems=sems, rows_of=rows_of):
-            return copy_to(total.at[c], rows_of(out_ref, c), sems.at[5, c], sems.at[6, c], axis, near)
-
-        def keep(c, total=total, out_ref=out_ref, sems=sems, rows_of=rows_of):
-            return pltpu.make_async_copy(total.at[c], rows_of(out_ref, c), sems.at[7, c])
+        def outward(c, total=total, out_ref=out_ref, sems=sems, rows_to=rows_to):
+            return copy_to(total.at[c], rows_to(out_ref, c), sems.at[5, c], sems.at[6, c], axis, near)
+
+        def keep(c, total=total, out_ref=out_ref, sems=sems, rows_to=rows_to):
+            return pltpu.make_async_copy(total.at[c], rows_to(out_ref, c), sems.at[7, c])
 
         groups.append((chunks, own, from_out, from_in, total, load, inward, middle, outward, keep))
 
@@ -1545,35 +1525,57 @@
         spread(k).wait_recv()
         total = total + parts[k]
     both_ref[...] = total
+    for copy in more:
+        copy.wait()
     for k in range(1, peers):
         spread(k).wait_send()
 
 
-def sum_over_line(arrays, widths, both, identity, sizes):
+def sum_over_line(small, stacked, summed, main, width, both, identity, sizes):
     if not square(sizes):
-        summed = lax.psum(tuple(a[:, :w] for a, w in zip(arrays, widths)), "dp")
-        return summed + (lax.psum(summed[0][:both], "tensor"),)
+        small, stacked, main = lax.psum((small, stacked, main[:, :width]), "dp")
+        return small, jnp.concatenate(stacked + summed, axis=0), main, lax.psum(small[:both], "tensor")
+    arrays = (small,) + stacked + (main,)
+    widths = (small.shape[1],) + tuple(a.shape[1] for a in stacked) + (width,)
+    places, at = [(0, 0)], 0
+    for a in stacked:
+        places.append((1, at))
+        at += a.shape[0]
+    places.append((2, 0))
+    copied = []
+    for a in summed:
+        copied.append((1, at))
+        at += a.shape[0]
     peers = sizes["tensor"]
-    scratch = [pltpu.VMEM((peers, both, widths[0]), arrays[0].dtype), pltpu.SemaphoreType.DMA((2, peers))]
-    spans = row_groups(arrays)
-    for i, _, chunk, chunks in spans:
+    scratch = [
+        pltpu.VMEM((peers, both, widths[0]), small.dtype),
+        pltpu.SemaphoreType.DMA((2, peers)),
+        pltpu.SemaphoreType.DMA((len(copied),)),
+    ]
+    spans = row_groups([a.shape[0] for a in arrays], places)
+    for i, _, chunk, chunks, _, _ in spans:
         scratch += [pltpu.VMEM((chunks, chunk, widths[i]), arrays[i].dtype)] * 4
         scratch.append(pltpu.SemaphoreType.DMA((8, chunks)))
-    anywhere = pl.BlockSpec(memory_space=pl.ANY)
     total = sum(a.shape[0] * w for a, w in zip(arrays, widths))
     return pl.pallas_call(
-        functools.partial(line_kernel, "dp", "tensor", tuple(widths), tuple(spans)),
-        out_shape=tuple(jax.ShapeDtypeStruct((a.shape[0], w), a.dtype) for a, w in zip(arrays, widths))
-        + (jax.ShapeDtypeStruct((both, widths[0]), arrays[0].dtype),),
-        in_specs=[anywhere] * len(arrays),
-        out_specs=(anywhere,) * len(arrays) + (pl.BlockSpec(memory_space=pltpu.VMEM),),
+        functools.partial(
+            line_kernel, "dp", "tensor", widths, tuple(spans), 3, tuple(copied)
+        ),
+        out_shape=(
+            jax.ShapeDtypeStruct(small.shape, small.dtype),
+            jax.ShapeDtypeStruct((at, stacked[0].shape[1]), bf16),
+            jax.ShapeDtypeStruct((main.shape[0], width), bf16),
+            jax.ShapeDtypeStruct((both, widths[0]), small.dtype),
+        ),
+        in_specs=[ANYWHERE] * (len(arrays) + len(summed)),
+        out_specs=(ANYWHERE,) * 3 + (IN_VMEM,),
         scratch_shapes=scratch,
         compiler_params=pltpu.CompilerParams(
             collective_id=identity, has_side_effects=True, vmem_limit_bytes=60 * 1024 * 1024
         ),
         cost_estimate=pl.CostEstimate(flops=0, bytes_accessed=200 * total, transcendentals=0),
         name="sum_over_line",
-    )(*arrays)
+    )(*arrays, *summed)
 
 
 def shards(
@@ -1611,15 +1613,8 @@
         tokens[0], gain_first, w_query, w_key, w_value, w_gate_out, w_alpha, w_beta, 0, sizes
     )
     main = w_in.shape[1] - EXTRA
-    extras = (
-        conv_query.astype(f32),
-        conv_key.astype(f32),
-        conv_value.astype(f32),
-        decay_log,
-        decay_bias,
-        out_gain.astype(f32),
-    )
-    mixed, final, states, inverse, update, raw = mixer_forward(projected, *extras, start_state[0])
+    params = pack_params(conv_query, conv_key, conv_value, decay_log, decay_bias, out_gain)
+    mixed, final, states, inverse, update, raw = mixer_forward(projected, params, start_state[0])
     grad_out_rows, gathered = lax.optimization_barrier((cotangent[0], gathered))
     grad_gathered = lax.all_gather(grad_out_rows, "tensor", axis=0, tiled=True)
     hidden, normed_ffn = attend(mixed, w_out, tokens[0], gain_second, 1, sizes)
@@ -1641,7 +1636,7 @@
     )
     grad_out_weight = cross_rows(mixed, grad_attended).astype(bf16)
     grad_projected, grad_tq, grad_tk, grad_tv, grad_dl, grad_db, grad_gain = mixer_backward(
-        projected, *extras, states, inverse, update, raw, grad_mixed
+        projected, params, states, inverse, update, raw, grad_mixed
     )
     part_normed = times_transposed(grad_projected, w_in).astype(bf16)
     grad_in = cross_rows(gathered, grad_projected).astype(bf16)
@@ -1676,13 +1671,20 @@
     ffn_out = scatter_rows(ffn_part)
     output = (hidden + ffn_out).astype(bf16)
     gains = 2 * width + out_gain.shape[0]
-    small_summed, grad_up_summed, grad_out_summed, grad_in_summed, gain_grads = sum_over_line(
-        (small.reshape(smalls_rows, 128), grad_up_weight, grad_out_weight, grad_in),
-        (128, width, width, main),
+    small_summed, ffn_summed, grad_in_summed, gain_grads = sum_over_line(
+        small.reshape(smalls_rows, 128),
+        (grad_up_weight, grad_out_weight),
+        (grad_down_summed, grad_gate_summed),
+        grad_in,
+        main,
         -(-gains // (16 * 128)) * 16,
         5,
         sizes,
     )
+    large, at = [], 0
+    for a in (grad_up_weight, grad_out_weight, grad_down_summed, grad_gate_summed):
+        large.append(ffn_summed[at : at + a.shape[0]].astype(f32))
+        at += a.shape[0]
     small_summed = small_summed.reshape(-1)
     gain_grads = gain_grads.reshape(-1)
     small_parts, at = [], gains
@@ -1712,11 +1714,11 @@
         small_parts[3],
         small_parts[4],
         gain_grads[2 * width : gains],
-        grad_out_summed.astype(f32),
+        large[1],
         gain_grads[width : 2 * width],
-        grad_gate_summed.astype(f32).T,
-        grad_up_summed.astype(f32).T,
-        grad_down_summed.astype(f32),
+        large[3].T,
+        large[0].T,
+        large[2],
     )
 
 

time: 733 us -> 735 us (level)
  no operation moved by 1% of the time
where the time goes in v9:
time: 735 us; the launch traced here: 729 us
  Pallas kernels  599 us (81%)
  matrix products  68.6 us (9%)
  other arithmetic  31.8 us (4%)
  local copies, waits for them, and re-layouts  14.8 us (2%)
  between operations  14.7 us (2%)
    pallas_call x1, Pallas kernels, sum_over_line(): pl.pallas_call(functools.partial(line_kernel, 'dp', 'tensor', widths, tup...  268 us
    pallas_call x1, Pallas kernels, mixer_backward(): pl.pallas_call(functools.partial(backward_kernel, heads, key_dim, value_d...  58.9 us
    pallas_call x1, Pallas kernels, attend(): pl.pallas_call(functools.partial(attend_kernel, 'tensor'), out_shape=(jax...  52.3 us
    pallas_call x1, Pallas kernels, return_hidden(): pl.pallas_call(functools.partial(return_kernel, 'tensor'), out_shape=(jax...  52 us
    pallas_call x1, Pallas kernels, gather_project(): pl.pallas_call(functools.partial(gather_project_kernel, 'tensor'), out_sh...  47.3 us
    pallas_call x1, Pallas kernels, gather_expand(): pl.pallas_call(functools.partial(gather_expand_kernel, 'tensor'), out_sha...  42.4 us
    pallas_call x1, Pallas kernels, gather_back(): pl.pallas_call(functools.partial(gather_back_kernel, 'tensor'), out_shape...  42.2 us
    pallas_call x1, Pallas kernels, mixer_forward(): pl.pallas_call(functools.partial(forward_kernel, heads, key_dim, value_di...  35.7 us
  transfers between devices with their start and end apart: 4, of which 0 were waited for; matrix products, arithmetic and copies ran while one was open for 12% of the time, Pallas kernels for 70%

profile of v9, /device:TPU:0, one launch (start us, length us, event | category | flops | bytes accessed | tf_op | source)
XLA Modules:
  0.0 729.2 jit_solution(14601469017857742480)
XLA Ops:
  7.2 0.0 all-gather.2.cloned.1.call-start
  7.2 1.3 convert_element_type.67
  8.5 0.0 copy-start.16
  8.5 0.0 copy-start.17
  8.6 0.0 copy-start.18
  8.6 47.3 %gather_project.1 = (bf16[2048,2048]{1,0:T(8,128)(2,1)}, bf16[2048,1664]{1,0:T(8,128)(2,1)}, f32[2048,1664]{1,0:T(8,128)}) custom-call(bf16[256,2048]{1,0:T(8,128)(2,1)} %bitcast.58, f32[1,2048]{1,0:T(1,128)} %bitcast.70, bf16[2,2048]{1,0:T(2,128)(2,1)} %bitcast.85, bf16[2,2048]{1,0:T(2,128)(2,1)} %bitcast.86, bf16[2048,256]{1,0:T(8,128)(2,1)} %wq_ref.1, ...), custom_call_target="tpu_custom_call" | custom-call | bytes 1000000 | tf_op jit(solution)/shard_map/gather_project/pallas_call | solution.py:873
  55.9 0.0 all-gather.2.cloned.1.call-update
  55.9 0.0 all-reduce.6.cloned.1.call-start
  56.0 0.0 copy-done.22
  56.1 0.6 broadcast_in_dim.52
  56.7 0.7 concatenate.10.param_ref
  57.4 35.7 %mixer_forward.1 = (bf16[2048,512]{1,0:T(8,128)(2,1)}, f32[2,128,256]{2,1,0:T(8,128)}, f32[8,2,128,256]{3,2,1,0:T(8,128)}, f32[8,2,256,256]{3,2,1,0:T(8,128)}, f32[2048,512]{1,0:T(8,128)}, /*index=5*/f32[2048,512]{1,0:T(8,128)}) custom-call(f32[2048,1664]{1,0:T(8,128)} %get-tuple-element.67.proj_ref.eq_ref.ek_ref.ev_ref, f32[8,1024]{1,0:T(8,128)} %concatenate.10.param_ref, ...), custom_call_target="tpu_custom_call" | custom-call | bytes 100000000 | tf_op jit(solution)/shard_map/mixer_forward/pallas_call | solution.py:296
  93.1 52.3 %attend.1 = (f32[256,2048]{1,0:T(8,128)}, bf16[256,2048]{1,0:T(8,128)(2,1)}) custom-call(bf16[2048,512]{1,0:T(8,128)(2,1)} %get-tuple-element.68.mixed_ref, bf16[512,2048]{1,0:T(8,128)(2,1)} %w_ref.3, bf16[256,2048]{1,0:T(8,128)(2,1)} %bitcast.59, f32[1,2048]{1,0:T(1,128)} %bitcast.71), custom_call_target="tpu_custom_call" | custom-call | bytes 1000000 | tf_op jit(solution)/shard_map/attend/pallas_call | solution.py:1272
  145.4 0.0 all-gather.2.cloned.1.call-done.cot_ref
  145.4 42.4 %gather_expand.1 = (bf16[2048,2048]{1,0:T(8,128)(2,1)}, bf16[688,2048]{1,0:T(8,128)(2,1)}, bf16[688,2048]{1,0:T(8,128)(2,1)}, bf16[688,2048]{1,0:T(8,128)(2,1)}) custom-call(bf16[256,2048]{1,0:T(8,128)(2,1)} %get-tuple-element.76.x_ref, bf16[2048,2048]{1,0:T(8,128)(2,1)} %all-gather.2.cloned.1.call-done.cot_ref, bf16[688,2048]{1,0:T(8,128)(2,1)} %bitcast.60, ...), custom_call_target="tpu_custom_call" | custom-call | bytes 1000000 | tf_op jit(solution)/shard_map/gather_expand/pallas_call | solution.py:996
  187.8 10.5 %convolution_convert_fusion.2 = bf16[688,2048]{1,0:T(8,128)(2,1)} fusion(bf16[688,2048]{1,0:T(8,128)(2,1)} %get-tuple-element.82.dgate_ref, bf16[2048,2048]{1,0:T(8,128)(2,1)} %get-tuple-element.81.normed_ref), kind=kOutput, calls=%fused_computation.5 | convolution fusion | flops 5772771328 | bytes 14024704 | tf_op jit(solution)/shard_map/dot_general | solution.py:1626
  198.3 7.3 convolution_convert_fusion.3
  205.6 0.0 all-reduce.6.cloned.1.call-update
  205.6 0.0 reduce-scatter.5.cloned.1.call-start
  205.6 52.0 %return_hidden.1 = (f32[256,2048]{1,0:T(8,128)}, bf16[256,2048]{1,0:T(8,128)(2,1)}, f32[1,2048]{1,0:T(1,128)}) custom-call(bf16[688,2048]{1,0:T(8,128)(2,1)} %get-tuple-element.82.dgate_ref, bf16[688,2048]{1,0:T(8,128)(2,1)} %get-tuple-element.83.dup_ref, bf16[688,2048]{1,0:T(8,128)(2,1)} %bitcast.61, bf16[688,2048]{1,0:T(8,128)(2,1)} %bitcast.63, ...), custom_call_target="tpu_custom_call" | custom-call | bytes 1000000 | tf_op jit(solution)/shard_map/return_hidden/pallas_call | solution.py:1341
  257.6 42.2 %gather_back.1 = (bf16[2048,2048]{1,0:T(8,128)(2,1)}, f32[2048,512]{1,0:T(8,128)}, bf16[2048,2048]{1,0:T(8,128)(2,1)}, bf16[688,2048]{1,0:T(8,128)(2,1)}) custom-call(bf16[256,2048]{1,0:T(8,128)(2,1)} %get-tuple-element.84.x_ref, bf16[512,2048]{1,0:T(8,128)(2,1)} %w_ref.3, bf16[688,2048]{1,0:T(8,128)(2,1)} %get-tuple-element.85.inner_ref, ...), custom_call_target="tpu_custom_call" | custom-call | bytes 1000000 | tf_op jit(solution)/shard_map/gather_back/pallas_call | solution.py:1129
  299.8 58.9 %mixer_backward.1 = (bf16[2048,1664]{1,0:T(8,128)(2,1)}, f32[4,256]{1,0:T(4,128)}, f32[4,256]{1,0:T(4,128)}, f32[4,512]{1,0:T(4,128)}, f32[1,2]{1,0:T(1,128)}, /*index=5*/f32[1,2]{1,0:T(1,128)}, f32[1,256]{1,0:T(1,128)}) custom-call(f32[2048,1664]{1,0:T(8,128)} %get-tuple-element.67.proj_ref.eq_ref.ek_ref.ev_ref, ...), custom_call_target="tpu_custom_call" | custom-call | bytes 100000000 | tf_op jit(solution)/shard_map/mixer_backward/pallas_call | solution.py:588
  358.8 0.0 copy-start.15
  358.8 0.0 copy-start.14
  358.8 0.0 copy-start.12
  358.8 0.0 copy-start.10
  358.8 20.8 %multiply_reduce_fusion = (f32[2048]{0:T(1024)S(1)}, bf16[2048,1664]{1,0:T(8,128)(2,1)S(1)}) fusion(bf16[2048,1664]{1,0:T(8,128)(2,1)} %get-tuple-element.89, bf16[2048,2048]{1,0:T(8,128)(2,1)} %get-tuple-element.71, bf16[2048,1664]{1,0:T(8,128)(2,1)} %get-tuple-element.87), kind=kOutput, calls=%fused_computation | convolution fusion | flops 13975681024 | bytes 28844032 | tf_op jit(solution)/shard_map/dot_general | solution.py:654
  379.6 0.0 copy-start.19
  379.6 0.0 copy-start.20
  379.6 0.0 copy-start.21
  379.6 0.0 copy-start.8
  379.7 3.0 copy-done.3
  382.7 0.1 convert_bitcast_fusion.2
  382.7 0.3 copy.44
  383.2 0.7 concatenate.11
  383.9 9.1 %convolution_convert_fusion.4.refs_2_ = bf16[512,2048]{1,0:T(8,128)(2,1)} fusion(bf16[2048,512]{1,0:T(8,128)(2,1)S(1)} %copy-done.8, bf16[2048,2048]{1,0:T(8,128)(2,1)} %get-tuple-element.98), kind=kOutput, calls=%fused_computation.7 | convolution fusion | flops 4296015872 | bytes 12582912 | tf_op jit(solution)/shard_map/dot_general | solution.py:654
  393.0 21.0 %convolution_convert_fusion = bf16[2048,2048]{1,0:T(8,128)(2,1)} fusion(bf16[2048,1664]{1,0:T(8,128)(2,1)} %get-tuple-element.87, bf16[2048,1664]{1,0:T(8,128)(2,1)} %get-tuple-element.89), kind=kOutput, calls=%fused_computation.1 | convolution fusion | flops 13962838016 | bytes 22020096 | tf_op jit(solution)/shard_map/dot_general | solution.py:658
  414.0 0.0 reduce-scatter.5.cloned.1.call-update
  414.0 0.0 copy-start
  414.0 0.0 reduce-scatter.3.cloned.1.call-start
  414.1 0.5 reduce-scatter.3.cloned.1.call-update
  414.6 0.6 copy-done
  415.3 0.3 fusion.7
  415.6 267.7 %sum_over_line.1 = (f32[144,128]{1,0:T(8,128)}, bf16[2576,2048]{1,0:T(8,128)(2,1)}, bf16[2048,1536]{1,0:T(8,128)(2,1)}, f32[48,128]{1,0:T(8,128)}) custom-call(f32[144,128]{1,0:T(8,128)} %bitcast.66, bf16[688,2048]{1,0:T(8,128)(2,1)} %get-tuple-element.104.refs_1_, bf16[512,2048]{1,0:T(8,128)(2,1)} %convolution_convert_fusion.4.refs_2_, ...), custom_call_target="tpu_custom_call" | custom-call | bytes 1124352000 | tf_op jit(solution)/shard_map/sum_over_line/pallas_call | solution.py:1560
  683.3 0.7 slice.95
  684.0 0.9 fusion.11
  684.9 0.6 slice.89
  685.5 0.6 slice.91
  686.1 0.8 fusion.10
  686.9 0.6 reshape.109
  687.5 0.6 reshape.110
  688.1 0.6 reshape.111
  688.7 1.3 fusion.9
  690.0 1.2 slice_bitcast_fusion.2
  691.2 1.3 slice_bitcast_fusion
  692.6 3.9 slice_convert_fusion.4
  696.5 4.3 slice_convert_fusion.1
  700.7 4.6 slice_convert_fusion.2
  705.3 10.3 %slice_convert_fusion = (f32[688,2048]{1,0:T(8,128)}, f32[2048,688]{0,1:T(8,128)}, f32[2048,688]{0,1:T(8,128)}) fusion(bf16[2576,2048]{1,0:T(8,128)(2,1)} %get-tuple-element.112), kind=kLoop, calls=%fused_computation.8 | loop fusion | flops 4227072 | bytes 25362432 | tf_op jit(solution)/shard_map/convert_element_type | solution.py:1686
  715.6 1.9 fusion.2
  717.6 0.0 reduce-scatter.3.cloned.1.call-done
  717.6 2.6 fusion.8
  720.2 0.0 copy-done.5
  720.3 2.0 fusion.6
  (49 shorter events, 0.1 us)
Async XLA Ops:
  7.2 138.2 %all-gather.2.cloned.1.call-start = ((), (), s32[]{:S(2)}) async-start(), calls=%async_computation.2 | async-start | bytes 9437184 | tf_op jit(solution)/shard_map/all_gather | solution.py:1619
  8.5 47.5 %copy-start.22 = (f32[2]{0:T(128)S(1)}, f32[2]{0:T(128)}, u32[]{:S(2)}) copy-start(f32[2]{0:T(128)} %param.33) | copy-start | bytes 28
  8.5 47.5 %copy-start.23 = (f32[2]{0:T(128)S(1)}, f32[2]{0:T(128)}, u32[]{:S(2)}) copy-start(f32[2]{0:T(128)} %param.34) | copy-start | bytes 28
  8.5 47.5 %copy-start.13 = (bf16[2048]{0:T(1024)(128)(2,1)S(1)}, bf16[2048]{0:T(1024)(128)(2,1)}, u32[]{:S(2)}) copy-start(bf16[2048]{0:T(1024)(128)(2,1)} %param.37) | copy-start | bytes 12292
  8.5 48.1 %copy-start.24 = (bf16[256]{0:T(256)(128)(2,1)S(1)}, bf16[256]{0:T(256)(128)(2,1)}, u32[]{:S(2)}) copy-start(bf16[256]{0:T(256)(128)(2,1)} %param.35) | copy-start | bytes 1540
  8.5 48.1 %copy-start.16 = (bf16[4,512]{1,0:T(4,128)(2,1)S(1)}, bf16[4,512]{1,0:T(4,128)(2,1)}, u32[]{:S(2)}) copy-start(bf16[4,512]{1,0:T(4,128)(2,1)} %param.32) | copy-start | bytes 12292
  8.5 48.1 %copy-start.17 = (bf16[4,256]{1,0:T(4,128)(2,1)S(1)}, bf16[4,256]{1,0:T(4,128)(2,1)}, u32[]{:S(2)}) copy-start(bf16[4,256]{1,0:T(4,128)(2,1)} %param.31) | copy-start | bytes 6148
  8.6 48.1 %copy-start.18 = (bf16[4,256]{1,0:T(4,128)(2,1)S(1)}, bf16[4,256]{1,0:T(4,128)(2,1)}, u32[]{:S(2)}) copy-start(bf16[4,256]{1,0:T(4,128)(2,1)} %param.30) | copy-start | bytes 6148
  55.9 358.1 %all-reduce.6.cloned.1.call-start = ((), (), s32[]{:S(2)}) async-start(), calls=%async_computation.5 | async-start | bytes 11272192 | tf_op jit(solution)/shard_map/psum | solution.py:1627
  187.8 10.5 %copy-start.2 = (bf16[2048,2048]{1,0:T(8,128)(2,1)S(1)}, bf16[2048,2048]{1,0:T(8,128)(2,1)}, u32[]{:S(2)}) copy-start(bf16[2048,2048]{1,0:T(8,128)(2,1)} %all-gather.2.cloned.1.call-done.cot_ref) | copy-start | bytes 25165828
  187.8 10.5 %copy-start.6 = (bf16[688,2048]{1,0:T(8,128)(2,1)S(1)}, bf16[688,2048]{1,0:T(8,128)(2,1)}, u32[]{:S(2)}) copy-start(bf16[688,2048]{1,0:T(8,128)(2,1)} %get-tuple-element.85.inner_ref) | copy-start | bytes 8454148
  205.6 510.0 %reduce-scatter.5.cloned.1.call-start = ((), (), s32[]{:S(2)}) async-start(), calls=%async_computation.4 | async-start | bytes 9437184 | tf_op jit(solution)/shard_map/reduce_scatter | solution.py:1361
  358.8 20.9 %copy-start.15 = (f32[4,256]{1,0:T(4,128)S(1)}, f32[4,256]{1,0:T(4,128)}, u32[]{:S(2)}) copy-start(f32[4,256]{1,0:T(4,128)} %get-tuple-element.92) | copy-start | bytes 12292
  358.8 20.9 %copy-start.14 = (f32[4,256]{1,0:T(4,128)S(1)}, f32[4,256]{1,0:T(4,128)}, u32[]{:S(2)}) copy-start(f32[4,256]{1,0:T(4,128)} %get-tuple-element.93) | copy-start | bytes 12292
  358.8 20.9 %copy-start.12 = (f32[4,512]{1,0:T(4,128)S(1)}, f32[4,512]{1,0:T(4,128)}, u32[]{:S(2)}) copy-start(f32[4,512]{1,0:T(4,128)} %get-tuple-element.94) | copy-start | bytes 24580
  358.8 24.3 %copy-start.10 = (bf16[2048]{0:T(1024)(128)(2,1)S(1)}, bf16[2048]{0:T(1024)(128)(2,1)}, u32[]{:S(2)}) copy-start(bf16[2048]{0:T(1024)(128)(2,1)} %param.23) | copy-start | bytes 12292
  379.6 3.1 copy-start.3
  379.6 3.5 copy-start.11
  379.6 3.5 copy-start.19
  379.6 3.5 copy-start.20
  379.6 3.5 copy-start.21
  379.6 4.2 copy-start.8
  414.0 1.2 copy-start
  414.0 303.5 %reduce-scatter.3.cloned.1.call-start = ((), (), s32[]{:S(2)}) async-start(), calls=%async_computation.3 | async-start | bytes 9437184 | tf_op jit(solution)/shard_map/reduce_scatter | solution.py:1361
  696.5 4.3 copy-start.4
  705.3 10.3 %copy-start.9 = (f32[2048]{0:T(1024)S(1)}, f32[2048]{0:T(1024)}, u32[]{:S(2)}) copy-start(f32[2048]{0:T(1024)} %convert_element_type.67) | copy-start | bytes 24580
  715.6 2.0 copy-start.1
  717.6 2.7 copy-start.5
  717.6 2.6 copy-start.7
Sparse Core Ops, SparseCore 0:
  56.1 61.0 all-gather.1
  205.7 201.9 all-reduce.5
  414.1 71.9 reduce-scatter.4
  489.9 71.2 reduce-scatter.2

commit v10 on v9

--- a/solution.py
+++ b/solution.py
@@ -1157,12 +1157,16 @@
     )(x, w, inner, down, dup, normed)
 
 
-def scatter_parts(axis, product, finish, mine, theirs, leaving, in_dx, in_dy, in_x, in_y, send, recv):
+def scatter_parts(
+    axis, product, finish, mine, theirs, leaving, in_dx, in_dy, in_x, in_y, send, recv, tick=None
+):
     me, other, along_x, along_y = neighbours(axis)
     rows = in_x.shape[0]
     half = rows // 2
     diagonal = along_x + along_y - me
-    greet(axis, (other, along_x, along_y))
+    if tick is None:
+        greet(axis, (other, along_x, along_y))
+        tick = lambda: None
     shift = other - me
     first, second = pl.ds(0, half), pl.ds(half, half)
     goals = (diagonal, along_x, along_y, me)
@@ -1186,19 +1190,26 @@
         mine[r] = (mine[r].astype(f32) + theirs[r].astype(f32)).astype(bf16)
 
     theirs_of(0)
+    tick()
     product(goals[0], mine.at[0])
     pair_sum(0)
     far_x = begin(mine.at[0, first, :], in_dx, along_x)
     far_y = begin(mine.at[0, second, :], in_dy, along_y)
+    tick()
     theirs_of(1)
+    tick()
     product(goals[1], mine.at[1])
+    tick()
     theirs_of(2)
     pair_sum(1)
     near_x0 = begin(mine.at[1, first, :], in_x.at[first, :], along_x)
+    tick()
     product(goals[2], mine.at[2])
     pair_sum(2)
     near_y1 = begin(mine.at[2, second, :], in_y.at[second, :], along_y)
+    tick()
     theirs_of(3)
+    tick()
     far_x.wait_recv()
     mine[2, first, :] = (mine[2, first, :].astype(f32) + in_dx[...].astype(f32)).astype(bf16)
     near_y0 = begin(mine.at[2, first, :], in_y.at[first, :], along_y)
@@ -1207,6 +1218,7 @@
     near_x1 = begin(mine.at[1, second, :], in_x.at[second, :], along_x)
     product(goals[3], mine.at[3])
     swaps[3].wait_recv()
+    tick()
     for at, near_x, near_y in ((first, near_x0, near_y0), (second, near_x1, near_y1)):
         near_x.wait_recv()
         near_y.wait_recv()
@@ -1217,6 +1229,7 @@
             + in_x[at, :].astype(f32)
             + in_y[at, :].astype(f32),
         )
+        tick()
     for copy in swaps + copies:
         copy.wait_send()
 
@@ -1364,32 +1377,27 @@
 CHUNK = 64
 
 
-def row_groups(heights, places):
+RING = 4
+
+
+def row_groups(arrays):
     groups = []
-    for i, (height, (output, row)) in enumerate(zip(heights, places)):
-        whole = height // CHUNK if i > 0 else 0
+    for i, a in enumerate(arrays):
+        whole = a.shape[0] // CHUNK if i > 0 else 0
         if whole > 0:
-            groups.append((i, 0, CHUNK, whole, output, row))
-        rest = height - whole * CHUNK
-        if rest > 0:
-            groups.append((i, whole * CHUNK, rest, 1, output, row + whole * CHUNK))
-    return groups
-
-
-def line_kernel(axis, cross, widths, spans, results, copied, *refs):
+            groups.append((i, 0, CHUNK, whole))
+        if a.shape[0] - whole * CHUNK > 0:
+            groups.append((i, whole * CHUNK, a.shape[0] - whole * CHUNK, 1))
+    lead = next(k for k, group in enumerate(groups) if group[0] == 1)
+    return [groups[lead]] + groups[:lead] + groups[lead + 1 :]
+
+
+def line_kernel(axis, cross, widths, spans, dproj_ref, w_ref, *refs):
     count = len(widths)
-    g_refs, more_refs, refs = refs[:count], refs[count : count + len(copied)], refs[count + len(copied) :]
-    out_refs, refs = refs[:results], refs[results:]
-    both_ref, parts, part_sems, more_sems = refs[:4]
-    scratch = refs[4:]
-    more = [
-        pltpu.make_async_copy(
-            ref, out_refs[output].at[pl.ds(row, ref.shape[0]), :], more_sems.at[k]
-        )
-        for k, (ref, (output, row)) in enumerate(zip(more_refs, copied))
-    ]
-    for copy in more:
-        copy.start()
+    g_refs, out_refs = refs[:count], refs[count : 2 * count]
+    both_ref, normed_ref, parts, part_sems, weights, rows_in, fetch = refs[2 * count : 2 * count + 7]
+    scattering = refs[2 * count + 7 : 2 * count + 16]
+    scratch = refs[2 * count + 16 :]
     peers = parts.shape[0]
     me = lax.axis_index(cross)
     z = lax.axis_index(axis)
@@ -1434,90 +1442,150 @@
             spread(k).start()
 
     groups = []
-    for k, (i, start, chunk, chunks, output, row) in enumerate(spans):
-        own, from_out, from_in, total, sems = scratch[5 * k : 5 * k + 5]
-        g_ref, out_ref = g_refs[i], out_refs[output]
+    for k, (i, start, chunk, chunks) in enumerate(spans):
+        own, from_out, from_in, sems = scratch[4 * k : 4 * k + 4]
+        g_ref, out_ref = g_refs[i], out_refs[i]
 
         def rows_of(ref, c, start=start, width=widths[i], chunk=chunk):
             return ref.at[pl.ds(pl.multiple_of(start + c * chunk, 16), chunk), pl.ds(0, width)]
 
-        def rows_to(ref, c, start=row, width=widths[i], chunk=chunk):
-            return ref.at[pl.ds(pl.multiple_of(start + c * chunk, 16), chunk), pl.ds(0, width)]
-
         def load(c, g_ref=g_ref, own=own, sems=sems, rows_of=rows_of):
-            return pltpu.make_async_copy(rows_of(g_ref, c), own.at[c], sems.at[0, c])
+            return pltpu.make_async_copy(rows_of(g_ref, c), own.at[c % own.shape[0]], sems.at[0, c])
 
         def inward(c, g_ref=g_ref, from_out=from_out, sems=sems, rows_of=rows_of):
             return copy_to(rows_of(g_ref, c), from_out.at[c], sems.at[1, c], sems.at[2, c], axis, near)
 
-        def middle(c, own=own, from_in=from_in, sems=sems):
-            return copy_to(own.at[c], from_in.at[c], sems.at[3, c], sems.at[4, c], axis, across)
-
-        def outward(c, total=total, out_ref=out_ref, sems=sems, rows_to=rows_to):
-            return copy_to(total.at[c], rows_to(out_ref, c), sems.at[5, c], sems.at[6, c], axis, near)
-
-        def keep(c, total=total, out_ref=out_ref, sems=sems, rows_to=rows_to):
-            return pltpu.make_async_copy(total.at[c], rows_to(out_ref, c), sems.at[7, c])
-
-        groups.append((chunks, own, from_out, from_in, total, load, inward, middle, outward, keep))
-
-    def each(chunks, body):
+        def middle(c, from_out=from_out, from_in=from_in, sems=sems):
+            return copy_to(from_out.at[c], from_in.at[c], sems.at[3, c], sems.at[4, c], axis, across)
+
+        def outward(c, from_in=from_in, out_ref=out_ref, sems=sems, rows_of=rows_of):
+            return copy_to(from_in.at[c], rows_of(out_ref, c), sems.at[5, c], sems.at[6, c], axis, near)
+
+        def keep(c, from_in=from_in, out_ref=out_ref, sems=sems, rows_of=rows_of):
+            return pltpu.make_async_copy(from_in.at[c], rows_of(out_ref, c), sems.at[7, c])
+
+        def first(c, own=own, from_out=from_out, chunks=chunks, load=load, inward=inward, middle=middle):
+            ring = own.shape[0]
+            load(c).wait()
+            inward(c).wait_recv()
+            from_out[c] = (own[c % ring].astype(f32) + from_out[c].astype(f32)).astype(own.dtype)
+            middle(c).start()
+            if chunks > ring:
+
+                @pl.when(c + ring < chunks)
+                def _():
+                    load(c + ring).start()
+
+        def second(c, from_out=from_out, from_in=from_in, middle=middle, outward=outward, keep=keep):
+            middle(c).wait_recv()
+            from_in[c] = (from_out[c].astype(f32) + from_in[c].astype(f32)).astype(from_in.dtype)
+            outward(c).start()
+            keep(c).start()
+
+        groups.append((i == 0, chunks, own.shape[0], load, inward, middle, outward, keep, first, second))
+
+    def each(low, high, body):
         def step(c, carry):
             body(c)
             return carry
 
-        lax.fori_loop(0, chunks, step, 0)
+        if high > low:
+            lax.fori_loop(low, high, step, 0)
 
     @pl.when(jnp.logical_not(inner))
     def _():
-        for chunks, _, _, _, _, _, inward, _, _, _ in groups:
-            each(chunks, lambda c: inward(c).start())
-        for i, (chunks, _, _, _, _, _, inward, _, outward, _) in enumerate(groups):
-            each(chunks, lambda c: outward(c).wait_recv())
-            each(chunks, lambda c: inward(c).wait_send())
-            if i == 0:
-                spread_all()
+        for _, chunks, _, _, inward, _, _, _, _, _ in groups:
+            each(0, chunks, lambda c: inward(c).start())
 
     @pl.when(inner)
     def _():
-        for chunks, _, _, _, _, load, _, _, _, _ in groups:
-            each(chunks, lambda c: load(c).start())
-        for i, group in enumerate(groups):
-            chunks, own, from_out, from_in, total, load, inward, middle, outward, keep = group
-
-            def first(c):
-                load(c).wait()
-                inward(c).wait_recv()
-                own[c] = (own[c].astype(f32) + from_out[c].astype(f32)).astype(own.dtype)
-                middle(c).start()
-
-            def second(c):
-                middle(c).wait_recv()
-                total[c] = (own[c].astype(f32) + from_in[c].astype(f32)).astype(total.dtype)
-                outward(c).start()
-                keep(c).start()
-
+        for _, _, ring, load, _, _, _, _, _, _ in groups:
+            for c in range(ring):
+                load(c).start()
+
+    _, lead, _, _, _, _, _, _, lead_first, lead_second = groups[0]
+    done = []
+
+    def tick():
+        k = len(done)
+        done.append(k)
+        if k > lead:
+            return
+
+        @pl.when(inner)
+        def _():
+            if k < lead:
+                lead_first(k)
+            if k > 0:
+                lead_second(k - 1)
+
+    rows, depth = normed_ref.shape
+    where = []
+    other = me + 1 - 2 * (me % 2)
+    along_x = me + 2 - 4 * ((me // 2) % 2)
+    along_y = me + 4 - 8 * (me // 4)
+    for goal in (along_x + along_y - me, along_x, along_y, me):
+        where += [goal + other - me, goal]
+    order = [0, 1, 2, 3, 4, 5, 6, 7]
+    fetches = [
+        pltpu.make_async_copy(rows_at(dproj_ref, where[n], rows), rows_in.at[n % 2], fetch.at[n]) for n in order
+    ]
+    take = pltpu.make_async_copy(w_ref, weights, fetch.at[8])
+    take.start()
+    fetches[0].start()
+    take.wait()
+    made = []
+
+    def product(shard, ref):
+        n = len(made)
+        made.append(n)
+        if n + 1 < 8:
+            fetches[n + 1].start()
+        fetches[n].wait()
+
+        def tile(here):
+            ref[:, here] = dot_nt(rows_in[n % 2], weights[here, :]).astype(bf16)
+
+        in_columns(depth, 512, tile)
+
+    def finish(at, value):
+        normed_ref[at, :] = value
+
+    scatter_parts(cross, product, finish, *scattering, tick=tick)
+    while len(done) <= lead:
+        tick()
+
+    @pl.when(jnp.logical_not(inner))
+    def _():
+        for is_small, chunks, _, _, inward, _, outward, _, _, _ in groups:
+            each(0, chunks, lambda c: outward(c).wait_recv())
+            each(0, chunks, lambda c: inward(c).wait_send())
+            if is_small:
+                spread_all()
+
+    @pl.when(inner)
+    def _():
+        for is_small, chunks, _, _, _, _, _, keep, first, second in groups[1:]:
             first(0)
 
-            def both(c):
+            def both(c, first=first, second=second):
                 first(c + 1)
                 second(c)
 
-            if chunks > 1:
-                each(chunks - 1, both)
+            each(0, chunks - 1, both)
             second(chunks - 1)
-            if i == 0:
-                each(chunks, lambda c: keep(c).wait())
+            if is_small:
+                each(0, chunks, lambda c: keep(c).wait())
                 spread_all()
-        for i, (chunks, _, _, _, _, _, _, middle, outward, keep) in enumerate(groups):
+        for is_small, chunks, _, _, _, middle, outward, keep, _, _ in groups:
 
             def settle(c):
                 middle(c).wait_send()
                 outward(c).wait_send()
-                if i > 0:
+                if not is_small:
                     keep(c).wait()
 
-            each(chunks, settle)
+            each(0, chunks, settle)
 
     own_part.wait()
     total = parts[0]
@@ -1525,57 +1593,47 @@
         spread(k).wait_recv()
         total = total + parts[k]
     both_ref[...] = total
-    for copy in more:
-        copy.wait()
     for k in range(1, peers):
         spread(k).wait_send()
 
 
-def sum_over_line(small, stacked, summed, main, width, both, identity, sizes):
+def sum_over_line(arrays, widths, both, dproj, w_in, identity, sizes):
     if not square(sizes):
-        small, stacked, main = lax.psum((small, stacked, main[:, :width]), "dp")
-        return small, jnp.concatenate(stacked + summed, axis=0), main, lax.psum(small[:both], "tensor")
-    arrays = (small,) + stacked + (main,)
-    widths = (small.shape[1],) + tuple(a.shape[1] for a in stacked) + (width,)
-    places, at = [(0, 0)], 0
-    for a in stacked:
-        places.append((1, at))
-        at += a.shape[0]
-    places.append((2, 0))
-    copied = []
-    for a in summed:
-        copied.append((1, at))
-        at += a.shape[0]
+        summed = lax.psum(tuple(a[:, :w] for a, w in zip(arrays, widths)), "dp")
+        part = times_transposed(dproj, w_in).astype(bf16)
+        return summed + (lax.psum(summed[0][:both], "tensor"), scatter_rows(part))
     peers = sizes["tensor"]
+    depth, inside = w_in.shape
+    rows = dproj.shape[0] // peers
     scratch = [
-        pltpu.VMEM((peers, both, widths[0]), small.dtype),
+        pltpu.VMEM((peers, both, widths[0]), arrays[0].dtype),
         pltpu.SemaphoreType.DMA((2, peers)),
-        pltpu.SemaphoreType.DMA((len(copied),)),
-    ]
-    spans = row_groups([a.shape[0] for a in arrays], places)
-    for i, _, chunk, chunks, _, _ in spans:
-        scratch += [pltpu.VMEM((chunks, chunk, widths[i]), arrays[i].dtype)] * 4
+        pltpu.VMEM((depth, inside), bf16),
+        pltpu.VMEM((2, rows, inside), bf16),
+        pltpu.SemaphoreType.DMA((9,)),
+    ] + scatter_scratch(rows, depth)
+    spans = row_groups(arrays)
+    for i, _, chunk, chunks in spans:
+        scratch.append(pltpu.VMEM((min(RING, chunks), chunk, widths[i]), arrays[i].dtype))
+        scratch += [pltpu.VMEM((chunks, chunk, widths[i]), arrays[i].dtype)] * 2
         scratch.append(pltpu.SemaphoreType.DMA((8, chunks)))
     total = sum(a.shape[0] * w for a, w in zip(arrays, widths))
     return pl.pallas_call(
-        functools.partial(
-            line_kernel, "dp", "tensor", widths, tuple(spans), 3, tuple(copied)
+        functools.partial(line_kernel, "dp", "tensor", tuple(widths), tuple(spans)),
+        out_shape=tuple(jax.ShapeDtypeStruct((a.shape[0], w), a.dtype) for a, w in zip(arrays, widths))
+        + (
+            jax.ShapeDtypeStruct((both, widths[0]), arrays[0].dtype),
+            jax.ShapeDtypeStruct((rows, depth), f32),
         ),
-        out_shape=(
-            jax.ShapeDtypeStruct(small.shape, small.dtype),
-            jax.ShapeDtypeStruct((at, stacked[0].shape[1]), bf16),
-            jax.ShapeDtypeStruct((main.shape[0], width), bf16),
-            jax.ShapeDtypeStruct((both, widths[0]), small.dtype),
-        ),
-        in_specs=[ANYWHERE] * (len(arrays) + len(summed)),
-        out_specs=(ANYWHERE,) * 3 + (IN_VMEM,),
+        in_specs=[ANYWHERE] * (2 + len(arrays)),
+        out_specs=(ANYWHERE,) * len(arrays) + (IN_VMEM,) * 2,
         scratch_shapes=scratch,
         compiler_params=pltpu.CompilerParams(
             collective_id=identity, has_side_effects=True, vmem_limit_bytes=60 * 1024 * 1024
         ),
         cost_estimate=pl.CostEstimate(flops=0, bytes_accessed=200 * total, transcendentals=0),
         name="sum_over_line",
-    )(*arrays, *summed)
+    )(dproj, w_in, *arrays)
 
 
 def shards(
@@ -1638,7 +1696,6 @@
     grad_projected, grad_tq, grad_tk, grad_tv, grad_dl, grad_db, grad_gain = mixer_backward(
         projected, params, states, inverse, update, raw, grad_mixed
     )
-    part_normed = times_transposed(grad_projected, w_in).astype(bf16)
     grad_in = cross_rows(gathered, grad_projected).astype(bf16)
     part_gain_attn = jnp.sum(grad_in.astype(f32) * w_in.astype(f32), 1) / gain_first
     grad_ab = grad_in[:, main : main + 2 * heads].astype(f32).T
@@ -1650,7 +1707,6 @@
         grad_in,
         grad_up_weight,
         small,
-        part_normed,
         ffn_part,
         grad_down_summed,
         grad_gate_summed,
@@ -1660,31 +1716,24 @@
             grad_in,
             grad_up_weight,
             small,
-            part_normed,
-            ffn_part,
+                ffn_part,
             grad_down_summed,
             grad_gate_summed,
             grad_out_weight,
         )
     )
-    grad_normed = scatter_rows(part_normed)
     ffn_out = scatter_rows(ffn_part)
     output = (hidden + ffn_out).astype(bf16)
     gains = 2 * width + out_gain.shape[0]
-    small_summed, ffn_summed, grad_in_summed, gain_grads = sum_over_line(
-        small.reshape(smalls_rows, 128),
-        (grad_up_weight, grad_out_weight),
-        (grad_down_summed, grad_gate_summed),
-        grad_in,
-        main,
+    small_summed, grad_up_summed, grad_out_summed, grad_in_summed, gain_grads, grad_normed = sum_over_line(
+        (small.reshape(smalls_rows, 128), grad_up_weight, grad_out_weight, grad_in),
+        (128, width, width, main),
         -(-gains // (16 * 128)) * 16,
+        grad_projected,
+        w_in,
         5,
         sizes,
     )
-    large, at = [], 0
-    for a in (grad_up_weight, grad_out_weight, grad_down_summed, grad_gate_summed):
-        large.append(ffn_summed[at : at + a.shape[0]].astype(f32))
-        at += a.shape[0]
     small_summed = small_summed.reshape(-1)
     gain_grads = gain_grads.reshape(-1)
     small_parts, at = [], gains
@@ -1714,11 +1763,11 @@
         small_parts[3],
         small_parts[4],
         gain_grads[2 * width : gains],
-        large[1],
+        grad_out_summed.astype(f32),
         gain_grads[width : 2 * width],
-        large[3].T,
-        large[0].T,
-        large[2],
+        grad_gate_summed.astype(f32).T,
+        grad_up_summed.astype(f32).T,
+        grad_down_summed.astype(f32),
     )
 
 

time: 735 us -> 749 us (1.019)
  Pallas kernels: 599 us -> 623 us
  matrix products: 68.6 us -> 47.6 us
  waiting for transfers between devices: 0.62 us -> 12.7 us
    pallas_call x1, Pallas kernels: 268 us -> 292 us  [sum_over_line(): pl.pallas_call(functools.partial(line_kernel, 'dp', 'tensor', tuple(width...]
    dot_general x1 -> x0, matrix products: 21 us -> none  [times_transposed(): lax.dot_general(left, right, (((1,), (1,)), ((), ())), preferred_element_...]
    psum x1, waiting for transfers between devices: 0.01 us -> 12.6 us  [shards(): lax.psum((grad_down, grad_gate_weight), 'dp')]
  transfers between devices with their start and end apart: 4 -> 3, of which waited for: 0 -> 1; matrix products, arithmetic and copies ran while one was open for 12% -> 9% of each run, Pallas kernels for 70% -> 72%
where the time goes in v10:
time: 749 us; the launch traced here: 743 us
  Pallas kernels  623 us (83%)
  matrix products  47.6 us (6%)
  other arithmetic  29.4 us (4%)
  local copies, waits for them, and re-layouts  16.2 us (2%)
  between operations  14.5 us (2%)
  waiting for transfers between devices  12.7 us (2%)
    pallas_call x1, Pallas kernels, sum_over_line(): pl.pallas_call(functools.partial(line_kernel, 'dp', 'tensor', tuple(width...  292 us
    pallas_call x1, Pallas kernels, mixer_backward(): pl.pallas_call(functools.partial(backward_kernel, heads, key_dim, value_d...  58.9 us
    pallas_call x1, Pallas kernels, attend(): pl.pallas_call(functools.partial(attend_kernel, 'tensor'), out_shape=(jax...  52.3 us
    pallas_call x1, Pallas kernels, return_hidden(): pl.pallas_call(functools.partial(return_kernel, 'tensor'), out_shape=(jax...  52 us
    pallas_call x1, Pallas kernels, gather_project(): pl.pallas_call(functools.partial(gather_project_kernel, 'tensor'), out_sh...  47.3 us
    pallas_call x1, Pallas kernels, gather_expand(): pl.pallas_call(functools.partial(gather_expand_kernel, 'tensor'), out_sha...  42.4 us
    pallas_call x1, Pallas kernels, gather_back(): pl.pallas_call(functools.partial(gather_back_kernel, 'tensor'), out_shape...  42.2 us
    pallas_call x1, Pallas kernels, mixer_forward(): pl.pallas_call(functools.partial(forward_kernel, heads, key_dim, value_di...  35.7 us
  transfers between devices with their start and end apart: 3, of which 1 were waited for; matrix products, arithmetic and copies ran while one was open for 9% of the time, Pallas kernels for 72%

profile of v10, /device:TPU:0, one launch (start us, length us, event | category | flops | bytes accessed | tf_op | source)
XLA Modules:
  0.0 743.1 jit_solution(17207423616002437421)
XLA Ops:
  7.2 0.0 all-gather.2.cloned.1.call-start
  7.2 1.3 convert_element_type.61
  8.5 0.0 copy-start.15
  8.5 0.0 copy-start.16
  8.6 0.0 copy-start.17
  8.6 47.3 %gather_project.1 = (bf16[2048,2048]{1,0:T(8,128)(2,1)}, bf16[2048,1664]{1,0:T(8,128)(2,1)}, f32[2048,1664]{1,0:T(8,128)}) custom-call(bf16[256,2048]{1,0:T(8,128)(2,1)} %bitcast.56, f32[1,2048]{1,0:T(1,128)} %bitcast.70, bf16[2,2048]{1,0:T(2,128)(2,1)} %bitcast.85, bf16[2,2048]{1,0:T(2,128)(2,1)} %bitcast.86, bf16[2048,256]{1,0:T(8,128)(2,1)} %wq_ref.1, ...), custom_call_target="tpu_custom_call" | custom-call | bytes 1000000 | tf_op jit(solution)/shard_map/gather_project/pallas_call | solution.py:873
  55.9 0.0 all-gather.2.cloned.1.call-update
  55.9 0.0 all-reduce.6.cloned.1.call-start
  56.0 0.0 copy-done.22
  56.0 0.6 broadcast_in_dim.52
  56.7 0.7 concatenate.10.param_ref
  57.4 35.7 %mixer_forward.1 = (bf16[2048,512]{1,0:T(8,128)(2,1)}, f32[2,128,256]{2,1,0:T(8,128)}, f32[8,2,128,256]{3,2,1,0:T(8,128)}, f32[8,2,256,256]{3,2,1,0:T(8,128)}, f32[2048,512]{1,0:T(8,128)}, /*index=5*/f32[2048,512]{1,0:T(8,128)}) custom-call(f32[2048,1664]{1,0:T(8,128)} %get-tuple-element.68.proj_ref.eq_ref.ek_ref.ev_ref, f32[8,1024]{1,0:T(8,128)} %concatenate.10.param_ref, ...), custom_call_target="tpu_custom_call" | custom-call | bytes 100000000 | tf_op jit(solution)/shard_map/mixer_forward/pallas_call | solution.py:296
  93.1 52.3 %attend.1 = (f32[256,2048]{1,0:T(8,128)}, bf16[256,2048]{1,0:T(8,128)(2,1)}) custom-call(bf16[2048,512]{1,0:T(8,128)(2,1)} %get-tuple-element.69.mixed_ref, bf16[512,2048]{1,0:T(8,128)(2,1)} %w_ref.3, bf16[256,2048]{1,0:T(8,128)(2,1)} %bitcast.57, f32[1,2048]{1,0:T(1,128)} %bitcast.71), custom_call_target="tpu_custom_call" | custom-call | bytes 1000000 | tf_op jit(solution)/shard_map/attend/pallas_call | solution.py:1285
  145.4 0.0 all-gather.2.cloned.1.call-done.cot_ref
  145.4 42.4 %gather_expand.1 = (bf16[2048,2048]{1,0:T(8,128)(2,1)}, bf16[688,2048]{1,0:T(8,128)(2,1)}, bf16[688,2048]{1,0:T(8,128)(2,1)}, bf16[688,2048]{1,0:T(8,128)(2,1)}) custom-call(bf16[256,2048]{1,0:T(8,128)(2,1)} %get-tuple-element.77.x_ref, bf16[2048,2048]{1,0:T(8,128)(2,1)} %all-gather.2.cloned.1.call-done.cot_ref, bf16[688,2048]{1,0:T(8,128)(2,1)} %bitcast.58, ...), custom_call_target="tpu_custom_call" | custom-call | bytes 1000000 | tf_op jit(solution)/shard_map/gather_expand/pallas_call | solution.py:996
  187.8 10.5 %convolution_convert_fusion.1 = bf16[688,2048]{1,0:T(8,128)(2,1)} fusion(bf16[688,2048]{1,0:T(8,128)(2,1)} %get-tuple-element.83.dgate_ref, bf16[2048,2048]{1,0:T(8,128)(2,1)} %get-tuple-element.82.normed_ref), kind=kOutput, calls=%fused_computation.4 | convolution fusion | flops 5772771328 | bytes 14024704 | tf_op jit(solution)/shard_map/dot_general | solution.py:1684
  198.3 0.0 copy-done.5
  198.3 7.3 convolution_convert_fusion.2
  205.6 0.0 all-reduce.6.cloned.1.call-update
  205.6 0.0 reduce-scatter.2.cloned.1.call-start
  205.6 52.0 %return_hidden.1 = (f32[256,2048]{1,0:T(8,128)}, bf16[256,2048]{1,0:T(8,128)(2,1)}, f32[1,2048]{1,0:T(1,128)}) custom-call(bf16[688,2048]{1,0:T(8,128)(2,1)} %get-tuple-element.83.dgate_ref, bf16[688,2048]{1,0:T(8,128)(2,1)} %get-tuple-element.84.dup_ref, bf16[688,2048]{1,0:T(8,128)(2,1)} %bitcast.59, bf16[688,2048]{1,0:T(8,128)(2,1)} %bitcast.61, ...), custom_call_target="tpu_custom_call" | custom-call | bytes 1000000 | tf_op jit(solution)/shard_map/return_hidden/pallas_call | solution.py:1354
  257.7 42.2 %gather_back.1 = (bf16[2048,2048]{1,0:T(8,128)(2,1)}, f32[2048,512]{1,0:T(8,128)}, bf16[2048,2048]{1,0:T(8,128)(2,1)}, bf16[688,2048]{1,0:T(8,128)(2,1)}) custom-call(bf16[256,2048]{1,0:T(8,128)(2,1)} %get-tuple-element.85.x_ref, bf16[512,2048]{1,0:T(8,128)(2,1)} %w_ref.3, bf16[688,2048]{1,0:T(8,128)(2,1)} %get-tuple-element.86.inner_ref, ...), custom_call_target="tpu_custom_call" | custom-call | bytes 1000000 | tf_op jit(solution)/shard_map/gather_back/pallas_call | solution.py:1129
  299.8 58.9 %mixer_backward.1 = (bf16[2048,1664]{1,0:T(8,128)(2,1)}, f32[4,256]{1,0:T(4,128)}, f32[4,256]{1,0:T(4,128)}, f32[4,512]{1,0:T(4,128)}, f32[1,2]{1,0:T(1,128)}, /*index=5*/f32[1,2]{1,0:T(1,128)}, f32[1,256]{1,0:T(1,128)}) custom-call(f32[2048,1664]{1,0:T(8,128)} %get-tuple-element.68.proj_ref.eq_ref.ek_ref.ev_ref, ...), custom_call_target="tpu_custom_call" | custom-call | bytes 100000000 | tf_op jit(solution)/shard_map/mixer_backward/pallas_call | solution.py:588
  358.8 0.7 copy.46
  359.5 0.7 copy.47
  360.2 0.7 copy.48
  360.9 0.0 copy-start.19
  360.9 0.0 copy-start.20
  360.9 20.8 %multiply_reduce_fusion = (f32[2048]{0:T(1024)S(1)}, bf16[2048,1664]{1,0:T(8,128)(2,1)S(1)}) fusion(bf16[2048,1664]{1,0:T(8,128)(2,1)} %get-tuple-element.90.w_ref, bf16[2048,2048]{1,0:T(8,128)(2,1)} %get-tuple-element.72, bf16[2048,1664]{1,0:T(8,128)(2,1)} %get-tuple-element.88.dproj_ref), kind=kOutput, calls=%fused_computation | convolution fusion | flops 13975681024 | bytes 28844032 | tf_op jit(solution)/shard_map/dot_general | solution.py:654
  381.7 0.0 copy-start.4
  381.7 0.0 copy-start.9
  381.7 3.0 copy-done.4
  384.7 0.1 convert_bitcast_fusion.2
  384.8 0.3 copy.44
  385.1 0.0 copy-done.11
  385.2 0.7 concatenate.11
  385.9 0.0 copy-done.9
  385.9 9.1 %convolution_convert_fusion.3.refs_2_ = bf16[512,2048]{1,0:T(8,128)(2,1)} fusion(bf16[2048,512]{1,0:T(8,128)(2,1)S(1)} %copy-done.9, bf16[2048,2048]{1,0:T(8,128)(2,1)} %get-tuple-element.99), kind=kOutput, calls=%fused_computation.6 | convolution fusion | flops 4296015872 | bytes 12582912 | tf_op jit(solution)/shard_map/dot_general | solution.py:654
  395.0 12.6 %all-reduce.6.cloned.1.call-done = (bf16[688,2048]{1,0:T(8,128)(2,1)}, bf16[688,2048]{1,0:T(8,128)(2,1)}) async-done(((bf16[688,2048]{1,0:T(8,128)(2,1)}, bf16[688,2048]{1,0:T(8,128)(2,1)}), (bf16[688,2048]{1,0:T(8,128)(2,1)}, bf16[688,2048]{1,0:T(8,128)(2,1)})) %all-reduce.6.cloned.1.call-update) | async-done | bytes 5636112 | tf_op jit(solution)/shard_map/psum | solution.py:1685
  407.7 0.0 reduce-scatter.2.cloned.1.call-update
  407.7 1.2 copy-done
  408.9 0.3 fusion.7
  409.2 291.8 %sum_over_line.1 = (f32[144,128]{1,0:T(8,128)}, bf16[688,2048]{1,0:T(8,128)(2,1)}, bf16[512,2048]{1,0:T(8,128)(2,1)}, bf16[2048,1536]{1,0:T(8,128)(2,1)}, f32[48,128]{1,0:T(8,128)}, /*index=5*/f32[256,2048]{1,0:T(8,128)}) custom-call(bf16[2048,1664]{1,0:T(8,128)(2,1)} %get-tuple-element.88.dproj_ref, bf16[2048,1664]{1,0:T(8,128)(2,1)} %get-tuple-element.90.w_ref, ...), custom_call_target="tpu_custom_call" | custom-call | bytes 1124352000 | tf_op jit(solution)/shard_map/sum_over_line/pallas_call | solution.py:1621
  701.0 0.7 slice.83
  701.7 0.9 fusion.11
  702.6 0.6 slice.77
  703.2 0.6 slice.79
  703.8 0.8 fusion.10
  704.6 0.6 reshape.109
  705.2 0.6 reshape.110
  705.8 0.6 reshape.111
  706.4 4.3 convert_element_type.76
  710.7 5.2 convert_element_type.77
  715.9 0.5 fusion.2
  716.4 1.3 fusion.9
  717.7 0.6 slice_bitcast_fusion.2
  718.3 0.6 slice_bitcast_fusion
  718.9 0.0 slice-done.1
  718.9 2.3 slice_convert_fusion.2
  721.2 0.1 copy-done.8
  721.3 1.9 fusion.6
  723.2 4.6 slice_convert_fusion
  727.8 5.9 convert_bitcast_fusion
  733.7 2.5 fusion.8
  (49 shorter events, 0.1 us)
Async XLA Ops:
  7.2 138.2 %all-gather.2.cloned.1.call-start = ((), (), s32[]{:S(2)}) async-start(), calls=%async_computation.1 | async-start | bytes 9437184 | tf_op jit(solution)/shard_map/all_gather | solution.py:1677
  8.5 47.5 %copy-start.21 = (f32[2]{0:T(128)S(1)}, f32[2]{0:T(128)}, u32[]{:S(2)}) copy-start(f32[2]{0:T(128)} %param.33) | copy-start | bytes 28
  8.5 47.5 %copy-start.22 = (f32[2]{0:T(128)S(1)}, f32[2]{0:T(128)}, u32[]{:S(2)}) copy-start(f32[2]{0:T(128)} %param.34) | copy-start | bytes 28
  8.5 47.5 %copy-start.14 = (bf16[2048]{0:T(1024)(128)(2,1)S(1)}, bf16[2048]{0:T(1024)(128)(2,1)}, u32[]{:S(2)}) copy-start(bf16[2048]{0:T(1024)(128)(2,1)} %param.37) | copy-start | bytes 12292
  8.5 48.1 %copy-start.23 = (bf16[256]{0:T(256)(128)(2,1)S(1)}, bf16[256]{0:T(256)(128)(2,1)}, u32[]{:S(2)}) copy-start(bf16[256]{0:T(256)(128)(2,1)} %param.35) | copy-start | bytes 1540
  8.5 48.1 %copy-start.15 = (bf16[4,512]{1,0:T(4,128)(2,1)S(1)}, bf16[4,512]{1,0:T(4,128)(2,1)}, u32[]{:S(2)}) copy-start(bf16[4,512]{1,0:T(4,128)(2,1)} %param.32) | copy-start | bytes 12292
  8.5 48.1 %copy-start.16 = (bf16[4,256]{1,0:T(4,128)(2,1)S(1)}, bf16[4,256]{1,0:T(4,128)(2,1)}, u32[]{:S(2)}) copy-start(bf16[4,256]{1,0:T(4,128)(2,1)} %param.31) | copy-start | bytes 6148
  8.6 48.1 %copy-start.17 = (bf16[4,256]{1,0:T(4,128)(2,1)S(1)}, bf16[4,256]{1,0:T(4,128)(2,1)}, u32[]{:S(2)}) copy-start(bf16[4,256]{1,0:T(4,128)(2,1)} %param.30) | copy-start | bytes 6148
  55.9 351.7 %all-reduce.6.cloned.1.call-start = ((), (), s32[]{:S(2)}) async-start(), calls=%async_computation.3 | async-start | bytes 11272192 | tf_op jit(solution)/shard_map/psum | solution.py:1685
  187.8 10.5 %copy-start.3 = (bf16[2048,2048]{1,0:T(8,128)(2,1)S(1)}, bf16[2048,2048]{1,0:T(8,128)(2,1)}, u32[]{:S(2)}) copy-start(bf16[2048,2048]{1,0:T(8,128)(2,1)} %all-gather.2.cloned.1.call-done.cot_ref) | copy-start | bytes 25165828
  187.8 10.5 %copy-start.5 = (bf16[688,2048]{1,0:T(8,128)(2,1)S(1)}, bf16[688,2048]{1,0:T(8,128)(2,1)}, u32[]{:S(2)}) copy-start(bf16[688,2048]{1,0:T(8,128)(2,1)} %get-tuple-element.86.inner_ref) | copy-start | bytes 8454148
  205.6 528.1 %reduce-scatter.2.cloned.1.call-start = ((), (), s32[]{:S(2)}) async-start(), calls=%async_computation.2 | async-start | bytes 9437184 | tf_op jit(solution)/shard_map/reduce_scatter | solution.py:1374
  360.9 24.3 %copy-start.11 = (bf16[2048]{0:T(1024)(128)(2,1)S(1)}, bf16[2048]{0:T(1024)(128)(2,1)}, u32[]{:S(2)}) copy-start(bf16[2048]{0:T(1024)(128)(2,1)} %param.23) | copy-start | bytes 12292
  360.9 24.3 %copy-start.13 = (f32[1,2048]{1,0:T(1,128)S(1)}, f32[1,2048]{1,0:T(1,128)}, u32[]{:S(2)}) copy-start(f32[1,2048]{1,0:T(1,128)} %get-tuple-element.91) | copy-start | bytes 24580
  360.9 24.3 %copy-start.18 = (f32[1,256]{1,0:T(1,128)S(1)}, f32[1,256]{1,0:T(1,128)}, u32[]{:S(2)}) copy-start(f32[1,256]{1,0:T(1,128)} %get-tuple-element.92) | copy-start | bytes 3076
  360.9 24.3 %copy-start.19 = (f32[1,2]{1,0:T(1,128)S(1)}, f32[1,2]{1,0:T(1,128)}, u32[]{:S(2)}) copy-start(f32[1,2]{1,0:T(1,128)} %get-tuple-element.96) | copy-start | bytes 28
  360.9 24.3 %copy-start.20 = (f32[1,2]{1,0:T(1,128)S(1)}, f32[1,2]{1,0:T(1,128)}, u32[]{:S(2)}) copy-start(f32[1,2]{1,0:T(1,128)} %get-tuple-element.97) | copy-start | bytes 28
  381.7 3.0 copy-start.4
  381.7 4.2 copy-start.9
  407.7 1.2 copy-start
  706.4 12.5 %slice-start = ((s8[6291456]{0:T(1024)(128)(4,1)}), s8[4194304]{0:T(1024)(128)(4,1)S(1)}, s32[]{:S(2)}) async-start(s8[6291456]{0:T(1024)(128)(4,1)} %bitcast.62), calls=%async_computation.4 | async-start | bytes 8388608
  710.7 5.2 copy-start.2
  710.7 5.2 copy-start.10
  710.7 8.2 %slice-start.1 = ((s8[6291456]{0:T(1024)(128)(4,1)}), s8[2097152]{0:T(1024)(128)(4,1)S(1)}, s32[]{:S(2)}) async-start(s8[6291456]{0:T(1024)(128)(4,1)} %bitcast.62), calls=%async_computation.5 | async-start | bytes 4194304
  715.9 1.9 copy-start.12
  718.9 2.4 copy-start.8
  723.2 4.6 copy-start.6
  723.2 4.6 copy-start.7
  727.8 5.9 copy-start.1
Sparse Core Ops, SparseCore 0:
  56.1 61.0 all-gather.1
  205.7 201.8 all-reduce.5
  411.1 93.6 reduce-scatter.1

commit v11 on v10

--- a/solution.py
+++ b/solution.py
@@ -1166,7 +1166,7 @@
     diagonal = along_x + along_y - me
     if tick is None:
         greet(axis, (other, along_x, along_y))
-        tick = lambda: None
+        tick = lambda times: None
     shift = other - me
     first, second = pl.ds(0, half), pl.ds(half, half)
     goals = (diagonal, along_x, along_y, me)
@@ -1190,35 +1190,36 @@
         mine[r] = (mine[r].astype(f32) + theirs[r].astype(f32)).astype(bf16)
 
     theirs_of(0)
-    tick()
+    tick(1)
     product(goals[0], mine.at[0])
     pair_sum(0)
     far_x = begin(mine.at[0, first, :], in_dx, along_x)
     far_y = begin(mine.at[0, second, :], in_dy, along_y)
-    tick()
+    tick(1)
     theirs_of(1)
-    tick()
+    tick(1)
     product(goals[1], mine.at[1])
-    tick()
+    tick(1)
     theirs_of(2)
     pair_sum(1)
     near_x0 = begin(mine.at[1, first, :], in_x.at[first, :], along_x)
-    tick()
+    tick(1)
     product(goals[2], mine.at[2])
     pair_sum(2)
     near_y1 = begin(mine.at[2, second, :], in_y.at[second, :], along_y)
-    tick()
+    tick(1)
     theirs_of(3)
-    tick()
+    tick(4)
     far_x.wait_recv()
     mine[2, first, :] = (mine[2, first, :].astype(f32) + in_dx[...].astype(f32)).astype(bf16)
     near_y0 = begin(mine.at[2, first, :], in_y.at[first, :], along_y)
     far_y.wait_recv()
     mine[1, second, :] = (mine[1, second, :].astype(f32) + in_dy[...].astype(f32)).astype(bf16)
     near_x1 = begin(mine.at[1, second, :], in_x.at[second, :], along_x)
+    tick(1)
     product(goals[3], mine.at[3])
+    tick(9)
     swaps[3].wait_recv()
-    tick()
     for at, near_x, near_y in ((first, near_x0, near_y0), (second, near_x1, near_y1)):
         near_x.wait_recv()
         near_y.wait_recv()
@@ -1229,7 +1230,7 @@
             + in_x[at, :].astype(f32)
             + in_y[at, :].astype(f32),
         )
-        tick()
+        tick(1)
     for copy in swaps + copies:
         copy.wait_send()
 
@@ -1388,7 +1389,7 @@
             groups.append((i, 0, CHUNK, whole))
         if a.shape[0] - whole * CHUNK > 0:
             groups.append((i, whole * CHUNK, a.shape[0] - whole * CHUNK, 1))
-    lead = next(k for k, group in enumerate(groups) if group[0] == 1)
+    lead = next(k for k, group in enumerate(groups) if group[0] == len(arrays) - 1)
     return [groups[lead]] + groups[:lead] + groups[lead + 1 :]
 
 
@@ -1506,18 +1507,21 @@
     _, lead, _, _, _, _, _, _, lead_first, lead_second = groups[0]
     done = []
 
-    def tick():
-        k = len(done)
-        done.append(k)
-        if k > lead:
-            return
+    def tick(times):
+        low = len(done)
+        high = min(low + times, lead)
+        done.extend(range(low, high))
 
         @pl.when(inner)
         def _():
-            if k < lead:
-                lead_first(k)
-            if k > 0:
-                lead_second(k - 1)
+            def both(c):
+                lead_first(c)
+
+                @pl.when(c > 0)
+                def _():
+                    lead_second(c - 1)
+
+            each(low, high, both)
 
     rows, depth = normed_ref.shape
     where = []
@@ -1552,8 +1556,7 @@
         normed_ref[at, :] = value
 
     scatter_parts(cross, product, finish, *scattering, tick=tick)
-    while len(done) <= lead:
-        tick()
+    tick(lead)
 
     @pl.when(jnp.logical_not(inner))
     def _():
@@ -1565,18 +1568,22 @@
 
     @pl.when(inner)
     def _():
-        for is_small, chunks, _, _, _, _, _, keep, first, second in groups[1:]:
-            first(0)
-
-            def both(c, first=first, second=second):
-                first(c + 1)
-                second(c)
-
-            each(0, chunks - 1, both)
-            second(chunks - 1)
-            if is_small:
-                each(0, chunks, lambda c: keep(c).wait())
+        for k in range(1, len(groups) + 1):
+            before = groups[k - 1]
+            if k < len(groups):
+                _, chunks, _, _, _, _, _, _, first, second = groups[k]
+                first(0)
+            before[9](before[1] - 1)
+            if before[0]:
+                each(0, before[1], lambda c: before[7](c).wait())
                 spread_all()
+            if k < len(groups):
+
+                def both(c, first=first, second=second):
+                    first(c + 1)
+                    second(c)
+
+                each(0, chunks - 1, both)
         for is_small, chunks, _, _, _, middle, outward, keep, _, _ in groups:
 
             def settle(c):
@@ -1681,7 +1688,8 @@
         normed_ffn, grad_gathered, gate_rows, up_rows, w_ffn_down, 2, sizes
     )
     grad_down = jnp.dot(inner, grad_gathered, preferred_element_type=f32).astype(bf16)
-    grad_gate_weight = jnp.dot(grad_gate_rows, gathered_ffn, preferred_element_type=f32).astype(bf16)
+    cut = grad_gate_rows.shape[0] * 7 // 8 // 16 * 16
+    grad_gate_weight = jnp.dot(grad_gate_rows[:cut], gathered_ffn, preferred_element_type=f32).astype(bf16)
     grad_down_summed, grad_gate_summed = lax.psum((grad_down, grad_gate_weight), "dp")
     grad_gate_rows, grad_up_rows, inner, grad_down, grad_gate_weight = lax.optimization_barrier(
         (grad_gate_rows, grad_up_rows, inner, grad_down, grad_gate_weight)
@@ -1693,6 +1701,7 @@
         grad_attended, w_out, inner, w_ffn_down, grad_up_rows, gathered_ffn, 4, sizes
     )
     grad_out_weight = cross_rows(mixed, grad_attended).astype(bf16)
+    grad_gate_rest = jnp.dot(grad_gate_rows[cut:], gathered_ffn, preferred_element_type=f32).astype(bf16)
     grad_projected, grad_tq, grad_tk, grad_tv, grad_dl, grad_db, grad_gain = mixer_backward(
         projected, params, states, inverse, update, raw, grad_mixed
     )
@@ -1706,6 +1715,7 @@
     (
         grad_in,
         grad_up_weight,
+        grad_gate_rest,
         small,
         ffn_part,
         grad_down_summed,
@@ -1715,6 +1725,7 @@
         (
             grad_in,
             grad_up_weight,
+            grad_gate_rest,
             small,
                 ffn_part,
             grad_down_summed,
@@ -1725,9 +1736,9 @@
     ffn_out = scatter_rows(ffn_part)
     output = (hidden + ffn_out).astype(bf16)
     gains = 2 * width + out_gain.shape[0]
-    small_summed, grad_up_summed, grad_out_summed, grad_in_summed, gain_grads, grad_normed = sum_over_line(
-        (small.reshape(smalls_rows, 128), grad_up_weight, grad_out_weight, grad_in),
-        (128, width, width, main),
+    small_summed, grad_up_summed, grad_rest_summed, grad_out_summed, grad_in_summed, gain_grads, grad_normed = sum_over_line(
+        (small.reshape(smalls_rows, 128), grad_up_weight, grad_gate_rest, grad_out_weight, grad_in),
+        (128, width, width, width, main),
         -(-gains // (16 * 128)) * 16,
         grad_projected,
         w_in,
@@ -1765,7 +1776,7 @@
         gain_grads[2 * width : gains],
         grad_out_summed.astype(f32),
         gain_grads[width : 2 * width],
-        grad_gate_summed.astype(f32).T,
+        jnp.concatenate([grad_gate_summed, grad_rest_summed], axis=0).astype(f32).T,
         grad_up_summed.astype(f32).T,
         grad_down_summed.astype(f32),
     )

time: 749 us -> 727 us (0.971)
  Pallas kernels: 623 us -> 607 us
  waiting for transfers between devices: 12.7 us -> 0.07 us
    pallas_call x1, Pallas kernels: 292 us -> 276 us  [sum_over_line(): pl.pallas_call(functools.partial(line_kernel, 'dp', 'tensor', tuple(width...]
    psum x1, waiting for transfers between devices: 12.6 us -> 0.01 us  [shards(): lax.psum((grad_down, grad_gate_weight), 'dp')]
    dot_general x1 -> x2, matrix products: 10.5 us -> 16.1 us  [the longest x1 10.3 us: shards(): jnp.dot(grad_gate_rows[:cut], gathered_ffn, preferred_element_type=f32)]
  transfers between devices with their start and end apart: 3 -> 3, of which waited for: 1 -> 0; matrix products, arithmetic and copies ran while one was open for 9% -> 10% of each run, Pallas kernels for 72% -> 72%
where the time goes in v11:
time: 727 us; the launch traced here: 720 us
  Pallas kernels  607 us (83%)
  matrix products  53.3 us (7%)
  other arithmetic  29.2 us (4%)
  local copies, waits for them, and re-layouts  15.9 us (2%)
  between operations  14.5 us (2%)
    pallas_call x1, Pallas kernels, sum_over_line(): pl.pallas_call(functools.partial(line_kernel, 'dp', 'tensor', tuple(width...  276 us
    pallas_call x1, Pallas kernels, mixer_backward(): pl.pallas_call(functools.partial(backward_kernel, heads, key_dim, value_d...  58.9 us
    pallas_call x1, Pallas kernels, attend(): pl.pallas_call(functools.partial(attend_kernel, 'tensor'), out_shape=(jax...  52.3 us
    pallas_call x1, Pallas kernels, return_hidden(): pl.pallas_call(functools.partial(return_kernel, 'tensor'), out_shape=(jax...  52.1 us
    pallas_call x1, Pallas kernels, gather_project(): pl.pallas_call(functools.partial(gather_project_kernel, 'tensor'), out_sh...  47.3 us
    pallas_call x1, Pallas kernels, gather_expand(): pl.pallas_call(functools.partial(gather_expand_kernel, 'tensor'), out_sha...  42.4 us
    pallas_call x1, Pallas kernels, gather_back(): pl.pallas_call(functools.partial(gather_back_kernel, 'tensor'), out_shape...  42.2 us
    pallas_call x1, Pallas kernels, mixer_forward(): pl.pallas_call(functools.partial(forward_kernel, heads, key_dim, value_di...  35.7 us
  transfers between devices with their start and end apart: 3, of which 0 were waited for; matrix products, arithmetic and copies ran while one was open for 10% of the time, Pallas kernels for 72%

profile of v11, /device:TPU:0, one launch (start us, length us, event | category | flops | bytes accessed | tf_op | source)
XLA Modules:
  0.0 720.5 jit_solution(3141884054945392012)
XLA Ops:
  7.2 0.0 all-gather.2.cloned.1.call-start
  7.2 1.3 convert_element_type.64
  8.5 0.0 copy-start.16
  8.5 0.0 copy-start.17
  8.6 0.0 copy-start.18
  8.6 47.3 %gather_project.1 = (bf16[2048,2048]{1,0:T(8,128)(2,1)}, bf16[2048,1664]{1,0:T(8,128)(2,1)}, f32[2048,1664]{1,0:T(8,128)}) custom-call(bf16[256,2048]{1,0:T(8,128)(2,1)} %bitcast.56, f32[1,2048]{1,0:T(1,128)} %bitcast.70, bf16[2,2048]{1,0:T(2,128)(2,1)} %bitcast.85, bf16[2,2048]{1,0:T(2,128)(2,1)} %bitcast.86, bf16[2048,256]{1,0:T(8,128)(2,1)} %wq_ref.1, ...), custom_call_target="tpu_custom_call" | custom-call | bytes 1000000 | tf_op jit(solution)/shard_map/gather_project/pallas_call | solution.py:873
  55.9 0.0 all-gather.2.cloned.1.call-update
  55.9 0.0 all-reduce.6.cloned.1.call-start
  56.0 0.0 copy-done.22
  56.0 0.0 copy-done.23
  56.0 0.0 copy-done.15
  56.0 0.6 broadcast_in_dim.52
  56.7 0.7 concatenate.13.param_ref
  57.3 35.7 %mixer_forward.1 = (bf16[2048,512]{1,0:T(8,128)(2,1)}, f32[2,128,256]{2,1,0:T(8,128)}, f32[8,2,128,256]{3,2,1,0:T(8,128)}, f32[8,2,256,256]{3,2,1,0:T(8,128)}, f32[2048,512]{1,0:T(8,128)}, /*index=5*/f32[2048,512]{1,0:T(8,128)}) custom-call(f32[2048,1664]{1,0:T(8,128)} %get-tuple-element.70.proj_ref.eq_ref.ek_ref.ev_ref, f32[8,1024]{1,0:T(8,128)} %concatenate.13.param_ref, ...), custom_call_target="tpu_custom_call" | custom-call | bytes 100000000 | tf_op jit(solution)/shard_map/mixer_forward/pallas_call | solution.py:296
  93.1 52.3 %attend.1 = (f32[256,2048]{1,0:T(8,128)}, bf16[256,2048]{1,0:T(8,128)(2,1)}) custom-call(bf16[2048,512]{1,0:T(8,128)(2,1)} %get-tuple-element.71.mixed_ref, bf16[512,2048]{1,0:T(8,128)(2,1)} %w_ref.3, bf16[256,2048]{1,0:T(8,128)(2,1)} %bitcast.57, f32[1,2048]{1,0:T(1,128)} %bitcast.71), custom_call_target="tpu_custom_call" | custom-call | bytes 1000000 | tf_op jit(solution)/shard_map/attend/pallas_call | solution.py:1286
  145.4 0.0 all-gather.2.cloned.1.call-done.cot_ref
  145.4 42.4 %gather_expand.1 = (bf16[2048,2048]{1,0:T(8,128)(2,1)}, bf16[688,2048]{1,0:T(8,128)(2,1)}, bf16[688,2048]{1,0:T(8,128)(2,1)}, bf16[688,2048]{1,0:T(8,128)(2,1)}) custom-call(bf16[256,2048]{1,0:T(8,128)(2,1)} %get-tuple-element.79.x_ref, bf16[2048,2048]{1,0:T(8,128)(2,1)} %all-gather.2.cloned.1.call-done.cot_ref, bf16[688,2048]{1,0:T(8,128)(2,1)} %bitcast.58, ...), custom_call_target="tpu_custom_call" | custom-call | bytes 1000000 | tf_op jit(solution)/shard_map/gather_expand/pallas_call | solution.py:996
  187.8 10.3 %convolution_convert_fusion.2 = bf16[592,2048]{1,0:T(8,128)(2,1)} fusion(bf16[2048,2048]{1,0:T(8,128)(2,1)} %get-tuple-element.84.normed_ref, bf16[688,2048]{1,0:T(8,128)(2,1)} %get-tuple-element.85.dgate_ref), kind=kOutput, calls=%fused_computation.5 | convolution fusion | flops 4967268352 | bytes 13238272 | tf_op jit(solution)/shard_map/dot_general | solution.py:1692
  198.1 7.3 %convolution_convert_fusion.1 = bf16[688,2048]{1,0:T(8,128)(2,1)} fusion(bf16[688,2048]{1,0:T(8,128)(2,1)S(1)} %copy-done.5, bf16[2048,2048]{1,0:T(8,128)(2,1)S(1)} %copy-done.3), kind=kOutput, calls=%fused_computation.4 | convolution fusion | flops 5772771328 | bytes 14024704 | tf_op jit(solution)/shard_map/dot_general | solution.py:1690
  205.4 0.0 all-reduce.6.cloned.1.call-update
  205.4 0.0 reduce-scatter.2.cloned.1.call-start
  205.5 52.1 %return_hidden.1 = (f32[256,2048]{1,0:T(8,128)}, bf16[256,2048]{1,0:T(8,128)(2,1)}, f32[1,2048]{1,0:T(1,128)}) custom-call(bf16[688,2048]{1,0:T(8,128)(2,1)} %get-tuple-element.85.dgate_ref, bf16[688,2048]{1,0:T(8,128)(2,1)} %get-tuple-element.86.dup_ref, bf16[688,2048]{1,0:T(8,128)(2,1)} %bitcast.59, bf16[688,2048]{1,0:T(8,128)(2,1)} %bitcast.61, ...), custom_call_target="tpu_custom_call" | custom-call | bytes 1000000 | tf_op jit(solution)/shard_map/return_hidden/pallas_call | solution.py:1355
  257.6 42.2 %gather_back.1 = (bf16[2048,2048]{1,0:T(8,128)(2,1)}, f32[2048,512]{1,0:T(8,128)}, bf16[2048,2048]{1,0:T(8,128)(2,1)}, bf16[688,2048]{1,0:T(8,128)(2,1)}) custom-call(bf16[256,2048]{1,0:T(8,128)(2,1)} %get-tuple-element.87.x_ref, bf16[512,2048]{1,0:T(8,128)(2,1)} %w_ref.3, bf16[688,2048]{1,0:T(8,128)(2,1)} %get-tuple-element.88.inner_ref, ...), custom_call_target="tpu_custom_call" | custom-call | bytes 1000000 | tf_op jit(solution)/shard_map/gather_back/pallas_call | solution.py:1129
  299.8 58.9 %mixer_backward.1 = (bf16[2048,1664]{1,0:T(8,128)(2,1)}, f32[4,256]{1,0:T(4,128)}, f32[4,256]{1,0:T(4,128)}, f32[4,512]{1,0:T(4,128)}, f32[1,2]{1,0:T(1,128)}, /*index=5*/f32[1,2]{1,0:T(1,128)}, f32[1,256]{1,0:T(1,128)}) custom-call(f32[2048,1664]{1,0:T(8,128)} %get-tuple-element.70.proj_ref.eq_ref.ek_ref.ev_ref, ...), custom_call_target="tpu_custom_call" | custom-call | bytes 100000000 | tf_op jit(solution)/shard_map/mixer_backward/pallas_call | solution.py:588
  358.7 0.7 copy.46
  359.4 0.7 copy.47
  360.1 0.7 copy.48
  360.8 0.0 copy-start.20
  360.8 0.0 copy-start.21
  360.8 20.8 %multiply_reduce_fusion = (f32[2048]{0:T(1024)S(1)}, bf16[2048,1664]{1,0:T(8,128)(2,1)S(1)}) fusion(bf16[2048,1664]{1,0:T(8,128)(2,1)} %get-tuple-element.92.w_ref, bf16[2048,2048]{1,0:T(8,128)(2,1)} %get-tuple-element.74, bf16[2048,1664]{1,0:T(8,128)(2,1)} %get-tuple-element.90.dproj_ref), kind=kOutput, calls=%fused_computation | convolution fusion | flops 13975681024 | bytes 28844032 | tf_op jit(solution)/shard_map/dot_general | solution.py:654
  381.7 2.8 copy-done.4
  384.5 0.1 convert_bitcast_fusion.2
  384.5 0.3 copy.44
  384.9 0.0 copy-done.12
  384.9 0.7 concatenate.14
  385.7 5.9 convolution_convert_fusion.4.refs_2_
  391.5 9.1 %convolution_convert_fusion.3.refs_3_ = bf16[512,2048]{1,0:T(8,128)(2,1)} fusion(bf16[2048,512]{1,0:T(8,128)(2,1)S(1)} %copy-done.9, bf16[2048,2048]{1,0:T(8,128)(2,1)} %get-tuple-element.101), kind=kOutput, calls=%fused_computation.6 | convolution fusion | flops 4296015872 | bytes 12582912 | tf_op jit(solution)/shard_map/dot_general | solution.py:654
  400.6 0.0 reduce-scatter.2.cloned.1.call-update
  400.6 1.2 copy-done
  401.8 0.3 fusion.8
  402.1 276.3 %sum_over_line.1 = (f32[144,128]{1,0:T(8,128)}, bf16[688,2048]{1,0:T(8,128)(2,1)}, bf16[96,2048]{1,0:T(8,128)(2,1)}, bf16[512,2048]{1,0:T(8,128)(2,1)}, bf16[204...) custom-call(bf16[2048,1664]{1,0:T(8,128)(2,1)} %get-tuple-element.90.dproj_ref, ...), custom_call_target="tpu_custom_call" | custom-call | bytes 1163673600 | tf_op jit(solution)/shard_map/sum_over_line/pallas_call | solution.py:1628
  678.5 0.7 slice.91
  679.2 0.6 reshape.111
  679.8 0.8 fusion.12
  680.6 0.6 reshape.110
  681.2 0.6 reshape.109
  681.8 0.9 fusion.13
  682.7 0.6 slice.87
  683.3 0.6 slice.85
  683.9 4.3 convert_element_type.80
  688.2 5.2 convert_element_type.81
  693.4 0.0 copy-done.11
  693.4 0.5 fusion.3
  693.9 1.3 fusion.11
  695.2 0.6 slice_bitcast_fusion.2
  695.8 0.6 slice_bitcast_fusion
  696.4 2.3 slice_convert_fusion.2
  698.7 0.1 copy-done.8
  698.8 1.9 fusion.7
  700.7 4.6 slice_convert_fusion
  705.3 0.0 copy-start.1
  705.3 5.7 convert_bitcast_fusion
  711.0 0.0 copy-done.1
  711.0 2.5 fusion.9
  (52 shorter events, 0.1 us)
Async XLA Ops:
  7.2 138.2 %all-gather.2.cloned.1.call-start = ((), (), s32[]{:S(2)}) async-start(), calls=%async_computation.1 | async-start | bytes 9437184 | tf_op jit(solution)/shard_map/all_gather | solution.py:1684
  8.5 47.5 %copy-start.22 = (f32[2]{0:T(128)S(1)}, f32[2]{0:T(128)}, u32[]{:S(2)}) copy-start(f32[2]{0:T(128)} %param.33) | copy-start | bytes 28
  8.5 47.5 %copy-start.23 = (f32[2]{0:T(128)S(1)}, f32[2]{0:T(128)}, u32[]{:S(2)}) copy-start(f32[2]{0:T(128)} %param.34) | copy-start | bytes 28
  8.5 47.5 %copy-start.15 = (bf16[2048]{0:T(1024)(128)(2,1)S(1)}, bf16[2048]{0:T(1024)(128)(2,1)}, u32[]{:S(2)}) copy-start(bf16[2048]{0:T(1024)(128)(2,1)} %param.37) | copy-start | bytes 12292
  8.5 48.1 %copy-start.24 = (bf16[256]{0:T(256)(128)(2,1)S(1)}, bf16[256]{0:T(256)(128)(2,1)}, u32[]{:S(2)}) copy-start(bf16[256]{0:T(256)(128)(2,1)} %param.35) | copy-start | bytes 1540
  8.5 48.1 %copy-start.16 = (bf16[4,512]{1,0:T(4,128)(2,1)S(1)}, bf16[4,512]{1,0:T(4,128)(2,1)}, u32[]{:S(2)}) copy-start(bf16[4,512]{1,0:T(4,128)(2,1)} %param.32) | copy-start | bytes 12292
  8.5 48.1 %copy-start.17 = (bf16[4,256]{1,0:T(4,128)(2,1)S(1)}, bf16[4,256]{1,0:T(4,128)(2,1)}, u32[]{:S(2)}) copy-start(bf16[4,256]{1,0:T(4,128)(2,1)} %param.31) | copy-start | bytes 6148
  8.6 48.1 %copy-start.18 = (bf16[4,256]{1,0:T(4,128)(2,1)S(1)}, bf16[4,256]{1,0:T(4,128)(2,1)}, u32[]{:S(2)}) copy-start(bf16[4,256]{1,0:T(4,128)(2,1)} %param.30) | copy-start | bytes 6148
  55.9 344.7 %all-reduce.6.cloned.1.call-start = ((), (), s32[]{:S(2)}) async-start(), calls=%async_computation.3 | async-start | bytes 10485760 | tf_op jit(solution)/shard_map/psum | solution.py:1693
  187.8 10.3 %copy-start.3 = (bf16[2048,2048]{1,0:T(8,128)(2,1)S(1)}, bf16[2048,2048]{1,0:T(8,128)(2,1)}, u32[]{:S(2)}) copy-start(bf16[2048,2048]{1,0:T(8,128)(2,1)} %all-gather.2.cloned.1.call-done.cot_ref) | copy-start | bytes 25165828
  187.8 10.3 %copy-start.5 = (bf16[688,2048]{1,0:T(8,128)(2,1)S(1)}, bf16[688,2048]{1,0:T(8,128)(2,1)}, u32[]{:S(2)}) copy-start(bf16[688,2048]{1,0:T(8,128)(2,1)} %get-tuple-element.88.inner_ref) | copy-start | bytes 8454148
  205.4 505.6 %reduce-scatter.2.cloned.1.call-start = ((), (), s32[]{:S(2)}) async-start(), calls=%async_computation.2 | async-start | bytes 9437184 | tf_op jit(solution)/shard_map/reduce_scatter | solution.py:1375
  360.8 24.1 %copy-start.12 = (bf16[2048]{0:T(1024)(128)(2,1)S(1)}, bf16[2048]{0:T(1024)(128)(2,1)}, u32[]{:S(2)}) copy-start(bf16[2048]{0:T(1024)(128)(2,1)} %param.23) | copy-start | bytes 12292
  360.8 24.1 %copy-start.14 = (f32[1,2048]{1,0:T(1,128)S(1)}, f32[1,2048]{1,0:T(1,128)}, u32[]{:S(2)}) copy-start(f32[1,2048]{1,0:T(1,128)} %get-tuple-element.93) | copy-start | bytes 24580
  360.8 24.1 %copy-start.19 = (f32[1,256]{1,0:T(1,128)S(1)}, f32[1,256]{1,0:T(1,128)}, u32[]{:S(2)}) copy-start(f32[1,256]{1,0:T(1,128)} %get-tuple-element.94) | copy-start | bytes 3076
  360.8 24.1 %copy-start.20 = (f32[1,2]{1,0:T(1,128)S(1)}, f32[1,2]{1,0:T(1,128)}, u32[]{:S(2)}) copy-start(f32[1,2]{1,0:T(1,128)} %get-tuple-element.98) | copy-start | bytes 28
  360.8 24.1 %copy-start.21 = (f32[1,2]{1,0:T(1,128)S(1)}, f32[1,2]{1,0:T(1,128)}, u32[]{:S(2)}) copy-start(f32[1,2]{1,0:T(1,128)} %get-tuple-element.99) | copy-start | bytes 28
  381.7 2.8 copy-start.4
  385.7 5.9 copy-start.9
  400.6 1.2 copy-start
  683.9 12.5 %slice-start = ((s8[6291456]{0:T(1024)(128)(4,1)}), s8[4194304]{0:T(1024)(128)(4,1)S(1)}, s32[]{:S(2)}) async-start(s8[6291456]{0:T(1024)(128)(4,1)} %bitcast.62), calls=%async_computation.4 | async-start | bytes 8388608
  688.2 5.2 copy-start.2
  688.2 5.2 copy-start.11
  688.2 8.2 %slice-start.1 = ((s8[6291456]{0:T(1024)(128)(4,1)}), s8[2097152]{0:T(1024)(128)(4,1)S(1)}, s32[]{:S(2)}) async-start(s8[6291456]{0:T(1024)(128)(4,1)} %bitcast.62), calls=%async_computation.5 | async-start | bytes 4194304
  693.4 1.8 copy-start.13
  696.4 2.4 copy-start.8
  700.7 4.6 copy-start.6
  700.7 4.6 copy-start.7
  700.7 4.6 copy-start.10
  705.3 5.7 copy-start.1
Sparse Core Ops, SparseCore 0:
  56.1 60.9 all-gather.1
  205.5 189.2 all-reduce.5
  400.8 93.0 reduce-scatter.1

commit v12 on v11

--- a/solution.py
+++ b/solution.py
@@ -898,11 +898,13 @@
 def gather_expand_kernel(
     axis,
     x_ref,
-    cot_ref,
+    mine_ref,
+    theirs_ref,
     wg_ref,
     wu_ref,
     wd_ref,
     all_ref,
+    cot_ref,
     inner_ref,
     dgate_ref,
     dup_ref,
@@ -929,9 +931,12 @@
         pltpu.make_async_copy(src, dst, load.at[k])
         for k, (src, dst) in enumerate(((wg_ref, w_gate), (wu_ref, w_up), (wd_ref, w_down)))
     ]
-    fetches = [
-        pltpu.make_async_copy(rows_at(cot_ref, order[i], rows), cots.at[i % 2], fetch.at[i])
-        for i in range(8)
+    sources = [
+        rows_at(mine_ref if i in (0, 2, 3, 6) else theirs_ref, order[i] // 2, rows) for i in range(8)
+    ]
+    fetches = [pltpu.make_async_copy(sources[i], cots.at[i % 2], fetch.at[i]) for i in range(8)]
+    saves = [
+        pltpu.make_async_copy(sources[i], rows_at(cot_ref, order[i], rows), fetch.at[8 + i]) for i in range(8)
     ]
     for copy in (loads[2], fetches[0], loads[0], loads[1]):
         copy.start()
@@ -975,11 +980,26 @@
     forward(1)
     for i in range(2, 8):
         backward(i)
+    for copy in saves:
+        copy.start()
     for i in range(2, 8):
         forward(i)
-    for copy in keeps + outs[6] + outs[7]:
+    for copy in saves + keeps + outs[6] + outs[7]:
         copy.wait()
     finish()
+
+
+def gather_sides(x, sizes):
+    if not square(sizes):
+        return (lax.all_gather(x, "tensor", axis=0, tiled=True),)
+    sides = [[0, 2, 4, 6], [1, 3, 5, 7]]
+    return (lax.all_gather(x, "tensor", axis=0, tiled=True, axis_index_groups=sides),)
+
+
+def other_side(mine, sizes):
+    if not square(sizes):
+        return mine
+    return mine + (lax.ppermute(mine[0], "tensor", [(i, i + 1 - 2 * (i % 2)) for i in range(8)]),)
 
 
 def gather_expand(x, cotangent, gate_rows, up_rows, down_rows, identity, sizes):
@@ -988,16 +1008,17 @@
     if not square(sizes):
         gathered = lax.all_gather(x, "tensor", axis=0, tiled=True)
         gate, up = times_transposed(gate_rows, gathered), times_transposed(up_rows, gathered)
-        dinner = times_transposed(down_rows, cotangent)
+        dinner = times_transposed(down_rows, cotangent[0])
         sig = sigmoid(gate)
         dgate = dinner * up * sig * (1.0 + gate * (1.0 - sig))
-        return gathered, (gate * sig * up).astype(bf16), dgate.astype(bf16), (dinner * gate * sig).astype(bf16)
+        inner = (gate * sig * up).astype(bf16)
+        return gathered, cotangent[0], inner, dgate.astype(bf16), (dinner * gate * sig).astype(bf16)
     by_token = jax.ShapeDtypeStruct((units, 8 * rows), bf16)
     return pl.pallas_call(
         functools.partial(gather_expand_kernel, "tensor"),
-        out_shape=(jax.ShapeDtypeStruct((8 * rows, depth), bf16), by_token, by_token, by_token),
-        in_specs=[ANYWHERE] * 5,
-        out_specs=(ANYWHERE,) * 4,
+        out_shape=(jax.ShapeDtypeStruct((8 * rows, depth), bf16),) * 2 + (by_token,) * 3,
+        in_specs=[ANYWHERE] * 6,
+        out_specs=(ANYWHERE,) * 5,
         scratch_shapes=[
             pltpu.VMEM((8 * rows, depth), bf16),
             pltpu.VMEM((units, depth), bf16),
@@ -1010,13 +1031,13 @@
             pltpu.VMEM((2, units, rows), bf16),
         ]
         + gather_scratch(rows, depth)
-        + [pltpu.SemaphoreType.DMA((3,)), pltpu.SemaphoreType.DMA((8,)), pltpu.SemaphoreType.DMA((3, 8))],
+        + [pltpu.SemaphoreType.DMA((3,)), pltpu.SemaphoreType.DMA((16,)), pltpu.SemaphoreType.DMA((3, 8))],
         compiler_params=pltpu.CompilerParams(
             collective_id=identity, has_side_effects=True, vmem_limit_bytes=60 * 1024 * 1024
         ),
         cost_estimate=pl.CostEstimate(flops=0, bytes_accessed=1_000_000, transcendentals=0),
         name="gather_expand",
-    )(x, cotangent, gate_rows, up_rows, down_rows)
+    )(x, *cotangent, gate_rows, up_rows, down_rows)
 
 
 def gather_back_kernel(
@@ -1026,6 +1047,7 @@
     inner_ref,
     down_ref,
     dup_ref,
+    rest_ref,
     normed_ref,
     all_ref,
     y_ref,
@@ -1049,10 +1071,20 @@
     out,
 ):
     rows, depth = x_ref.shape
+    units = inner.shape[0]
+    rest = dup.shape[0] - units
     ready, finish, _ = gather_parts(axis, x_ref, held, send, recv, local)
     loads = [
         pltpu.make_async_copy(src, dst, load.at[k])
-        for k, (src, dst) in enumerate(((w_ref, weights), (inner_ref, inner), (down_ref, down), (dup_ref, dup)))
+        for k, (src, dst) in enumerate(
+            (
+                (w_ref, weights),
+                (inner_ref, inner),
+                (down_ref, down),
+                (dup_ref, dup.at[pl.ds(0, units), :]),
+                (rest_ref.at[pl.ds(units - rest, rest), :], dup.at[pl.ds(units, rest), :]),
+            )
+        )
     ]
     for copy in loads:
         copy.start()
@@ -1118,13 +1150,15 @@
     finish()
 
 
-def gather_back(x, w, inner, down, dup, normed, identity, sizes):
+def gather_back(x, w, inner, down, dup, dgate, cut, normed, identity, sizes):
     rows, depth = x.shape
     width, units = w.shape[0], inner.shape[0]
+    tall = 2 * units - cut
     if not square(sizes):
         gathered = lax.all_gather(x, "tensor", axis=0, tiled=True)
         part = cross_rows(inner, down).astype(bf16)
-        dw = jnp.dot(dup, normed, preferred_element_type=f32).astype(bf16)
+        both = jnp.concatenate([dup, dgate[cut:]], axis=0)
+        dw = jnp.dot(both, normed, preferred_element_type=f32).astype(bf16)
         return gathered, times_transposed(gathered, w), part, dw
     return pl.pallas_call(
         functools.partial(gather_back_kernel, "tensor"),
@@ -1132,9 +1166,9 @@
             jax.ShapeDtypeStruct((8 * rows, depth), bf16),
             jax.ShapeDtypeStruct((8 * rows, width), f32),
             jax.ShapeDtypeStruct((8 * rows, depth), bf16),
-            jax.ShapeDtypeStruct((units, depth), bf16),
+            jax.ShapeDtypeStruct((tall, depth), bf16),
         ),
-        in_specs=[ANYWHERE] * 6,
+        in_specs=[ANYWHERE] * 7,
         out_specs=(ANYWHERE,) * 4,
         scratch_shapes=[
             pltpu.VMEM((8 * rows, depth), bf16),
@@ -1142,19 +1176,19 @@
             pltpu.VMEM((2, rows, width), f32),
             pltpu.VMEM((units, 8 * rows), bf16),
             pltpu.VMEM((units, depth), bf16),
-            pltpu.VMEM((units, 8 * rows), bf16),
+            pltpu.VMEM((tall, 8 * rows), bf16),
             pltpu.VMEM((2, 8 * rows, depth // 8), bf16),
             pltpu.VMEM((2, rows, depth), bf16),
-            pltpu.VMEM((2, units, depth // 8), bf16),
+            pltpu.VMEM((2, tall, depth // 8), bf16),
         ]
         + gather_scratch(rows, depth)
-        + [pltpu.SemaphoreType.DMA((4,)), pltpu.SemaphoreType.DMA((8,)), pltpu.SemaphoreType.DMA((3, 8))],
+        + [pltpu.SemaphoreType.DMA((5,)), pltpu.SemaphoreType.DMA((8,)), pltpu.SemaphoreType.DMA((3, 8))],
         compiler_params=pltpu.CompilerParams(
             collective_id=identity, has_side_effects=True, vmem_limit_bytes=60 * 1024 * 1024
         ),
         cost_estimate=pl.CostEstimate(flops=0, bytes_accessed=1_000_000, transcendentals=0),
         name="gather_back",
-    )(x, w, inner, down, dup, normed)
+    )(x, w, inner, down, dup, dgate, normed)
 
 
 def scatter_parts(
@@ -1681,14 +1715,17 @@
     params = pack_params(conv_query, conv_key, conv_value, decay_log, decay_bias, out_gain)
     mixed, final, states, inverse, update, raw = mixer_forward(projected, params, start_state[0])
     grad_out_rows, gathered = lax.optimization_barrier((cotangent[0], gathered))
-    grad_gathered = lax.all_gather(grad_out_rows, "tensor", axis=0, tiled=True)
+    sides = gather_sides(grad_out_rows, sizes)
+    sides, mixed = lax.optimization_barrier((sides, mixed))
+    sides = other_side(sides, sizes)
     hidden, normed_ffn = attend(mixed, w_out, tokens[0], gain_second, 1, sizes)
     gate_rows, up_rows = w_ffn_gate.T, w_ffn_up.T
-    gathered_ffn, inner, grad_gate_rows, grad_up_rows = gather_expand(
-        normed_ffn, grad_gathered, gate_rows, up_rows, w_ffn_down, 2, sizes
+    gathered_ffn, grad_gathered, inner, grad_gate_rows, grad_up_rows = gather_expand(
+        normed_ffn, sides, gate_rows, up_rows, w_ffn_down, 2, sizes
     )
     grad_down = jnp.dot(inner, grad_gathered, preferred_element_type=f32).astype(bf16)
-    cut = grad_gate_rows.shape[0] * 7 // 8 // 16 * 16
+    units = grad_gate_rows.shape[0]
+    cut = units * 7 // 8 // 16 * 16
     grad_gate_weight = jnp.dot(grad_gate_rows[:cut], gathered_ffn, preferred_element_type=f32).astype(bf16)
     grad_down_summed, grad_gate_summed = lax.psum((grad_down, grad_gate_weight), "dp")
     grad_gate_rows, grad_up_rows, inner, grad_down, grad_gate_weight = lax.optimization_barrier(
@@ -1698,10 +1735,9 @@
         grad_gate_rows, grad_up_rows, gate_rows, up_rows, hidden, grad_out_rows, gain_second, 3, sizes
     )
     grad_attended, grad_mixed, ffn_part, grad_up_weight = gather_back(
-        grad_attended, w_out, inner, w_ffn_down, grad_up_rows, gathered_ffn, 4, sizes
+        grad_attended, w_out, inner, w_ffn_down, grad_up_rows, grad_gate_rows, cut, gathered_ffn, 4, sizes
     )
     grad_out_weight = cross_rows(mixed, grad_attended).astype(bf16)
-    grad_gate_rest = jnp.dot(grad_gate_rows[cut:], gathered_ffn, preferred_element_type=f32).astype(bf16)
     grad_projected, grad_tq, grad_tk, grad_tv, grad_dl, grad_db, grad_gain = mixer_backward(
         projected, params, states, inverse, update, raw, grad_mixed
     )
@@ -1715,7 +1751,6 @@
     (
         grad_in,
         grad_up_weight,
-        grad_gate_rest,
         small,
         ffn_part,
         grad_down_summed,
@@ -1725,7 +1760,6 @@
         (
             grad_in,
             grad_up_weight,
-            grad_gate_rest,
             small,
                 ffn_part,
             grad_down_summed,
@@ -1736,9 +1770,9 @@
     ffn_out = scatter_rows(ffn_part)
     output = (hidden + ffn_out).astype(bf16)
     gains = 2 * width + out_gain.shape[0]
-    small_summed, grad_up_summed, grad_rest_summed, grad_out_summed, grad_in_summed, gain_grads, grad_normed = sum_over_line(
-        (small.reshape(smalls_rows, 128), grad_up_weight, grad_gate_rest, grad_out_weight, grad_in),
-        (128, width, width, width, main),
+    small_summed, grad_up_summed, grad_out_summed, grad_in_summed, gain_grads, grad_normed = sum_over_line(
+        (small.reshape(smalls_rows, 128), grad_up_weight, grad_out_weight, grad_in),
+        (128, width, width, main),
         -(-gains // (16 * 128)) * 16,
         grad_projected,
         w_in,
@@ -1776,8 +1810,8 @@
         gain_grads[2 * width : gains],
         grad_out_summed.astype(f32),
         gain_grads[width : 2 * width],
-        jnp.concatenate([grad_gate_summed, grad_rest_summed], axis=0).astype(f32).T,
-        grad_up_summed.astype(f32).T,
+        jnp.concatenate([grad_gate_summed, grad_up_summed[units:]], axis=0).astype(f32).T,
+        grad_up_summed[:units].astype(f32).T,
         grad_down_summed.astype(f32),
     )
 

time: 727 us -> 965 us (1.33)
  Pallas kernels: 607 us -> 836 us
  waiting for transfers between devices: 0.07 us -> 16.6 us
    pallas_call x1, Pallas kernels: 42.4 us -> 277 us  [gather_expand(): pl.pallas_call(functools.partial(gather_expand_kernel, 'tensor'), out_sha...]
    all_gather x1, waiting for transfers between devices: 0.02 us -> 16.5 us  [gather_sides(): lax.all_gather(x, 'tensor', axis=0, tiled=True, axis_index_groups=sides)]
  transfers between devices with their start and end apart: 3 -> 4, of which waited for: 0 -> 1; matrix products, arithmetic and copies ran while one was open for 10% -> 7% of each run, Pallas kernels for 72% -> 53%
where the time goes in v12:
time: 965 us; the launch traced here: 959 us
  Pallas kernels  836 us (87%)
  matrix products  46.8 us (5%)
  other arithmetic  27.2 us (3%)
  local copies, waits for them, and re-layouts  17.2 us (2%)
  waiting for transfers between devices  16.6 us (2%)
  between operations  14.6 us (2%)
    pallas_call x1, Pallas kernels, gather_expand(): pl.pallas_call(functools.partial(gather_expand_kernel, 'tensor'), out_sha...  277 us
    pallas_call x1, Pallas kernels, sum_over_line(): pl.pallas_call(functools.partial(line_kernel, 'dp', 'tensor', tuple(width...  276 us
    pallas_call x1, Pallas kernels, mixer_backward(): pl.pallas_call(functools.partial(backward_kernel, heads, key_dim, value_d...  58.9 us
    pallas_call x1, Pallas kernels, return_hidden(): pl.pallas_call(functools.partial(return_kernel, 'tensor'), out_shape=(jax...  52.1 us
    pallas_call x1, Pallas kernels, gather_project(): pl.pallas_call(functools.partial(gather_project_kernel, 'tensor'), out_sh...  47.3 us
    pallas_call x1, Pallas kernels, attend(): pl.pallas_call(functools.partial(attend_kernel, 'tensor'), out_shape=(jax...  47.3 us
    pallas_call x1, Pallas kernels, gather_back(): pl.pallas_call(functools.partial(gather_back_kernel, 'tensor'), out_shape...  42.5 us
    pallas_call x1, Pallas kernels, mixer_forward(): pl.pallas_call(functools.partial(forward_kernel, heads, key_dim, value_di...  35.7 us
  transfers between devices with their start and end apart: 4, of which 1 were waited for; matrix products, arithmetic and copies ran while one was open for 7% of the time, Pallas kernels for 53%

profile of v12, /device:TPU:0, one launch (start us, length us, event | category | flops | bytes accessed | tf_op | source)
XLA Modules:
  0.0 958.7 jit_solution(18420968578263671313)
XLA Ops:
  7.2 0.0 all-gather.2.cloned.1.call-start
  7.2 1.3 convert_element_type.61
  8.5 0.0 copy-start.17
  8.5 0.0 copy-start.18
  8.6 47.3 %gather_project.1 = (bf16[2048,2048]{1,0:T(8,128)(2,1)}, bf16[2048,1664]{1,0:T(8,128)(2,1)}, f32[2048,1664]{1,0:T(8,128)}) custom-call(bf16[256,2048]{1,0:T(8,128)(2,1)} %bitcast.55, f32[1,2048]{1,0:T(1,128)} %bitcast.69, bf16[2,2048]{1,0:T(2,128)(2,1)} %bitcast.84, bf16[2,2048]{1,0:T(2,128)(2,1)} %bitcast.85, bf16[2048,256]{1,0:T(8,128)(2,1)} %wq_ref.1, ...), custom_call_target="tpu_custom_call" | custom-call | bytes 1000000 | tf_op jit(solution)/shard_map/gather_project/pallas_call | solution.py:873
  55.9 0.0 all-gather.2.cloned.1.call-update
  55.9 0.0 all-reduce.6.cloned.1.call-start
  56.0 0.0 copy-done.22
  56.1 0.7 concatenate.13.param_ref
  56.7 35.7 %mixer_forward.1 = (bf16[2048,512]{1,0:T(8,128)(2,1)}, f32[2,128,256]{2,1,0:T(8,128)}, f32[8,2,128,256]{3,2,1,0:T(8,128)}, f32[8,2,256,256]{3,2,1,0:T(8,128)}, f32[2048,512]{1,0:T(8,128)}, /*index=5*/f32[2048,512]{1,0:T(8,128)}) custom-call(f32[2048,1664]{1,0:T(8,128)} %get-tuple-element.73.proj_ref.eq_ref.ek_ref.ev_ref, f32[8,1024]{1,0:T(8,128)} %concatenate.13.param_ref, ...), custom_call_target="tpu_custom_call" | custom-call | bytes 100000000 | tf_op jit(solution)/shard_map/mixer_forward/pallas_call | solution.py:296
  92.5 16.5 %all-gather.2.cloned.1.call-done.mine_ref = bf16[1024,2048]{1,0:T(8,128)(2,1)} async-done(((bf16[256,2048]{1,0:T(8,128)(2,1)}), bf16[1024,2048]{1,0:T(8,128)(2,1)}) %all-gather.2.cloned.1.call-update) | async-done | bytes 4194320 | tf_op jit(solution)/shard_map/all_gather | solution.py:996
  109.0 0.0 collective-permute-start
  109.0 0.6 broadcast_in_dim.52
  109.6 47.3 %attend.1 = (f32[256,2048]{1,0:T(8,128)}, bf16[256,2048]{1,0:T(8,128)(2,1)}) custom-call(bf16[2048,512]{1,0:T(8,128)(2,1)} %get-tuple-element.75.mixed_ref, bf16[512,2048]{1,0:T(8,128)(2,1)} %w_ref.3, bf16[256,2048]{1,0:T(8,128)(2,1)} %bitcast.56, f32[1,2048]{1,0:T(1,128)} %bitcast.70), custom_call_target="tpu_custom_call" | custom-call | bytes 1000000 | tf_op jit(solution)/shard_map/attend/pallas_call | solution.py:1320
  156.9 0.0 collective-permute-done.theirs_ref
  156.9 276.7 %gather_expand.1 = (bf16[2048,2048]{1,0:T(8,128)(2,1)}, bf16[2048,2048]{1,0:T(8,128)(2,1)}, bf16[688,2048]{1,0:T(8,128)(2,1)}, bf16[688,2048]{1,0:T(8,128)(2,1)}, bf16[688,2048]{1,0:T(8,128)(2,1)}) custom-call(bf16[256,2048]{1,0:T(8,128)(2,1)} %get-tuple-element.82.x_ref, bf16[1024,2048]{1,0:T(8,128)(2,1)} %all-gather.2.cloned.1.call-done.mine_ref, ...), custom_call_target="tpu_custom_call" | custom-call | bytes 1000000 | tf_op jit(solution)/shard_map/gather_expand/pallas_call | solution.py:1017
  433.7 10.5 %convolution_convert_fusion.1 = bf16[688,2048]{1,0:T(8,128)(2,1)} fusion(bf16[688,2048]{1,0:T(8,128)(2,1)} %get-tuple-element.92.inner_ref, bf16[2048,2048]{1,0:T(8,128)(2,1)} %get-tuple-element.87), kind=kOutput, calls=%fused_computation.4 | convolution fusion | flops 5772771328 | bytes 14024704 | tf_op jit(solution)/shard_map/dot_general | solution.py:1726
  444.1 6.4 convolution_convert_fusion.2
  450.5 0.0 all-reduce.6.cloned.1.call-update
  450.6 0.0 reduce-scatter.2.cloned.1.call-start
  450.6 52.1 %return_hidden.1 = (f32[256,2048]{1,0:T(8,128)}, bf16[256,2048]{1,0:T(8,128)(2,1)}, f32[1,2048]{1,0:T(1,128)}) custom-call(bf16[688,2048]{1,0:T(8,128)(2,1)} %get-tuple-element.89.dgate_ref.rest_ref, bf16[688,2048]{1,0:T(8,128)(2,1)} %get-tuple-element.90.dup_ref, bf16[688,2048]{1,0:T(8,128)(2,1)} %bitcast.58, bf16[688,2048]{1,0:T(8,128)(2,1)} %bitcast.60, ...), custom_call_target="tpu_custom_call" | custom-call | bytes 1000000 | tf_op jit(solution)/shard_map/return_hidden/pallas_call | solution.py:1389
  502.7 42.5 %gather_back.1 = (bf16[2048,2048]{1,0:T(8,128)(2,1)}, f32[2048,512]{1,0:T(8,128)}, bf16[2048,2048]{1,0:T(8,128)(2,1)}, bf16[784,2048]{1,0:T(8,128)(2,1)}) custom-call(bf16[256,2048]{1,0:T(8,128)(2,1)} %get-tuple-element.91.x_ref, bf16[512,2048]{1,0:T(8,128)(2,1)} %w_ref.3, bf16[688,2048]{1,0:T(8,128)(2,1)} %get-tuple-element.92.inner_ref, ...), custom_call_target="tpu_custom_call" | custom-call | bytes 1000000 | tf_op jit(solution)/shard_map/gather_back/pallas_call | solution.py:1163
  545.2 58.9 %mixer_backward.1 = (bf16[2048,1664]{1,0:T(8,128)(2,1)}, f32[4,256]{1,0:T(4,128)}, f32[4,256]{1,0:T(4,128)}, f32[4,512]{1,0:T(4,128)}, f32[1,2]{1,0:T(1,128)}, /*index=5*/f32[1,2]{1,0:T(1,128)}, f32[1,256]{1,0:T(1,128)}) custom-call(f32[2048,1664]{1,0:T(8,128)} %get-tuple-element.73.proj_ref.eq_ref.ek_ref.ev_ref, ...), custom_call_target="tpu_custom_call" | custom-call | bytes 100000000 | tf_op jit(solution)/shard_map/mixer_backward/pallas_call | solution.py:588
  604.1 0.7 copy.46
  604.8 0.7 copy.47
  605.5 0.7 copy.48
  606.2 0.0 copy-start.20
  606.2 0.0 copy-start.21
  606.3 20.8 %multiply_reduce_fusion = (f32[2048]{0:T(1024)S(1)}, bf16[2048,1664]{1,0:T(8,128)(2,1)S(1)}) fusion(bf16[2048,1664]{1,0:T(8,128)(2,1)} %get-tuple-element.96.w_ref, bf16[2048,2048]{1,0:T(8,128)(2,1)} %get-tuple-element.77, bf16[2048,1664]{1,0:T(8,128)(2,1)} %get-tuple-element.94.dproj_ref), kind=kOutput, calls=%fused_computation | convolution fusion | flops 13975681024 | bytes 28844032 | tf_op jit(solution)/shard_map/dot_general | solution.py:654
  627.1 0.0 copy-start.5
  627.1 0.0 copy-start.10
  627.1 3.0 copy-done.5
  630.1 0.1 convert_bitcast_fusion.2
  630.2 0.3 copy.44
  630.5 0.0 copy-done.12
  630.6 0.7 concatenate.14
  631.3 9.1 convolution_convert_fusion.3.refs_2_
  640.4 0.0 reduce-scatter.2.cloned.1.call-update
  640.4 1.2 copy-done
  641.6 0.3 fusion.8
  641.9 275.6 %sum_over_line.1 = (f32[144,128]{1,0:T(8,128)}, bf16[784,2048]{1,0:T(8,128)(2,1)}, bf16[512,2048]{1,0:T(8,128)(2,1)}, bf16[2048,1536]{1,0:T(8,128)(2,1)}, f32[48,128]{1,0:T(8,128)}, /*index=5*/f32[256,2048]{1,0:T(8,128)}) custom-call(bf16[2048,1664]{1,0:T(8,128)(2,1)} %get-tuple-element.94.dproj_ref, bf16[2048,1664]{1,0:T(8,128)(2,1)} %get-tuple-element.96.w_ref, ...), custom_call_target="tpu_custom_call" | custom-call | bytes 1163673600 | tf_op jit(solution)/shard_map/sum_over_line/pallas_call | solution.py:1662
  917.6 0.7 slice.93
  918.3 0.9 fusion.12
  919.2 0.6 slice.87
  919.8 0.6 slice.89
  920.4 0.8 fusion.11
  921.2 0.6 reshape.109
  921.8 0.6 reshape.110
  922.4 0.6 reshape.111
  923.0 4.3 convert_element_type.76
  927.3 1.0 slice.100
  928.3 0.0 copy-start.11
  928.3 0.0 slice-start.1
  928.3 3.2 convert_element_type.77
  931.6 0.5 fusion.3
  932.1 1.3 fusion.10
  933.4 0.6 slice_bitcast_fusion.2
  934.0 0.6 slice_bitcast_fusion
  934.6 2.3 slice_convert_fusion.2
  936.9 0.1 copy-done.9
  937.0 1.9 fusion.7
  938.9 4.6 slice_convert_fusion
  943.5 5.7 convert_bitcast_fusion
  949.2 2.5 fusion.9
  (54 shorter events, 0.1 us)
Async XLA Ops:
  7.2 101.8 %all-gather.2.cloned.1.call-start = ((), (), s32[]{:S(2)}) async-start(), calls=%async_computation.1 | async-start | bytes 5242880 | tf_op jit(solution)/shard_map/all_gather | solution.py:996
  8.5 47.4 %copy-start.22 = (f32[2]{0:T(128)S(1)}, f32[2]{0:T(128)}, u32[]{:S(2)}) copy-start(f32[2]{0:T(128)} %param.33) | copy-start | bytes 28
  8.5 47.5 %copy-start.23 = (f32[2]{0:T(128)S(1)}, f32[2]{0:T(128)}, u32[]{:S(2)}) copy-start(f32[2]{0:T(128)} %param.34) | copy-start | bytes 28
  8.5 47.5 %copy-start.24 = (bf16[256]{0:T(256)(128)(2,1)S(1)}, bf16[256]{0:T(256)(128)(2,1)}, u32[]{:S(2)}) copy-start(bf16[256]{0:T(256)(128)(2,1)} %param.35) | copy-start | bytes 1540
  8.5 47.5 %copy-start.16 = (bf16[4,512]{1,0:T(4,128)(2,1)S(1)}, bf16[4,512]{1,0:T(4,128)(2,1)}, u32[]{:S(2)}) copy-start(bf16[4,512]{1,0:T(4,128)(2,1)} %param.32) | copy-start | bytes 12292
  8.5 47.5 %copy-start.17 = (bf16[4,256]{1,0:T(4,128)(2,1)S(1)}, bf16[4,256]{1,0:T(4,128)(2,1)}, u32[]{:S(2)}) copy-start(bf16[4,256]{1,0:T(4,128)(2,1)} %param.31) | copy-start | bytes 6148
  8.5 47.5 %copy-start.18 = (bf16[4,256]{1,0:T(4,128)(2,1)S(1)}, bf16[4,256]{1,0:T(4,128)(2,1)}, u32[]{:S(2)}) copy-start(bf16[4,256]{1,0:T(4,128)(2,1)} %param.30) | copy-start | bytes 6148
  55.9 584.5 %all-reduce.6.cloned.1.call-start = ((), (), s32[]{:S(2)}) async-start(), calls=%async_computation.3 | async-start | bytes 10485760 | tf_op jit(solution)/shard_map/psum | solution.py:1730
  56.7 52.3 %copy-start.15 = (bf16[2048]{0:T(1024)(128)(2,1)S(1)}, bf16[2048]{0:T(1024)(128)(2,1)}, u32[]{:S(2)}) copy-start(bf16[2048]{0:T(1024)(128)(2,1)} %param.37) | copy-start | bytes 12292
  109.0 47.9 %collective-permute-start = (bf16[1024,2048]{1,0:T(8,128)(2,1)}, bf16[1024,2048]{1,0:T(8,128)(2,1)}, u32[]{:S(2)}, u32[]{:S(2)}) collective-permute-start(bf16[1024,2048]{1,0:T(8,128)(2,1)} %all-gather.2.cloned.1.call-done.mine_ref), channel_id=1, source_target_pairs={{0,1},{1,0},{2,3},{3,2},{4,5},{5,4},{6,7},{7,6},{8,9},{9,8},{10,11... | collective-permute-start | bytes 12582920 | tf_op jit(solution)/shard_map/ppermute | solution.py:1002
  433.6 10.5 %copy-start.1 = (bf16[688,2048]{1,0:T(8,128)(2,1)S(1)}, bf16[688,2048]{1,0:T(8,128)(2,1)}, u32[]{:S(2)}) copy-start(bf16[688,2048]{1,0:T(8,128)(2,1)} %get-tuple-element.89.dgate_ref.rest_ref) | copy-start | bytes 8454148
  433.7 10.5 %copy-start.4 = (bf16[2048,2048]{1,0:T(8,128)(2,1)S(1)}, bf16[2048,2048]{1,0:T(8,128)(2,1)}, u32[]{:S(2)}) copy-start(bf16[2048,2048]{1,0:T(8,128)(2,1)} %get-tuple-element.88.normed_ref) | copy-start | bytes 25165828
  450.6 498.6 %reduce-scatter.2.cloned.1.call-start = ((), (), s32[]{:S(2)}) async-start(), calls=%async_computation.2 | async-start | bytes 9437184 | tf_op jit(solution)/shard_map/reduce_scatter | solution.py:1409
  606.2 24.3 %copy-start.12 = (bf16[2048]{0:T(1024)(128)(2,1)S(1)}, bf16[2048]{0:T(1024)(128)(2,1)}, u32[]{:S(2)}) copy-start(bf16[2048]{0:T(1024)(128)(2,1)} %param.23) | copy-start | bytes 12292
  606.2 24.3 %copy-start.14 = (f32[1,2048]{1,0:T(1,128)S(1)}, f32[1,2048]{1,0:T(1,128)}, u32[]{:S(2)}) copy-start(f32[1,2048]{1,0:T(1,128)} %get-tuple-element.97) | copy-start | bytes 24580
  606.2 24.3 %copy-start.19 = (f32[1,256]{1,0:T(1,128)S(1)}, f32[1,256]{1,0:T(1,128)}, u32[]{:S(2)}) copy-start(f32[1,256]{1,0:T(1,128)} %get-tuple-element.98) | copy-start | bytes 3076
  606.2 24.3 %copy-start.20 = (f32[1,2]{1,0:T(1,128)S(1)}, f32[1,2]{1,0:T(1,128)}, u32[]{:S(2)}) copy-start(f32[1,2]{1,0:T(1,128)} %get-tuple-element.102) | copy-start | bytes 28
  606.2 24.3 %copy-start.21 = (f32[1,2]{1,0:T(1,128)S(1)}, f32[1,2]{1,0:T(1,128)}, u32[]{:S(2)}) copy-start(f32[1,2]{1,0:T(1,128)} %get-tuple-element.103) | copy-start | bytes 28
  627.1 3.0 copy-start.5
  627.1 4.2 copy-start.10
  640.4 1.2 copy-start
  923.0 5.3 copy-start.7
  923.0 11.6 %slice-start = ((s8[6291456]{0:T(1024)(128)(4,1)}), s8[4194304]{0:T(1024)(128)(4,1)S(1)}, s32[]{:S(2)}) async-start(s8[6291456]{0:T(1024)(128)(4,1)} %bitcast.61), calls=%async_computation.4 | async-start | bytes 8388608
  928.3 3.3 copy-start.3
  928.3 3.3 copy-start.11
  928.3 6.3 slice-start.1
  931.6 1.8 copy-start.13
  934.6 2.4 copy-start.9
  938.9 4.6 copy-start.6
  938.9 4.6 copy-start.8
  943.5 5.7 copy-start.2
Sparse Core Ops, SparseCore 0:
  56.0 52.9 all-gather.1
  450.7 189.2 all-reduce.5
  643.5 92.7 reduce-scatter.1

commit v13 on v12

--- a/solution.py
+++ b/solution.py
@@ -898,13 +898,11 @@
 def gather_expand_kernel(
     axis,
     x_ref,
-    mine_ref,
-    theirs_ref,
+    cot_ref,
     wg_ref,
     wu_ref,
     wd_ref,
     all_ref,
-    cot_ref,
     inner_ref,
     dgate_ref,
     dup_ref,
@@ -931,12 +929,9 @@
         pltpu.make_async_copy(src, dst, load.at[k])
         for k, (src, dst) in enumerate(((wg_ref, w_gate), (wu_ref, w_up), (wd_ref, w_down)))
     ]
-    sources = [
-        rows_at(mine_ref if i in (0, 2, 3, 6) else theirs_ref, order[i] // 2, rows) for i in range(8)
-    ]
-    fetches = [pltpu.make_async_copy(sources[i], cots.at[i % 2], fetch.at[i]) for i in range(8)]
-    saves = [
-        pltpu.make_async_copy(sources[i], rows_at(cot_ref, order[i], rows), fetch.at[8 + i]) for i in range(8)
+    fetches = [
+        pltpu.make_async_copy(rows_at(cot_ref, order[i], rows), cots.at[i % 2], fetch.at[i])
+        for i in range(8)
     ]
     for copy in (loads[2], fetches[0], loads[0], loads[1]):
         copy.start()
@@ -980,26 +975,11 @@
     forward(1)
     for i in range(2, 8):
         backward(i)
-    for copy in saves:
-        copy.start()
     for i in range(2, 8):
         forward(i)
-    for copy in saves + keeps + outs[6] + outs[7]:
+    for copy in keeps + outs[6] + outs[7]:
         copy.wait()
     finish()
-
-
-def gather_sides(x, sizes):
-    if not square(sizes):
-        return (lax.all_gather(x, "tensor", axis=0, tiled=True),)
-    sides = [[0, 2, 4, 6], [1, 3, 5, 7]]
-    return (lax.all_gather(x, "tensor", axis=0, tiled=True, axis_index_groups=sides),)
-
-
-def other_side(mine, sizes):
-    if not square(sizes):
-        return mine
-    return mine + (lax.ppermute(mine[0], "tensor", [(i, i + 1 - 2 * (i % 2)) for i in range(8)]),)
 
 
 def gather_expand(x, cotangent, gate_rows, up_rows, down_rows, identity, sizes):
@@ -1008,17 +988,16 @@
     if not square(sizes):
         gathered = lax.all_gather(x, "tensor", axis=0, tiled=True)
         gate, up = times_transposed(gate_rows, gathered), times_transposed(up_rows, gathered)
-        dinner = times_transposed(down_rows, cotangent[0])
+        dinner = times_transposed(down_rows, cotangent)
         sig = sigmoid(gate)
         dgate = dinner * up * sig * (1.0 + gate * (1.0 - sig))
-        inner = (gate * sig * up).astype(bf16)
-        return gathered, cotangent[0], inner, dgate.astype(bf16), (dinner * gate * sig).astype(bf16)
+        return gathered, (gate * sig * up).astype(bf16), dgate.astype(bf16), (dinner * gate * sig).astype(bf16)
     by_token = jax.ShapeDtypeStruct((units, 8 * rows), bf16)
     return pl.pallas_call(
         functools.partial(gather_expand_kernel, "tensor"),
-        out_shape=(jax.ShapeDtypeStruct((8 * rows, depth), bf16),) * 2 + (by_token,) * 3,
-        in_specs=[ANYWHERE] * 6,
-        out_specs=(ANYWHERE,) * 5,
+        out_shape=(jax.ShapeDtypeStruct((8 * rows, depth), bf16), by_token, by_token, by_token),
+        in_specs=[ANYWHERE] * 5,
+        out_specs=(ANYWHERE,) * 4,
         scratch_shapes=[
             pltpu.VMEM((8 * rows, depth), bf16),
             pltpu.VMEM((units, depth), bf16),
@@ -1031,13 +1010,13 @@
             pltpu.VMEM((2, units, rows), bf16),
         ]
         + gather_scratch(rows, depth)
-        + [pltpu.SemaphoreType.DMA((3,)), pltpu.SemaphoreType.DMA((16,)), pltpu.SemaphoreType.DMA((3, 8))],
+        + [pltpu.SemaphoreType.DMA((3,)), pltpu.SemaphoreType.DMA((8,)), pltpu.SemaphoreType.DMA((3, 8))],
         compiler_params=pltpu.CompilerParams(
             collective_id=identity, has_side_effects=True, vmem_limit_bytes=60 * 1024 * 1024
         ),
         cost_estimate=pl.CostEstimate(flops=0, bytes_accessed=1_000_000, transcendentals=0),
         name="gather_expand",
-    )(x, *cotangent, gate_rows, up_rows, down_rows)
+    )(x, cotangent, gate_rows, up_rows, down_rows)
 
 
 def gather_back_kernel(
@@ -1715,13 +1694,11 @@
     params = pack_params(conv_query, conv_key, conv_value, decay_log, decay_bias, out_gain)
     mixed, final, states, inverse, update, raw = mixer_forward(projected, params, start_state[0])
     grad_out_rows, gathered = lax.optimization_barrier((cotangent[0], gathered))
-    sides = gather_sides(grad_out_rows, sizes)
-    sides, mixed = lax.optimization_barrier((sides, mixed))
-    sides = other_side(sides, sizes)
+    grad_gathered = lax.all_gather(grad_out_rows, "tensor", axis=0, tiled=True)
     hidden, normed_ffn = attend(mixed, w_out, tokens[0], gain_second, 1, sizes)
     gate_rows, up_rows = w_ffn_gate.T, w_ffn_up.T
-    gathered_ffn, grad_gathered, inner, grad_gate_rows, grad_up_rows = gather_expand(
-        normed_ffn, sides, gate_rows, up_rows, w_ffn_down, 2, sizes
+    gathered_ffn, inner, grad_gate_rows, grad_up_rows = gather_expand(
+        normed_ffn, grad_gathered, gate_rows, up_rows, w_ffn_down, 2, sizes
     )
     grad_down = jnp.dot(inner, grad_gathered, preferred_element_type=f32).astype(bf16)
     units = grad_gate_rows.shape[0]

time: 965 us -> 720 us (0.75)
  Pallas kernels: 836 us -> 607 us
  waiting for transfers between devices: 16.6 us -> 0.07 us
    pallas_call x1, Pallas kernels: 277 us -> 42.3 us  [gather_expand(): pl.pallas_call(functools.partial(gather_expand_kernel, 'tensor'), out_sha...]
    all_gather x1, waiting for transfers between devices: 16.5 us -> 0.02 us  [shards(): grad_gathered = lax.all_gather(grad_out_rows, 'tensor', axis=0, tiled=True)]
  transfers between devices with their start and end apart: 4 -> 3, of which waited for: 1 -> 0; matrix products, arithmetic and copies ran while one was open for 7% -> 9% of each run, Pallas kernels for 53% -> 72%
where the time goes in v13:
time: 720 us; the launch traced here: 713 us
  Pallas kernels  607 us (84%)
  matrix products  47.5 us (7%)
  other arithmetic  27.2 us (4%)
  local copies, waits for them, and re-layouts  17.2 us (2%)
  between operations  14.6 us (2%)
    pallas_call x1, Pallas kernels, sum_over_line(): pl.pallas_call(functools.partial(line_kernel, 'dp', 'tensor', tuple(width...  275 us
    pallas_call x1, Pallas kernels, mixer_backward(): pl.pallas_call(functools.partial(backward_kernel, heads, key_dim, value_d...  58.9 us
    pallas_call x1, Pallas kernels, attend(): pl.pallas_call(functools.partial(attend_kernel, 'tensor'), out_shape=(jax...  52.3 us
    pallas_call x1, Pallas kernels, return_hidden(): pl.pallas_call(functools.partial(return_kernel, 'tensor'), out_shape=(jax...  52.2 us
    pallas_call x1, Pallas kernels, gather_project(): pl.pallas_call(functools.partial(gather_project_kernel, 'tensor'), out_sh...  47.3 us
    pallas_call x1, Pallas kernels, gather_back(): pl.pallas_call(functools.partial(gather_back_kernel, 'tensor'), out_shape...  42.5 us
    pallas_call x1, Pallas kernels, gather_expand(): pl.pallas_call(functools.partial(gather_expand_kernel, 'tensor'), out_sha...  42.3 us
    pallas_call x1, Pallas kernels, mixer_forward(): pl.pallas_call(functools.partial(forward_kernel, heads, key_dim, value_di...  35.7 us
  transfers between devices with their start and end apart: 3, of which 0 were waited for; matrix products, arithmetic and copies ran while one was open for 9% of the time, Pallas kernels for 72%

profile of v13, /device:TPU:0, one launch (start us, length us, event | category | flops | bytes accessed | tf_op | source)
XLA Modules:
  0.0 713.4 jit_solution(9531001653359770375)
XLA Ops:
  7.2 0.0 all-gather.2.cloned.1.call-start
  7.2 1.3 convert_element_type.61
  8.5 0.0 copy-start.16
  8.5 0.0 copy-start.17
  8.6 0.0 copy-start.18
  8.6 47.3 %gather_project.1 = (bf16[2048,2048]{1,0:T(8,128)(2,1)}, bf16[2048,1664]{1,0:T(8,128)(2,1)}, f32[2048,1664]{1,0:T(8,128)}) custom-call(bf16[256,2048]{1,0:T(8,128)(2,1)} %bitcast.55, f32[1,2048]{1,0:T(1,128)} %bitcast.69, bf16[2,2048]{1,0:T(2,128)(2,1)} %bitcast.84, bf16[2,2048]{1,0:T(2,128)(2,1)} %bitcast.85, bf16[2048,256]{1,0:T(8,128)(2,1)} %wq_ref.1, ...), custom_call_target="tpu_custom_call" | custom-call | bytes 1000000 | tf_op jit(solution)/shard_map/gather_project/pallas_call | solution.py:873
  55.9 0.0 all-gather.2.cloned.1.call-update
  55.9 0.0 all-reduce.6.cloned.1.call-start
  56.0 0.0 copy-done.23
  56.0 0.6 broadcast_in_dim.52
  56.7 0.7 concatenate.13.param_ref
  57.3 35.7 %mixer_forward.1 = (bf16[2048,512]{1,0:T(8,128)(2,1)}, f32[2,128,256]{2,1,0:T(8,128)}, f32[8,2,128,256]{3,2,1,0:T(8,128)}, f32[8,2,256,256]{3,2,1,0:T(8,128)}, f32[2048,512]{1,0:T(8,128)}, /*index=5*/f32[2048,512]{1,0:T(8,128)}) custom-call(f32[2048,1664]{1,0:T(8,128)} %get-tuple-element.68.proj_ref.eq_ref.ek_ref.ev_ref, f32[8,1024]{1,0:T(8,128)} %concatenate.13.param_ref, ...), custom_call_target="tpu_custom_call" | custom-call | bytes 100000000 | tf_op jit(solution)/shard_map/mixer_forward/pallas_call | solution.py:296
  93.1 52.3 %attend.1 = (f32[256,2048]{1,0:T(8,128)}, bf16[256,2048]{1,0:T(8,128)(2,1)}) custom-call(bf16[2048,512]{1,0:T(8,128)(2,1)} %get-tuple-element.69.mixed_ref, bf16[512,2048]{1,0:T(8,128)(2,1)} %w_ref.3, bf16[256,2048]{1,0:T(8,128)(2,1)} %bitcast.56, f32[1,2048]{1,0:T(1,128)} %bitcast.70), custom_call_target="tpu_custom_call" | custom-call | bytes 1000000 | tf_op jit(solution)/shard_map/attend/pallas_call | solution.py:1299
  145.4 0.0 all-gather.2.cloned.1.call-done.cot_ref
  145.4 42.3 %gather_expand.1 = (bf16[2048,2048]{1,0:T(8,128)(2,1)}, bf16[688,2048]{1,0:T(8,128)(2,1)}, bf16[688,2048]{1,0:T(8,128)(2,1)}, bf16[688,2048]{1,0:T(8,128)(2,1)}) custom-call(bf16[256,2048]{1,0:T(8,128)(2,1)} %get-tuple-element.77.x_ref, bf16[2048,2048]{1,0:T(8,128)(2,1)} %all-gather.2.cloned.1.call-done.cot_ref, bf16[688,2048]{1,0:T(8,128)(2,1)} %bitcast.57, ...), custom_call_target="tpu_custom_call" | custom-call | bytes 1000000 | tf_op jit(solution)/shard_map/gather_expand/pallas_call | solution.py:996
  187.8 0.0 copy-start.3
  187.8 0.0 copy-start.7
  187.8 10.3 %convolution_convert_fusion.2 = bf16[592,2048]{1,0:T(8,128)(2,1)} fusion(bf16[2048,2048]{1,0:T(8,128)(2,1)} %get-tuple-element.82.normed_ref, bf16[688,2048]{1,0:T(8,128)(2,1)} %get-tuple-element.83.dgate_ref.rest_ref), kind=kOutput, calls=%fused_computation.5 | convolution fusion | flops 4967268352 | bytes 13238272 | tf_op jit(solution)/shard_map/dot_general | solution.py:1706
  198.1 0.0 copy-done.3
  198.1 7.3 %convolution_convert_fusion.1 = bf16[688,2048]{1,0:T(8,128)(2,1)} fusion(bf16[688,2048]{1,0:T(8,128)(2,1)S(1)} %copy-done.7, bf16[2048,2048]{1,0:T(8,128)(2,1)S(1)} %copy-done.3), kind=kOutput, calls=%fused_computation.4 | convolution fusion | flops 5772771328 | bytes 14024704 | tf_op jit(solution)/shard_map/dot_general | solution.py:1703
  205.3 0.0 all-reduce.6.cloned.1.call-update
  205.4 0.0 reduce-scatter.2.cloned.1.call-start
  205.4 52.2 %return_hidden.1 = (f32[256,2048]{1,0:T(8,128)}, bf16[256,2048]{1,0:T(8,128)(2,1)}, f32[1,2048]{1,0:T(1,128)}) custom-call(bf16[688,2048]{1,0:T(8,128)(2,1)} %get-tuple-element.83.dgate_ref.rest_ref, bf16[688,2048]{1,0:T(8,128)(2,1)} %get-tuple-element.84.dup_ref, bf16[688,2048]{1,0:T(8,128)(2,1)} %bitcast.58, bf16[688,2048]{1,0:T(8,128)(2,1)} %bitcast.60, ...), custom_call_target="tpu_custom_call" | custom-call | bytes 1000000 | tf_op jit(solution)/shard_map/return_hidden/pallas_call | solution.py:1368
  257.6 42.5 %gather_back.1 = (bf16[2048,2048]{1,0:T(8,128)(2,1)}, f32[2048,512]{1,0:T(8,128)}, bf16[2048,2048]{1,0:T(8,128)(2,1)}, bf16[784,2048]{1,0:T(8,128)(2,1)}) custom-call(bf16[256,2048]{1,0:T(8,128)(2,1)} %get-tuple-element.85.x_ref, bf16[512,2048]{1,0:T(8,128)(2,1)} %w_ref.3, bf16[688,2048]{1,0:T(8,128)(2,1)} %get-tuple-element.86.inner_ref, ...), custom_call_target="tpu_custom_call" | custom-call | bytes 1000000 | tf_op jit(solution)/shard_map/gather_back/pallas_call | solution.py:1142
  300.1 58.9 %mixer_backward.1 = (bf16[2048,1664]{1,0:T(8,128)(2,1)}, f32[4,256]{1,0:T(4,128)}, f32[4,256]{1,0:T(4,128)}, f32[4,512]{1,0:T(4,128)}, f32[1,2]{1,0:T(1,128)}, /*index=5*/f32[1,2]{1,0:T(1,128)}, f32[1,256]{1,0:T(1,128)}) custom-call(f32[2048,1664]{1,0:T(8,128)} %get-tuple-element.68.proj_ref.eq_ref.ek_ref.ev_ref, ...), custom_call_target="tpu_custom_call" | custom-call | bytes 100000000 | tf_op jit(solution)/shard_map/mixer_backward/pallas_call | solution.py:588
  359.0 0.7 copy.46
  359.7 0.7 copy.47
  360.4 0.7 copy.48
  361.1 0.0 copy-start.20
  361.1 0.0 copy-start.21
  361.1 20.8 %multiply_reduce_fusion = (f32[2048]{0:T(1024)S(1)}, bf16[2048,1664]{1,0:T(8,128)(2,1)S(1)}) fusion(bf16[2048,1664]{1,0:T(8,128)(2,1)} %get-tuple-element.90.w_ref, bf16[2048,2048]{1,0:T(8,128)(2,1)} %get-tuple-element.72, bf16[2048,1664]{1,0:T(8,128)(2,1)} %get-tuple-element.88.dproj_ref), kind=kOutput, calls=%fused_computation | convolution fusion | flops 13975681024 | bytes 28844032 | tf_op jit(solution)/shard_map/dot_general | solution.py:654
  382.0 0.0 copy-start.10
  382.0 3.0 copy-done.4
  385.0 0.1 convert_bitcast_fusion.2
  385.1 0.3 copy.44
  385.5 0.7 concatenate.14
  386.2 9.1 %convolution_convert_fusion.3.refs_2_ = bf16[512,2048]{1,0:T(8,128)(2,1)} fusion(bf16[2048,512]{1,0:T(8,128)(2,1)S(1)} %copy-done.10, bf16[2048,2048]{1,0:T(8,128)(2,1)} %get-tuple-element.99), kind=kOutput, calls=%fused_computation.6 | convolution fusion | flops 4296015872 | bytes 12582912 | tf_op jit(solution)/shard_map/dot_general | solution.py:654
  395.3 0.0 reduce-scatter.2.cloned.1.call-update
  395.3 1.2 copy-done
  396.5 0.3 fusion.8
  396.8 275.4 %sum_over_line.1 = (f32[144,128]{1,0:T(8,128)}, bf16[784,2048]{1,0:T(8,128)(2,1)}, bf16[512,2048]{1,0:T(8,128)(2,1)}, bf16[2048,1536]{1,0:T(8,128)(2,1)}, f32[48,128]{1,0:T(8,128)}, /*index=5*/f32[256,2048]{1,0:T(8,128)}) custom-call(bf16[2048,1664]{1,0:T(8,128)(2,1)} %get-tuple-element.88.dproj_ref, bf16[2048,1664]{1,0:T(8,128)(2,1)} %get-tuple-element.90.w_ref, ...), custom_call_target="tpu_custom_call" | custom-call | bytes 1163673600 | tf_op jit(solution)/shard_map/sum_over_line/pallas_call | solution.py:1641
  672.3 0.7 slice.93
  673.0 0.9 fusion.12
  673.9 0.6 slice.87
  674.5 0.6 slice.89
  675.1 0.8 fusion.11
  675.9 0.6 reshape.109
  676.5 0.6 reshape.110
  677.1 0.6 reshape.111
  677.7 4.3 convert_element_type.76
  682.0 1.0 slice.100
  683.0 0.0 copy-start.11
  683.0 0.0 slice-start.1
  683.0 3.2 convert_element_type.77
  686.3 0.5 fusion.3
  686.8 1.3 fusion.10
  688.1 0.6 slice_bitcast_fusion.2
  688.7 0.6 slice_bitcast_fusion
  689.3 2.3 slice_convert_fusion.2
  691.6 0.1 copy-done.9
  691.7 1.9 fusion.7
  693.6 4.6 slice_convert_fusion
  698.2 5.7 convert_bitcast_fusion
  703.9 2.5 fusion.9
  (52 shorter events, 0.1 us)
Async XLA Ops:
  7.2 138.2 %all-gather.2.cloned.1.call-start = ((), (), s32[]{:S(2)}) async-start(), calls=%async_computation.1 | async-start | bytes 9437184 | tf_op jit(solution)/shard_map/all_gather | solution.py:1697
  8.5 47.5 %copy-start.22 = (f32[2]{0:T(128)S(1)}, f32[2]{0:T(128)}, u32[]{:S(2)}) copy-start(f32[2]{0:T(128)} %param.33) | copy-start | bytes 28
  8.5 47.5 %copy-start.23 = (f32[2]{0:T(128)S(1)}, f32[2]{0:T(128)}, u32[]{:S(2)}) copy-start(f32[2]{0:T(128)} %param.34) | copy-start | bytes 28
  8.5 47.5 %copy-start.15 = (bf16[2048]{0:T(1024)(128)(2,1)S(1)}, bf16[2048]{0:T(1024)(128)(2,1)}, u32[]{:S(2)}) copy-start(bf16[2048]{0:T(1024)(128)(2,1)} %param.37) | copy-start | bytes 12292
  8.5 48.1 %copy-start.24 = (bf16[256]{0:T(256)(128)(2,1)S(1)}, bf16[256]{0:T(256)(128)(2,1)}, u32[]{:S(2)}) copy-start(bf16[256]{0:T(256)(128)(2,1)} %param.35) | copy-start | bytes 1540
  8.5 48.1 %copy-start.16 = (bf16[4,512]{1,0:T(4,128)(2,1)S(1)}, bf16[4,512]{1,0:T(4,128)(2,1)}, u32[]{:S(2)}) copy-start(bf16[4,512]{1,0:T(4,128)(2,1)} %param.32) | copy-start | bytes 12292
  8.5 48.1 %copy-start.17 = (bf16[4,256]{1,0:T(4,128)(2,1)S(1)}, bf16[4,256]{1,0:T(4,128)(2,1)}, u32[]{:S(2)}) copy-start(bf16[4,256]{1,0:T(4,128)(2,1)} %param.31) | copy-start | bytes 6148
  8.6 48.1 %copy-start.18 = (bf16[4,256]{1,0:T(4,128)(2,1)S(1)}, bf16[4,256]{1,0:T(4,128)(2,1)}, u32[]{:S(2)}) copy-start(bf16[4,256]{1,0:T(4,128)(2,1)} %param.30) | copy-start | bytes 6148
  55.9 339.4 %all-reduce.6.cloned.1.call-start = ((), (), s32[]{:S(2)}) async-start(), calls=%async_computation.3 | async-start | bytes 10485760 | tf_op jit(solution)/shard_map/psum | solution.py:1707
  187.8 10.3 %copy-start.3 = (bf16[2048,2048]{1,0:T(8,128)(2,1)S(1)}, bf16[2048,2048]{1,0:T(8,128)(2,1)}, u32[]{:S(2)}) copy-start(bf16[2048,2048]{1,0:T(8,128)(2,1)} %all-gather.2.cloned.1.call-done.cot_ref) | copy-start | bytes 25165828
  187.8 10.3 %copy-start.7 = (bf16[688,2048]{1,0:T(8,128)(2,1)S(1)}, bf16[688,2048]{1,0:T(8,128)(2,1)}, u32[]{:S(2)}) copy-start(bf16[688,2048]{1,0:T(8,128)(2,1)} %get-tuple-element.86.inner_ref) | copy-start | bytes 8454148
  205.4 498.6 %reduce-scatter.2.cloned.1.call-start = ((), (), s32[]{:S(2)}) async-start(), calls=%async_computation.2 | async-start | bytes 9437184 | tf_op jit(solution)/shard_map/reduce_scatter | solution.py:1388
  361.1 24.3 %copy-start.12 = (bf16[2048]{0:T(1024)(128)(2,1)S(1)}, bf16[2048]{0:T(1024)(128)(2,1)}, u32[]{:S(2)}) copy-start(bf16[2048]{0:T(1024)(128)(2,1)} %param.23) | copy-start | bytes 12292
  361.1 24.3 %copy-start.14 = (f32[1,2048]{1,0:T(1,128)S(1)}, f32[1,2048]{1,0:T(1,128)}, u32[]{:S(2)}) copy-start(f32[1,2048]{1,0:T(1,128)} %get-tuple-element.91) | copy-start | bytes 24580
  361.1 24.3 %copy-start.19 = (f32[1,256]{1,0:T(1,128)S(1)}, f32[1,256]{1,0:T(1,128)}, u32[]{:S(2)}) copy-start(f32[1,256]{1,0:T(1,128)} %get-tuple-element.92) | copy-start | bytes 3076
  361.1 24.3 %copy-start.20 = (f32[1,2]{1,0:T(1,128)S(1)}, f32[1,2]{1,0:T(1,128)}, u32[]{:S(2)}) copy-start(f32[1,2]{1,0:T(1,128)} %get-tuple-element.96) | copy-start | bytes 28
  361.1 24.3 %copy-start.21 = (f32[1,2]{1,0:T(1,128)S(1)}, f32[1,2]{1,0:T(1,128)}, u32[]{:S(2)}) copy-start(f32[1,2]{1,0:T(1,128)} %get-tuple-element.97) | copy-start | bytes 28
  382.0 3.0 copy-start.4
  382.0 4.2 copy-start.10
  395.3 1.2 copy-start
  677.7 5.3 copy-start.6
  677.7 11.6 %slice-start = ((s8[6291456]{0:T(1024)(128)(4,1)}), s8[4194304]{0:T(1024)(128)(4,1)S(1)}, s32[]{:S(2)}) async-start(s8[6291456]{0:T(1024)(128)(4,1)} %bitcast.61), calls=%async_computation.4 | async-start | bytes 8388608
  683.0 3.3 copy-start.2
  683.0 3.3 copy-start.11
  683.0 6.3 slice-start.1
  686.3 1.9 copy-start.13
  689.3 2.4 copy-start.9
  693.6 4.6 copy-start.5
  693.6 4.6 copy-start.8
  698.2 5.7 copy-start.1
Sparse Core Ops, SparseCore 0:
  56.1 60.9 all-gather.1
  205.5 189.2 all-reduce.5
  398.3 92.6 reduce-scatter.1
